TPU v7x, 32 devices: a whole 2x2x4 slice. The times are simulated.
32 devices in a mesh: rep: 4 (over z), shard: 8 (over y, x, core).
Axes of the slice: x: 2, y: 2, z: 4, core: 2. Of those that a mesh axis runs over, the one named last changes fastest.
Arguments:
- block_input: bfloat16 [32, 1024, 1024], P(('rep', 'shard')), may hold values from -6 to 6
- document_numbers: int32 [32, 1024], P(('rep', 'shard')), may hold values from 0 to 3, as said below
- attn_gain: bfloat16 [1024], P('shard'), may hold values from 0.099609375 to 1.8984375
- w_query: bfloat16 [1024, 1024], P('shard'), may hold values from -0.1875 to 0.1875
- key_weight: bfloat16 [1024, 512], P('shard'), may hold values from -0.1875 to 0.1875
- value_weight: bfloat16 [1024, 512], P('shard'), may hold values from -0.1875 to 0.1875
- query_gain: bfloat16 [64], P('shard'), may hold values from 0.796875 to 1.796875
- key_gain: bfloat16 [64], P('shard'), may hold values from 0.796875 to 1.796875
- w_output: bfloat16 [1024, 1024], P('shard'), may hold values from -0.75 to 0.75
- ffn_gain: bfloat16 [1024], P('shard'), may hold values from 0.099609375 to 1.8984375
- w_gate: bfloat16 [1024, 4608], P('shard'), may hold values from -0.1875 to 0.1875
- w_up: bfloat16 [1024, 4608], P('shard'), may hold values from -0.1875 to 0.1875
- w_down: bfloat16 [4608, 1024], P('shard'), may hold values from -0.09375 to 0.09375
- cotangent: bfloat16 [32, 1024, 1024], P(('rep', 'shard')), may hold values from -6 to 6
Outputs:
- block_output: bfloat16 [32, 1024, 1024], P(('rep', 'shard'))
- input_grad: float32 [32, 1024, 1024], P(('rep', 'shard'))
- grad_attn_gain: float32 [1024], P('shard')
- grad_w_query: float32 [1024, 1024], P('shard')
- grad_w_key: float32 [1024, 512], P('shard')
- grad_w_value: float32 [1024, 512], P('shard')
- grad_query_gain: float32 [64], P('shard')
- grad_key_gain: float32 [64], P('shard')
- grad_w_output: float32 [1024, 1024], P('shard')
- grad_ffn_gain: float32 [1024], P('shard')
- grad_w_gate: float32 [1024, 4608], P('shard')
- grad_w_up: float32 [1024, 4608], P('shard')
- grad_w_down: float32 [4608, 1024], P('shard')
Inputs may be any that keep to these rules, and one draw needn't show every extreme that they name: `document_numbers`: within each sequence the ids start at 0 on its first token, never fall, and reach 3 on its last token; a document is a run of equal ids, and an id may skip values.
All inputs are finite; a program needn't handle non-finite values.
Results may differ from a plain program's by a relative error of at most 0.02.
Values may be sent and summed in bfloat16 or wider, within the bound.
No kernel may reach another device: no remote copies, remote signals or barrier semaphores. Data moves between devices by JAX's collectives and lax.ppermute only.
A program may use at most 256 MiB of HBM per device.

v0:
```python
import jax
import jax.numpy as jnp
from jax import lax
from jax.sharding import PartitionSpec as P

QUERY_HEADS = 16
KEY_VALUE_HEADS = 8
HEAD_SIZE = 64
FF = 4608


EPS = 1e-05
rope_base = 1000000.0


def einsum_result(form, left, right):
    return jnp.einsum(form, left, right, preferred_element_type=jnp.float32)


def unit_rows(value_rows):
    inverse = lax.rsqrt(jnp.mean(value_rows * value_rows, axis=-1, keepdims=True) + EPS)
    return (value_rows * inverse, inverse)


def unit_back(grad_out, unit_part, inverse, gain):
    scaled = grad_out * gain
    return inverse * (scaled - unit_part * jnp.mean(scaled * unit_part, axis=-1, keepdims=True))


def rope_tables(document_numbers):
    sequence_count, token_length = document_numbers.shape
    indices = jnp.arange(token_length, dtype=jnp.int32)
    starts = jnp.concatenate(
        [
            jnp.ones((sequence_count, 1), dtype=bool),
            document_numbers[:, 1:] != document_numbers[:, :-1],
        ],
        axis=1,
    )
    begins = lax.cummax(
        jnp.where(starts, indices[None, :], jnp.zeros_like(document_numbers)), axis=1
    )
    offsets = (
        (indices[None, :] - begins).astype(jnp.float32).reshape(sequence_count * token_length, 1, 1)
    )
    frequency = rope_base ** (-jnp.arange(0, HEAD_SIZE, 2).astype(jnp.float32) / HEAD_SIZE)
    angles = offsets * frequency
    angles = jnp.concatenate([angles, angles], axis=-1)
    return (jnp.cos(angles), jnp.sin(angles))


def rotate(value_rows, cosine, sine):
    half_dim = value_rows.shape[-1] // 2
    turned = jnp.concatenate([-value_rows[..., half_dim:], value_rows[..., :half_dim]], axis=-1)
    return value_rows * cosine + turned * sine


def rotate_back(grads, cosine, sine):
    half_dim = grads.shape[-1] // 2
    moved = grads * sine
    return grads * cosine + jnp.concatenate(
        [moved[..., half_dim:], -moved[..., :half_dim]], axis=-1
    )


def split_heads(value_rows, sequence_count, token_length):
    reshaped_array = value_rows.reshape(
        sequence_count, token_length, KEY_VALUE_HEADS, -1, HEAD_SIZE
    )
    return reshaped_array.transpose(0, 2, 1, 3, 4).reshape(
        sequence_count * KEY_VALUE_HEADS, token_length, -1, HEAD_SIZE
    )


def join_heads(value_rows, sequence_count, token_length):
    reshaped_array = value_rows.reshape(
        sequence_count, KEY_VALUE_HEADS, token_length, -1, HEAD_SIZE
    )
    return reshaped_array.transpose(0, 2, 1, 3, 4).reshape(sequence_count * token_length, -1)


def masked_scores(query_rows, key_rows, seg_row):
    scaling = HEAD_SIZE ** (-0.5)
    scores = einsum_result("qgd,pd->gqp", query_rows, key_rows) * scaling
    indices = jnp.arange(seg_row.shape[0])
    allowed = (indices[:, None] >= indices[None, :]) & (seg_row[:, None] == seg_row[None, :])
    return jnp.where(allowed[None], scores, -1e30)


def attend_item(pieces):
    query_rows, key_rows, value_rows, seg_row = pieces
    scores = masked_scores(query_rows, key_rows, seg_row)
    highest = jnp.max(scores, axis=-1, keepdims=True)
    weights = jnp.exp(scores - highest)
    totals = jnp.sum(weights, axis=-1, keepdims=True)
    probabilities = (weights / totals).astype(jnp.bfloat16)
    attended = einsum_result("gqp,pd->qgd", probabilities, value_rows)
    return (attended.astype(jnp.bfloat16), (highest + jnp.log(totals))[..., 0])


def attend_back(pieces):
    query_rows, key_rows, value_rows, seg_row, log_total, back_attended = pieces
    scaling = HEAD_SIZE ** (-0.5)
    probabilities = jnp.exp(masked_scores(query_rows, key_rows, seg_row) - log_total[..., None])
    back_probs = einsum_result("qgd,pd->gqp", back_attended, value_rows)
    centre = jnp.sum(probabilities * back_probs, axis=-1, keepdims=True)
    back_scores = (probabilities * (back_probs - centre)).astype(jnp.bfloat16)
    back_queries = einsum_result("gqp,pd->qgd", back_scores, key_rows) * scaling
    back_keys = einsum_result("gqp,qgd->pd", back_scores, query_rows) * scaling
    back_values = einsum_result("gqp,qgd->pd", probabilities.astype(jnp.bfloat16), back_attended)
    return (back_queries, back_keys, back_values.astype(jnp.bfloat16))


def on_device(
    block_input,
    document_numbers,
    attn_gain,
    w_query,
    key_weight,
    value_weight,
    query_gain,
    key_gain,
    w_output,
    ffn_gain,
    w_gate,
    w_up,
    w_down,
    cotangent,
):
    sequence_count, token_length, features = block_input.shape
    local_rows = sequence_count * token_length
    inputs = block_input.reshape(local_rows, features).astype(jnp.float32)
    collected_rows = (
        lax.all_gather(attn_gain, "shard", axis=0, tiled=True),
        lax.all_gather(query_gain, "shard", axis=0, tiled=True),
        lax.all_gather(key_gain, "shard", axis=0, tiled=True),
        lax.all_gather(ffn_gain, "shard", axis=0, tiled=True),
        lax.all_gather(w_query, "shard", axis=0, tiled=True),
        lax.all_gather(key_weight, "shard", axis=0, tiled=True),
        lax.all_gather(value_weight, "shard", axis=0, tiled=True),
        lax.all_gather(w_output, "shard", axis=0, tiled=True),
    )
    gain_attn, gain_query, gain_key, gain_ffn = [
        member.astype(jnp.float32) for member in collected_rows[:4]
    ]
    unit_one, inverse_one = unit_rows(inputs)
    first_normed = (unit_one * gain_attn).astype(jnp.bfloat16)
    query_raw = einsum_result("vp,pl->vl", first_normed, collected_rows[4]).reshape(
        local_rows, QUERY_HEADS, HEAD_SIZE
    )
    key_unrotated = einsum_result("vp,pl->vl", first_normed, collected_rows[5]).reshape(
        local_rows, KEY_VALUE_HEADS, HEAD_SIZE
    )
    value_rows = (
        einsum_result("vp,pl->vl", first_normed, collected_rows[6])
        .astype(jnp.bfloat16)
        .reshape(local_rows, KEY_VALUE_HEADS, HEAD_SIZE)
    )
    cosine, sine = rope_tables(document_numbers)
    query_unit, query_inverse = unit_rows(query_raw)
    key_unit, key_inverse = unit_rows(key_unrotated)
    query_rows = rotate(query_unit * gain_query, cosine, sine).astype(jnp.bfloat16)
    key_rows = rotate(key_unit * gain_key, cosine, sine).astype(jnp.bfloat16)
    query_items = split_heads(query_rows, sequence_count, token_length)
    key_items = split_heads(key_rows, sequence_count, token_length)[:, :, 0, :]
    value_items = split_heads(value_rows, sequence_count, token_length)[:, :, 0, :]
    segment_items = jnp.repeat(document_numbers, KEY_VALUE_HEADS, axis=0)
    attended_items, log_totals = lax.map(
        attend_item, (query_items, key_items, value_items, segment_items)
    )
    attended = join_heads(attended_items, sequence_count, token_length)
    first_sum = inputs + einsum_result("nh,hd->nd", attended, collected_rows[7])
    unit_two, inverse_two = unit_rows(first_sum)
    normed_two = (unit_two * gain_ffn).astype(jnp.bfloat16)
    columns = normed_two
    gate_value = einsum_result(
        "nc,cf->nf", columns, lax.all_gather(w_gate, "shard", axis=0, tiled=True)
    )
    up_value = einsum_result(
        "nc,cf->nf", columns, lax.all_gather(w_up, "shard", axis=0, tiled=True)
    )
    sigmoid_gate = jax.nn.sigmoid(gate_value)
    swish_gate = gate_value * sigmoid_gate
    hidden = (swish_gate * up_value).astype(jnp.bfloat16)
    columns = hidden
    ffn_out = einsum_result(
        "nf,fd->nd", columns, lax.all_gather(w_down, "shard", axis=0, tiled=True)
    )
    block_output = (
        (first_sum + ffn_out).astype(jnp.bfloat16).reshape(sequence_count, token_length, features)
    )
    back_ffn = cotangent.reshape(local_rows, features)
    back_hidden = einsum_result(
        "nd,fd->nf", back_ffn, lax.all_gather(w_down, "shard", axis=0, tiled=True)
    )
    back_up = (back_hidden * swish_gate).astype(jnp.bfloat16)
    back_gate = (
        back_hidden * up_value * sigmoid_gate * (1.0 + gate_value * (1.0 - sigmoid_gate))
    ).astype(jnp.bfloat16)
    weight_rows = lax.all_gather(jnp.stack((w_gate, w_up), axis=1), "shard", axis=0, tiled=True)
    back_two = einsum_result("nf,cf->nc", back_gate, weight_rows[:, 0]) + einsum_result(
        "nf,cf->nc", back_up, weight_rows[:, 1]
    )
    grad_gain_ffn = jnp.sum(back_two * unit_two, axis=0)
    back_first = back_ffn.astype(jnp.float32) + unit_back(back_two, unit_two, inverse_two, gain_ffn)
    back_attn = back_first.astype(jnp.bfloat16)
    weights_again = (
        lax.all_gather(w_query, "shard", axis=0, tiled=True),
        lax.all_gather(key_weight, "shard", axis=0, tiled=True),
        lax.all_gather(value_weight, "shard", axis=0, tiled=True),
        lax.all_gather(w_output, "shard", axis=0, tiled=True),
    )
    back_attended = einsum_result("nd,hd->nh", back_attn, weights_again[3]).astype(jnp.bfloat16)
    back_items = split_heads(
        back_attended.reshape(local_rows, QUERY_HEADS, HEAD_SIZE), sequence_count, token_length
    )
    back_query_items, back_key_items, back_value_items = lax.map(
        attend_back, (query_items, key_items, value_items, segment_items, log_totals, back_items)
    )
    back_queries = join_heads(back_query_items, sequence_count, token_length).reshape(
        local_rows, QUERY_HEADS, HEAD_SIZE
    )
    back_keys = join_heads(back_key_items[:, :, None, :], sequence_count, token_length).reshape(
        local_rows, KEY_VALUE_HEADS, HEAD_SIZE
    )
    back_values = join_heads(back_value_items[:, :, None, :], sequence_count, token_length)
    query_turned = rotate_back(back_queries, cosine, sine)
    key_turned = rotate_back(back_keys, cosine, sine)
    grad_gain_query = jnp.sum(query_turned * query_unit, axis=(0, 1))
    grad_gain_key = jnp.sum(key_turned * key_unit, axis=(0, 1))
    back_query_raw = (
        unit_back(query_turned, query_unit, query_inverse, gain_query)
        .astype(jnp.bfloat16)
        .reshape(local_rows, QUERY_HEADS * HEAD_SIZE)
    )
    back_key_raw = (
        unit_back(key_turned, key_unit, key_inverse, gain_key)
        .astype(jnp.bfloat16)
        .reshape(local_rows, KEY_VALUE_HEADS * HEAD_SIZE)
    )
    back_one = (
        einsum_result("nh,ch->nc", back_query_raw, weights_again[0])
        + einsum_result("nh,ch->nc", back_key_raw, weights_again[1])
        + einsum_result("nh,ch->nc", back_values, weights_again[2])
    )
    grad_gain_attn = jnp.sum(back_one * unit_one, axis=0)
    input_grad = back_first + unit_back(back_one, unit_one, inverse_one, gain_attn)
    gain_sums = (
        lax.psum_scatter(grad_gain_attn, "shard", scatter_dimension=0, tiled=True),
        lax.psum_scatter(grad_gain_query, "shard", scatter_dimension=0, tiled=True),
        lax.psum_scatter(grad_gain_key, "shard", scatter_dimension=0, tiled=True),
        lax.psum_scatter(grad_gain_ffn, "shard", scatter_dimension=0, tiled=True),
    )
    grad_down = lax.psum_scatter(
        einsum_result("nf,nd->fd", hidden, back_ffn).astype(jnp.bfloat16),
        "shard",
        scatter_dimension=0,
        tiled=True,
    ).astype(jnp.float32)
    grad_pair = lax.psum_scatter(
        jnp.concatenate(
            [
                einsum_result("nc,nf->cf", normed_two, back_gate),
                einsum_result("nc,nf->cf", normed_two, back_up),
            ],
            axis=1,
        ).astype(jnp.bfloat16),
        "shard",
        scatter_dimension=0,
        tiled=True,
    ).astype(jnp.float32)
    grad_output = lax.psum_scatter(
        einsum_result("nh,nd->hd", attended, back_attn).astype(jnp.bfloat16),
        "shard",
        scatter_dimension=0,
        tiled=True,
    ).astype(jnp.float32)
    grad_inputs = lax.psum_scatter(
        jnp.concatenate(
            [
                einsum_result("nc,nh->ch", first_normed, back_query_raw),
                einsum_result("nc,nh->ch", first_normed, back_key_raw),
                einsum_result("nc,nh->ch", first_normed, back_values),
            ],
            axis=1,
        ).astype(jnp.bfloat16),
        "shard",
        scatter_dimension=0,
        tiled=True,
    ).astype(jnp.float32)
    query_cols = QUERY_HEADS * HEAD_SIZE
    key_columns = KEY_VALUE_HEADS * HEAD_SIZE
    shards = (
        gain_sums[0],
        grad_inputs[:, :query_cols],
        grad_inputs[:, query_cols : query_cols + key_columns],
        grad_inputs[:, query_cols + key_columns :],
        gain_sums[1],
        gain_sums[2],
        grad_output,
        gain_sums[3],
        grad_pair[:, :FF],
        grad_pair[:, FF:],
        grad_down,
    )
    summed = (
        lax.psum(shards[0].astype(jnp.bfloat16), "rep").astype(jnp.float32),
        lax.psum(shards[1].astype(jnp.bfloat16), "rep").astype(jnp.float32),
        lax.psum(shards[2].astype(jnp.bfloat16), "rep").astype(jnp.float32),
        lax.psum(shards[3].astype(jnp.bfloat16), "rep").astype(jnp.float32),
        lax.psum(shards[4].astype(jnp.bfloat16), "rep").astype(jnp.float32),
        lax.psum(shards[5].astype(jnp.bfloat16), "rep").astype(jnp.float32),
        lax.psum(shards[6].astype(jnp.bfloat16), "rep").astype(jnp.float32),
        lax.psum(shards[7].astype(jnp.bfloat16), "rep").astype(jnp.float32),
        lax.psum(shards[8].astype(jnp.bfloat16), "rep").astype(jnp.float32),
        lax.psum(shards[9].astype(jnp.bfloat16), "rep").astype(jnp.float32),
        lax.psum(shards[10].astype(jnp.bfloat16), "rep").astype(jnp.float32),
    )
    return (block_output, input_grad.reshape(sequence_count, token_length, features)) + tuple(
        summed
    )


def solution(mesh):
    in_specs = (
        P(("rep", "shard"), None, None),
        P(("rep", "shard"), None),
        P("shard"),
        P("shard", None),
        P("shard", None),
        P("shard", None),
        P("shard"),
        P("shard"),
        P("shard", None),
        P("shard"),
        P("shard", None),
        P("shard", None),
        P("shard", None),
        P(("rep", "shard"), None, None),
    )
    out_specs = (
        P(("rep", "shard"), None, None),
        P(("rep", "shard"), None, None),
        P("shard"),
        P("shard", None),
        P("shard", None),
        P("shard", None),
        P("shard"),
        P("shard"),
        P("shard", None),
        P("shard"),
        P("shard", None),
        P("shard", None),
        P("shard", None),
    )
    return jax.shard_map(
        on_device, mesh=mesh, in_specs=in_specs, out_specs=out_specs, check_vma=False
    )
```

profile of v0, /device:TPU:0, one launch (start us, length us, event | category | flops | bytes accessed | tf_op | source)
XLA Modules:
  0.0 1109.8 jit_solution(7073934975808297929)
XLA Ops:
  17.2 10.2 all-gather
  29.1 13.2 %all-reduce.7 = (bf16[64]{0:T(256)(128)(2,1)S(1)}, bf16[64]{0:T(256)(128)(2,1)S(1)}) all-reduce(bf16[64]{0:T(256)(128)(2,1)S(1)} %dynamic-update-slice, bf16[64]{0:T(256)(128)(2,1)S(1)} %dynamic-update-slice.1), channel_id=1, replica_groups=mesh['rep'=4,'shard'=8] {'shard'}, use_global_device_ids=true, to_apply=%add | all-reduce | flops 128 | bytes 512
  44.4 9.2 all-gather.1
  53.6 3.9 copy.79
  69.0 22.5 %all-gather.15.cloned.1.call-done = bf16[1024,1024]{1,0:T(8,128)(2,1)} async-done(((bf16[128,1024]{1,0:T(8,128)(2,1)}), bf16[1024,1024]{1,0:T(8,128)(2,1)}) %all-gather.15.cloned.1.call-update) | async-done | bytes 2097168 | tf_op jit(solution)/shard_map/all_gather | solution.py:138
  95.4 4.1 multiply_reduce_fusion.5
  104.2 84.0 %while.26 = (s32[]{:T(128)}, bf16[8,1024,2,64]{1,3,2,0:T(8,128)(2,1)}, f32[8,2,1024]{2,1,0:T(2,128)}, bf16[8,1024,64]{1,2,0:T(8,128)(2,1)}, s32[8,1024]{1,0:T(8,...) while((s32[]{:T(128)}, bf16[8,1024,2,64]{1,3,2,0:T(8,128)(2,1)}, ...), condition=%wide.region_8.9_spmd, body=%wide.region_5.8_spmd.sunk | while | flops 565311488 | bytes 30227032 | solution.py:168
  110.5 4.4 fusion.199
  121.0 4.4 fusion.199
  131.5 4.4 fusion.199
  142.0 4.4 fusion.199
  152.4 4.4 fusion.199
  163.0 4.4 fusion.199
  173.5 4.4 fusion.199
  183.9 4.4 fusion.199
  188.3 5.1 multiply_reduce_fusion.4
  197.3 16.4 %fusion.97 = f32[1024,4608]{1,0:T(8,128)} fusion(bf16[4608,1024]{1,0:T(8,128)(2,1)} %all-gather.23.cloned.1.call-done, bf16[1,1024,1024]{2,1,0:T(8,128)(2,1)S(1)} %copy-done.18), kind=kOutput, calls=%fused_computation.135 | convolution fusion | flops 9663676416 | bytes 30408704 | tf_op jit(solution)/shard_map/nd,fd->nf/dot_general | solution.py:17
  213.7 28.7 %all-gather.21.cloned.1.call-done = bf16[1024,4608]{1,0:T(8,128)(2,1)} async-done(((bf16[128,4608]{1,0:T(8,128)(2,1)}), bf16[1024,4608]{1,0:T(8,128)(2,1)}) %all-gather.21.cloned.1.call-update) | async-done | bytes 9437200 | tf_op jit(solution)/shard_map/all_gather | solution.py:180
  242.3 17.1 %fusion.140 = f32[1024,4608]{1,0:T(8,128)} fusion(bf16[1024,1024]{0,1:T(8,128)(2,1)} %multiply_convert_fusion.4, bf16[1024,4608]{1,0:T(8,128)(2,1)} %all-gather.21.cloned.1.call-done), kind=kOutput, calls=%fused_computation.197 | convolution fusion | flops 9663676416 | bytes 30408704 | tf_op jit(solution)/shard_map/nc,cf->nf/dot_general | solution.py:17
  259.5 43.6 %all-gather.19.cloned.1.call-done = bf16[1024,4608]{1,0:T(8,128)(2,1)} async-done(((bf16[128,4608]{1,0:T(8,128)(2,1)}), bf16[1024,4608]{1,0:T(8,128)(2,1)}) %all-gather.19.cloned.1.call-update) | async-done | bytes 9437200 | tf_op jit(solution)/shard_map/all_gather | solution.py:177
  303.1 31.7 %multiply_convert_fusion.1 = (bf16[1024,4608]{1,0:T(8,128)(2,1)}, bf16[1024,4608]{1,0:T(8,128)(2,1)}, bf16[1024,4608]{1,0:T(8,128)(2,1)}) fusion(f32[1024,4608]{1,0:T(8,128)} %fusion.97, f32[1024,4608]{1,0:T(8,128)} %fusion.140, bf16[1024,1024]{0,1:T(8,128)(2,1)S(1)} %copy-done.20, bf16[1024,4608]{1,0:T(8,128)(2,1)} %all-gather.19.cloned.1.call-done), kind=kOutput, calls=%fused_computation.75 | convolution fusion | flops 9734455296 | bytes 77594624 | tf_op jit(solution)/shard_map/nc,cf->nf/dot_general | solution.py:17
  334.8 69.6 %all-gather.25.cloned.1.call-done = bf16[1024,2,4608]{2,0,1:T(8,128)(2,1)} async-done(((bf16[128,2,4608]{2,0,1:T(8,128)(2,1)}), bf16[1024,2,4608]{2,0,1:T(8,128)(2,1)}) %all-gather.25.cloned.1.call-update) | async-done | bytes 18874384 | tf_op jit(solution)/shard_map/all_gather | solution.py:200
  404.3 16.6 %fusion.69 = f32[1024,1024]{0,1:T(8,128)} fusion(bf16[1024,4608]{1,0:T(8,128)(2,1)} %get-tuple-element.215, bf16[1024,2,4608]{2,0,1:T(8,128)(2,1)} %all-gather.25.cloned.1.call-done), kind=kOutput, calls=%fused_computation.83 | convolution fusion | flops 9663676416 | bytes 23068672 | tf_op jit(solution)/shard_map/nf,cf->nc/dot_general | solution.py:17
  421.0 17.1 %multiply_reduce_fusion = (f32[1024]{0:T(1024)}, f32[1024]{0:T(1024)S(1)}, f32[1024,1024]{0,1:T(8,128)S(1)}) fusion(f32[1024,1024]{0,1:T(8,128)S(1)} %copy-done.7, f32[1024]{0:T(1024)S(1)} %add_rsqrt_fusion.2, f32[1024]{0:T(1024)S(1)} %bitcast.405, f32[1024,1024]{0,1:T(8,128)} %fusion.69, bf16[1024,4608]{1,0:T(8,128)(2,1)} %get-tuple-element.214, ...), kind=kOutput, calls=%fused_computation.112 | convolution fusion | flops 9671014400 | bytes 31473664 | tf_op jit(solution)/shard_map/nf,cf->nc/dot_general | solution.py:17
  443.3 150.0 %while.27 = (s32[]{:T(128)}, f32[8,1024,2,64]{1,3,2,0:T(8,128)}, f32[8,1024,64]{1,2,0:T(8,128)S(1)}, bf16[8,1024,64]{1,2,0:T(8,128)(2,1)S(1)}, bf16[8,1024,64]{1...) while((s32[]{:T(128)}, f32[8,1024,2,64]{1,3,2,0:T(8,128)}, ...), condition=%wide.region_13.14_spmd, body=%wide.region_11.13_spmd.sunk | while | flops 1377040384 | bytes 69543024 | solution.py:217
  447.1 4.0 fusion.210
  465.8 4.0 fusion.210
  484.5 4.0 fusion.210
  503.2 4.0 fusion.210
  521.9 4.0 fusion.210
  540.6 4.0 fusion.210
  559.3 4.0 fusion.210
  578.0 4.0 fusion.210
  613.7 6.5 copy.104
  620.2 13.4 %convolution_convert_fusion = bf16[1024,4608]{1,0:T(8,128)(2,1)S(1)} fusion(bf16[1024,1024]{0,1:T(8,128)(2,1)} %multiply_convert_fusion.4, bf16[1024,4608]{1,0:T(8,128)(2,1)} %get-tuple-element.215), kind=kOutput, calls=%fused_computation.79 | convolution fusion | flops 9668395008 | bytes 20971520 | tf_op jit(solution)/shard_map/nc,nf->cf/dot_general | solution.py:17
  633.7 13.3 %convolution_convert_fusion.1 = bf16[1024,4608]{1,0:T(8,128)(2,1)S(1)} fusion(bf16[1024,1024]{0,1:T(8,128)(2,1)} %multiply_convert_fusion.4, bf16[1024,4608]{1,0:T(8,128)(2,1)} %get-tuple-element.214), kind=kOutput, calls=%fused_computation.80 | convolution fusion | flops 9668395008 | bytes 20971520 | tf_op jit(solution)/shard_map/nc,nf->cf/dot_general | solution.py:17
  646.9 11.0 pad_maximum_fusion
  658.0 17.0 %convolution_convert_fusion.2 = bf16[4608,1024]{1,0:T(8,128)(2,1)} fusion(bf16[1024,4608]{1,0:T(8,128)(2,1)} %get-tuple-element.216, bf16[1,1024,1024]{2,1,0:T(8,128)(2,1)} %param.31), kind=kOutput, calls=%fused_computation.81 | convolution fusion | flops 9668395008 | bytes 20971520 | tf_op jit(solution)/shard_map/nf,nd->fd/dot_general | solution.py:17
  675.1 6.5 convolution_convert_fusion.4
  687.5 114.2 %reduce-scatter.9.cloned.1.call-done = bf16[128,9216]{1,0:T(8,128)(2,1)} async-done(((bf16[1024,9216]{1,0:T(8,128)(2,1)}), bf16[128,9216]{1,0:T(8,128)(2,1)}) %reduce-scatter.9.cloned.1.call-update) | async-done | bytes 2359312 | tf_op jit(solution)/shard_map/reduce_scatter | solution.py:260
  805.0 77.2 %reduce-scatter.11.cloned.1.call-done = bf16[576,1024]{1,0:T(8,128)(2,1)} async-done(((bf16[4608,1024]{1,0:T(8,128)(2,1)}), bf16[576,1024]{1,0:T(8,128)(2,1)}) %reduce-scatter.11.cloned.1.call-update) | async-done | bytes 1179664 | tf_op jit(solution)/shard_map/reduce_scatter | solution.py:254
  882.2 45.3 %reduce-scatter.7.cloned.1.call-done = bf16[128,1024]{1,0:T(8,128)(2,1)} async-done(((bf16[1024,1024]{1,0:T(8,128)(2,1)}), bf16[128,1024]{1,0:T(8,128)(2,1)}) %reduce-scatter.7.cloned.1.call-update) | async-done | bytes 262160 | tf_op jit(solution)/shard_map/reduce_scatter | solution.py:272
  927.5 17.0 %fusion.91 = bf16[1,1024,1024]{1,2,0:T(8,128)(2,1)} fusion(f32[1024,1024]{0,1:T(8,128)} %copy-done.6, bf16[1024,4608]{1,0:T(8,128)(2,1)} %get-tuple-element.216, bf16[4608,1024]{1,0:T(8,128)(2,1)} %all-gather.23.cloned.1.call-done), kind=kOutput, calls=%fused_computation.126 | convolution fusion | flops 9665773568 | bytes 25165824 | tf_op jit(solution)/shard_map/nf,fd->nd/dot_general | solution.py:17
  957.4 24.7 %all-reduce.6 = (bf16[1024]{0:T(1024)(128)(2,1)S(1)}, bf16[64]{0:T(256)(128)(2,1)S(1)}, bf16[64]{0:T(256)(128)(2,1)S(1)}, bf16[1024]{0:T(1024)(128)(2,1)S(1)}) all-reduce(f32[1024]{0:T(1024)S(1)} %get-tuple-element.153, f32[64]{0:T(128)S(1)} %copy-done.47, f32[64]{0:T(128)S(1)} %copy-done.46, ...), channel_id=2, replica_groups=mesh['rep'=4,'shard'=8] {'shard'}, use_global_device_ids=true, to_apply=%region_18.19.clone | all-reduce | flops 2176 | bytes 13056
  982.3 12.4 %all-reduce.8 = (bf16[128]{0:T(256)(128)(2,1)S(1)}, bf16[8]{0:T(256)(128)(2,1)S(1)}, bf16[8]{0:T(256)(128)(2,1)S(1)}, bf16[128]{0:T(256)(128)(2,1)S(1)}) all-reduce(bf16[128]{0:T(256)(128)(2,1)S(1)} %dynamic-slice.17, bf16[8]{0:T(256)(128)(2,1)S(1)} %dynamic-slice.16, ...), channel_id=1, replica_groups=mesh['rep'=4,'shard'=8] {'rep'}, use_global_device_ids=true, to_apply=%region_19.20 | all-reduce | flops 272 | bytes 1088 | tf_op jit(solution)/shard_map/psum | solution.py:307
  996.8 6.4 fusion.83
  1003.3 5.4 copy.86
  1008.7 84.5 %all-reduce.12.cloned.1.call-done = (bf16[128,1024]{0,1:T(8,128)(2,1)}, bf16[128,512]{0,1:T(8,128)(2,1)}, bf16[128,512]{0,1:T(8,128)(2,1)}, bf16[128,1024]{1,0:T...) async-done(((bf16[128,1024]{0,1:T(8,128)(2,1)}, bf16[128,512]{0,1:T(8,128)(2,1)}, bf16[128,512]{0,1:T(8,128)(2,1)}, ...) | async-done | bytes 4325392 | tf_op jit(solution)/shard_map/psum | solution.py:308
  (331 shorter events, 261.2 us)
Async XLA Ops:
  7.2 4.8 copy-start.16
  7.2 4.8 copy-start.17
  7.2 50.4 %all-gather.13.cloned.1.call-start = ((), (), s32[]{:S(2)}) async-start(), calls=%async_computation.5 | async-start | bytes 1179648 | tf_op jit(solution)/shard_map/all_gather | solution.py:139
  7.9 57.5 %all-gather.11.cloned.1.call-start = ((), (), s32[]{:S(2)}) async-start(), calls=%async_computation.4 | async-start | bytes 1179648 | tf_op jit(solution)/shard_map/all_gather | solution.py:140
  8.7 82.8 %all-gather.15.cloned.1.call-start = ((), (), s32[]{:S(2)}) async-start(), calls=%async_computation.6 | async-start | bytes 2359296 | tf_op jit(solution)/shard_map/all_gather | solution.py:138
  9.4 178.9 %all-gather.17.cloned.1.call-start = ((), (), s32[]{:S(2)}) async-start(), calls=%async_computation.7 | async-start | bytes 2359296 | tf_op jit(solution)/shard_map/all_gather | solution.py:141
  10.0 187.3 %all-gather.23.cloned.1.call-start = ((), (), s32[]{:S(2)}) async-start(), calls=%async_computation.10 | async-start | bytes 10616832 | tf_op jit(solution)/shard_map/all_gather | solution.py:187
  10.6 231.8 %all-gather.21.cloned.1.call-start = ((), (), s32[]{:S(2)}) async-start(), calls=%async_computation.9 | async-start | bytes 10616832 | tf_op jit(solution)/shard_map/all_gather | solution.py:180
  11.2 291.9 %all-gather.19.cloned.1.call-start = ((), (), s32[]{:S(2)}) async-start(), calls=%async_computation.8 | async-start | bytes 10616832 | tf_op jit(solution)/shard_map/all_gather | solution.py:177
  11.9 392.4 %all-gather.25.cloned.1.call-start = ((), (), s32[]{:S(2)}) async-start(), calls=%async_computation.11 | async-start | bytes 21233664 | tf_op jit(solution)/shard_map/all_gather | solution.py:200
  13.6 3.6 copy-start.49
  13.6 13.8 %copy-start.48 = (u32[32]{0:T(128)S(1)}, u32[32]{0:T(128)}, u32[]{:S(2)}) copy-start(u32[32]{0:T(128)} %constant.98) | copy-start | bytes 388
  13.6 15.0 %copy-start.52 = (bf16[8]{0:T(256)(128)(2,1)S(1)}, bf16[8]{0:T(256)(128)(2,1)}, u32[]{:S(2)}) copy-start(bf16[8]{0:T(256)(128)(2,1)} %param.25) | copy-start | bytes 52
  13.6 15.3 %copy-start.53 = (bf16[8]{0:T(256)(128)(2,1)S(1)}, bf16[8]{0:T(256)(128)(2,1)}, u32[]{:S(2)}) copy-start(bf16[8]{0:T(256)(128)(2,1)} %param.24) | copy-start | bytes 52
  13.6 28.8 %copy-start.36 = (s32[1,1024]{1,0:T(1,128)S(1)}, s32[1,1024]{1,0:T(1,128)}, u32[]{:S(2)}) copy-start(s32[1,1024]{1,0:T(1,128)} %param.19) | copy-start | bytes 12292
  13.6 30.8 %copy-start.50 = (bf16[128]{0:T(256)(128)(2,1)S(1)}, bf16[128]{0:T(256)(128)(2,1)}, u32[]{:S(2)}) copy-start(bf16[128]{0:T(256)(128)(2,1)} %param.27) | copy-start | bytes 772
  13.6 669.3 %reduce-scatter.13.cloned.1.call-start = ((), (), s32[]{:S(2)}) async-start(), calls=%async_computation.15 | async-start | bytes 4718592
  16.6 171.7 %copy-start.4 = (bf16[1,1024,1024]{1,2,0:T(8,128)(2,1)}, bf16[1,1024,1024]{1,2,0:T(8,128)(2,1)S(1)}, u32[]{:S(2)}) copy-start(bf16[1,1024,1024]{1,2,0:T(8,128)(2,1)S(1)} %copy.73) | copy-start | bytes 6291460
  17.1 78.3 %copy-start.37 = (f32[1024]{0:T(1024)}, f32[1024]{0:T(1024)S(1)}, u32[]{:S(2)}) copy-start(f32[1024]{0:T(1024)S(1)} %add_rsqrt_fusion.3) | copy-start | bytes 12292
  27.4 68.0 %copy-start.39 = (f32[8,1,128]{2,1,0:T(1,128)}, f32[8,1,128]{2,1,0:T(1,128)S(1)}, u32[]{:S(2)}) copy-start(f32[8,1,128]{2,1,0:T(1,128)S(1)} %convert_element_type.217) | copy-start | bytes 12292
  42.4 58.4 %copy-start.41 = (f32[64]{0:T(128)}, f32[64]{0:T(128)S(1)}, u32[]{:S(2)}) copy-start(f32[64]{0:T(128)S(1)} %convert_element_type.186) | copy-start | bytes 772
  44.4 56.4 %copy-start.12 = (f32[1024,64]{0,1:T(8,128)}, f32[1024,64]{0,1:T(8,128)S(1)}, u32[]{:S(2)}) copy-start(f32[1024,64]{0,1:T(8,128)S(1)} %get-tuple-element.229) | copy-start | bytes 786436
  44.4 56.4 %copy-start.14 = (f32[1024,64]{0,1:T(8,128)}, f32[1024,64]{0,1:T(8,128)S(1)}, u32[]{:S(2)}) copy-start(f32[1024,64]{0,1:T(8,128)S(1)} %get-tuple-element.230) | copy-start | bytes 786436
  44.4 18.8 %copy-start.43 = (f32[64]{0:T(128)}, f32[64]{0:T(128)S(1)}, u32[]{:S(2)}) copy-start(f32[64]{0:T(128)S(1)} %convert_element_type.182) | copy-start | bytes 772
  193.4 3.9 copy-start.18
  213.7 89.4 %copy-start.20 = (bf16[1024,1024]{0,1:T(8,128)(2,1)S(1)}, bf16[1024,1024]{0,1:T(8,128)(2,1)}, u32[]{:S(2)}) copy-start(bf16[1024,1024]{0,1:T(8,128)(2,1)} %multiply_convert_fusion.4) | copy-start | bytes 6291460
  404.3 16.6 %copy-start.7 = (f32[1024,1024]{0,1:T(8,128)S(1)}, f32[1024,1024]{0,1:T(8,128)}, u32[]{:S(2)}) copy-start(f32[1024,1024]{0,1:T(8,128)} %copy-done.6) | copy-start | bytes 12582916
  421.0 17.1 %copy-start.11 = (bf16[1,1024,1024]{1,2,0:T(8,128)(2,1)S(1)}, bf16[1,1024,1024]{1,2,0:T(8,128)(2,1)}, u32[]{:S(2)}) copy-start(bf16[1,1024,1024]{1,2,0:T(8,128)(2,1)} %copy.79) | copy-start | bytes 6291460
  439.6 3.7 copy-start.9
  439.6 3.7 copy-start.10
  439.6 3.7 copy-start.28
  443.3 150.0 %copy-start.15 = (f32[1024,64]{0,1:T(8,128)S(1)}, f32[1024,64]{0,1:T(8,128)}, u32[]{:S(2)}) copy-start(f32[1024,64]{0,1:T(8,128)} %copy-done.14) | copy-start | bytes 786436
  607.4 2.5 copy-start.21
  620.2 181.6 %reduce-scatter.9.cloned.1.call-start = ((), (), s32[]{:S(2)}) async-start(), calls=%async_computation.13 | async-start | bytes 21233664 | tf_op jit(solution)/shard_map/reduce_scatter | solution.py:260
  657.9 224.2 %reduce-scatter.11.cloned.1.call-start = ((), (), s32[]{:S(2)}) async-start(), calls=%async_computation.14 | async-start | bytes 10616832 | tf_op jit(solution)/shard_map/reduce_scatter | solution.py:254
  675.0 252.5 %reduce-scatter.7.cloned.1.call-start = ((), (), s32[]{:S(2)}) async-start(), calls=%async_computation.12 | async-start | bytes 2359296 | tf_op jit(solution)/shard_map/reduce_scatter | solution.py:272
  681.6 411.6 %all-reduce.12.cloned.1.call-start = ((), (), s32[]{:S(2)}) async-start(), calls=%async_computation.16 | async-start | bytes 8650752 | tf_op jit(solution)/shard_map/psum | solution.py:308
  948.5 3.0 copy-start.19
  948.5 3.0 copy-start.22
  953.8 3.5 copy-start.45
  953.8 3.5 copy-start.46
  953.9 3.5 copy-start.47
  1093.2 3.1 copy-start.26
  1093.2 4.7 copy-start.25
  1096.3 3.4 copy-start.33
  1096.3 4.2 copy-start.32
  1096.3 5.1 copy-start.35
  1096.3 6.0 copy-start.34
  (19 other events, 34.8 us)
Sparse Core Ops, SparseCore 0:
  9.9 26.3 all-gather.12
  38.2 23.4 all-gather.10
  63.5 27.8 all-gather.14
  93.2 27.8 all-gather.16
  122.9 58.8 all-gather.22
  183.5 58.8 all-gather.20
  244.2 58.8 all-gather.18
  305.6 98.7 all-gather.24
  620.3 51.3 reduce-scatter.12
  675.6 126.0 reduce-scatter.8
  805.7 76.4 reduce-scatter.10
  886.3 41.2 reduce-scatter.6
  931.6 161.5 all-reduce.11
where the time goes:
time: 1120 us; the launch traced here: 1110 us
  waiting for transfers between devices  490 us (44%)
  matrix products  374 us (33%)
  other arithmetic  102 us (9%)
  blocking collectives  69.8 us (6%)
  local copies, waits for them, and re-layouts  55.1 us (5%)
  between operations  16.8 us (2%)
    dot_general x77, matrix products, einsum_result(): return jnp.einsum(form, left, right, preferred_element_type=jnp.float32)  374 us
    reduce_scatter x1, waiting for transfers between devices, on_device(): lax.psum_scatter(jnp.concatenate([einsum_result('nc,nf->cf', normed_two,...  114 us
    psum x1, waiting for transfers between devices, on_device(): lax.psum(shards[1].astype(jnp.bfloat16), 'rep').astype(jnp.float32)  84.5 us
    reduce_scatter x1, waiting for transfers between devices, on_device(): lax.psum_scatter(einsum_result('nf,nd->fd', hidden, back_ffn).astype(jnp....  77.2 us
    all_gather x1, waiting for transfers between devices, on_device(): lax.all_gather(jnp.stack((w_gate, w_up), axis=1), 'shard', axis=0, tiled=...  69.6 us
    reduce_scatter x1, waiting for transfers between devices, on_device(): lax.psum_scatter(einsum_result('nh,nd->hd', attended, back_attn).astype(j...  45.3 us
    all_gather x1, waiting for transfers between devices, on_device(): lax.all_gather(w_gate, 'shard', axis=0, tiled=True)  43.6 us
    unnamed x2, blocking collectives  37.9 us
  transfers between devices with their start and end apart: 13, of which 8 were waited for; matrix products, arithmetic and copies ran while one was open for 27% of the time, Pallas kernels for 0%

commit v1 on v0

v1 whole, which is shorter than its diff:
```python
import jax
import jax.numpy as jnp
from jax import lax
from jax.experimental import pallas as pl
from jax.experimental.pallas import tpu as pltpu
from jax.sharding import PartitionSpec as P

QUERY_HEADS = 16
KEY_VALUE_HEADS = 8
HEAD_SIZE = 64
FF = 4608
EPS = 1e-05
ROPE_BASE = 1000000.0
FAR = 32768.0
TILE = 256
VMEM_LIMIT = 56 * 1024 * 1024
NT = ((1,), (1,))
NN = ((1,), (0,))


def dot(left, right, dims=NN):
    return lax.dot_general(left, right, (dims, ((), ())), preferred_element_type=jnp.float32)


def einsum_result(form, left, right):
    return jnp.einsum(form, left, right, preferred_element_type=jnp.float32)


def unit_rows(rows):
    inverse = lax.rsqrt(jnp.mean(rows * rows, axis=-1, keepdims=True) + EPS)
    return rows * inverse, inverse


def unit_back(grad_out, unit_part, inverse, gain):
    scaled = grad_out * gain
    return inverse * (scaled - unit_part * jnp.mean(scaled * unit_part, axis=-1, keepdims=True))


def split3(value):
    high = value.astype(jnp.bfloat16).astype(jnp.float32)
    rest = value - high
    middle = rest.astype(jnp.bfloat16).astype(jnp.float32)
    return high, middle, rest - middle


def causal(query_axis):
    first = lax.broadcasted_iota(jnp.int32, (TILE, TILE), 0)
    second = lax.broadcasted_iota(jnp.int32, (TILE, TILE), 1)
    return (first >= second) if query_axis == 0 else (second >= first)


def attend_kernel(q_ref, k_ref, v_ref, o_ref, qb_ref):
    tiles = q_ref.shape[1] // TILE
    keep = causal(0)
    lane = lax.broadcasted_iota(jnp.int32, (TILE, 128), 1)
    for i in range(tiles):
        rows = slice(i * TILE, (i + 1) * TILE)
        halves = []
        for h in range(2):
            q = q_ref[h, rows, :]
            out = None
            for j in range(i + 1):
                cols = slice(j * TILE, (j + 1) * TILE)
                weights = jnp.exp(dot(q, k_ref[0, cols, :], NT))
                if j == i:
                    weights = jnp.where(keep, weights, 0.0)
                part = dot(weights.astype(jnp.bfloat16), v_ref[0, cols, :])
                out = part if out is None else out + part
            total = out[:, 64:65]
            halves.append(out / total)
            high, middle, low = split3(-jnp.log(total))
            extra = jnp.where(
                lane == 68, high, jnp.where(lane == 69, middle, jnp.where(lane == 70, low, 0.0))
            )
            qb_ref[h, rows, :] = (q.astype(jnp.float32) + extra).astype(jnp.bfloat16)
        both = jnp.where(lane < 64, halves[0], pltpu.roll(halves[1], 64, 1))
        o_ref[rows, :] = both.astype(jnp.bfloat16)


def attend(q_aug, k_aug, v_aug):
    heads, length, _ = q_aug.shape
    groups = k_aug.shape[0]
    return pl.pallas_call(
        attend_kernel,
        grid=(groups,),
        in_specs=[
            pl.BlockSpec((2, length, 128), lambda g: (g, 0, 0)),
            pl.BlockSpec((1, length, 128), lambda g: (g, 0, 0)),
            pl.BlockSpec((1, length, 128), lambda g: (g, 0, 0)),
        ],
        out_specs=[
            pl.BlockSpec((length, 128), lambda g: (0, g)),
            pl.BlockSpec((2, length, 128), lambda g: (g, 0, 0)),
        ],
        out_shape=[
            jax.ShapeDtypeStruct((length, groups * 128), jnp.bfloat16),
            jax.ShapeDtypeStruct((heads, length, 128), jnp.bfloat16),
        ],
        compiler_params=pltpu.CompilerParams(vmem_limit_bytes=VMEM_LIMIT),
        cost_estimate=pl.CostEstimate(
            flops=20 * 10**9, bytes_accessed=16 * 2**20, transcendentals=10 * 2**20
        ),
        name="attend",
    )(q_aug, k_aug, v_aug)


def attend_back_kernel(q_ref, k_ref, v_ref, o_ref, do_ref, dq_ref, dkv_ref, do_aug, k_t, dq_t):
    length = q_ref.shape[1]
    tiles = length // TILE
    keep = causal(1)
    lane = lax.broadcasted_iota(jnp.int32, (length, 128), 1)
    back = do_ref[...].astype(jnp.float32)
    product = back * o_ref[...].astype(jnp.float32)
    for h in range(2):
        own = (lane < 64) if h == 0 else (lane >= 64)
        centre = jnp.sum(jnp.where(own, product, 0.0), axis=1, keepdims=True)
        moved = back if h == 0 else pltpu.roll(back, 64, 1)
        high, middle, low = split3(-centre)
        extra = jnp.where(
            lane == 64, high, jnp.where(lane == 65, middle, jnp.where(lane == 66, low, 0.0))
        )
        do_aug[h] = jnp.where(lane < 64, moved, extra).astype(jnp.bfloat16)
    k_t[...] = k_ref[0].astype(jnp.float32).T[:64, :].astype(jnp.bfloat16)
    low_half = lax.broadcasted_iota(jnp.int32, (TILE, 128), 1) < 64
    for j in range(tiles):
        cols = slice(j * TILE, (j + 1) * TILE)
        k = k_ref[0, cols, :]
        v = v_ref[0, cols, :]
        dk = None
        dv = None
        for i in range(j, tiles):
            rows = slice(i * TILE, (i + 1) * TILE)
            for h in range(2):
                q = q_ref[h, rows, :]
                do = do_aug[h, rows, :]
                probs = jnp.exp(dot(k, q, NT))
                if i == j:
                    probs = jnp.where(keep, probs, 0.0)
                scores = (probs * dot(v, do, NT)).astype(jnp.bfloat16)
                to_v = dot(probs.astype(jnp.bfloat16), do)
                to_k = dot(scores, q)
                dv = to_v if dv is None else dv + to_v
                dk = to_k if dk is None else dk + to_k
                to_q = dot(k_t[:, cols], scores)
                if j == 0:
                    dq_t[h * 64 : (h + 1) * 64, rows] = to_q
                else:
                    dq_t[h * 64 : (h + 1) * 64, rows] += to_q
        dkv_ref[cols, :] = jnp.where(low_half, dk, pltpu.roll(dv, 64, 1))
    dq_ref[...] = dq_t[...].T


def attend_back(q_back, k_aug, v_aug, attended, back_attended):
    _, length, _ = q_back.shape
    groups = k_aug.shape[0]
    by_group = pl.BlockSpec((length, 128), lambda g: (0, g))
    return pl.pallas_call(
        attend_back_kernel,
        grid=(groups,),
        in_specs=[
            pl.BlockSpec((2, length, 128), lambda g: (g, 0, 0)),
            pl.BlockSpec((1, length, 128), lambda g: (g, 0, 0)),
            pl.BlockSpec((1, length, 128), lambda g: (g, 0, 0)),
            by_group,
            by_group,
        ],
        out_specs=[by_group, by_group],
        out_shape=[jax.ShapeDtypeStruct((length, groups * 128), jnp.float32)] * 2,
        scratch_shapes=[
            pltpu.VMEM((2, length, 128), jnp.bfloat16),
            pltpu.VMEM((64, length), jnp.bfloat16),
            pltpu.VMEM((128, length), jnp.float32),
        ],
        compiler_params=pltpu.CompilerParams(vmem_limit_bytes=VMEM_LIMIT),
        cost_estimate=pl.CostEstimate(
            flops=38 * 10**9, bytes_accessed=24 * 2**20, transcendentals=10 * 2**20
        ),
        name="attend_back",
    )(q_back, k_aug, v_aug, attended, back_attended)


def rope_tables(numbers):
    length = numbers.shape[0]
    indices = jnp.arange(length, dtype=jnp.int32)
    starts = jnp.concatenate([jnp.ones((1,), dtype=bool), numbers[1:] != numbers[:-1]])
    begins = lax.cummax(jnp.where(starts, indices, jnp.zeros_like(numbers)), axis=0)
    offsets = (indices - begins).astype(jnp.float32).reshape(length, 1)
    frequency = ROPE_BASE ** (-jnp.arange(0, HEAD_SIZE, 2).astype(jnp.float32) / HEAD_SIZE)
    angles = offsets * frequency
    cosine = jnp.cos(angles)
    sine = jnp.sin(angles)
    return (
        jnp.concatenate([cosine, cosine], axis=-1)[:, None, :],
        jnp.concatenate([sine, sine], axis=-1)[:, None, :],
    )


def rotate(rows, cosine, sine):
    half = rows.shape[-1] // 2
    turned = jnp.concatenate([-rows[..., half:], rows[..., :half]], axis=-1)
    return rows * cosine + turned * sine


def rotate_back(grads, cosine, sine):
    half = grads.shape[-1] // 2
    moved = grads * sine
    return grads * cosine + jnp.concatenate([moved[..., half:], -moved[..., :half]], axis=-1)


def augment(q, k, v, numbers):
    length = numbers.shape[0]
    same = (numbers[:, None] == jnp.arange(4)[None]).astype(jnp.float32)
    q_more = jnp.concatenate([-FAR * same, jnp.zeros((length, 60))], 1)
    k_more = jnp.concatenate([1 - same, jnp.ones((length, 3)), jnp.zeros((length, 57))], 1)
    v_more = jnp.concatenate([jnp.ones((length, 3)), jnp.zeros((length, 61))], 1)

    def join(rows, more):
        rows = rows.transpose(1, 0, 2)
        more = jnp.broadcast_to(more.astype(jnp.bfloat16), rows.shape)
        return jnp.concatenate([rows, more], 2)

    return (
        join(q * jnp.bfloat16(HEAD_SIZE**-0.5), q_more),
        join(k, k_more),
        join(v, v_more),
    )


def gather(array):
    return lax.all_gather(array, "shard", axis=0, tiled=True)


def scatter(array):
    return lax.psum_scatter(array, "shard", scatter_dimension=0, tiled=True)


def block_step(
    inputs,
    numbers,
    gain_attn,
    gain_query,
    gain_key,
    gain_ffn,
    attn_pack,
    pair,
    down,
    cotangent,
):
    rows = inputs.shape[0]
    w_query = attn_pack[:, :1024]
    w_key = attn_pack[:, 1024:1536]
    w_value = attn_pack[:, 1536:2048]
    w_output = attn_pack[:, 2048:]
    unit_one, inverse_one = unit_rows(inputs)
    normed_one = (unit_one * gain_attn).astype(jnp.bfloat16)
    raw = einsum_result("vp,pl->vl", normed_one, attn_pack[:, :2048])
    query_raw = raw[:, :1024].reshape(rows, QUERY_HEADS, HEAD_SIZE)
    key_raw = raw[:, 1024:1536].reshape(rows, KEY_VALUE_HEADS, HEAD_SIZE)
    values = raw[:, 1536:].astype(jnp.bfloat16).reshape(rows, KEY_VALUE_HEADS, HEAD_SIZE)
    cosine, sine = rope_tables(numbers)
    query_unit, query_inverse = unit_rows(query_raw)
    key_unit, key_inverse = unit_rows(key_raw)
    queries = rotate(query_unit * gain_query, cosine, sine).astype(jnp.bfloat16)
    keys = rotate(key_unit * gain_key, cosine, sine).astype(jnp.bfloat16)
    q_aug, k_aug, v_aug = augment(queries, keys, values, numbers)
    attended, q_back = attend(q_aug, k_aug, v_aug)
    first_sum = inputs + einsum_result("nh,hd->nd", attended, w_output)
    unit_two, inverse_two = unit_rows(first_sum)
    normed_two = (unit_two * gain_ffn).astype(jnp.bfloat16)
    gate_value = einsum_result("nc,cf->nf", normed_two, pair[:, :FF])
    up_value = einsum_result("nc,cf->nf", normed_two, pair[:, FF:])
    sigmoid_gate = jax.nn.sigmoid(gate_value)
    swish_gate = gate_value * sigmoid_gate
    hidden = (swish_gate * up_value).astype(jnp.bfloat16)
    grad_down = scatter(einsum_result("nf,nd->fd", hidden, cotangent).astype(jnp.bfloat16))
    back_hidden = einsum_result("nd,fd->nf", cotangent, down)
    back_up = (back_hidden * swish_gate).astype(jnp.bfloat16)
    back_gate = (
        back_hidden * up_value * sigmoid_gate * (1.0 + gate_value * (1.0 - sigmoid_gate))
    ).astype(jnp.bfloat16)
    grad_gate = scatter(einsum_result("nc,nf->cf", normed_two, back_gate).astype(jnp.bfloat16))
    grad_up = scatter(einsum_result("nc,nf->cf", normed_two, back_up).astype(jnp.bfloat16))
    back_two = einsum_result("nf,cf->nc", back_gate, pair[:, :FF]) + einsum_result(
        "nf,cf->nc", back_up, pair[:, FF:]
    )
    grad_gain_ffn = jnp.sum(back_two * unit_two, axis=0)
    back_first = cotangent.astype(jnp.float32) + unit_back(
        back_two, unit_two, inverse_two, gain_ffn
    )
    back_attn = back_first.astype(jnp.bfloat16)
    back_attended = einsum_result("nd,hd->nh", back_attn, w_output).astype(jnp.bfloat16)
    grad_out = einsum_result("nh,nd->hd", attended, back_attn).astype(jnp.bfloat16)
    dq, dkv = attend_back(q_back, k_aug, v_aug, attended, back_attended)
    dkv = dkv.reshape(rows, KEY_VALUE_HEADS, 2 * HEAD_SIZE)
    scaling = HEAD_SIZE**-0.5
    back_queries = dq.reshape(rows, QUERY_HEADS, HEAD_SIZE) * scaling
    back_keys = dkv[:, :, :HEAD_SIZE]
    back_values = dkv[:, :, HEAD_SIZE:].astype(jnp.bfloat16).reshape(rows, 512)
    query_turned = rotate_back(back_queries, cosine, sine)
    key_turned = rotate_back(back_keys, cosine, sine)
    grad_gain_query = jnp.sum(query_turned * query_unit, axis=(0, 1))
    grad_gain_key = jnp.sum(key_turned * key_unit, axis=(0, 1))
    back_query_raw = unit_back(query_turned, query_unit, query_inverse, gain_query)
    back_key_raw = unit_back(key_turned, key_unit, key_inverse, gain_key)
    back_raw = jnp.concatenate(
        [
            back_query_raw.astype(jnp.bfloat16).reshape(rows, 1024),
            back_key_raw.astype(jnp.bfloat16).reshape(rows, 512),
            back_values,
        ],
        axis=1,
    )
    back_one = einsum_result("nh,ch->nc", back_raw, attn_pack[:, :2048])
    grad_gain_attn = jnp.sum(back_one * unit_one, axis=0)
    input_grad = back_first + unit_back(back_one, unit_one, inverse_one, gain_attn)
    grad_attn = scatter(
        jnp.concatenate(
            [einsum_result("nc,nh->ch", normed_one, back_raw).astype(jnp.bfloat16), grad_out],
            axis=1,
        )
    )
    ffn_out = einsum_result("nf,fd->nd", hidden, down)
    block_output = (first_sum + ffn_out).astype(jnp.bfloat16)
    gains = [grad_gain_attn, grad_gain_query, grad_gain_key, grad_gain_ffn]
    return block_output, input_grad, grad_down, grad_gate, grad_up, grad_attn, gains


def on_device(
    block_input,
    document_numbers,
    attn_gain,
    w_query,
    key_weight,
    value_weight,
    query_gain,
    key_gain,
    w_output,
    ffn_gain,
    w_gate,
    w_up,
    w_down,
    cotangent,
):
    _, length, features = block_input.shape
    parts = features // attn_gain.shape[0]
    widths = [attn_gain.shape[0], query_gain.shape[0], key_gain.shape[0], ffn_gain.shape[0]]
    gains = lax.all_gather(
        jnp.concatenate([attn_gain, query_gain, key_gain, ffn_gain]), "shard", axis=0, tiled=False
    ).astype(jnp.float32)
    offsets = [sum(widths[:i]) for i in range(5)]
    gain_attn, gain_query, gain_key, gain_ffn = [
        gains[:, offsets[i] : offsets[i + 1]].reshape(-1) for i in range(4)
    ]
    attn_pack = gather(jnp.concatenate([w_query, key_weight, value_weight, w_output], axis=1))
    pair = gather(jnp.concatenate([w_gate, w_up], axis=1))
    down = gather(w_down)
    inputs = block_input.reshape(length, features).astype(jnp.float32)
    back_ffn = cotangent.reshape(length, features)
    (block_output, input_grad, grad_down, grad_gate, grad_up, grad_attn, gain_grads) = block_step(
        inputs,
        document_numbers.reshape(length),
        gain_attn,
        gain_query,
        gain_key,
        gain_ffn,
        attn_pack,
        pair,
        down,
        back_ffn,
    )

    def over(array):
        return lax.psum(array, "rep")

    sum_down = over(grad_down)
    grad_gate, sum_down = lax.optimization_barrier((grad_gate, sum_down))
    sum_gate = over(grad_gate)
    grad_up, sum_gate = lax.optimization_barrier((grad_up, sum_gate))
    sum_up = over(grad_up)
    grad_attn, sum_up = lax.optimization_barrier((grad_attn, sum_up))
    sum_attn = over(grad_attn).astype(jnp.float32)
    gain_grads = jnp.concatenate([part.reshape(parts, -1) for part in gain_grads], axis=1)
    sums = lax.psum(
        lax.psum_scatter(gain_grads, "shard", scatter_dimension=0, tiled=True), "rep"
    ).reshape(-1)
    return (
        block_output[None],
        input_grad[None],
        sums[offsets[0] : offsets[1]],
        sum_attn[:, :1024],
        sum_attn[:, 1024:1536],
        sum_attn[:, 1536:2048],
        sums[offsets[1] : offsets[2]],
        sums[offsets[2] : offsets[3]],
        sum_attn[:, 2048:],
        sums[offsets[3] : offsets[4]],
        sum_gate.astype(jnp.float32),
        sum_up.astype(jnp.float32),
        sum_down.astype(jnp.float32),
    )


def solution(mesh):
    in_specs = (
        P(("rep", "shard"), None, None),
        P(("rep", "shard"), None),
        P("shard"),
        P("shard", None),
        P("shard", None),
        P("shard", None),
        P("shard"),
        P("shard"),
        P("shard", None),
        P("shard"),
        P("shard", None),
        P("shard", None),
        P("shard", None),
        P(("rep", "shard"), None, None),
    )
    out_specs = (
        P(("rep", "shard"), None, None),
        P(("rep", "shard"), None, None),
        P("shard"),
        P("shard", None),
        P("shard", None),
        P("shard", None),
        P("shard"),
        P("shard"),
        P("shard", None),
        P("shard"),
        P("shard", None),
        P("shard", None),
        P("shard", None),
    )
    return jax.shard_map(
        on_device, mesh=mesh, in_specs=in_specs, out_specs=out_specs, check_vma=False
    )
```

time: 1120 us -> 840 us (0.75)
  waiting for transfers between devices: 490 us -> 248 us
  matrix products: 374 us -> 209 us
  local copies, waits for them, and re-layouts: 55.1 us -> 128 us
  Pallas kernels: 0 us -> 70.2 us
  blocking collectives: 69.8 us -> 51.4 us
    dot_general x77 -> x15, matrix products: 374 us -> 209 us  [einsum_result(): return jnp.einsum(form, left, right, preferred_element_type=jnp.float32)]
    reduce_scatter x3 -> x4, waiting for transfers between devices: 237 us -> 93.6 us  [scatter(): return lax.psum_scatter(array, 'shard', scatter_dimension=0, tiled=True)]
    all_gather x8 -> x3, waiting for transfers between devices: 164 us -> 55.7 us  [gather(): return lax.all_gather(array, 'shard', axis=0, tiled=True)]
    pallas_call x0 -> x2, Pallas kernels: none -> 70.2 us  [the longest x1 45.1 us: attend_back(): pl.pallas_call(attend_back_kernel, grid=(groups,), in_specs=[pl.BlockSpec...]
    convert_element_type x25 -> x6, other arithmetic: 37.3 us -> 9.82 us  [the longest x1 2.95 us: block_step(): back_key_raw.astype(jnp.bfloat16).reshape(rows, 512)]
    mul x0 -> x11, local copies, waits for them, and re-layouts: none -> 25.6 us  [the longest x2 8.42 us: unit_back(): unit_part * jnp.mean(scaled * unit_part, axis=-1, keepdims=True)]
    reshape x1 -> x8, local copies, waits for them, and re-layouts: 0.01 us -> 23.2 us  [the longest x1 7.02 us: block_step(): back_queries = dq.reshape(rows, QUERY_HEADS, HEAD_SIZE) * scaling]
    slice x4 -> x14, local copies, waits for them, and re-layouts: 5.56 us -> 25.4 us  [the longest x2 8.4 us: block_step(): query_raw = raw[:, :1024].reshape(rows, QUERY_HEADS, HEAD_SIZE)]
  transfers between devices with their start and end apart: 13 -> 11, of which waited for: 8 -> 6; matrix products, arithmetic and copies ran while one was open for 27% -> 44% of each run, Pallas kernels for 0% -> 8%
where the time goes in v1:
time: 840 us; the launch traced here: 834 us
  waiting for transfers between devices  248 us (30%)
  matrix products  209 us (25%)
  local copies, waits for them, and re-layouts  128 us (15%)
  other arithmetic  111 us (13%)
  Pallas kernels  70.2 us (8%)
  blocking collectives  51.4 us (6%)
  between operations  15.9 us (2%)
    dot_general x15, matrix products, einsum_result(): return jnp.einsum(form, left, right, preferred_element_type=jnp.float32)  209 us
    psum x4, waiting for transfers between devices, over(): return lax.psum(array, 'rep')  97.7 us
    reduce_scatter x4, waiting for transfers between devices, scatter(): return lax.psum_scatter(array, 'shard', scatter_dimension=0, tiled=True)  93.6 us
    all_gather x3, waiting for transfers between devices, gather(): return lax.all_gather(array, 'shard', axis=0, tiled=True)  55.7 us
    pallas_call x1, Pallas kernels, attend_back(): pl.pallas_call(attend_back_kernel, grid=(groups,), in_specs=[pl.BlockSpec...  45.1 us
    unnamed x2, blocking collectives  41.2 us
    unnamed x134, local copies, waits for them, and re-layouts  28.3 us
    pallas_call x1, Pallas kernels, attend(): pl.pallas_call(attend_kernel, grid=(groups,), in_specs=[pl.BlockSpec((2,...  25.1 us
  transfers between devices with their start and end apart: 11, of which 6 were waited for; matrix products, arithmetic and copies ran while one was open for 44% of the time, Pallas kernels for 8%

profile of v1, /device:TPU:0, one launch (start us, length us, event | category | flops | bytes accessed | tf_op | source)
XLA Modules:
  0.0 834.2 jit_solution(14057266160527745649)
XLA Ops:
  16.7 16.0 %all-reduce.1 = bf16[2176]{0:T(1024)(128)(2,1)S(1)} all-reduce(bf16[2176]{0:T(1024)(128)(2,1)S(1)} %dynamic-update-slice), channel_id=2, replica_groups=mesh['rep'=4,'shard'=8] {'shard'}, use_global_device_ids=true, to_apply=%add.1 | all-reduce | flops 2176 | bytes 8704
  38.8 20.2 %all-gather.5.cloned.1.call-done = bf16[1024,3072]{1,0:T(8,128)(2,1)} async-done(((bf16[128,3072]{1,0:T(8,128)(2,1)}), bf16[1024,3072]{1,0:T(8,128)(2,1)}) %all-gather.5.cloned.1.call-update) | async-done | bytes 6291472 | tf_op jit(solution)/shard_map/all_gather | solution.py:230
  59.0 6.9 fusion.29
  77.7 5.3 copy.109
  83.0 6.9 copy.110
  95.4 3.6 multiply_multiply_fusion.1
  113.7 7.6 slice_negate_fusion.1
  121.3 8.3 fusion.24
  130.5 3.7 pad_maximum_fusion.2.q_ref
  134.1 25.1 %attend.1 = (bf16[1024,1024]{1,0:T(8,128)(2,1)}, bf16[16,1024,128]{2,1,0:T(8,128)(2,1)}) custom-call(bf16[16,1024,128]{2,1,0:T(8,128)(2,1)} %pad_maximum_fusion.2.q_ref, bf16[8,1024,128]{2,1,0:T(8,128)(2,1)} %pad_maximum_fusion.5.k_ref, bf16[8,1024,128]{2,1,0:T(8,128)(2,1)} %pad_maximum_fusion.6.v_ref), custom_call_target="tpu_custom_call" | custom-call | flops 20000000000 | bytes 16777216 | tf_op jit(solution)/shard_map/attend/pallas_call | solution.py:83
  159.3 4.8 multiply_reduce_fusion.6
  168.1 17.3 %fusion.37 = f32[1024,4608]{1,0:T(8,128)} fusion(bf16[4608,1024]{1,0:T(8,128)(2,1)} %all-gather.9.cloned.1.call-done, bf16[1,1024,1024]{2,1,0:T(8,128)(2,1)S(1)} %copy-done.19), kind=kOutput, calls=%fused_computation.79 | convolution fusion | flops 9663676416 | bytes 30408704 | tf_op jit(solution)/shard_map/nd,fd->nf/dot_general | solution.py:26
  185.5 35.5 %all-gather.7.cloned.1.call-done = bf16[1024,9216]{1,0:T(8,128)(2,1)} async-done(((bf16[128,9216]{1,0:T(8,128)(2,1)}), bf16[1024,9216]{1,0:T(8,128)(2,1)}) %all-gather.7.cloned.1.call-update) | async-done | bytes 18874384 | tf_op jit(solution)/shard_map/all_gather | solution.py:230
  221.0 16.9 %fusion.5 = f32[1024,4608]{1,0:T(8,128)} fusion(bf16[1024,1024]{0,1:T(8,128)(2,1)} %multiply_convert_fusion.5, bf16[1024,9216]{1,0:T(8,128)(2,1)} %all-gather.7.cloned.1.call-done), kind=kOutput, calls=%fused_computation.17 | convolution fusion | flops 9663676416 | bytes 30408704 | tf_op jit(solution)/shard_map/nc,cf->nf/dot_general | solution.py:26
  237.9 36.6 %multiply_convert_fusion.1 = (bf16[1024,4608]{1,0:T(8,128)(2,1)}, bf16[1024,4608]{1,0:T(8,128)(2,1)}, bf16[1024,4608]{1,0:T(8,128)(2,1)}) fusion(f32[1024,4608]{1,0:T(8,128)} %fusion.37, f32[1024,4608]{1,0:T(8,128)} %fusion.5, bf16[1024,1024]{0,1:T(8,128)(2,1)} %multiply_convert_fusion.5, bf16[1024,9216]{1,0:T(8,128)(2,1)} %all-gather.7.cloned.1.call-done), kind=kOutput, calls=%fused_computation.1 | convolution fusion | flops 9734455296 | bytes 77594624 | tf_op jit(solution)/shard_map/nc,cf->nf/dot_general | solution.py:26
  274.5 16.1 %convolution_convert_fusion.2 = bf16[4608,1024]{1,0:T(8,128)(2,1)} fusion(bf16[1024,4608]{1,0:T(8,128)(2,1)} %get-tuple-element.96, bf16[1,1024,1024]{2,1,0:T(8,128)(2,1)S(1)} %copy-done.19), kind=kOutput, calls=%fused_computation.7 | convolution fusion | flops 9668395008 | bytes 20971520 | tf_op jit(solution)/shard_map/nf,nd->fd/dot_general | solution.py:26
  292.2 15.6 %convolution_convert_fusion = bf16[1024,4608]{1,0:T(8,128)(2,1)} fusion(bf16[1024,1024]{0,1:T(8,128)(2,1)S(1)} %copy-done.21, bf16[1024,4608]{1,0:T(8,128)(2,1)} %get-tuple-element.94), kind=kOutput, calls=%fused_computation.5 | convolution fusion | flops 9668395008 | bytes 20971520 | tf_op jit(solution)/shard_map/nc,nf->cf/dot_general | solution.py:26
  307.9 3.3 copy.116
  314.0 5.5 copy.121
  322.7 5.7 copy.129
  328.4 38.9 %reduce-scatter.11.cloned.1.call-done = bf16[576,1024]{1,0:T(8,128)(2,1)} async-done(((bf16[4608,1024]{1,0:T(8,128)(2,1)}), bf16[576,1024]{1,0:T(8,128)(2,1)}) %reduce-scatter.11.cloned.1.call-update) | async-done | bytes 1179664 | tf_op jit(solution)/shard_map/reduce_scatter | solution.py:234
  367.4 16.7 %convolution_convert_fusion.1 = bf16[1024,4608]{1,0:T(8,128)(2,1)} fusion(bf16[1024,1024]{0,1:T(8,128)(2,1)} %multiply_convert_fusion.5, bf16[1024,4608]{1,0:T(8,128)(2,1)} %get-tuple-element.95), kind=kOutput, calls=%fused_computation.6 | convolution fusion | flops 9668395008 | bytes 20971520 | tf_op jit(solution)/shard_map/nc,nf->cf/dot_general | solution.py:26
  384.2 17.2 %fusion.3 = f32[1024,1024]{0,1:T(8,128)} fusion(bf16[1024,4608]{1,0:T(8,128)(2,1)} %get-tuple-element.95, bf16[1024,9216]{1,0:T(8,128)(2,1)} %all-gather.7.cloned.1.call-done), kind=kOutput, calls=%fused_computation.15 | convolution fusion | flops 9663676416 | bytes 23068672 | tf_op jit(solution)/shard_map/nf,cf->nc/dot_general | solution.py:26
  401.4 17.5 %multiply_reduce_fusion.1 = (f32[1024]{0:T(1024)}, f32[1024]{0:T(1024)S(1)}, f32[1024,1024]{0,1:T(8,128)S(1)}) fusion(f32[1024,1024]{0,1:T(8,128)S(1)} %copy-done.8, f32[1024]{0:T(1024)S(1)} %copy-done.38, f32[1024]{0:T(1024)S(1)} %copy-done.40, f32[1024,1024]{0,1:T(8,128)} %fusion.3, bf16[1024,4608]{1,0:T(8,128)(2,1)} %get-tuple-element.94, ...), kind=kOutput, calls=%fused_computation.50 | convolution fusion | flops 9671014400 | bytes 31473664 | tf_op jit(solution)/shard_map/nf,cf->nc/dot_general | solution.py:26
  419.9 6.8 convolution_convert_fusion.5.do_ref
  426.7 45.1 %attend_back.1 = (f32[1024,1024]{1,0:T(8,128)}, f32[1024,1024]{1,0:T(8,128)}) custom-call(bf16[16,1024,128]{2,1,0:T(8,128)(2,1)} %get-tuple-element.24.q_ref, bf16[8,1024,128]{2,1,0:T(8,128)(2,1)} %pad_maximum_fusion.5.k_ref, bf16[8,1024,128]{2,1,0:T(8,128)(2,1)} %pad_maximum_fusion.6.v_ref, bf16[1024,1024]{1,0:T(8,128)(2,1)} %get-tuple-element.23.o_ref, ...), custom_call_target="tpu_custom_call" | custom-call | flops 38000001024 | bytes 25165824 | tf_op jit(solution)/shard_map/attend_back/pallas_call | solution.py:157
  471.8 5.4 copy.130
  481.6 5.5 copy.122
  487.2 7.0 copy.123
  494.2 4.2 broadcast_multiply_fusion
  498.4 7.2 fusion.48
  505.7 15.2 %multiply_reduce_fusion = (f32[1024,16]{0,1:T(8,128)S(1)}, f32[1024,16,64]{2,0,1:T(8,128)}) fusion(f32[1024,16,64]{2,0,1:T(8,128)} %copy.123, f32[1024,16,64]{2,0,1:T(8,128)S(1)} %bitcast.82, f32[1024,64]{1,0:T(8,128)S(1)} %copy-done.18, f32[64]{0:T(128)S(1)} %copy-done.48, f32[1024,16]{0,1:T(8,128)S(1)} %copy-done.25, ...), kind=kLoop, calls=%fused_computation.14 | loop fusion | flops 7323648 | bytes 17170688 | tf_op jit(solution)/shard_map/reduce_sum | solution.py:36
  523.8 5.6 copy.128
  529.4 7.0 copy.124
  536.3 5.4 copy.125
  550.8 3.7 multiply_reduce_fusion.2
  562.0 12.1 %multiply_reduce_fusion.3 = (f32[1024]{0:T(1024)S(1)}, bf16[1024,1024]{1,0:T(8,128)(2,1)}) fusion(f32[1024,1024]{1,0:T(8,128)} %copy.129, f32[1024,1024]{1,0:T(8,128)} %copy.125, f32[1024,1024]{1,0:T(8,128)} %get-tuple-element.25, f32[1024,1024]{1,0:T(8,128)} %copy.121, f32[1024,2048]{1,0:T(8,128)} %copy-done.11, f32[1024,1024]{1,0:T(8,128)} %copy.128, ...), kind=kLoop, calls=%fused_computation.52 | loop fusion | flops 10484736 | bytes 27271168 | tf_op jit(solution)/shard_map/reduce_sum | solution.py:301
  574.3 6.7 convolution_convert_fusion.3
  583.4 3.2 pad_maximum_fusion.1
  586.6 17.1 %fusion.34 = bf16[1,1024,1024]{1,2,0:T(8,128)(2,1)} fusion(f32[1024,1024]{0,1:T(8,128)} %copy-done.7, bf16[1024,4608]{1,0:T(8,128)(2,1)} %get-tuple-element.96, bf16[4608,1024]{1,0:T(8,128)(2,1)} %all-gather.9.cloned.1.call-done), kind=kOutput, calls=%fused_computation.72 | convolution fusion | flops 9665773568 | bytes 25165824 | tf_op jit(solution)/shard_map/nf,fd->nd/dot_general | solution.py:26
  603.8 39.4 %all-reduce.10.cloned.1.call-done = bf16[128,4608]{1,0:T(8,128)(2,1)} async-done(((bf16[128,4608]{1,0:T(8,128)(2,1)}), bf16[128,4608]{1,0:T(8,128)(2,1)}) %all-reduce.10.cloned.1.call-update) | async-done | bytes 1179664 | tf_op jit(solution)/shard_map/psum | solution.py:373
  643.3 9.9 %fusion.21 = (f32[1024]{0:T(1024)S(1)}, f32[1024]{0:T(1024)S(1)}, f32[1024,1024]{0,1:T(8,128)}) fusion(bf16[1,1024,1024]{1,2,0:T(8,128)(2,1)S(1)} %copy-done.6, f32[1024]{0:T(1024)S(1)} %copy-done.43, f32[1024]{0:T(1024)S(1)} %copy-done.45, bf16[1024,3072]{1,0:T(8,128)(2,1)} %all-gather.5.cloned.1.call-done, bf16[1024,512]{1,0:T(8,128)(2,1)} %copy.134, ...), kind=kOutput, calls=%fused_computation.38 | convolution fusion | flops 4314888192 | bytes 14696448 | tf_op jit(solution)/shard_map/nh,ch->nc/dot_general | solution.py:26
  653.2 54.7 %reduce-scatter.5.cloned.1.call-done = bf16[128,3072]{1,0:T(8,128)(2,1)} async-done(((bf16[1024,3072]{1,0:T(8,128)(2,1)}), bf16[128,3072]{1,0:T(8,128)(2,1)}) %reduce-scatter.5.cloned.1.call-update) | async-done | bytes 786448 | tf_op jit(solution)/shard_map/reduce_scatter | solution.py:234
  707.9 58.3 %all-reduce.12.cloned.1.call-done = bf16[128,4608]{1,0:T(8,128)(2,1)} async-done(((bf16[128,4608]{1,0:T(8,128)(2,1)}), bf16[128,4608]{1,0:T(8,128)(2,1)}) %all-reduce.12.cloned.1.call-update) | async-done | bytes 1179664 | tf_op jit(solution)/shard_map/psum | solution.py:373
  766.2 6.4 fusion.20
  772.9 5.5 copy.139
  781.1 25.2 %all-reduce.2 = f32[8,272]{1,0:T(8,128)S(1)} all-reduce(f32[8,272]{1,0:T(8,128)S(1)} %pad_maximum_fusion.12), channel_id=3, replica_groups=mesh['rep'=4,'shard'=8] {'shard'}, use_global_device_ids=true, to_apply=%region_15.16.clone | all-reduce | flops 2176 | bytes 17408
  806.9 10.2 %psum.35 = f32[1,272]{1,0:T(1,128)S(1)} all-reduce(f32[1,272]{1,0:T(1,128)S(1)} %constant_dynamic-slice_fusion), channel_id=1, replica_groups=mesh['rep'=4,'shard'=8] {'rep'}, use_global_device_ids=true, to_apply=%region_16.17 | all-reduce | flops 272 | bytes 2176 | tf_op jit(solution)/shard_map/psum | solution.py:383
  (240 shorter events, 100.1 us)
Async XLA Ops:
  7.2 51.8 %all-gather.5.cloned.1.call-start = ((), (), s32[]{:S(2)}) async-start(), calls=%async_computation.4 | async-start | bytes 7077888 | tf_op jit(solution)/shard_map/all_gather | solution.py:230
  9.5 158.6 %all-gather.9.cloned.1.call-start = ((), (), s32[]{:S(2)}) async-start(), calls=%async_computation.6 | async-start | bytes 10616832 | tf_op jit(solution)/shard_map/all_gather | solution.py:230
  10.3 210.7 %all-gather.7.cloned.1.call-start = ((), (), s32[]{:S(2)}) async-start(), calls=%async_computation.5 | async-start | bytes 21233664 | tf_op jit(solution)/shard_map/all_gather | solution.py:230
  12.0 21.0 %copy-start.36 = (s32[1,1024]{1,0:T(1,128)S(1)}, s32[1,1024]{1,0:T(1,128)}, u32[]{:S(2)}) copy-start(s32[1,1024]{1,0:T(1,128)} %param.15) | copy-start | bytes 12292
  12.0 355.2 %reduce-scatter.11.cloned.1.call-start = ((), (), s32[]{:S(2)}) async-start(), calls=%async_computation.10 | async-start | bytes 10616832 | tf_op jit(solution)/shard_map/reduce_scatter | solution.py:234
  15.0 51.0 %copy-start.4 = (bf16[1,1024,1024]{1,2,0:T(8,128)(2,1)}, bf16[1,1024,1024]{1,2,0:T(8,128)(2,1)S(1)}, u32[]{:S(2)}) copy-start(bf16[1,1024,1024]{1,2,0:T(8,128)(2,1)S(1)} %copy.108) | copy-start | bytes 6291460
  33.0 67.5 %copy-start.49 = (f32[64]{0:T(128)}, f32[64]{0:T(128)S(1)}, u32[]{:S(2)}) copy-start(f32[64]{0:T(128)S(1)} %mul.366) | copy-start | bytes 772
  33.8 87.5 %copy-start.46 = (f32[64]{0:T(128)}, f32[64]{0:T(128)S(1)}, u32[]{:S(2)}) copy-start(f32[64]{0:T(128)S(1)} %mul.347) | copy-start | bytes 772
  37.5 83.8 %copy-start.12 = (f32[1024,64]{1,0:T(8,128)}, f32[1024,64]{1,0:T(8,128)S(1)}, u32[]{:S(2)}) copy-start(f32[1024,64]{1,0:T(8,128)S(1)} %get-tuple-element.133) | copy-start | bytes 786436
  37.5 83.8 %copy-start.14 = (f32[1024,64]{1,0:T(8,128)}, f32[1024,64]{1,0:T(8,128)S(1)}, u32[]{:S(2)}) copy-start(f32[1024,64]{1,0:T(8,128)S(1)} %get-tuple-element.112) | copy-start | bytes 786436
  38.0 28.0 %copy-start.42 = (f32[1024]{0:T(1024)}, f32[1024]{0:T(1024)S(1)}, u32[]{:S(2)}) copy-start(f32[1024]{0:T(1024)S(1)} %add_rsqrt_fusion.3) | copy-start | bytes 12292
  38.0 27.9 %copy-start.44 = (f32[1024]{0:T(1024)}, f32[1024]{0:T(1024)S(1)}, u32[]{:S(2)}) copy-start(f32[1024]{0:T(1024)S(1)} %get-tuple-element.116) | copy-start | bytes 12292
  38.0 126.1 %copy-start.39 = (f32[1024]{0:T(1024)}, f32[1024]{0:T(1024)S(1)}, u32[]{:S(2)}) copy-start(f32[1024]{0:T(1024)S(1)} %get-tuple-element.115) | copy-start | bytes 12292
  66.0 5.9 copy-start.11
  95.4 5.1 copy-start.33
  104.2 5.9 slice-start
  111.2 10.1 %copy-start.23 = (f32[1024,16]{0,1:T(8,128)}, f32[1024,16]{0,1:T(8,128)S(1)}, u32[]{:S(2)}) copy-start(f32[1024,16]{0,1:T(8,128)S(1)} %add_rsqrt_fusion) | copy-start | bytes 196612
  134.1 25.1 %copy-start.5 = (bf16[1,1024,1024]{1,2,0:T(8,128)(2,1)S(1)}, bf16[1,1024,1024]{1,2,0:T(8,128)(2,1)}, u32[]{:S(2)}) copy-start(bf16[1,1024,1024]{1,2,0:T(8,128)(2,1)} %copy-done.4) | copy-start | bytes 6291460
  290.6 283.5 %reduce-scatter.9.cloned.1.call-start = ((), (), s32[]{:S(2)}) async-start(), calls=%async_computation.9 | async-start | bytes 10616832 | tf_op jit(solution)/shard_map/reduce_scatter | solution.py:234
  307.9 266.2 %all-reduce.8.cloned.1.call-start = ((), (), s32[]{:S(2)}) async-start(), calls=%async_computation.11 | async-start | bytes 2359296 | tf_op jit(solution)/shard_map/psum | solution.py:373
  314.0 5.5 copy-start.47
  314.0 6.2 copy-start.24
  367.3 236.5 %reduce-scatter.7.cloned.1.call-start = ((), (), s32[]{:S(2)}) async-start(), calls=%async_computation.8 | async-start | bytes 10616832 | tf_op jit(solution)/shard_map/reduce_scatter | solution.py:234
  384.1 17.2 %copy-start.38 = (f32[1024]{0:T(1024)S(1)}, f32[1024]{0:T(1024)}, u32[]{:S(2)}) copy-start(f32[1024]{0:T(1024)} %copy-done.37) | copy-start | bytes 12292
  384.1 17.2 %copy-start.40 = (f32[1024]{0:T(1024)S(1)}, f32[1024]{0:T(1024)}, u32[]{:S(2)}) copy-start(f32[1024]{0:T(1024)} %copy-done.39) | copy-start | bytes 12292
  384.1 259.0 %all-reduce.10.cloned.1.call-start = ((), (), s32[]{:S(2)}) async-start(), calls=%async_computation.12 | async-start | bytes 2359296 | tf_op jit(solution)/shard_map/psum | solution.py:373
  384.2 17.2 %copy-start.8 = (f32[1024,1024]{0,1:T(8,128)S(1)}, f32[1024,1024]{0,1:T(8,128)}, u32[]{:S(2)}) copy-start(f32[1024,1024]{0,1:T(8,128)} %copy-done.7) | copy-start | bytes 12582916
  419.9 6.8 copy-start.9
  487.2 7.0 copy-start.22
  494.2 11.4 %slice-start.2 = ((s8[8388608]{0:T(1024)(128)(4,1)}), s8[4194304]{0:T(1024)(128)(4,1)S(1)}, s32[]{:S(2)}) async-start(s8[8388608]{0:T(1024)(128)(4,1)} %bitcast.81), calls=%async_computation.17 | async-start | bytes 8388608
  498.4 7.3 slice-start.3
  498.4 7.3 copy-start.18
  498.4 7.3 copy-start.25
  498.4 7.3 copy-start.48
  557.5 4.5 copy-start.41
  562.0 12.2 %copy-start.6 = (bf16[1,1024,1024]{1,2,0:T(8,128)(2,1)S(1)}, bf16[1,1024,1024]{1,2,0:T(8,128)(2,1)}, u32[]{:S(2)}) copy-start(bf16[1,1024,1024]{1,2,0:T(8,128)(2,1)} %copy-done.4) | copy-start | bytes 6291460
  562.0 12.2 %copy-start.32 = (bf16[1024,512]{1,0:T(8,128)(2,1)S(1)}, bf16[1024,512]{1,0:T(8,128)(2,1)}, u32[]{:S(2)}) copy-start(bf16[1024,512]{1,0:T(8,128)(2,1)} %copy.133) | copy-start | bytes 3145732
  562.0 12.2 %copy-start.43 = (f32[1024]{0:T(1024)S(1)}, f32[1024]{0:T(1024)}, u32[]{:S(2)}) copy-start(f32[1024]{0:T(1024)} %copy-done.42) | copy-start | bytes 12292
  562.0 12.2 %copy-start.45 = (f32[1024]{0:T(1024)S(1)}, f32[1024]{0:T(1024)}, u32[]{:S(2)}) copy-start(f32[1024]{0:T(1024)} %copy-done.44) | copy-start | bytes 12292
  574.2 133.7 %reduce-scatter.5.cloned.1.call-start = ((), (), s32[]{:S(2)}) async-start(), calls=%async_computation.7 | async-start | bytes 7077888 | tf_op jit(solution)/shard_map/reduce_scatter | solution.py:234
  574.2 6.7 copy-start.10
  574.2 6.7 copy-start.57
  586.6 179.6 %all-reduce.12.cloned.1.call-start = ((), (), s32[]{:S(2)}) async-start(), calls=%async_computation.13 | async-start | bytes 2359296 | tf_op jit(solution)/shard_map/psum | solution.py:373
  643.2 180.1 %all-reduce.14.cloned.1.call-start = ((), (), s32[]{:S(2)}) async-start(), calls=%async_computation.14 | async-start | bytes 1572864 | tf_op jit(solution)/shard_map/psum | solution.py:373
  772.9 5.5 copy-start.20
  778.4 39.9 %copy-start.26 = (bf16[576,1024]{1,0:T(8,128)(2,1)S(1)}, bf16[576,1024]{1,0:T(8,128)(2,1)}, u32[]{:S(2)}) copy-start(bf16[576,1024]{1,0:T(8,128)(2,1)} %all-reduce.8.cloned.1.call-done) | copy-start | bytes 3538948
  781.0 39.0 %copy-start.27 = (bf16[128,4608]{1,0:T(8,128)(2,1)S(1)}, bf16[128,4608]{1,0:T(8,128)(2,1)}, u32[]{:S(2)}) copy-start(bf16[128,4608]{1,0:T(8,128)(2,1)} %all-reduce.10.cloned.1.call-done) | copy-start | bytes 3538948
  817.1 4.5 copy-start.28
  (25 other events, 80.2 us)
Sparse Core Ops, SparseCore 0:
  10.5 48.4 all-gather.4
  60.9 58.8 all-gather.8
  122.2 98.7 all-gather.6
  290.7 76.4 reduce-scatter.10
  370.6 76.4 reduce-scatter.8
  449.4 55.8 all-reduce.7
  508.8 76.0 reduce-scatter.6
  587.2 55.8 all-reduce.9
  646.6 61.2 reduce-scatter.4
  710.2 55.8 all-reduce.11
  768.7 43.2 all-reduce.13

commit v2 on v1

v2 whole, which is shorter than its diff:
```python
import jax
import jax.numpy as jnp
from jax import lax
from jax.experimental import pallas as pl
from jax.experimental.pallas import tpu as pltpu
from jax.sharding import PartitionSpec as P

QUERY_HEADS = 16
KEY_VALUE_HEADS = 8
HEAD_SIZE = 64
EPS = 1e-05
ROPE_BASE = 1000000.0
FAR = 32768.0
TILE = 256
SLAB = 512
VMEM_LIMIT = 60 * 1024 * 1024
NT = ((1,), (1,))
NN = ((1,), (0,))
TN = ((0,), (0,))
BF16 = jnp.bfloat16
F32 = jnp.float32
SMALL = pl.BlockSpec(memory_space=pltpu.SMEM)


def dot(left, right, dims=NN):
    return lax.dot_general(left, right, (dims, ((), ())), preferred_element_type=F32)


def params():
    return pltpu.CompilerParams(vmem_limit_bytes=VMEM_LIMIT)


def cost(giga_flops, mega_bytes, exps=0):
    return pl.CostEstimate(
        flops=int(giga_flops * 10**6),
        bytes_accessed=int(mega_bytes * 10**3),
        transcendentals=exps // 1000,
    )


def fixed(shape, where=None):
    index = (0,) * len(shape) if where is None else where
    return pl.BlockSpec(shape, lambda *_: index, pipeline_mode=pl.Buffered(1))


def by_rows(width, rows=TILE):
    return pl.BlockSpec((rows, width), lambda i: (i, 0))


class Pieces:
    def __init__(self, groups=None, stacked=None):
        self.stacked = stacked
        self.count = len(groups) if stacked is None else stacked.shape[0]
        self.groups = groups if stacked is None else [[stacked]] * self.count
        self.arrays = [array for group in self.groups for array in group]
        self.layout = [len(group) for group in self.groups]

    def specs(self, rows, start):
        once = pl.Buffered(1) if start(0) == start(1) else None
        found = []
        for k, group in enumerate(self.groups):
            for array in group:
                shape = (pl.Element(rows), pl.Element(array.shape[-1]))
                if self.stacked is None:
                    found.append(
                        pl.BlockSpec(shape, lambda i: (start(i), 0), pipeline_mode=once)
                    )
                else:
                    found.append(
                        pl.BlockSpec(
                            (pl.Squeezed(),) + shape,
                            lambda i, k=k: (k, start(i), 0),
                            pipeline_mode=once,
                        )
                    )
        return found


def grouped(refs, layout):
    groups, at = [], 0
    for size in layout:
        groups.append(refs[at : at + size])
        at += size
    return groups


def fill(target, at, group, rows):
    left = 0
    for ref in group:
        right = left + ref.shape[1]
        target[at, left:right] = ref[rows, :]
        left = right


def split3(value):
    high = value.astype(BF16).astype(F32)
    rest = value - high
    middle = rest.astype(BF16).astype(F32)
    return high, middle, rest - middle


def aligned(index, rows):
    return pl.ds(pl.multiple_of(index * rows, rows), rows)


def unit_of(rows):
    inverse = lax.rsqrt(jnp.mean(rows * rows, axis=-1, keepdims=True) + EPS)
    return rows * inverse, inverse


def head_blocks():
    first = lax.broadcasted_iota(jnp.int32, (128, 128), 0) // HEAD_SIZE
    second = lax.broadcasted_iota(jnp.int32, (128, 128), 1) // HEAD_SIZE
    return (first == second).astype(BF16)


def head_mean(rows, blocks):
    return dot(rows.astype(BF16), blocks) * (1.0 / HEAD_SIZE)


def swap_halves(rows, first):
    return jnp.where(first, pltpu.roll(rows, 96, 1), pltpu.roll(rows, 32, 1))


def lanes(rows=TILE):
    return lax.broadcasted_iota(jnp.int32, (rows, 128), 1)


def load_pairs(parts, me_ref, refs, w_all):
    rows = w_all.shape[0] // parts

    @pl.when(pl.program_id(0) == 0)
    def _():
        for k in range(parts):
            at = aligned(me_ref[0] ^ k, rows)
            w_all[at, :1024] = refs[2 * k][...]
            w_all[at, 1024:] = refs[2 * k + 1][...]


def pair_specs(pieces, rows):
    arrays, specs = [], []
    for piece in pieces:
        left, right, at = piece
        arrays += [left, right]
        specs += [fixed((rows, 1024)), fixed((rows, 1024), (at, 0))]
    return arrays, specs


def project_kernel(parts, me_ref, x_ref, cos_ref, sin_ref, qx_ref, kx_ref, *refs):
    gain_refs = refs[2 * parts : 3 * parts]
    n_ref, unit_ref, scale_ref, q_ref, k_ref, v_ref, gain_ref, w_all = refs[3 * parts :]
    load_pairs(parts, me_ref, refs, w_all)

    @pl.when(pl.program_id(0) == 0)
    def _():
        total = gain_refs[0][...].astype(F32)
        for ref in gain_refs[1:]:
            total = total + ref[...].astype(F32)
        gain_ref[...] = total

    unit, _ = unit_of(x_ref[...].astype(F32))
    normed = (unit * gain_ref[0:1, :]).astype(BF16)
    n_ref[...] = normed
    raw = dot(normed, w_all[...])
    blocks = head_blocks()
    lane = lanes()
    first = (lane % HEAD_SIZE) < HEAD_SIZE // 2
    low = lane < HEAD_SIZE
    cosine, sine = cos_ref[...], sin_ref[...]
    for p in range(12):
        at = slice(p * 128, (p + 1) * 128)
        rows_in = raw[:, at]
        inverse = lax.rsqrt(head_mean(rows_in * rows_in, blocks) + EPS)
        unit = rows_in * inverse
        unit_ref[:, at] = unit.astype(BF16)
        scale_ref[:, at] = inverse.astype(BF16)
        scaled = unit * gain_ref[1 + p // 8 : 2 + p // 8, :128]
        turned = scaled * cosine + swap_halves(scaled, first) * sine
        if p < 8:
            turned = turned * HEAD_SIZE**-0.5
            out, more, at = q_ref, qx_ref[...], 2 * p
        else:
            out, more, at = k_ref, kx_ref[...], 2 * (p - 8)
        out[at] = jnp.where(low, turned, more).astype(BF16)
        out[at + 1] = jnp.where(low, pltpu.roll(turned, 64, 1), more).astype(BF16)
    more = ((lane >= 64) & (lane < 67)).astype(F32)
    for p in range(4):
        rows_in = raw[:, 1536 + p * 128 : 1664 + p * 128]
        v_ref[2 * p] = jnp.where(low, rows_in, more).astype(BF16)
        v_ref[2 * p + 1] = jnp.where(low, pltpu.roll(rows_in, 64, 1), more).astype(BF16)


def project(pieces, me, x, tables):
    length, width = x.shape
    parts = len(pieces)
    rows = width // parts
    arrays, specs = pair_specs(pieces, rows)
    gains = [(piece[1], (piece[2] + 1) * rows // 16) for piece in pieces]

    def heads(count):
        return pl.BlockSpec((count, TILE, 128), lambda i: (0, i, 0))

    return pl.pallas_call(
        lambda *refs: project_kernel(parts, *refs),
        grid=(length // TILE,),
        in_specs=[SMALL, by_rows(width)]
        + [by_rows(128)] * 4
        + specs
        + [fixed((16, 1024), (at, 0)) for _, at in gains],
        out_specs=[by_rows(width), by_rows(1536), by_rows(1536), heads(16), heads(8), heads(8)]
        + [fixed((16, 1024))],
        out_shape=[
            jax.ShapeDtypeStruct((length, width), BF16),
            jax.ShapeDtypeStruct((length, 1536), BF16),
            jax.ShapeDtypeStruct((length, 1536), BF16),
            jax.ShapeDtypeStruct((16, length, 128), BF16),
            jax.ShapeDtypeStruct((8, length, 128), BF16),
            jax.ShapeDtypeStruct((8, length, 128), BF16),
            jax.ShapeDtypeStruct((16, 1024), F32),
        ],
        scratch_shapes=[pltpu.VMEM((width, 2048), BF16)],
        compiler_params=params(),
        cost_estimate=cost(8, 25),
        name="project",
    )(me, x, *tables, *arrays, *[array for array, _ in gains])


def causal(query_axis):
    first = lax.broadcasted_iota(jnp.int32, (TILE, TILE), 0)
    second = lax.broadcasted_iota(jnp.int32, (TILE, TILE), 1)
    return (first >= second) if query_axis == 0 else (second >= first)


def attend_kernel(q_ref, k_ref, v_ref, o_ref, qb_ref):
    tiles = q_ref.shape[1] // TILE
    keep = causal(0)
    lane = lax.broadcasted_iota(jnp.int32, (TILE, 128), 1)
    for i in range(tiles):
        rows = slice(i * TILE, (i + 1) * TILE)
        halves = []
        for h in range(2):
            q = q_ref[h, rows, :]
            out = None
            for j in range(i + 1):
                cols = slice(j * TILE, (j + 1) * TILE)
                weights = jnp.exp(dot(q, k_ref[0, cols, :], NT))
                if j == i:
                    weights = jnp.where(keep, weights, 0.0)
                part = dot(weights.astype(BF16), v_ref[0, cols, :])
                out = part if out is None else out + part
            total = out[:, 64:65]
            halves.append(out / total)
            high, middle, low = split3(-jnp.log(total))
            extra = jnp.where(
                lane == 68, high, jnp.where(lane == 69, middle, jnp.where(lane == 70, low, 0.0))
            )
            qb_ref[h, rows, :] = (q.astype(F32) + extra).astype(BF16)
        both = jnp.where(lane < 64, halves[0], pltpu.roll(halves[1], 64, 1))
        o_ref[rows, :] = both.astype(BF16)


def attend(q_aug, k_aug, v_aug, begin, groups):
    _, length, _ = q_aug.shape
    return pl.pallas_call(
        attend_kernel,
        grid=(groups,),
        in_specs=[
            pl.BlockSpec((2, length, 128), lambda g: (g + begin, 0, 0)),
            pl.BlockSpec((1, length, 128), lambda g: (g + begin, 0, 0)),
            pl.BlockSpec((1, length, 128), lambda g: (g + begin, 0, 0)),
        ],
        out_specs=[
            pl.BlockSpec((length, 128), lambda g: (0, g)),
            pl.BlockSpec((2, length, 128), lambda g: (g, 0, 0)),
        ],
        out_shape=[
            jax.ShapeDtypeStruct((length, groups * 128), BF16),
            jax.ShapeDtypeStruct((2 * groups, length, 128), BF16),
        ],
        compiler_params=params(),
        cost_estimate=cost(2.5 * groups, 2 * groups, groups * 2**20),
        name="attend",
    )(q_aug, k_aug, v_aug)


def attend_back_kernel(q_ref, k_ref, v_ref, o_ref, do_ref, dq_ref, dkv_ref, do_aug, k_t, dq_t):
    length = q_ref.shape[1]
    tiles = length // TILE
    keep = causal(1)
    lane = lax.broadcasted_iota(jnp.int32, (length, 128), 1)
    back = do_ref[...].astype(F32)
    product = back * o_ref[...].astype(F32)
    for h in range(2):
        own = (lane < 64) if h == 0 else (lane >= 64)
        centre = jnp.sum(jnp.where(own, product, 0.0), axis=1, keepdims=True)
        moved = back if h == 0 else pltpu.roll(back, 64, 1)
        high, middle, low = split3(-centre)
        extra = jnp.where(
            lane == 64, high, jnp.where(lane == 65, middle, jnp.where(lane == 66, low, 0.0))
        )
        do_aug[h] = jnp.where(lane < 64, moved, extra).astype(BF16)
    k_t[...] = k_ref[0].astype(F32).T[:64, :].astype(BF16)
    low_half = lax.broadcasted_iota(jnp.int32, (TILE, 128), 1) < 64
    for j in range(tiles):
        cols = slice(j * TILE, (j + 1) * TILE)
        k = k_ref[0, cols, :]
        v = v_ref[0, cols, :]
        dk = None
        dv = None
        for i in range(j, tiles):
            rows = slice(i * TILE, (i + 1) * TILE)
            for h in range(2):
                q = q_ref[h, rows, :]
                do = do_aug[h, rows, :]
                probs = jnp.exp(dot(k, q, NT))
                if i == j:
                    probs = jnp.where(keep, probs, 0.0)
                scores = (probs * dot(v, do, NT)).astype(BF16)
                to_v = dot(probs.astype(BF16), do)
                to_k = dot(scores, q)
                dv = to_v if dv is None else dv + to_v
                dk = to_k if dk is None else dk + to_k
                to_q = dot(k_t[:, cols], scores)
                if j == 0:
                    dq_t[h * 64 : (h + 1) * 64, rows] = to_q
                else:
                    dq_t[h * 64 : (h + 1) * 64, rows] += to_q
        dkv_ref[cols, :] = jnp.where(low_half, dk, pltpu.roll(dv, 64, 1))
    dq_ref[...] = dq_t[...].T


def attend_back(q_back, k_aug, v_aug, attended, back_attended, begin, groups):
    _, length, _ = q_back.shape
    by_group = pl.BlockSpec((length, 128), lambda g: (0, g + begin))
    out_group = pl.BlockSpec((length, 128), lambda g: (0, g))
    return pl.pallas_call(
        attend_back_kernel,
        grid=(groups,),
        in_specs=[
            pl.BlockSpec((2, length, 128), lambda g: (g, 0, 0)),
            pl.BlockSpec((1, length, 128), lambda g: (g + begin, 0, 0)),
            pl.BlockSpec((1, length, 128), lambda g: (g + begin, 0, 0)),
            out_group,
            by_group,
        ],
        out_specs=[out_group, out_group],
        out_shape=[jax.ShapeDtypeStruct((length, groups * 128), F32)] * 2,
        scratch_shapes=[
            pltpu.VMEM((2, length, 128), BF16),
            pltpu.VMEM((64, length), BF16),
            pltpu.VMEM((128, length), F32),
        ],
        compiler_params=params(),
        cost_estimate=cost(5 * groups, 3 * groups, groups * 2**20),
        name="attend_back",
    )(q_back, k_aug, v_aug, attended, back_attended)


def output_kernel(layout, me_ref, o0_ref, o1_ref, x_ref, gain_ref, *refs):
    sum_ref, n_ref, nt_ref, w_all = refs[-4:]
    rows = w_all.shape[0] // len(layout)

    @pl.when(pl.program_id(0) == 0)
    def _():
        for k, group in enumerate(grouped(refs, layout)):
            fill(w_all, aligned(me_ref[0] ^ k, rows), group, slice(None))

    total = x_ref[...].astype(F32) + dot(o0_ref[...], w_all[:512, :])
    total = total + dot(o1_ref[...], w_all[512:, :])
    sum_ref[...] = total
    unit, _ = unit_of(total)
    normed = unit * gain_ref[3:4, :]
    n_ref[...] = normed.astype(BF16)
    nt_ref[...] = normed.T.astype(BF16)


def output_rows(pieces, me, attended, x, gain):
    length, width = x.shape
    parts = pieces.count
    rows = width // parts
    return pl.pallas_call(
        lambda *refs: output_kernel(pieces.layout, *refs),
        grid=(length // TILE,),
        in_specs=[SMALL, by_rows(512), by_rows(512), by_rows(width), fixed((16, 1024))]
        + pieces.specs(rows, lambda i: 0),
        out_specs=[by_rows(width), by_rows(width), pl.BlockSpec((width, TILE), lambda i: (0, i))],
        out_shape=[
            jax.ShapeDtypeStruct((length, width), F32),
            jax.ShapeDtypeStruct((length, width), BF16),
            jax.ShapeDtypeStruct((width, length), BF16),
        ],
        scratch_shapes=[pltpu.VMEM((1024, width), BF16)],
        compiler_params=params(),
        cost_estimate=cost(5, 15),
        name="output_rows",
    )(me, *attended, x, gain, *pieces.arrays)


def scatter_rows(me, parts, value, rows, own_ref, sib_ref, at):
    half = me >> 1
    core = me & 1
    for q in range(parts // 2):
        for s, ref in enumerate((own_ref, sib_ref)):
            source = 2 * q + (core ^ s)
            ref[q ^ half, at : at + rows, :] = value[aligned(source, rows), :]


def feed_kernel(layout, paired, me_ref, n_ref, nt_ref, c_ref, *refs):
    parts = len(layout)
    f_ref, b_ref, *grad_refs = refs[sum(layout) : -7]
    w_all, d_all, back, w_grad, d_grad, f_sum, b_sum = refs[-7:]
    me = me_ref[0]
    rows = w_all.shape[0] // parts
    seg = SLAB // parts
    for k, group in enumerate(grouped(refs, layout)):
        fill(w_all, aligned(me ^ k, rows), group, slice(0, rows))
        fill(d_all, aligned(me ^ k, seg), group, slice(rows, rows + seg))
    both = dot(n_ref[...], w_all[...])
    gate = both[:, :SLAB]
    up = both[:, SLAB:]
    sig = 1.0 / (1.0 + jnp.exp(-gate))
    swish = gate * sig
    hidden = (swish * up).astype(BF16)
    back_hidden = dot(c_ref[...], d_all[...], NT)
    back[:, SLAB:] = (back_hidden * swish).astype(BF16)
    back[:, :SLAB] = (back_hidden * up * sig * (1.0 + gate * (1.0 - sig))).astype(BF16)
    out = dot(hidden, d_all[...])
    w_grad[...] = dot(nt_ref[...], back[...]).astype(BF16)
    d_grad[...] = dot(hidden, c_ref[...], TN).astype(BF16)
    back_in = dot(back[...], w_all[...], NT)

    step = pl.program_id(0)

    @pl.when(step == 0)
    def _():
        f_sum[...] = out
        b_sum[...] = back_in

    @pl.when(step > 0)
    def _():
        f_sum[...] += out
        b_sum[...] += back_in

    @pl.when(step == pl.num_programs(0) - 1)
    def _():
        f_ref[...] = f_sum[...].astype(BF16)
        b_ref[...] = b_sum[...].astype(BF16)

    if paired:
        own_ref, sib_ref = grad_refs
        scatter_rows(me, parts, w_grad, rows, own_ref, sib_ref, 0)
        scatter_rows(me, parts, d_grad, seg, own_ref, sib_ref, rows)
    else:
        for d in range(parts):
            grad_refs[0][d, :rows, :] = w_grad[d * rows : (d + 1) * rows, :]
            grad_refs[0][d, rows:, :] = d_grad[d * seg : (d + 1) * seg, :]


def feed(pieces, me, begin, slabs, normed, normed_t, cotangent, paired):
    length, width = normed.shape
    parts = pieces.count
    rows = width // parts + SLAB // parts
    depth = parts // 2 if paired else parts
    count = 2 if paired else 1
    grads = pl.BlockSpec((depth, rows, 2 * SLAB), lambda i: (0, i, 0))
    return pl.pallas_call(
        lambda *refs: feed_kernel(pieces.layout, paired, *refs),
        grid=(slabs,),
        in_specs=[SMALL, fixed((length, width)), fixed((width, length)), fixed((length, width))]
        + pieces.specs(rows, lambda i: (begin // 16 + i * (rows // 16)) * 16),
        out_specs=[fixed((length, width)), fixed((length, width))] + [grads] * count,
        out_shape=[
            jax.ShapeDtypeStruct((length, width), BF16),
            jax.ShapeDtypeStruct((length, width), BF16),
        ]
        + [jax.ShapeDtypeStruct((depth, slabs * rows, 2 * SLAB), BF16)] * count,
        scratch_shapes=[
            pltpu.VMEM((width, 2 * SLAB), BF16),
            pltpu.VMEM((SLAB, width), BF16),
            pltpu.VMEM((length, 2 * SLAB), BF16),
            pltpu.VMEM((width, 2 * SLAB), BF16),
            pltpu.VMEM((SLAB, width), BF16),
            pltpu.VMEM((length, width), F32),
            pltpu.VMEM((length, width), F32),
        ],
        compiler_params=params(),
        cost_estimate=cost(12.5 * slabs, 20 + 6 * slabs),
        name="feed",
    )(me, normed, normed_t, cotangent, *pieces.arrays)


def middle_kernel(layout, sums, me_ref, s_ref, c_ref, o0_ref, o1_ref, gain_ref, *refs):
    b_refs = refs[:sums]
    f_ref, a_ref, g_ref, w_all, total = refs[-5:]
    rows = w_all.shape[0] // len(layout)
    step = pl.program_id(0)

    @pl.when(step == 0)
    def _():
        for k, group in enumerate(grouped(refs[sums:], layout)):
            fill(w_all, aligned(me_ref[0] ^ k, rows), group, slice(None))

    back = b_refs[0][...].astype(F32)
    for ref in b_refs[1:]:
        back = back + ref[...].astype(F32)
    unit, inverse = unit_of(s_ref[...])
    scaled = back * gain_ref[3:4, :]
    first = c_ref[...].astype(F32) + inverse * (
        scaled - unit * jnp.mean(scaled * unit, axis=-1, keepdims=True)
    )
    f_ref[...] = first
    short = first.astype(BF16)
    a_ref[...] = dot(short, w_all[...], NT).astype(BF16)
    grads = [dot(ref[...], short, TN) for ref in (o0_ref, o1_ref)]

    @pl.when(step == 0)
    def _():
        total[:512, :] = grads[0]
        total[512:, :] = grads[1]

    @pl.when(step > 0)
    def _():
        total[:512, :] += grads[0]
        total[512:, :] += grads[1]

    @pl.when(step == pl.num_programs(0) - 1)
    def _():
        g_ref[...] = total[...].astype(BF16)


def middle(pieces, me, first_sum, cotangent, attended, gain, backs):
    length, width = first_sum.shape
    parts = pieces.count
    rows = width // parts
    return pl.pallas_call(
        lambda *refs: middle_kernel(pieces.layout, len(backs), *refs),
        grid=(length // TILE,),
        in_specs=[SMALL, by_rows(width), by_rows(width), by_rows(512), by_rows(512), fixed((16, 1024))]
        + [by_rows(width)] * len(backs)
        + pieces.specs(rows, lambda i: 0),
        out_specs=[by_rows(width), by_rows(1024), fixed((1024, width))],
        out_shape=[
            jax.ShapeDtypeStruct((length, width), F32),
            jax.ShapeDtypeStruct((length, 1024), BF16),
            jax.ShapeDtypeStruct((1024, width), BF16),
        ],
        scratch_shapes=[pltpu.VMEM((1024, width), BF16), pltpu.VMEM((1024, width), F32)],
        compiler_params=params(),
        cost_estimate=cost(9, 32),
        name="middle",
    )(me, first_sum, cotangent, *attended, gain, *backs, *pieces.arrays)


def raw_back_kernel(
    parts, me_ref, dq0_ref, dq1_ref, dkv0_ref, dkv1_ref, unit_ref, scale_ref, n_ref, cos_ref, sin_ref, gain_ref, wo_ref,
    b_ref, own_ref, sib_ref, total, gains,
):
    step = pl.program_id(0)
    rows = total.shape[0] // parts
    blocks = head_blocks()
    lane = lanes()
    first = (lane % HEAD_SIZE) < HEAD_SIZE // 2
    low = lane < HEAD_SIZE
    cosine, sine = cos_ref[...], sin_ref[...]
    sums = [None, None]
    for p in range(12):
        at = slice(p * 128, (p + 1) * 128)
        if p < 8:
            dq_ref = dq0_ref if p < 4 else dq1_ref
            grads = dq_ref[:, (p % 4) * 128 : (p % 4 + 1) * 128] * HEAD_SIZE**-0.5
        else:
            dkv_ref = dkv0_ref if p < 10 else dkv1_ref
            left = dkv_ref[:, (p % 2) * 256 : (p % 2) * 256 + 128]
            right = dkv_ref[:, (p % 2) * 256 + 128 : (p % 2) * 256 + 256]
            grads = jnp.where(low, left, pltpu.roll(right, 64, 1))
            values = jnp.where(low, pltpu.roll(left, 64, 1), right)
            b_ref[:, 512 + p * 128 : 640 + p * 128] = values.astype(BF16)
        turned = grads * cosine + swap_halves(grads * sine, first)
        unit = unit_ref[:, at].astype(F32)
        inverse = scale_ref[:, at].astype(F32)
        kind = 0 if p < 8 else 1
        part = jnp.sum(turned * unit, axis=0, keepdims=True)
        sums[kind] = part if sums[kind] is None else sums[kind] + part
        scaled = turned * gain_ref[1 + kind : 2 + kind, :128]
        b_ref[:, at] = (inverse * (scaled - unit * head_mean(scaled * unit, blocks))).astype(BF16)
    grad = dot(n_ref[...], b_ref[...], TN)

    @pl.when(step == 0)
    def _():
        total[...] = grad
        gains[...] = jnp.zeros_like(gains)

    @pl.when(step > 0)
    def _():
        total[...] += grad

    gains[0:1, :] += sums[0]
    gains[1:2, :] += sums[1]

    @pl.when(step == pl.num_programs(0) - 1)
    def _():
        me = me_ref[0]
        half = me >> 1
        core = me & 1
        more = gains[...].astype(BF16)
        for q in range(parts // 2):
            for s, ref in enumerate((own_ref, sib_ref)):
                source = aligned(2 * q + (core ^ s), rows)
                block = total[source, :].astype(BF16)
                ref[q ^ half, :rows, :] = block[:, :1024]
                ref[q ^ half, rows : 2 * rows, :] = block[:, 1024:]
                ref[q ^ half, 2 * rows : 3 * rows, :] = wo_ref[source, :]
                ref[q ^ half, 3 * rows :, :] = jnp.zeros((16, 1024), BF16)
                ref[q ^ half, 3 * rows :, :128] = more


def raw_back(parts, me, halves, units, normed, cosine, sine, gains, grad_out):
    length, width = normed.shape
    rows = 3 * (width // parts) + 16
    grads = fixed((parts // 2, rows, 1024))
    return pl.pallas_call(
        lambda *refs: raw_back_kernel(parts, *refs),
        grid=(length // TILE,),
        in_specs=[SMALL] + [by_rows(512)] * 4 + [by_rows(1536)] * 2 + [by_rows(width)]
        + [by_rows(128)] * 2
        + [fixed((16, 1024)), fixed((1024, width))],
        out_specs=[by_rows(2048), grads, grads],
        out_shape=[jax.ShapeDtypeStruct((length, 2048), BF16)]
        + [jax.ShapeDtypeStruct((parts // 2, rows, 1024), BF16)] * 2,
        scratch_shapes=[pltpu.VMEM((width, 2048), F32), pltpu.VMEM((16, 128), F32)],
        compiler_params=params(),
        cost_estimate=cost(10, 30),
        name="raw_back",
    )(me, *halves, *units, normed, cosine, sine, gains, grad_out)


def input_kernel(parts, me_ref, b_ref, x_ref, f_ref, gain_ref, *refs):
    out_ref, w_all = refs[2 * parts :]
    load_pairs(parts, me_ref, refs, w_all)
    unit, inverse = unit_of(x_ref[...].astype(F32))
    scaled = dot(b_ref[...], w_all[...], NT) * gain_ref[0:1, :]
    out_ref[...] = f_ref[...] + inverse * (
        scaled - unit * jnp.mean(scaled * unit, axis=-1, keepdims=True)
    )


def input_back(pieces, me, back_raw, x, back_first, gain):
    length, width = x.shape
    parts = len(pieces)
    arrays, specs = pair_specs(pieces, width // parts)
    return pl.pallas_call(
        lambda *refs: input_kernel(parts, *refs),
        grid=(length // TILE,),
        in_specs=[SMALL, by_rows(2048), by_rows(width), by_rows(width), fixed((16, 1024))] + specs,
        out_specs=by_rows(width),
        out_shape=jax.ShapeDtypeStruct((length, width), F32),
        scratch_shapes=[pltpu.VMEM((width, 2048), BF16)],
        compiler_params=params(),
        cost_estimate=cost(6, 18),
        name="input_back",
    )(me, back_raw, x, back_first, gain, *arrays)


def tables_of(numbers):
    length = numbers.shape[0]
    indices = jnp.arange(length, dtype=jnp.int32)
    starts = jnp.concatenate([jnp.ones((1,), dtype=bool), numbers[1:] != numbers[:-1]])
    begins = lax.cummax(jnp.where(starts, indices, jnp.zeros_like(numbers)), axis=0)
    offsets = (indices - begins).astype(F32).reshape(length, 1)
    frequency = ROPE_BASE ** (-jnp.arange(0, HEAD_SIZE, 2).astype(F32) / HEAD_SIZE)
    angles = offsets * frequency
    cosine = jnp.cos(angles)
    sine = jnp.sin(angles)
    same = (numbers[:, None] == jnp.arange(4)[None]).astype(F32)
    empty = jnp.zeros((length, 64), F32)
    return (
        jnp.concatenate([cosine] * 4, axis=1),
        jnp.concatenate([-sine, sine, -sine, sine], axis=1),
        jnp.concatenate([empty, -FAR * same, empty[:, :60]], axis=1),
        jnp.concatenate([empty, 1 - same, jnp.ones((length, 3)), empty[:, :57]], axis=1),
    )


def pack_kernel(chunks, o_ref, gate_ref, up_ref, down_ref, *out_refs):
    low = lanes(128) < 64
    out_refs[0][:128, :] = o_ref[...]
    places = [(c, i) for c, n in enumerate(chunks) for i in range(n)]
    for t, (c, i) in enumerate(places):
        row = i * 192 + (0 if c else 128)
        for side, ref in enumerate((gate_ref, up_ref)):
            for e in range(4):
                left, right = (18 * e + t) // 2, (18 * e + 9 + t) // 2
                a = ref[:, left * 128 : left * 128 + 128].astype(F32)
                b = ref[:, right * 128 : right * 128 + 128].astype(F32)
                both = pltpu.roll(jnp.where(low, b, a), 64, 1) if t % 2 else jnp.where(low, a, b)
                at = side * SLAB + e * 128
                out_refs[c][row : row + 128, at : at + 128] = both.astype(BF16)
        out_refs[c][row + 128 : row + 192, :] = down_ref[t * 64 : t * 64 + 64, :]


def pack_rows(chunks, w_output, w_gate, w_up, w_down):
    return pl.pallas_call(
        lambda *refs: pack_kernel(chunks, *refs),
        out_shape=[
            jax.ShapeDtypeStruct((n * 192 + (0 if c else 128), 1024), BF16)
            for c, n in enumerate(chunks)
        ],
        compiler_params=params(),
        cost_estimate=cost(0, 7),
        name="pack_rows",
    )(w_output, w_gate, w_up, w_down)


def unpack_kernel(*refs):
    *in_refs, gate_ref, up_ref, down_ref = refs
    low = lanes(128) < 64

    def rows_of(at, size, columns):
        for ref in in_refs:
            if at < ref.shape[0]:
                return ref[at : at + size, columns].astype(F32)
            at -= ref.shape[0]

    def segment(side, s, half):
        d = s // 9
        at = side * SLAB + (d // 2) * 128
        tile = rows_of((s % 9) * 192, 128, slice(at, at + 128))
        return tile if d % 2 == half else pltpu.roll(tile, 64, 1)

    for side, out in enumerate((gate_ref, up_ref)):
        for m in range(36):
            out[:, m * 128 : m * 128 + 128] = jnp.where(
                low, segment(side, 2 * m, 0), segment(side, 2 * m + 1, 1)
            )
    for t in range(9):
        down_ref[t * 64 : t * 64 + 64, :] = rows_of(t * 192 + 128, 64, slice(None))


def unpack_rows(*totals):
    return pl.pallas_call(
        unpack_kernel,
        out_shape=[
            jax.ShapeDtypeStruct((128, 4608), F32),
            jax.ShapeDtypeStruct((128, 4608), F32),
            jax.ShapeDtypeStruct((576, 1024), F32),
        ],
        compiler_params=params(),
        cost_estimate=cost(0, 14),
        name="unpack_rows",
    )(*totals)


def tie(*values):
    return lax.optimization_barrier(values)


def after(value, *tokens):
    return tie(value, *tokens)[0]


def hop(array, bit):
    return lax.ppermute(array, "shard", [(i, i ^ bit) for i in range(8)])


def gather_all(pack):
    return lax.all_gather(pack, "shard", axis=0, tiled=False)


def scatter_all(every):
    return lax.psum_scatter(every, "shard", scatter_dimension=0, tiled=True)[0]


def weave(near, far):
    groups = []
    for one, two in zip(near, far):
        groups += [list(one), list(two)]
    return Pieces(groups)


def add_parts(k, own, other, *more):
    total = own[k].astype(F32) + other[k].astype(F32)
    for term in more:
        total = total + term.astype(F32)
    return total


def rep_hop(array, pairs):
    return lax.ppermute(array.astype(BF16), "rep", pairs)


INWARD = [(0, 1), (3, 2)]
ACROSS = [(1, 2), (2, 1)]
OUTWARD = [(1, 0), (2, 3)]


def at_end(inner, outer):
    place = lax.axis_index("rep")
    return jnp.where((place == 0) | (place == 3), outer.astype(F32), inner)


def on_device(sizes, *arrays):
    (
        block_input, document_numbers, attn_gain, w_query, key_weight, value_weight, query_gain,
        key_gain, w_output, ffn_gain, w_gate, w_up, w_down, cotangent,
    ) = arrays
    reps, parts = sizes
    _, length, width = block_input.shape
    ff = w_gate.shape[1]
    paired = parts == 8 and reps == 4
    me = lax.axis_index("shard").astype(jnp.int32)
    place = me.reshape(1) if paired else jnp.zeros((1,), jnp.int32)
    x = block_input.reshape(length, width)
    back_out = cotangent.reshape(length, width)
    numbers = document_numbers.reshape(length)
    rows = width // parts
    seg = SLAB // parts
    slabs = ff // SLAB
    few = query_gain.shape[0]

    lane = jnp.arange(width)

    def spot(gain, times, size):
        share = gain.shape[0]
        wide = jnp.tile(gain, width // share)
        return jnp.where((lane < size * times) & ((lane % size) // share == me), wide, 0)

    empty = jnp.zeros((width,), BF16)
    gain_rows = [
        spot(attn_gain, 1, width),
        spot(query_gain, 2, HEAD_SIZE),
        spot(key_gain, 2, HEAD_SIZE),
        spot(ffn_gain, 1, width),
    ]
    first_pack = jnp.concatenate(
        [
            w_query,
            jnp.concatenate([key_weight, value_weight], axis=1),
            jnp.stack(gain_rows + [empty] * 12),
        ]
    )
    tables = tables_of(numbers)
    run = block_paired if paired else block_simple
    args = (me, place, x, back_out, tables, first_pack, w_output, w_gate, w_up, w_down)
    block_output, input_grad, attn_grad, feed_grads = run(*args)
    grad_gate, grad_up, grad_down = feed_grads
    grad_query = attn_grad[:rows]
    grad_key = attn_grad[rows : 2 * rows, :512]
    grad_value = attn_grad[rows : 2 * rows, 512:]

    def diagonal(*pairs):
        total = 0.0
        for weight, grad in pairs:
            total = total + jnp.sum(weight.astype(F32) * grad, axis=1)
        return total

    grad_gain_attn = diagonal(
        (w_query, grad_query), (key_weight, grad_key), (value_weight, grad_value)
    ) / attn_gain.astype(F32)
    grad_gain_ffn = diagonal((w_gate, grad_gate), (w_up, grad_up)) / ffn_gain.astype(F32)

    def small(row):
        both = attn_grad[3 * rows + row, :64] + attn_grad[3 * rows + row, 64:128]
        return lax.dynamic_slice(both, (me * few,), (few,))

    return (
        block_output[None],
        input_grad[None],
        grad_gain_attn,
        grad_query,
        grad_key,
        grad_value,
        small(0),
        small(1),
        attn_grad[2 * rows : 3 * rows],
        grad_gain_ffn,
        grad_gate,
        grad_up,
        grad_down,
    )


def block_simple(me, place, x, back_out, tables, first_pack, w_output, w_gate, w_up, w_down):
    rows, ff = w_gate.shape
    parts = x.shape[1] // rows
    seg = SLAB // parts
    slabs = ff // SLAB
    tall = rows + seg

    def columns(weight):
        cut = weight.reshape(rows, parts, slabs, seg).transpose(2, 0, 1, 3)
        return cut.reshape(slabs, rows, SLAB)

    pack = jnp.concatenate(
        [
            jnp.concatenate([columns(w_gate), columns(w_up)], axis=2),
            w_down.reshape(slabs, seg, x.shape[1]),
        ],
        axis=1,
    ).reshape(slabs * tall, 2 * SLAB)
    every = gather_all(first_pack)
    pairs = [(every[k], every[k], 1) for k in range(parts)]
    pieces = Pieces(stacked=gather_all(jnp.concatenate([w_output, pack])))
    normed_one, *units, q_aug, k_aug, v_aug, gains = project(pairs, place, x, tables)
    attended_0, q_back_0 = attend(q_aug, k_aug, v_aug, 0, 4)
    attended_1, q_back_1 = attend(q_aug, k_aug, v_aug, 4, 4)
    attended = (attended_0, attended_1)
    first_sum, normed_two, normed_two_t = output_rows(pieces, place, attended, x, gains)
    out, back, grads = feed(
        pieces, place, rows, slabs, normed_two, normed_two_t, back_out, False
    )
    total = lax.psum(scatter_all(grads), "rep").astype(F32).reshape(slabs, tall, 2 * SLAB)
    back_first, back_attended, grad_out = middle(
        pieces, place, first_sum, back_out, attended, gains, [back]
    )
    halves_0 = attend_back(q_back_0, k_aug, v_aug, attended_0, back_attended, 0, 4)
    halves_1 = attend_back(q_back_1, k_aug, v_aug, attended_1, back_attended, 4, 4)
    back_raw, own, sib = raw_back(
        parts, place, (halves_0[0], halves_1[0], halves_0[1], halves_1[1]), units, normed_one,
        tables[0], tables[1], gains, grad_out,
    )
    every = jnp.stack([own, sib], axis=1).reshape((parts,) + own.shape[1:])
    attn_grad = lax.psum(scatter_all(every), "rep").astype(F32)
    input_grad = input_back(pairs, place, back_raw, x, back_first, gains)

    def uncut(block):
        return block.reshape(slabs, rows, parts, seg).transpose(1, 2, 0, 3).reshape(rows, ff)

    feed_grads = (
        uncut(total[:, :rows, :SLAB]),
        uncut(total[:, :rows, SLAB:]),
        total[:, rows:, :].reshape(slabs * seg, x.shape[1]),
    )
    return (first_sum + out).astype(BF16), input_grad, attn_grad, feed_grads


def fence(outputs, *hops):
    found = tie(*outputs, *hops)
    return found[: len(outputs)], list(found[len(outputs) :])


def block_paired(me, place, x, back_out, tables, first_pack, w_output, w_gate, w_up, w_down):
    rows = w_gate.shape[0]
    chunks = (4, 3, 2)

    first = hop(first_pack, 2)
    second = hop(first_pack, 4)
    twin = hop(first_pack, 1)
    made, (first, second, twin) = fence(
        [*pack_rows(chunks, w_output, w_gate, w_up, w_down), *tables], first, second, twin
    )
    packs, tables = list(made[:3]), made[3:]
    corner_a = hop(second[:rows], 2)
    corner_b = hop(first[rows:], 4)
    far = [twin] + [hop(piece, 1) for piece in (first, second, corner_a, corner_b)]
    near = [first_pack, first, second, corner_a, corner_b]
    pairs = []
    for k in range(3):
        pairs += [(near[k], near[k], 1), (far[k], far[k], 1)]
    pairs += [(near[3], near[4], 0), (far[3], far[4], 0)]

    pack = after(packs[0], corner_a, corner_b)
    first, second, twin = hop(pack, 2), hop(pack, 4), hop(pack, 1)
    normed_one, *units, q_aug, k_aug, v_aug, gains = project(pairs, place, x, tables)
    (attended_0, q_back_0, k_aug), (first, second, twin) = fence(
        [*attend(q_aug, k_aug, v_aug, 0, 4), k_aug], first, second, twin
    )
    corner_a, corner_b = hop(second[:, :512], 2), hop(first[:, 512:], 4)
    far = [hop(first, 1), hop(second, 1)]
    packs[1] = after(packs[1], first, second)
    waiting = [hop(packs[1], bit) for bit in (1, 2, 4, 6)]
    (attended_1, q_back_1), (corner_a, corner_b, *far) = fence(
        attend(q_aug, k_aug, v_aug, 4, 4), corner_a, corner_b, *far
    )
    attended = (attended_0, attended_1)
    early = weave(
        [[pack], [first], [second], [corner_a, corner_b]],
        [[twin], [far[0]], [far[1]], [hop(corner_a, 1), hop(corner_b, 1)]],
    )
    first_sum, normed_two, normed_two_t = output_rows(early, place, attended, x, gains)

    def finish(pack, twin, first, second, corner):
        near = (first, second, corner)
        far = [hop(piece, 1) for piece in near]
        return weave([[pack]] + [[a] for a in near], [[twin]] + [[a] for a in far])

    def feed_step(pieces, begin, n, paired):
        return feed(pieces, place, begin, n, normed_two, normed_two_t, back_out, paired)

    (out_0, back_0, own_0, sib_0, normed_two), waiting = fence(
        [*feed_step(early, rows, chunks[0], True), normed_two], *waiting
    )
    later = finish(packs[1], *waiting)
    waiting = [hop(packs[2], bit) for bit in (1, 2, 4, 6)]
    other_0 = hop(after(sib_0, *later.arrays), 1)
    (out_1, back_1, stack_1, normed_two), (other_0, *waiting) = fence(
        [*feed_step(later, 0, chunks[1], False), normed_two], other_0, *waiting
    )
    grads_1 = scatter_all(stack_1)
    last = finish(packs[2], *waiting)
    moved_0 = hop(add_parts(3, own_0, other_0).astype(BF16), 2)
    (out_2, back_2, own_2, sib_2), (moved_0,) = fence(
        feed_step(last, 0, chunks[2], True), moved_0
    )
    other_2 = hop(sib_2, 1)
    first_0 = hop(add_parts(1, own_0, other_0).astype(BF16), 2)
    second_0 = hop(add_parts(2, own_0, other_0, moved_0).astype(BF16), 4)
    middles = middle(
        early, place, first_sum, back_out, attended, gains, [back_0, back_1, back_2]
    )
    (back_first, back_attended, grad_out), (other_2,) = fence(middles, other_2)
    moved_2 = hop(add_parts(3, own_2, other_2).astype(BF16), 4)
    halves = attend_back(q_back_0, k_aug, v_aug, attended_0, back_attended, 0, 4)
    (dq_0, dkv_0, back_attended), (first_0, second_0, grads_1) = fence(
        [*halves, back_attended], first_0, second_0, grads_1
    )
    total_1 = lax.psum(grads_1, "rep")
    grads_0 = add_parts(0, own_0, other_0, first_0, second_0)
    grads_0, back_attended = tie(grads_0, back_attended)
    inward_0 = rep_hop(grads_0, INWARD)
    halves = attend_back(q_back_1, k_aug, v_aug, attended_1, back_attended, 4, 4)
    (dq_1, dkv_1), (moved_2,) = fence(halves, moved_2)
    first_2 = hop(add_parts(1, own_2, other_2, moved_2).astype(BF16), 2)
    second_2 = hop(add_parts(2, own_2, other_2).astype(BF16), 4)
    result = raw_back(
        8, place, (dq_0, dq_1, dkv_0, dkv_1), units, normed_one, tables[0], tables[1], gains,
        grad_out,
    )
    (back_raw, own, sib), (first_2, second_2, inward_0, total_1) = fence(
        result, first_2, second_2, inward_0, total_1
    )
    other = hop(sib, 1)
    half_0 = grads_0 + inward_0.astype(F32)
    grads_2 = add_parts(0, own_2, other_2, first_2, second_2)
    back_raw, other, half_0, grads_2 = tie(back_raw, other, half_0, grads_2)
    terms = [add_parts(k, own, other).astype(BF16) for k in (1, 2, 3)]
    back_raw, *terms = tie(back_raw, *terms)
    steps = [hop(term, 2 * k) for k, term in zip((1, 2, 3), terms)]
    across_0 = rep_hop(half_0, ACROSS)
    inward_2 = rep_hop(grads_2, INWARD)
    input_grad = input_back(pairs, place, back_raw, x, back_first, gains)
    (input_grad,), (inward_2, across_0, *steps) = fence([input_grad], inward_2, across_0, *steps)
    attn_grad = add_parts(0, own, other, *steps)
    attn_grad, inward_2, across_0, first_sum = tie(attn_grad, inward_2, across_0, first_sum)
    inward = rep_hop(attn_grad, INWARD)
    total_0 = half_0 + across_0.astype(F32)
    outward_0 = rep_hop(total_0, OUTWARD)
    half_2 = grads_2 + inward_2.astype(F32)
    across_2 = rep_hop(half_2, ACROSS)
    outs = out_0.astype(F32) + out_1.astype(F32) + out_2.astype(F32)
    block_output = (first_sum + outs).astype(BF16)
    (block_output,), (inward, across_2) = fence([block_output], inward, across_2)
    half = attn_grad + inward.astype(F32)
    half, across_2 = tie(half, across_2)
    across = rep_hop(half, ACROSS)
    total_2 = half_2 + across_2.astype(F32)
    outward_2 = rep_hop(total_2, OUTWARD)
    total_2, across = tie(total_2, across)
    total = half + across.astype(F32)
    total, outward_2, outward_0 = tie(total, outward_2, outward_0)
    outward = rep_hop(total, OUTWARD)
    feed_grads = unpack_rows(at_end(total_0, outward_0), total_1, at_end(total_2, outward_2))
    (*feed_grads,), (outward,) = fence(feed_grads, outward)
    return block_output, input_grad, at_end(total, outward), feed_grads


def solution(mesh):
    sizes = (mesh.shape["rep"], mesh.shape["shard"])
    whole = P(("rep", "shard"), None, None)
    matrix = P("shard", None)
    vector = P("shard")
    in_specs = (
        whole, P(("rep", "shard"), None), vector, matrix, matrix, matrix, vector, vector, matrix,
        vector, matrix, matrix, matrix, whole,
    )
    out_specs = (
        whole, whole, vector, matrix, matrix, matrix, vector, vector, matrix, vector, matrix,
        matrix, matrix,
    )
    return jax.shard_map(
        lambda *arrays: on_device(sizes, *arrays),
        mesh=mesh,
        in_specs=in_specs,
        out_specs=out_specs,
        check_vma=False,
    )
```

time: 840 us -> 600 us (0.71)
  Pallas kernels: 70.2 us -> 296 us
  matrix products: 209 us -> 0 us
  local copies, waits for them, and re-layouts: 128 us -> 15.5 us
  waiting for transfers between devices: 248 us -> 146 us
  starting transfers between devices: 0.44 us -> 55.1 us
  blocking collectives: 51.4 us -> 0 us
  other arithmetic: 111 us -> 63.9 us
    pallas_call x0 -> x10, Pallas kernels: none -> 211 us  [the longest x3 129 us: feed(): pl.pallas_call(lambda *refs: feed_kernel(pieces.layout, paired, *refs), g...]
    dot_general x15 -> x0, matrix products: 209 us -> none  [einsum_result(): return jnp.einsum(form, left, right, preferred_element_type=jnp.float32)]
    ppermute x0 -> x53, waiting for transfers between devices: none -> 121 us  [the longest x44 68.1 us: hop(): return lax.ppermute(array, 'shard', [(i, i ^ bit) for i in range(8)])]
    reduce_scatter x4 -> x1, waiting for transfers between devices: 93.6 us -> 0.01 us  [scatter_all(): return lax.psum_scatter(every, 'shard', scatter_dimension=0, tiled=True)[0]]
    psum x4 -> x1, waiting for transfers between devices: 97.7 us -> 25.7 us  [block_paired(): total_1 = lax.psum(grads_1, 'rep')]
    all_gather x3 -> x0, waiting for transfers between devices: 55.7 us -> none  [gather(): return lax.all_gather(array, 'shard', axis=0, tiled=True)]
    ppermute x0 -> x53, starting transfers between devices: none -> 55 us  [the longest x44 31 us: hop(): return lax.ppermute(array, 'shard', [(i, i ^ bit) for i in range(8)])]
    unnamed x2 -> x0, blocking collectives: 41.2 us -> none
  transfers between devices with their start and end apart: 11 -> 55, of which waited for: 6 -> 25; matrix products, arithmetic and copies ran while one was open for 44% -> 9% of each run, Pallas kernels for 8% -> 50%
where the time goes in v2:
time: 600 us; the launch traced here: 592 us
  Pallas kernels  296 us (49%)
  waiting for transfers between devices  146 us (24%)
  other arithmetic  63.9 us (11%)
  starting transfers between devices  55.1 us (9%)
  local copies, waits for them, and re-layouts  15.5 us (3%)
  between operations  15 us (2%)
    pallas_call x3, Pallas kernels, feed(): pl.pallas_call(lambda *refs: feed_kernel(pieces.layout, paired, *refs), g...  129 us
    ppermute x44, waiting for transfers between devices, hop(): return lax.ppermute(array, 'shard', [(i, i ^ bit) for i in range(8)])  68.1 us
    ppermute x9, waiting for transfers between devices, rep_hop(): return lax.ppermute(array.astype(BF16), 'rep', pairs)  52.5 us
    pallas_call x2, Pallas kernels, attend_back(): pl.pallas_call(attend_back_kernel, grid=(groups,), in_specs=[pl.BlockSpec...  47.6 us
    pallas_call x2, Pallas kernels, attend(): pl.pallas_call(attend_kernel, grid=(groups,), in_specs=[pl.BlockSpec((2,...  37.6 us
    ppermute x44, starting transfers between devices, hop(): return lax.ppermute(array, 'shard', [(i, i ^ bit) for i in range(8)])  31 us
    psum x1, waiting for transfers between devices, block_paired(): total_1 = lax.psum(grads_1, 'rep')  25.7 us
    ppermute x9, starting transfers between devices, rep_hop(): return lax.ppermute(array.astype(BF16), 'rep', pairs)  24 us
  transfers between devices with their start and end apart: 55, of which 25 were waited for; matrix products, arithmetic and copies ran while one was open for 9% of the time, Pallas kernels for 50%

profile of v2, /device:TPU:0, one launch (start us, length us, event | category | flops | bytes accessed | tf_op | source)
XLA Modules:
  0.0 591.6 jit_solution(12283699723777018106)
XLA Ops:
  12.8 2.6 collective-permute-start.1
  21.7 4.6 pack_rows.1
  32.3 5.9 collective-permute-done.5.refs_18_.refs_17_
  46.7 16.0 %project.1 = (bf16[1024,1024]{1,0:T(8,128)(2,1)}, bf16[1024,1536]{1,0:T(8,128)(2,1)}, bf16[1024,1536]{1,0:T(8,128)(2,1)}, bf16[16,1024,128]{2,1,0:T(8,128)(2,1)}...) custom-call(s32[1]{0:T(128)} %bitcast.refs_0_, bf16[1024,1024]{1,0:T(8,128)(2,1)} %bitcast.69, ...), custom_call_target="tpu_custom_call" | custom-call | flops 8000000 | bytes 25000 | tf_op jit(solution)/shard_map/project/pallas_call | solution.py:203
  62.7 13.5 %attend.2 = (bf16[1024,512]{1,0:T(8,128)(2,1)}, bf16[8,1024,128]{2,1,0:T(8,128)(2,1)}) custom-call(bf16[16,1024,128]{2,1,0:T(8,128)(2,1)} %get-tuple-element.166.q_ref, bf16[8,1024,128]{2,1,0:T(8,128)(2,1)} %get-tuple-element.174.k_ref, bf16[8,1024,128]{2,1,0:T(8,128)(2,1)} %get-tuple-element.168.v_ref), custom_call_target="tpu_custom_call" | custom-call | flops 10000000 | bytes 8000 | tf_op jit(solution)/shard_map/attend/pallas_call | solution.py:264
  76.2 4.9 collective-permute-done.10.refs_9_.refs_8_.refs_13_
  83.7 2.2 slice.138
  88.2 24.1 %attend.3 = (bf16[1024,512]{1,0:T(8,128)(2,1)}, bf16[8,1024,128]{2,1,0:T(8,128)(2,1)}) custom-call(bf16[16,1024,128]{2,1,0:T(8,128)(2,1)} %get-tuple-element.166.q_ref, bf16[8,1024,128]{2,1,0:T(8,128)(2,1)} %get-tuple-element.174.k_ref, bf16[8,1024,128]{2,1,0:T(8,128)(2,1)} %get-tuple-element.168.v_ref), custom_call_target="tpu_custom_call" | custom-call | flops 10000000 | bytes 8000 | tf_op jit(solution)/shard_map/attend/pallas_call | solution.py:264
  116.5 3.6 collective-permute-done.17.refs_14_.refs_13_.refs_18_
  121.1 8.3 %output_rows.1 = (f32[1024,1024]{1,0:T(8,128)}, bf16[1024,1024]{1,0:T(8,128)(2,1)}, bf16[1024,1024]{1,0:T(8,128)(2,1)}) custom-call(s32[1]{0:T(128)} %bitcast.refs_0_, bf16[1024,512]{1,0:T(8,128)(2,1)} %get-tuple-element.175.refs_1_.refs_3_.o_ref, bf16[1024,512]{1,0:T(8,128)(2,1)} %get-tuple-element.180.refs_2_.refs_4_.o_ref, bf16[1024,1024]{1,0:T(8,128)(2,1)} %bitcast.70, ...), custom_call_target="tpu_custom_call" | custom-call | flops 5000000 | bytes 15000 | tf_op jit(solution)/shard_map/output_rows/pallas_call | solution.py:381
  129.4 54.0 %feed.3 = (bf16[1024,1024]{1,0:T(8,128)(2,1)}, bf16[1024,1024]{1,0:T(8,128)(2,1)}, bf16[4,768,1024]{2,1,0:T(8,128)(2,1)}, bf16[4,768,1024]{2,1,0:T(8,128)(2,1)}) custom-call(s32[1]{0:T(128)} %bitcast.refs_0_, bf16[1024,1024]{1,0:T(8,128)(2,1)} %get-tuple-element.209.refs_1_, bf16[1024,1024]{1,0:T(8,128)(2,1)} %get-tuple-element.189.refs_2_, ...), custom_call_target="tpu_custom_call" | custom-call | flops 50000000 | bytes 44000 | tf_op jit(solution)/shard_map/feed/pallas_call | solution.py:466
  184.1 2.4 collective-permute-done.22.refs_7_
  186.6 3.4 collective-permute-done.23.refs_9_
  194.7 42.6 %feed.4 = (bf16[1024,1024]{1,0:T(8,128)(2,1)}, bf16[1024,1024]{1,0:T(8,128)(2,1)}, bf16[8,576,1024]{2,1,0:T(8,128)(2,1)}) custom-call(s32[1]{0:T(128)} %bitcast.refs_0_, bf16[1024,1024]{1,0:T(8,128)(2,1)} %get-tuple-element.209.refs_1_, bf16[1024,1024]{1,0:T(8,128)(2,1)} %get-tuple-element.189.refs_2_, bf16[1024,1024]{1,0:T(8,128)(2,1)} %bitcast.66, ...), custom_call_target="tpu_custom_call" | custom-call | flops 37500000 | bytes 38000 | tf_op jit(solution)/shard_map/feed/pallas_call | solution.py:466
  237.4 5.6 fusion.6
  244.3 2.9 collective-permute-done.30.refs_7_
  250.0 32.6 %feed.5 = (bf16[1024,1024]{1,0:T(8,128)(2,1)}, bf16[1024,1024]{1,0:T(8,128)(2,1)}, bf16[4,384,1024]{2,1,0:T(8,128)(2,1)}, bf16[4,384,1024]{2,1,0:T(8,128)(2,1)}) custom-call(s32[1]{0:T(128)} %bitcast.refs_0_, bf16[1024,1024]{1,0:T(8,128)(2,1)} %get-tuple-element.209.refs_1_, bf16[1024,1024]{1,0:T(8,128)(2,1)} %get-tuple-element.189.refs_2_, ...), custom_call_target="tpu_custom_call" | custom-call | flops 25000000 | bytes 32000 | tf_op jit(solution)/shard_map/feed/pallas_call | solution.py:466
  282.6 10.1 %collective-permute-done.33 = bf16[768,1024]{1,0:T(8,128)(2,1)S(1)} collective-permute-done((bf16[768,1024]{1,0:T(8,128)(2,1)S(1)}, bf16[768,1024]{1,0:T(8,128)(2,1)S(1)}, u32[]{:S(2)}, u32[]{:S(2)}) %collective-permute-start.33) | collective-permute-done | bytes 1572896 | tf_op jit(solution)/shard_map/ppermute | solution.py:762
  293.5 4.3 fusion.1
  298.7 14.7 %middle.1 = (f32[1024,1024]{1,0:T(8,128)}, bf16[1024,1024]{1,0:T(8,128)(2,1)}, bf16[1024,1024]{1,0:T(8,128)(2,1)}) custom-call(s32[1]{0:T(128)} %bitcast.refs_0_, f32[1024,1024]{1,0:T(8,128)} %get-tuple-element.273.refs_1_, bf16[1024,1024]{1,0:T(8,128)(2,1)} %bitcast.68, bf16[1024,512]{1,0:T(8,128)(2,1)} %get-tuple-element.175.refs_1_.refs_3_.o_ref, ...), custom_call_target="tpu_custom_call" | custom-call | flops 9000000 | bytes 32000 | tf_op jit(solution)/shard_map/middle/pallas_call | solution.py:535
  313.4 3.2 fusion.14
  317.7 23.7 %attend_back.2 = (f32[1024,512]{1,0:T(8,128)}, f32[1024,512]{1,0:T(8,128)}) custom-call(bf16[8,1024,128]{2,1,0:T(8,128)(2,1)} %get-tuple-element.173.q_ref, bf16[8,1024,128]{2,1,0:T(8,128)(2,1)} %get-tuple-element.174.k_ref, bf16[8,1024,128]{2,1,0:T(8,128)(2,1)} %get-tuple-element.168.v_ref, bf16[1024,512]{1,0:T(8,128)(2,1)} %get-tuple-element.175.refs_1_.refs_3_.o_ref, ...), custom_call_target="tpu_custom_call" | custom-call | flops 20000000 | bytes 12000 | tf_op jit(solution)/shard_map/attend_back/pallas_call | solution.py:336
  341.3 10.2 %collective-permute-done.35 = bf16[768,1024]{1,0:T(8,128)(2,1)} collective-permute-done((bf16[768,1024]{1,0:T(8,128)(2,1)}, bf16[768,1024]{1,0:T(8,128)(2,1)}, u32[]{:S(2)}, u32[]{:S(2)}) %collective-permute-start.35) | collective-permute-done | bytes 1572896 | tf_op jit(solution)/shard_map/ppermute | solution.py:762
  351.5 4.2 fusion
  357.9 4.7 collective-permute-start.40
  363.9 24.0 %attend_back.3 = (f32[1024,512]{1,0:T(8,128)}, f32[1024,512]{1,0:T(8,128)}) custom-call(bf16[8,1024,128]{2,1,0:T(8,128)(2,1)} %get-tuple-element.231.q_ref, bf16[8,1024,128]{2,1,0:T(8,128)(2,1)} %get-tuple-element.174.k_ref, bf16[8,1024,128]{2,1,0:T(8,128)(2,1)} %get-tuple-element.168.v_ref, bf16[1024,512]{1,0:T(8,128)(2,1)} %get-tuple-element.180.refs_2_.refs_4_.o_ref, ...), custom_call_target="tpu_custom_call" | custom-call | flops 20000000 | bytes 12000 | tf_op jit(solution)/shard_map/attend_back/pallas_call | solution.py:336
  387.9 2.7 fusion.8
  391.1 19.8 %raw_back.1 = (bf16[1024,2048]{1,0:T(8,128)(2,1)}, bf16[4,400,1024]{2,1,0:T(8,128)(2,1)}, bf16[4,400,1024]{2,1,0:T(8,128)(2,1)}) custom-call(s32[1]{0:T(128)} %bitcast.refs_0_, f32[1024,512]{1,0:T(8,128)} %get-tuple-element.230.refs_1_, f32[1024,512]{1,0:T(8,128)} %get-tuple-element.240.refs_2_, f32[1024,512]{1,0:T(8,128)} %get-tuple-element.241.refs_3_, ...), custom_call_target="tpu_custom_call" | custom-call | flops 10000000 | bytes 30000 | tf_op jit(solution)/shard_map/raw_back/pallas_call | solution.py:621
  410.9 25.7 %all-reduce.2.cloned.1.call-done.refs_1_ = bf16[576,1024]{1,0:T(8,128)(2,1)} async-done(((bf16[576,1024]{1,0:T(8,128)(2,1)}), bf16[576,1024]{1,0:T(8,128)(2,1)}) %all-reduce.2.cloned.1.call-update) | async-done | bytes 1179664 | tf_op jit(solution)/shard_map/psum | solution.py:1016
  436.7 2.3 fusion.7
  439.2 2.7 convert_add_fusion.1
  444.1 2.0 collective-permute-start.43
  446.1 2.2 fusion.12
  452.9 5.3 collective-permute-start.42
  458.2 11.1 %input_back.1 = f32[1024,1024]{1,0:T(8,128)} custom-call(s32[1]{0:T(128)} %bitcast.refs_0_, bf16[1024,2048]{1,0:T(8,128)(2,1)} %get-tuple-element.261.refs_1_, bf16[1024,1024]{1,0:T(8,128)(2,1)} %bitcast.71, f32[1024,1024]{1,0:T(8,128)} %get-tuple-element.262.refs_3_, f32[16,1024]{1,0:T(8,128)} %get-tuple-element.181.refs_4_.refs_5_.refs_10_, ...), custom_call_target="tpu_custom_call" | custom-call | flops 6000000 | bytes 18000 | tf_op jit(solution)/shard_map/input_back/pallas_call | solution.py:651
  469.3 4.4 collective-permute-done.42
  473.7 14.1 %collective-permute-done.45 = bf16[400,1024]{1,0:T(8,128)(2,1)} collective-permute-done((bf16[400,1024]{1,0:T(8,128)(2,1)}, bf16[400,1024]{1,0:T(8,128)(2,1)}, u32[]{:S(2)}, u32[]{:S(2)}) %collective-permute-start.45) | collective-permute-done | bytes 819232 | tf_op jit(solution)/shard_map/ppermute | solution.py:762
  487.8 2.9 fusion.4
  493.2 6.5 %collective-permute-start.47 = (bf16[400,1024]{1,0:T(8,128)(2,1)S(1)}, bf16[400,1024]{1,0:T(8,128)(2,1)S(1)}, u32[]{:S(2)}, u32[]{:S(2)}) collective-permute-start(bf16[400,1024]{1,0:T(8,128)(2,1)S(1)} %convert_element_type.340), channel_id=1, source_target_pairs={{0,8},{24,16},{1,9},{25,17},{2,10},{26,18},{3,11},{27,19},{4,12},{... | collective-permute-start | bytes 2457608 | tf_op jit(solution)/shard_map/ppermute | solution.py:788
  503.0 3.0 add_convert_fusion
  506.0 9.7 %collective-permute-done.47 = bf16[400,1024]{1,0:T(8,128)(2,1)S(1)} collective-permute-done((bf16[400,1024]{1,0:T(8,128)(2,1)S(1)}, bf16[400,1024]{1,0:T(8,128)(2,1)S(1)}, u32[]{:S(2)}, u32[]{:S(2)}) %collective-permute-start.47) | collective-permute-done | bytes 819232 | tf_op jit(solution)/shard_map/ppermute | solution.py:788
  516.8 2.7 fusion.18
  521.2 19.7 %collective-permute-done.51 = bf16[768,1024]{1,0:T(8,128)(2,1)S(1)} collective-permute-done((bf16[768,1024]{1,0:T(8,128)(2,1)S(1)}, bf16[768,1024]{1,0:T(8,128)(2,1)S(1)}, u32[]{:S(2)}, u32[]{:S(2)}) %collective-permute-start.51) | collective-permute-done | bytes 1572896 | tf_op jit(solution)/shard_map/ppermute | solution.py:788
  540.9 14.0 %collective-permute-done.50 = bf16[384,1024]{1,0:T(8,128)(2,1)S(1)} collective-permute-done((bf16[384,1024]{1,0:T(8,128)(2,1)S(1)}, bf16[384,1024]{1,0:T(8,128)(2,1)S(1)}, u32[]{:S(2)}, u32[]{:S(2)}) %collective-permute-start.50) | collective-permute-done | bytes 786464 | tf_op jit(solution)/shard_map/ppermute | solution.py:788
  557.7 2.7 convert_select_fusion.2.refs_2_
  560.4 3.8 convert_select_fusion.refs_0_
  564.2 6.8 %unpack_rows.1 = (f32[128,4608]{1,0:T(8,128)}, f32[128,4608]{1,0:T(8,128)}, f32[576,1024]{1,0:T(8,128)}) custom-call(f32[768,1024]{1,0:T(8,128)} %convert_select_fusion.refs_0_, bf16[576,1024]{1,0:T(8,128)(2,1)} %all-reduce.2.cloned.1.call-done.refs_1_, f32[384,1024]{1,0:T(8,128)} %convert_select_fusion.2.refs_2_), custom_call_target="tpu_custom_call" | custom-call | bytes 14000 | tf_op jit(solution)/shard_map/unpack_rows/pallas_call | solution.py:740
  571.1 4.7 collective-permute-done.52
  (237 shorter events, 79.3 us)
Async XLA Ops:
  7.2 344.3 %reduce-scatter.2.cloned.1.call-start = ((), (), s32[]{:S(2)}) async-start(), calls=%async_computation.1 | async-start | bytes 10616832 | tf_op jit(solution)/shard_map/reduce_scatter | solution.py:770
  12.3 15.5 %collective-permute-start.2 = (bf16[272,1024]{1,0:T(8,128)(2,1)S(1)}, bf16[272,1024]{1,0:T(8,128)(2,1)S(1)}, u32[]{:S(2)}, u32[]{:S(2)}) collective-permute-start(bf16[272,1024]{1,0:T(8,128)(2,1)S(1)} %concatenate.38.refs_6_.refs_7_.refs_22_.refs_5_), channel_id=1, source_target_pairs={{0,1},{1,0},{2,3},{3,2},{4,5},{5,4},{6,7},{7,6},{8,9},{9,8},{10,11... | collective-permute-start | bytes 1671176 | tf_op jit(solution)/shard_map/ppermute | solution.py:762
  12.8 15.8 %collective-permute-start.1 = (bf16[272,1024]{1,0:T(8,128)(2,1)S(1)}, bf16[272,1024]{1,0:T(8,128)(2,1)S(1)}, u32[]{:S(2)}, u32[]{:S(2)}) collective-permute-start(bf16[272,1024]{1,0:T(8,128)(2,1)S(1)} %concatenate.38.refs_6_.refs_7_.refs_22_.refs_5_), channel_id=1, source_target_pairs={{0,4},{1,5},{2,6},{3,7},{4,0},{5,1},{6,2},{7,3},{8,12},{9,13},{10,... | collective-permute-start | bytes 1671176 | tf_op jit(solution)/shard_map/ppermute | solution.py:762
  15.4 14.7 %collective-permute-start = (bf16[272,1024]{1,0:T(8,128)(2,1)S(1)}, bf16[272,1024]{1,0:T(8,128)(2,1)S(1)}, u32[]{:S(2)}, u32[]{:S(2)}) collective-permute-start(bf16[272,1024]{1,0:T(8,128)(2,1)S(1)} %concatenate.38.refs_6_.refs_7_.refs_22_.refs_5_), channel_id=1, source_target_pairs={{0,2},{1,3},{2,0},{3,1},{4,6},{5,7},{6,4},{7,5},{8,10},{9,11},{10,... | collective-permute-start | bytes 1671176 | tf_op jit(solution)/shard_map/ppermute | solution.py:762
  30.1 8.3 %collective-permute-start.6 = (bf16[144,1024]{1,0:T(8,128)(2,1)S(1)}, bf16[144,1024]{1,0:T(8,128)(2,1)S(1)}, u32[]{:S(2)}, u32[]{:S(2)}) collective-permute-start(bf16[144,1024]{1,0:T(8,128)(2,1)S(1)} %slice.136), channel_id=1, source_target_pairs={{0,4},{1,5},{2,6},{3,7},{4,0},{5,1},{6,2},{7,3},{8,12},{9,13},{10,... | collective-permute-start | bytes 884744 | tf_op jit(solution)/shard_map/ppermute | solution.py:762
  30.5 7.7 %collective-permute-start.5 = (bf16[128,1024]{1,0:T(8,128)(2,1)S(1)}, bf16[128,1024]{1,0:T(8,128)(2,1)S(1)}, u32[]{:S(2)}, u32[]{:S(2)}) collective-permute-start(bf16[128,1024]{1,0:T(8,128)(2,1)S(1)} %slice.135), channel_id=1, source_target_pairs={{0,2},{1,3},{2,0},{3,1},{4,6},{5,7},{6,4},{7,5},{8,10},{9,11},{10,... | collective-permute-start | bytes 786440 | tf_op jit(solution)/shard_map/ppermute | solution.py:762
  38.5 37.7 %collective-permute-start.11 = (bf16[896,1024]{1,0:T(8,128)(2,1)}, bf16[896,1024]{1,0:T(8,128)(2,1)}, u32[]{:S(2)}, u32[]{:S(2)}) collective-permute-start(bf16[896,1024]{1,0:T(8,128)(2,1)} %get-tuple-element.172.refs_5_.refs_4_.refs_9_), channel_id=1, source_target_pairs={{0,1},{1,0},{2,3},{3,2},{4,5},{5,4},{6,7},{7,6},{8,9},{9,8},{10,11... | collective-permute-start | bytes 5505032 | tf_op jit(solution)/shard_map/ppermute | solution.py:762
  38.5 42.6 %collective-permute-start.10 = (bf16[896,1024]{1,0:T(8,128)(2,1)}, bf16[896,1024]{1,0:T(8,128)(2,1)S(1)}, u32[]{:S(2)}, u32[]{:S(2)}) collective-permute-start(bf16[896,1024]{1,0:T(8,128)(2,1)} %get-tuple-element.172.refs_5_.refs_4_.refs_9_), channel_id=1, source_target_pairs={{0,4},{1,5},{2,6},{3,7},{4,0},{5,1},{6,2},{7,3},{8,12},{9,13},{10,... | collective-permute-start | bytes 5505032 | tf_op jit(solution)/shard_map/ppermute | solution.py:762
  39.7 42.4 %collective-permute-start.9 = (bf16[896,1024]{1,0:T(8,128)(2,1)}, bf16[896,1024]{1,0:T(8,128)(2,1)}, u32[]{:S(2)}, u32[]{:S(2)}) collective-permute-start(bf16[896,1024]{1,0:T(8,128)(2,1)} %get-tuple-element.172.refs_5_.refs_4_.refs_9_), channel_id=1, source_target_pairs={{0,2},{1,3},{2,0},{3,1},{4,6},{5,7},{6,4},{7,5},{8,10},{9,11},{10,... | collective-permute-start | bytes 5505032 | tf_op jit(solution)/shard_map/ppermute | solution.py:762
  82.1 30.2 %collective-permute-start.15 = (bf16[896,1024]{1,0:T(8,128)(2,1)S(1)}, bf16[896,1024]{1,0:T(8,128)(2,1)}, u32[]{:S(2)}, u32[]{:S(2)}) collective-permute-start(bf16[896,1024]{1,0:T(8,128)(2,1)S(1)} %collective-permute-done.10.refs_9_.refs_8_.refs_13_), channel_id=1, source_target_pairs={{0,1},{1,0},{2,3},{3,2},{4,5},{5,4},{6,7},{7,6},{8,9},{9,8},{10,11... | collective-permute-start | bytes 5505032 | tf_op jit(solution)/shard_map/ppermute | solution.py:762
  82.1 30.2 %collective-permute-start.14 = (bf16[896,1024]{1,0:T(8,128)(2,1)}, bf16[896,1024]{1,0:T(8,128)(2,1)}, u32[]{:S(2)}, u32[]{:S(2)}) collective-permute-start(bf16[896,1024]{1,0:T(8,128)(2,1)} %collective-permute-done.9.refs_7_.refs_6_.refs_11_), channel_id=1, source_target_pairs={{0,1},{1,0},{2,3},{3,2},{4,5},{5,4},{6,7},{7,6},{8,9},{9,8},{10,11... | collective-permute-start | bytes 5505032 | tf_op jit(solution)/shard_map/ppermute | solution.py:762
  85.9 26.4 %collective-permute-start.13 = (bf16[896,512]{1,0:T(8,128)(2,1)}, bf16[896,512]{1,0:T(8,128)(2,1)S(1)}, u32[]{:S(2)}, u32[]{:S(2)}) collective-permute-start(bf16[896,512]{1,0:T(8,128)(2,1)} %slice.138), channel_id=1, source_target_pairs={{0,4},{1,5},{2,6},{3,7},{4,0},{5,1},{6,2},{7,3},{8,12},{9,13},{10,... | collective-permute-start | bytes 2752520 | tf_op jit(solution)/shard_map/ppermute | solution.py:762
  86.7 25.6 %collective-permute-start.12 = (bf16[896,512]{1,0:T(8,128)(2,1)}, bf16[896,512]{1,0:T(8,128)(2,1)}, u32[]{:S(2)}, u32[]{:S(2)}) collective-permute-start(bf16[896,512]{1,0:T(8,128)(2,1)} %slice.137), channel_id=1, source_target_pairs={{0,2},{1,3},{2,0},{3,1},{4,6},{5,7},{6,4},{7,5},{8,10},{9,11},{10,... | collective-permute-start | bytes 2752520 | tf_op jit(solution)/shard_map/ppermute | solution.py:762
  112.4 70.9 %collective-permute-start.21 = (bf16[576,1024]{1,0:T(8,128)(2,1)}, bf16[576,1024]{1,0:T(8,128)(2,1)S(1)}, u32[]{:S(2)}, u32[]{:S(2)}) collective-permute-start(bf16[576,1024]{1,0:T(8,128)(2,1)} %get-tuple-element.195.refs_4_), channel_id=1, source_target_pairs={{0,6},{1,7},{2,4},{3,5},{4,2},{5,3},{6,0},{7,1},{8,14},{9,15},{10,... | collective-permute-start | bytes 3538952 | tf_op jit(solution)/shard_map/ppermute | solution.py:762
  113.7 69.7 %collective-permute-start.20 = (bf16[576,1024]{1,0:T(8,128)(2,1)}, bf16[576,1024]{1,0:T(8,128)(2,1)}, u32[]{:S(2)}, u32[]{:S(2)}) collective-permute-start(bf16[576,1024]{1,0:T(8,128)(2,1)} %get-tuple-element.195.refs_4_), channel_id=1, source_target_pairs={{0,4},{1,5},{2,6},{3,7},{4,0},{5,1},{6,2},{7,3},{8,12},{9,13},{10,... | collective-permute-start | bytes 3538952 | tf_op jit(solution)/shard_map/ppermute | solution.py:762
  114.5 68.9 %collective-permute-start.19 = (bf16[576,1024]{1,0:T(8,128)(2,1)}, bf16[576,1024]{1,0:T(8,128)(2,1)}, u32[]{:S(2)}, u32[]{:S(2)}) collective-permute-start(bf16[576,1024]{1,0:T(8,128)(2,1)} %get-tuple-element.195.refs_4_), channel_id=1, source_target_pairs={{0,2},{1,3},{2,0},{3,1},{4,6},{5,7},{6,4},{7,5},{8,10},{9,11},{10,... | collective-permute-start | bytes 3538952 | tf_op jit(solution)/shard_map/ppermute | solution.py:762
  116.0 67.4 %collective-permute-start.18 = (bf16[576,1024]{1,0:T(8,128)(2,1)}, bf16[576,1024]{1,0:T(8,128)(2,1)}, u32[]{:S(2)}, u32[]{:S(2)}) collective-permute-start(bf16[576,1024]{1,0:T(8,128)(2,1)} %get-tuple-element.195.refs_4_), channel_id=1, source_target_pairs={{0,1},{1,0},{2,3},{3,2},{4,5},{5,4},{6,7},{7,6},{8,9},{9,8},{10,11... | collective-permute-start | bytes 3538952 | tf_op jit(solution)/shard_map/ppermute | solution.py:762
  116.0 4.1 collective-permute-start.17
  183.6 6.3 %collective-permute-start.23 = (bf16[576,1024]{1,0:T(8,128)(2,1)}, bf16[576,1024]{1,0:T(8,128)(2,1)S(1)}, u32[]{:S(2)}, u32[]{:S(2)}) collective-permute-start(bf16[576,1024]{1,0:T(8,128)(2,1)} %collective-permute-done.20.refs_8_), channel_id=1, source_target_pairs={{0,1},{1,0},{2,3},{3,2},{4,5},{5,4},{6,7},{7,6},{8,9},{9,8},{10,11... | collective-permute-start | bytes 3538952 | tf_op jit(solution)/shard_map/ppermute | solution.py:762
  184.0 5.9 %collective-permute-start.24 = (bf16[576,1024]{1,0:T(8,128)(2,1)S(1)}, bf16[576,1024]{1,0:T(8,128)(2,1)S(1)}, u32[]{:S(2)}, u32[]{:S(2)}) collective-permute-start(bf16[576,1024]{1,0:T(8,128)(2,1)S(1)} %collective-permute-done.21.refs_10_), channel_id=1, source_target_pairs={{0,1},{1,0},{2,3},{3,2},{4,5},{5,4},{6,7},{7,6},{8,9},{9,8},{10,11... | collective-permute-start | bytes 3538952 | tf_op jit(solution)/shard_map/ppermute | solution.py:762
  191.0 46.3 %collective-permute-start.25 = (bf16[4,768,1024]{2,1,0:T(8,128)(2,1)}, bf16[4,768,1024]{2,1,0:T(8,128)(2,1)}, u32[]{:S(2)}, u32[]{:S(2)}) collective-permute-start(bf16[4,768,1024]{2,1,0:T(8,128)(2,1)} %get-tuple-element.206), channel_id=1, source_target_pairs={{0,1},{1,0},{2,3},{3,2},{4,5},{5,4},{6,7},{7,6},{8,9},{9,8},{10,11... | collective-permute-start | bytes 18874376 | tf_op jit(solution)/shard_map/ppermute | solution.py:762
  191.2 46.1 %collective-permute-start.29 = (bf16[384,1024]{1,0:T(8,128)(2,1)}, bf16[384,1024]{1,0:T(8,128)(2,1)}, u32[]{:S(2)}, u32[]{:S(2)}) collective-permute-start(bf16[384,1024]{1,0:T(8,128)(2,1)} %get-tuple-element.207.refs_4_), channel_id=1, source_target_pairs={{0,6},{1,7},{2,4},{3,5},{4,2},{5,3},{6,0},{7,1},{8,14},{9,15},{10,... | collective-permute-start | bytes 2359304 | tf_op jit(solution)/shard_map/ppermute | solution.py:762
  192.4 44.9 %collective-permute-start.28 = (bf16[384,1024]{1,0:T(8,128)(2,1)}, bf16[384,1024]{1,0:T(8,128)(2,1)}, u32[]{:S(2)}, u32[]{:S(2)}) collective-permute-start(bf16[384,1024]{1,0:T(8,128)(2,1)} %get-tuple-element.207.refs_4_), channel_id=1, source_target_pairs={{0,4},{1,5},{2,6},{3,7},{4,0},{5,1},{6,2},{7,3},{8,12},{9,13},{10,... | collective-permute-start | bytes 2359304 | tf_op jit(solution)/shard_map/ppermute | solution.py:762
  193.2 44.1 %collective-permute-start.27 = (bf16[384,1024]{1,0:T(8,128)(2,1)}, bf16[384,1024]{1,0:T(8,128)(2,1)}, u32[]{:S(2)}, u32[]{:S(2)}) collective-permute-start(bf16[384,1024]{1,0:T(8,128)(2,1)} %get-tuple-element.207.refs_4_), channel_id=1, source_target_pairs={{0,2},{1,3},{2,0},{3,1},{4,6},{5,7},{6,4},{7,5},{8,10},{9,11},{10,... | collective-permute-start | bytes 2359304 | tf_op jit(solution)/shard_map/ppermute | solution.py:762
  194.7 42.6 %collective-permute-start.26 = (bf16[384,1024]{1,0:T(8,128)(2,1)}, bf16[384,1024]{1,0:T(8,128)(2,1)}, u32[]{:S(2)}, u32[]{:S(2)}) collective-permute-start(bf16[384,1024]{1,0:T(8,128)(2,1)} %get-tuple-element.207.refs_4_), channel_id=1, source_target_pairs={{0,1},{1,0},{2,3},{3,2},{4,5},{5,4},{6,7},{7,6},{8,9},{9,8},{10,11... | collective-permute-start | bytes 2359304 | tf_op jit(solution)/shard_map/ppermute | solution.py:762
  237.3 199.3 %all-reduce.2.cloned.1.call-start = ((), (), s32[]{:S(2)}) async-start(), calls=%async_computation.2 | async-start | bytes 2359296 | tf_op jit(solution)/shard_map/psum | solution.py:1016
  243.0 49.7 %collective-permute-start.33 = (bf16[768,1024]{1,0:T(8,128)(2,1)S(1)}, bf16[768,1024]{1,0:T(8,128)(2,1)S(1)}, u32[]{:S(2)}, u32[]{:S(2)}) collective-permute-start(bf16[768,1024]{1,0:T(8,128)(2,1)S(1)} %get-tuple-element.308), channel_id=1, source_target_pairs={{0,2},{1,3},{2,0},{3,1},{4,6},{5,7},{6,4},{7,5},{8,10},{9,11},{10,... | collective-permute-start | bytes 4718600 | tf_op jit(solution)/shard_map/ppermute | solution.py:762
  243.8 4.6 collective-permute-start.31
  244.1 6.0 %collective-permute-start.32 = (bf16[384,1024]{1,0:T(8,128)(2,1)}, bf16[384,1024]{1,0:T(8,128)(2,1)}, u32[]{:S(2)}, u32[]{:S(2)}) collective-permute-start(bf16[384,1024]{1,0:T(8,128)(2,1)} %collective-permute-done.29.refs_10_), channel_id=1, source_target_pairs={{0,1},{1,0},{2,3},{3,2},{4,5},{5,4},{6,7},{7,6},{8,9},{9,8},{10,11... | collective-permute-start | bytes 2359304 | tf_op jit(solution)/shard_map/ppermute | solution.py:762
  292.7 20.7 %collective-permute-start.34 = (bf16[4,384,1024]{2,1,0:T(8,128)(2,1)}, bf16[4,384,1024]{2,1,0:T(8,128)(2,1)}, u32[]{:S(2)}, u32[]{:S(2)}) collective-permute-start(bf16[4,384,1024]{2,1,0:T(8,128)(2,1)} %get-tuple-element.224), channel_id=1, source_target_pairs={{0,1},{1,0},{2,3},{3,2},{4,5},{5,4},{6,7},{7,6},{8,9},{9,8},{10,11... | collective-permute-start | bytes 9437192 | tf_op jit(solution)/shard_map/ppermute | solution.py:762
  292.7 58.8 %collective-permute-start.35 = (bf16[768,1024]{1,0:T(8,128)(2,1)}, bf16[768,1024]{1,0:T(8,128)(2,1)}, u32[]{:S(2)}, u32[]{:S(2)}) collective-permute-start(bf16[768,1024]{1,0:T(8,128)(2,1)} %get-tuple-element.307), channel_id=1, source_target_pairs={{0,2},{1,3},{2,0},{3,1},{4,6},{5,7},{6,4},{7,5},{8,10},{9,11},{10,... | collective-permute-start | bytes 4718600 | tf_op jit(solution)/shard_map/ppermute | solution.py:762
  297.8 53.8 %collective-permute-start.36 = (bf16[768,1024]{1,0:T(8,128)(2,1)}, bf16[768,1024]{1,0:T(8,128)(2,1)}, u32[]{:S(2)}, u32[]{:S(2)}) collective-permute-start(bf16[768,1024]{1,0:T(8,128)(2,1)} %fusion.1), channel_id=1, source_target_pairs={{0,4},{1,5},{2,6},{3,7},{4,0},{5,1},{6,2},{7,3},{8,12},{9,13},{10,... | collective-permute-start | bytes 4718600 | tf_op jit(solution)/shard_map/ppermute | solution.py:762
  316.6 71.3 %collective-permute-start.37 = (bf16[384,1024]{1,0:T(8,128)(2,1)}, bf16[384,1024]{1,0:T(8,128)(2,1)}, u32[]{:S(2)}, u32[]{:S(2)}) collective-permute-start(bf16[384,1024]{1,0:T(8,128)(2,1)} %get-tuple-element.313), channel_id=1, source_target_pairs={{0,4},{1,5},{2,6},{3,7},{4,0},{5,1},{6,2},{7,3},{8,12},{9,13},{10,... | collective-permute-start | bytes 2359304 | tf_op jit(solution)/shard_map/ppermute | solution.py:762
  357.9 78.8 %collective-permute-start.40 = (bf16[768,1024]{1,0:T(8,128)(2,1)}, bf16[768,1024]{1,0:T(8,128)(2,1)}, u32[]{:S(2)}, u32[]{:S(2)}) collective-permute-start(bf16[768,1024]{1,0:T(8,128)(2,1)} %convert_element_type.311), channel_id=1, source_target_pairs={{0,8},{24,16},{1,9},{25,17},{2,10},{26,18},{3,11},{27,19},{4,12},{... | collective-permute-start | bytes 4718600 | tf_op jit(solution)/shard_map/ppermute | solution.py:788
  362.6 48.3 %collective-permute-start.39 = (bf16[384,1024]{1,0:T(8,128)(2,1)}, bf16[384,1024]{1,0:T(8,128)(2,1)}, u32[]{:S(2)}, u32[]{:S(2)}) collective-permute-start(bf16[384,1024]{1,0:T(8,128)(2,1)} %get-tuple-element.312), channel_id=1, source_target_pairs={{0,4},{1,5},{2,6},{3,7},{4,0},{5,1},{6,2},{7,3},{8,12},{9,13},{10,... | collective-permute-start | bytes 2359304 | tf_op jit(solution)/shard_map/ppermute | solution.py:762
  390.5 20.4 %collective-permute-start.38 = (bf16[384,1024]{1,0:T(8,128)(2,1)}, bf16[384,1024]{1,0:T(8,128)(2,1)}, u32[]{:S(2)}, u32[]{:S(2)}) collective-permute-start(bf16[384,1024]{1,0:T(8,128)(2,1)} %fusion.8), channel_id=1, source_target_pairs={{0,2},{1,3},{2,0},{3,1},{4,6},{5,7},{6,4},{7,5},{8,10},{9,11},{10,... | collective-permute-start | bytes 2359304 | tf_op jit(solution)/shard_map/ppermute | solution.py:762
  436.6 6.1 %collective-permute-start.41 = (bf16[4,400,1024]{2,1,0:T(8,128)(2,1)}, bf16[4,400,1024]{2,1,0:T(8,128)(2,1)S(1)}, u32[]{:S(2)}, u32[]{:S(2)}) collective-permute-start(bf16[4,400,1024]{2,1,0:T(8,128)(2,1)} %get-tuple-element.255), channel_id=1, source_target_pairs={{0,1},{1,0},{2,3},{3,2},{4,5},{5,4},{6,7},{7,6},{8,9},{9,8},{10,11... | collective-permute-start | bytes 9830408 | tf_op jit(solution)/shard_map/ppermute | solution.py:762
  444.1 43.8 %collective-permute-start.43 = (bf16[768,1024]{1,0:T(8,128)(2,1)}, bf16[768,1024]{1,0:T(8,128)(2,1)}, u32[]{:S(2)}, u32[]{:S(2)}) collective-permute-start(bf16[768,1024]{1,0:T(8,128)(2,1)} %convert_element_type.332), channel_id=1, source_target_pairs={{8,16},{16,8},{9,17},{17,9},{10,18},{18,10},{11,19},{19,11},{12,20... | collective-permute-start | bytes 4718600 | tf_op jit(solution)/shard_map/ppermute | solution.py:788
  448.4 25.4 %collective-permute-start.44 = (bf16[400,1024]{1,0:T(8,128)(2,1)}, bf16[400,1024]{1,0:T(8,128)(2,1)}, u32[]{:S(2)}, u32[]{:S(2)}) collective-permute-start(bf16[400,1024]{1,0:T(8,128)(2,1)} %get-tuple-element.265), channel_id=1, source_target_pairs={{0,2},{1,3},{2,0},{3,1},{4,6},{5,7},{6,4},{7,5},{8,10},{9,11},{10,... | collective-permute-start | bytes 2457608 | tf_op jit(solution)/shard_map/ppermute | solution.py:762
  449.8 38.0 %collective-permute-start.45 = (bf16[400,1024]{1,0:T(8,128)(2,1)}, bf16[400,1024]{1,0:T(8,128)(2,1)}, u32[]{:S(2)}, u32[]{:S(2)}) collective-permute-start(bf16[400,1024]{1,0:T(8,128)(2,1)} %get-tuple-element.266), channel_id=1, source_target_pairs={{0,4},{1,5},{2,6},{3,7},{4,0},{5,1},{6,2},{7,3},{8,12},{9,13},{10,... | collective-permute-start | bytes 2457608 | tf_op jit(solution)/shard_map/ppermute | solution.py:762
  451.3 36.5 %collective-permute-start.46 = (bf16[400,1024]{1,0:T(8,128)(2,1)}, bf16[400,1024]{1,0:T(8,128)(2,1)}, u32[]{:S(2)}, u32[]{:S(2)}) collective-permute-start(bf16[400,1024]{1,0:T(8,128)(2,1)} %get-tuple-element.267), channel_id=1, source_target_pairs={{0,6},{1,7},{2,4},{3,5},{4,2},{5,3},{6,0},{7,1},{8,14},{9,15},{10,... | collective-permute-start | bytes 2457608 | tf_op jit(solution)/shard_map/ppermute | solution.py:762
  452.9 20.9 %collective-permute-start.42 = (bf16[384,1024]{1,0:T(8,128)(2,1)}, bf16[384,1024]{1,0:T(8,128)(2,1)}, u32[]{:S(2)}, u32[]{:S(2)}) collective-permute-start(bf16[384,1024]{1,0:T(8,128)(2,1)} %convert_element_type.331), channel_id=1, source_target_pairs={{0,8},{24,16},{1,9},{25,17},{2,10},{26,18},{3,11},{27,19},{4,12},{... | collective-permute-start | bytes 2359304 | tf_op jit(solution)/shard_map/ppermute | solution.py:788
  492.3 13.7 %collective-permute-start.48 = (bf16[384,1024]{1,0:T(8,128)(2,1)S(1)}, bf16[384,1024]{1,0:T(8,128)(2,1)S(1)}, u32[]{:S(2)}, u32[]{:S(2)}) collective-permute-start(bf16[384,1024]{1,0:T(8,128)(2,1)S(1)} %fusion.9), channel_id=1, source_target_pairs={{8,16},{16,8},{9,17},{17,9},{10,18},{18,10},{11,19},{19,11},{12,20... | collective-permute-start | bytes 2359304 | tf_op jit(solution)/shard_map/ppermute | solution.py:788
  493.2 22.6 %collective-permute-start.47 = (bf16[400,1024]{1,0:T(8,128)(2,1)S(1)}, bf16[400,1024]{1,0:T(8,128)(2,1)S(1)}, u32[]{:S(2)}, u32[]{:S(2)}) collective-permute-start(bf16[400,1024]{1,0:T(8,128)(2,1)S(1)} %convert_element_type.340), channel_id=1, source_target_pairs={{0,8},{24,16},{1,9},{25,17},{2,10},{26,18},{3,11},{27,19},{4,12},{... | collective-permute-start | bytes 2457608 | tf_op jit(solution)/shard_map/ppermute | solution.py:788
  501.7 39.2 %collective-permute-start.51 = (bf16[768,1024]{1,0:T(8,128)(2,1)S(1)}, bf16[768,1024]{1,0:T(8,128)(2,1)S(1)}, u32[]{:S(2)}, u32[]{:S(2)}) collective-permute-start(bf16[768,1024]{1,0:T(8,128)(2,1)S(1)} %fusion.2), channel_id=1, source_target_pairs={{8,0},{16,24},{9,1},{17,25},{10,2},{18,26},{11,3},{19,27},{12,4},{... | collective-permute-start | bytes 4718600 | tf_op jit(solution)/shard_map/ppermute | solution.py:788
  516.1 4.8 collective-permute-start.49
  519.6 35.3 %collective-permute-start.50 = (bf16[384,1024]{1,0:T(8,128)(2,1)S(1)}, bf16[384,1024]{1,0:T(8,128)(2,1)S(1)}, u32[]{:S(2)}, u32[]{:S(2)}) collective-permute-start(bf16[384,1024]{1,0:T(8,128)(2,1)S(1)} %get-tuple-element.305), channel_id=1, source_target_pairs={{8,0},{16,24},{9,1},{17,25},{10,2},{18,26},{11,3},{19,27},{12,4},{... | collective-permute-start | bytes 2359304 | tf_op jit(solution)/shard_map/ppermute | solution.py:788
  556.2 19.6 %collective-permute-start.52 = (bf16[400,1024]{1,0:T(8,128)(2,1)}, bf16[400,1024]{1,0:T(8,128)(2,1)}, u32[]{:S(2)}, u32[]{:S(2)}) collective-permute-start(bf16[400,1024]{1,0:T(8,128)(2,1)} %convert_element_type.353), channel_id=1, source_target_pairs={{8,0},{16,24},{9,1},{17,25},{10,2},{18,26},{11,3},{19,27},{12,4},{... | collective-permute-start | bytes 2457608 | tf_op jit(solution)/shard_map/ppermute | solution.py:788
  (52 other events, 331.1 us)
Sparse Core Ops, SparseCore 0:
  237.4 112.4 reduce-scatter.1
  362.7 73.8 all-reduce.1

commit v3 on v2

--- a/solution.py
+++ b/solution.py
@@ -940,7 +940,7 @@
 
 def block_paired(me, place, x, back_out, tables, first_pack, w_output, w_gate, w_up, w_down):
     rows = w_gate.shape[0]
-    chunks = (4, 3, 2)
+    chunks = (3, 3, 3)
 
     first = hop(first_pack, 2)
     second = hop(first_pack, 4)
@@ -986,79 +986,65 @@
     def feed_step(pieces, begin, n, paired):
         return feed(pieces, place, begin, n, normed_two, normed_two_t, back_out, paired)
 
-    (out_0, back_0, own_0, sib_0, normed_two), waiting = fence(
-        [*feed_step(early, rows, chunks[0], True), normed_two], *waiting
-    )
+    (out_0, back_0, stack_0, normed_two), waiting = fence(
+        [*feed_step(early, rows, chunks[0], False), normed_two], *waiting
+    )
+    grads_0 = scatter_all(stack_0)
     later = finish(packs[1], *waiting)
     waiting = [hop(packs[2], bit) for bit in (1, 2, 4, 6)]
-    other_0 = hop(after(sib_0, *later.arrays), 1)
-    (out_1, back_1, stack_1, normed_two), (other_0, *waiting) = fence(
-        [*feed_step(later, 0, chunks[1], False), normed_two], other_0, *waiting
-    )
-    grads_1 = scatter_all(stack_1)
+    (out_1, back_1, stack_1, normed_two), waiting = fence(
+        [*feed_step(later, 0, chunks[1], False), normed_two], *waiting
+    )
     last = finish(packs[2], *waiting)
-    moved_0 = hop(add_parts(3, own_0, other_0).astype(BF16), 2)
-    (out_2, back_2, own_2, sib_2), (moved_0,) = fence(
-        feed_step(last, 0, chunks[2], True), moved_0
-    )
+    (out_2, back_2, own_2, sib_2), (grads_0,) = fence(
+        feed_step(last, 0, chunks[2], True), grads_0
+    )
+    grads_1 = scatter_all(after(stack_1, grads_0))
     other_2 = hop(sib_2, 1)
-    first_0 = hop(add_parts(1, own_0, other_0).astype(BF16), 2)
-    second_0 = hop(add_parts(2, own_0, other_0, moved_0).astype(BF16), 4)
     middles = middle(
         early, place, first_sum, back_out, attended, gains, [back_0, back_1, back_2]
     )
     (back_first, back_attended, grad_out), (other_2,) = fence(middles, other_2)
     moved_2 = hop(add_parts(3, own_2, other_2).astype(BF16), 4)
     halves = attend_back(q_back_0, k_aug, v_aug, attended_0, back_attended, 0, 4)
-    (dq_0, dkv_0, back_attended), (first_0, second_0, grads_1) = fence(
-        [*halves, back_attended], first_0, second_0, grads_1
-    )
-    total_1 = lax.psum(grads_1, "rep")
-    grads_0 = add_parts(0, own_0, other_0, first_0, second_0)
-    grads_0, back_attended = tie(grads_0, back_attended)
-    inward_0 = rep_hop(grads_0, INWARD)
-    halves = attend_back(q_back_1, k_aug, v_aug, attended_1, back_attended, 4, 4)
-    (dq_1, dkv_1), (moved_2,) = fence(halves, moved_2)
+    (dq_0, dkv_0, back_attended), (moved_2,) = fence([*halves, back_attended], moved_2)
     first_2 = hop(add_parts(1, own_2, other_2, moved_2).astype(BF16), 2)
     second_2 = hop(add_parts(2, own_2, other_2).astype(BF16), 4)
+    halves = attend_back(q_back_1, k_aug, v_aug, attended_1, back_attended, 4, 4)
+    (dq_1, dkv_1), (first_2, second_2) = fence(halves, first_2, second_2)
+    grads_2 = add_parts(0, own_2, other_2, first_2, second_2)
+    inward_2 = rep_hop(grads_2, INWARD)
     result = raw_back(
         8, place, (dq_0, dq_1, dkv_0, dkv_1), units, normed_one, tables[0], tables[1], gains,
         grad_out,
     )
-    (back_raw, own, sib), (first_2, second_2, inward_0, total_1) = fence(
-        result, first_2, second_2, inward_0, total_1
-    )
+    (back_raw, own, sib), (inward_2, grads_1) = fence(result, inward_2, grads_1)
     other = hop(sib, 1)
-    half_0 = grads_0 + inward_0.astype(F32)
-    grads_2 = add_parts(0, own_2, other_2, first_2, second_2)
-    back_raw, other, half_0, grads_2 = tie(back_raw, other, half_0, grads_2)
+    both = jnp.concatenate([grads_0, grads_1])
+    back_raw, both = tie(back_raw, both)
+    total_01 = lax.psum(both, "rep")
+    half_2 = grads_2 + inward_2.astype(F32)
+    back_raw, other, half_2 = tie(back_raw, other, half_2)
     terms = [add_parts(k, own, other).astype(BF16) for k in (1, 2, 3)]
     back_raw, *terms = tie(back_raw, *terms)
     steps = [hop(term, 2 * k) for k, term in zip((1, 2, 3), terms)]
-    across_0 = rep_hop(half_0, ACROSS)
-    inward_2 = rep_hop(grads_2, INWARD)
+    across_2 = rep_hop(half_2, ACROSS)
     input_grad = input_back(pairs, place, back_raw, x, back_first, gains)
-    (input_grad,), (inward_2, across_0, *steps) = fence([input_grad], inward_2, across_0, *steps)
-    attn_grad = add_parts(0, own, other, *steps)
-    attn_grad, inward_2, across_0, first_sum = tie(attn_grad, inward_2, across_0, first_sum)
-    inward = rep_hop(attn_grad, INWARD)
-    total_0 = half_0 + across_0.astype(F32)
-    outward_0 = rep_hop(total_0, OUTWARD)
-    half_2 = grads_2 + inward_2.astype(F32)
-    across_2 = rep_hop(half_2, ACROSS)
+    (input_grad,), (across_2, *steps) = fence([input_grad], across_2, *steps)
+    grads = add_parts(0, own, other, *steps)
+    grads, across_2, first_sum = tie(grads, across_2, first_sum)
+    inward = rep_hop(grads, INWARD)
+    total_2 = half_2 + across_2.astype(F32)
+    outward_2 = rep_hop(total_2, OUTWARD)
     outs = out_0.astype(F32) + out_1.astype(F32) + out_2.astype(F32)
     block_output = (first_sum + outs).astype(BF16)
-    (block_output,), (inward, across_2) = fence([block_output], inward, across_2)
-    half = attn_grad + inward.astype(F32)
-    half, across_2 = tie(half, across_2)
+    (block_output,), (inward,) = fence([block_output], inward)
+    half = grads + inward.astype(F32)
     across = rep_hop(half, ACROSS)
-    total_2 = half_2 + across_2.astype(F32)
-    outward_2 = rep_hop(total_2, OUTWARD)
-    total_2, across = tie(total_2, across)
     total = half + across.astype(F32)
-    total, outward_2, outward_0 = tie(total, outward_2, outward_0)
+    total, total_01 = tie(total, total_01)
     outward = rep_hop(total, OUTWARD)
-    feed_grads = unpack_rows(at_end(total_0, outward_0), total_1, at_end(total_2, outward_2))
+    feed_grads = unpack_rows(total_01, at_end(total_2, outward_2))
     (*feed_grads,), (outward,) = fence(feed_grads, outward)
     return block_output, input_grad, at_end(total, outward), feed_grads
 

time: 600 us -> 623 us (1.038)
  waiting for transfers between devices: 146 us -> 184 us
  Pallas kernels: 296 us -> 285 us
  other arithmetic: 63.9 us -> 54.4 us
    ppermute x44 -> x40, waiting for transfers between devices: 68.1 us -> 114 us  [hop(): return lax.ppermute(array, 'shard', [(i, i ^ bit) for i in range(8)])]
    ppermute x9 -> x6, waiting for transfers between devices: 52.5 us -> 40.7 us  [rep_hop(): return lax.ppermute(array.astype(BF16), 'rep', pairs)]
    pallas_call x2, Pallas kernels: 37.6 us -> 27.4 us  [attend(): pl.pallas_call(attend_kernel, grid=(groups,), in_specs=[pl.BlockSpec((2,...]
    convert_element_type x2 -> x0, other arithmetic: 9.94 us -> none  [the longest x1 5.64 us: block_paired(): first_0 = hop(add_parts(1, own_0, other_0).astype(BF16), 2)]
    ppermute x9 -> x6, starting transfers between devices: 24 us -> 30.9 us  [rep_hop(): return lax.ppermute(array.astype(BF16), 'rep', pairs)]
    add x3 -> x1, other arithmetic: 9.46 us -> 3.1 us  [add_parts(): total = total + term.astype(F32)]
    ppermute x44 -> x40, starting transfers between devices: 31 us -> 28.6 us  [hop(): return lax.ppermute(array, 'shard', [(i, i ^ bit) for i in range(8)])]
  transfers between devices with their start and end apart: 55 -> 49, of which waited for: 25 -> 26; matrix products, arithmetic and copies ran while one was open for 9% -> 8% of each run, Pallas kernels for 50% -> 46%
where the time goes in v3:
time: 623 us; the launch traced here: 613 us
  Pallas kernels  285 us (46%)
  waiting for transfers between devices  184 us (30%)
  starting transfers between devices  59.7 us (10%)
  other arithmetic  54.4 us (9%)
  local copies, waits for them, and re-layouts  15.4 us (2%)
  between operations  14.7 us (2%)
    pallas_call x3, Pallas kernels, feed(): pl.pallas_call(lambda *refs: feed_kernel(pieces.layout, paired, *refs), g...  129 us
    ppermute x40, waiting for transfers between devices, hop(): return lax.ppermute(array, 'shard', [(i, i ^ bit) for i in range(8)])  114 us
    pallas_call x2, Pallas kernels, attend_back(): pl.pallas_call(attend_back_kernel, grid=(groups,), in_specs=[pl.BlockSpec...  47.2 us
    ppermute x6, waiting for transfers between devices, rep_hop(): return lax.ppermute(array.astype(BF16), 'rep', pairs)  40.7 us
    ppermute x6, starting transfers between devices, rep_hop(): return lax.ppermute(array.astype(BF16), 'rep', pairs)  30.9 us
    psum x1, waiting for transfers between devices, block_paired(): total_01 = lax.psum(both, 'rep')  29.1 us
    ppermute x40, starting transfers between devices, hop(): return lax.ppermute(array, 'shard', [(i, i ^ bit) for i in range(8)])  28.6 us
    pallas_call x2, Pallas kernels, attend(): pl.pallas_call(attend_kernel, grid=(groups,), in_specs=[pl.BlockSpec((2,...  27.4 us
  transfers between devices with their start and end apart: 49, of which 26 were waited for; matrix products, arithmetic and copies ran while one was open for 8% of the time, Pallas kernels for 46%

profile of v3, /device:TPU:0, one launch (start us, length us, event | category | flops | bytes accessed | tf_op | source)
XLA Modules:
  0.0 613.2 jit_solution(2273243112201221595)
XLA Ops:
  12.8 2.6 collective-permute-start.1
  18.4 1.9 fusion.13
  20.3 1.8 pad_maximum_fusion.1
  22.4 4.5 pack_rows.1
  30.5 1.8 collective-permute-start.5
  32.3 5.9 collective-permute-done.5.refs_18_.refs_17_
  41.8 1.8 collective-permute-done.7.refs_20_.refs_19_
  46.7 15.9 %project.1 = (bf16[1024,1024]{1,0:T(8,128)(2,1)}, bf16[1024,1536]{1,0:T(8,128)(2,1)}, bf16[1024,1536]{1,0:T(8,128)(2,1)}, bf16[16,1024,128]{2,1,0:T(8,128)(2,1)}...) custom-call(s32[1]{0:T(128)} %bitcast.refs_0_, bf16[1024,1024]{1,0:T(8,128)(2,1)} %bitcast.62, ...), custom_call_target="tpu_custom_call" | custom-call | flops 8000000 | bytes 25000 | tf_op jit(solution)/shard_map/project/pallas_call | solution.py:203
  62.6 13.5 %attend.2 = (bf16[1024,512]{1,0:T(8,128)(2,1)}, bf16[8,1024,128]{2,1,0:T(8,128)(2,1)}) custom-call(bf16[16,1024,128]{2,1,0:T(8,128)(2,1)} %get-tuple-element.151.q_ref, bf16[8,1024,128]{2,1,0:T(8,128)(2,1)} %get-tuple-element.159.k_ref, bf16[8,1024,128]{2,1,0:T(8,128)(2,1)} %get-tuple-element.153.v_ref), custom_call_target="tpu_custom_call" | custom-call | flops 10000000 | bytes 8000 | tf_op jit(solution)/shard_map/attend/pallas_call | solution.py:264
  80.8 13.9 %attend.3 = (bf16[1024,512]{1,0:T(8,128)(2,1)}, bf16[8,1024,128]{2,1,0:T(8,128)(2,1)}) custom-call(bf16[16,1024,128]{2,1,0:T(8,128)(2,1)} %get-tuple-element.151.q_ref, bf16[8,1024,128]{2,1,0:T(8,128)(2,1)} %get-tuple-element.159.k_ref, bf16[8,1024,128]{2,1,0:T(8,128)(2,1)} %get-tuple-element.153.v_ref), custom_call_target="tpu_custom_call" | custom-call | flops 10000000 | bytes 8000 | tf_op jit(solution)/shard_map/attend/pallas_call | solution.py:264
  94.7 2.5 collective-permute-done.13.refs_12_.refs_11_.refs_16_
  102.0 3.4 collective-permute-done.17.refs_14_.refs_13_.refs_18_
  106.3 8.3 %output_rows.1 = (f32[1024,1024]{1,0:T(8,128)}, bf16[1024,1024]{1,0:T(8,128)(2,1)}, bf16[1024,1024]{1,0:T(8,128)(2,1)}) custom-call(s32[1]{0:T(128)} %bitcast.refs_0_, bf16[1024,512]{1,0:T(8,128)(2,1)} %get-tuple-element.160.refs_1_.refs_3_.o_ref, bf16[1024,512]{1,0:T(8,128)(2,1)} %get-tuple-element.165.refs_2_.refs_4_.o_ref, bf16[1024,1024]{1,0:T(8,128)(2,1)} %bitcast.63, ...), custom_call_target="tpu_custom_call" | custom-call | flops 5000000 | bytes 15000 | tf_op jit(solution)/shard_map/output_rows/pallas_call | solution.py:381
  114.5 42.2 %feed.3 = (bf16[1024,1024]{1,0:T(8,128)(2,1)}, bf16[1024,1024]{1,0:T(8,128)(2,1)}, bf16[8,576,1024]{2,1,0:T(8,128)(2,1)}) custom-call(s32[1]{0:T(128)} %bitcast.refs_0_, bf16[1024,1024]{1,0:T(8,128)(2,1)} %get-tuple-element.191.refs_1_, bf16[1024,1024]{1,0:T(8,128)(2,1)} %get-tuple-element.174.refs_2_, bf16[1024,1024]{1,0:T(8,128)(2,1)} %bitcast.58, ...), custom_call_target="tpu_custom_call" | custom-call | flops 37500000 | bytes 38000 | tf_op jit(solution)/shard_map/feed/pallas_call | solution.py:466
  164.4 44.1 %feed.4 = (bf16[1024,1024]{1,0:T(8,128)(2,1)}, bf16[1024,1024]{1,0:T(8,128)(2,1)}, bf16[8,576,1024]{2,1,0:T(8,128)(2,1)}) custom-call(s32[1]{0:T(128)} %bitcast.refs_0_, bf16[1024,1024]{1,0:T(8,128)(2,1)} %get-tuple-element.191.refs_1_, bf16[1024,1024]{1,0:T(8,128)(2,1)} %get-tuple-element.174.refs_2_, bf16[1024,1024]{1,0:T(8,128)(2,1)} %bitcast.59, ...), custom_call_target="tpu_custom_call" | custom-call | flops 37500000 | bytes 38000 | tf_op jit(solution)/shard_map/feed/pallas_call | solution.py:466
  208.5 29.5 %collective-permute-done.27.refs_8_ = bf16[576,1024]{1,0:T(8,128)(2,1)} collective-permute-done((bf16[576,1024]{1,0:T(8,128)(2,1)S(1)}, bf16[576,1024]{1,0:T(8,128)(2,1)}, u32[]{:S(2)}, u32[]{:S(2)}) %collective-permute-start.27) | collective-permute-done | bytes 1179680 | tf_op jit(solution)/shard_map/ppermute | solution.py:762
  238.6 2.5 collective-permute-done.29.refs_7_
  241.1 1.7 collective-permute-done.30.refs_9_
  242.8 1.7 collective-permute-done.31.refs_11_
  245.6 42.6 %feed.5 = (bf16[1024,1024]{1,0:T(8,128)(2,1)}, bf16[1024,1024]{1,0:T(8,128)(2,1)}, bf16[4,576,1024]{2,1,0:T(8,128)(2,1)}, bf16[4,576,1024]{2,1,0:T(8,128)(2,1)}) custom-call(s32[1]{0:T(128)} %bitcast.refs_0_, bf16[1024,1024]{1,0:T(8,128)(2,1)} %get-tuple-element.191.refs_1_, bf16[1024,1024]{1,0:T(8,128)(2,1)} %get-tuple-element.174.refs_2_, ...), custom_call_target="tpu_custom_call" | custom-call | flops 37500000 | bytes 38000 | tf_op jit(solution)/shard_map/feed/pallas_call | solution.py:466
  288.4 14.9 %middle.1 = (f32[1024,1024]{1,0:T(8,128)}, bf16[1024,1024]{1,0:T(8,128)(2,1)}, bf16[1024,1024]{1,0:T(8,128)(2,1)}) custom-call(s32[1]{0:T(128)} %bitcast.refs_0_, f32[1024,1024]{1,0:T(8,128)} %get-tuple-element.250.refs_1_, bf16[1024,1024]{1,0:T(8,128)(2,1)} %bitcast.61, bf16[1024,512]{1,0:T(8,128)(2,1)} %get-tuple-element.160.refs_1_.refs_3_.o_ref, ...), custom_call_target="tpu_custom_call" | custom-call | flops 9000000 | bytes 32000 | tf_op jit(solution)/shard_map/middle/pallas_call | solution.py:535
  303.4 4.5 fusion.6
  309.9 23.6 %attend_back.2 = (f32[1024,512]{1,0:T(8,128)}, f32[1024,512]{1,0:T(8,128)}) custom-call(bf16[8,1024,128]{2,1,0:T(8,128)(2,1)} %get-tuple-element.158.q_ref, bf16[8,1024,128]{2,1,0:T(8,128)(2,1)} %get-tuple-element.159.k_ref, bf16[8,1024,128]{2,1,0:T(8,128)(2,1)} %get-tuple-element.153.v_ref, bf16[1024,512]{1,0:T(8,128)(2,1)} %get-tuple-element.160.refs_1_.refs_3_.o_ref, ...), custom_call_target="tpu_custom_call" | custom-call | flops 20000000 | bytes 12000 | tf_op jit(solution)/shard_map/attend_back/pallas_call | solution.py:336
  333.6 22.0 %collective-permute-done.33 = bf16[576,1024]{1,0:T(8,128)(2,1)} collective-permute-done((bf16[576,1024]{1,0:T(8,128)(2,1)S(1)}, bf16[576,1024]{1,0:T(8,128)(2,1)}, u32[]{:S(2)}, u32[]{:S(2)}) %collective-permute-start.33) | collective-permute-done | bytes 1179680 | tf_op jit(solution)/shard_map/ppermute | solution.py:762
  355.6 3.9 fusion.1
  360.4 23.6 %attend_back.3 = (f32[1024,512]{1,0:T(8,128)}, f32[1024,512]{1,0:T(8,128)}) custom-call(bf16[8,1024,128]{2,1,0:T(8,128)(2,1)} %get-tuple-element.212.q_ref, bf16[8,1024,128]{2,1,0:T(8,128)(2,1)} %get-tuple-element.159.k_ref, bf16[8,1024,128]{2,1,0:T(8,128)(2,1)} %get-tuple-element.153.v_ref, bf16[1024,512]{1,0:T(8,128)(2,1)} %get-tuple-element.165.refs_2_.refs_4_.o_ref, ...), custom_call_target="tpu_custom_call" | custom-call | flops 20000000 | bytes 12000 | tf_op jit(solution)/shard_map/attend_back/pallas_call | solution.py:336
  384.0 12.7 %collective-permute-done.35 = bf16[576,1024]{1,0:T(8,128)(2,1)S(1)} collective-permute-done((bf16[576,1024]{1,0:T(8,128)(2,1)S(1)}, bf16[576,1024]{1,0:T(8,128)(2,1)S(1)}, u32[]{:S(2)}, u32[]{:S(2)}) %collective-permute-start.35) | collective-permute-done | bytes 1179680 | tf_op jit(solution)/shard_map/ppermute | solution.py:762
  397.2 4.1 fusion.12
  401.3 3.8 collective-permute-start.36
  405.2 20.1 %raw_back.1 = (bf16[1024,2048]{1,0:T(8,128)(2,1)}, bf16[4,400,1024]{2,1,0:T(8,128)(2,1)}, bf16[4,400,1024]{2,1,0:T(8,128)(2,1)}) custom-call(s32[1]{0:T(128)} %bitcast.refs_0_, f32[1024,512]{1,0:T(8,128)} %get-tuple-element.211.refs_1_, f32[1024,512]{1,0:T(8,128)} %get-tuple-element.217.refs_2_, f32[1024,512]{1,0:T(8,128)} %get-tuple-element.218.refs_3_, ...), custom_call_target="tpu_custom_call" | custom-call | flops 10000000 | bytes 30000 | tf_op jit(solution)/shard_map/raw_back/pallas_call | solution.py:621
  425.3 3.8 collective-permute-done.36
  429.1 3.3 pad_maximum_fusion
  432.4 3.6 convert_add_fusion.1
  438.4 3.9 fusion.10
  445.8 11.4 %input_back.1 = f32[1024,1024]{1,0:T(8,128)} custom-call(s32[1]{0:T(128)} %bitcast.refs_0_, bf16[1024,2048]{1,0:T(8,128)(2,1)} %get-tuple-element.240.refs_1_, bf16[1024,1024]{1,0:T(8,128)(2,1)} %bitcast.64, f32[1024,1024]{1,0:T(8,128)} %get-tuple-element.241.refs_3_, f32[16,1024]{1,0:T(8,128)} %get-tuple-element.166.refs_4_.refs_5_.refs_10_, ...), custom_call_target="tpu_custom_call" | custom-call | flops 6000000 | bytes 18000 | tf_op jit(solution)/shard_map/input_back/pallas_call | solution.py:651
  457.2 6.5 %collective-permute-done.39 = bf16[400,1024]{1,0:T(8,128)(2,1)} collective-permute-done((bf16[400,1024]{1,0:T(8,128)(2,1)}, bf16[400,1024]{1,0:T(8,128)(2,1)}, u32[]{:S(2)}, u32[]{:S(2)}) %collective-permute-start.39) | collective-permute-done | bytes 819232 | tf_op jit(solution)/shard_map/ppermute | solution.py:762
  463.7 16.3 %collective-permute-done.40 = bf16[400,1024]{1,0:T(8,128)(2,1)} collective-permute-done((bf16[400,1024]{1,0:T(8,128)(2,1)}, bf16[400,1024]{1,0:T(8,128)(2,1)}, u32[]{:S(2)}, u32[]{:S(2)}) %collective-permute-start.40) | collective-permute-done | bytes 819232 | tf_op jit(solution)/shard_map/ppermute | solution.py:762
  479.9 1.8 collective-permute-done.41
  481.7 3.1 fusion.3
  484.9 23.0 %collective-permute-start.42 = (bf16[400,1024]{1,0:T(8,128)(2,1)S(1)}, bf16[400,1024]{1,0:T(8,128)(2,1)S(1)}, u32[]{:S(2)}, u32[]{:S(2)}) collective-permute-start(bf16[400,1024]{1,0:T(8,128)(2,1)S(1)} %convert_element_type.249), channel_id=1, source_target_pairs={{0,8},{24,16},{1,9},{25,17},{2,10},{26,18},{3,11},{27,19},{4,12},{... | collective-permute-start | bytes 2457608 | tf_op jit(solution)/shard_map/ppermute | solution.py:788
  507.9 5.2 add_convert_fusion
  513.2 19.7 %collective-permute-done.42 = bf16[400,1024]{1,0:T(8,128)(2,1)S(1)} collective-permute-done((bf16[400,1024]{1,0:T(8,128)(2,1)S(1)}, bf16[400,1024]{1,0:T(8,128)(2,1)S(1)}, u32[]{:S(2)}, u32[]{:S(2)}) %collective-permute-start.42) | collective-permute-done | bytes 819232 | tf_op jit(solution)/shard_map/ppermute | solution.py:788
  538.2 29.1 %all-reduce.2.cloned.1.call-done.refs_0_ = bf16[1152,1024]{1,0:T(8,128)(2,1)} async-done(((bf16[1152,1024]{1,0:T(8,128)(2,1)}), bf16[1152,1024]{1,0:T(8,128)(2,1)}) %all-reduce.2.cloned.1.call-update) | async-done | bytes 2359312 | tf_op jit(solution)/shard_map/psum | solution.py:1025
  567.3 2.4 convert_element_type.257
  571.0 12.6 %collective-permute-done.44 = bf16[576,1024]{1,0:T(8,128)(2,1)} collective-permute-done((bf16[576,1024]{1,0:T(8,128)(2,1)}, bf16[576,1024]{1,0:T(8,128)(2,1)}, u32[]{:S(2)}, u32[]{:S(2)}) %collective-permute-start.44) | collective-permute-done | bytes 1179680 | tf_op jit(solution)/shard_map/ppermute | solution.py:788
  583.7 3.2 convert_select_fusion.refs_1_
  586.9 6.3 %unpack_rows.1 = (f32[128,4608]{1,0:T(8,128)}, f32[128,4608]{1,0:T(8,128)}, f32[576,1024]{1,0:T(8,128)}) custom-call(bf16[1152,1024]{1,0:T(8,128)(2,1)} %all-reduce.2.cloned.1.call-done.refs_0_, f32[576,1024]{1,0:T(8,128)} %convert_select_fusion.refs_1_), custom_call_target="tpu_custom_call" | custom-call | bytes 14000 | tf_op jit(solution)/shard_map/unpack_rows/pallas_call | solution.py:740
  593.1 4.5 collective-permute-done.45
  (204 shorter events, 63.6 us)
Async XLA Ops:
  7.2 281.0 %reduce-scatter.3.cloned.1.call-start = ((), (), s32[]{:S(2)}) async-start(), calls=%async_computation.2 | async-start | bytes 10616832 | tf_op jit(solution)/shard_map/reduce_scatter | solution.py:770
  12.3 16.2 %collective-permute-start.2 = (bf16[272,1024]{1,0:T(8,128)(2,1)S(1)}, bf16[272,1024]{1,0:T(8,128)(2,1)S(1)}, u32[]{:S(2)}, u32[]{:S(2)}) collective-permute-start(bf16[272,1024]{1,0:T(8,128)(2,1)S(1)} %concatenate.41.refs_6_.refs_7_.refs_22_.refs_5_), channel_id=1, source_target_pairs={{0,1},{1,0},{2,3},{3,2},{4,5},{5,4},{6,7},{7,6},{8,9},{9,8},{10,11... | collective-permute-start | bytes 1671176 | tf_op jit(solution)/shard_map/ppermute | solution.py:762
  12.8 15.8 %collective-permute-start.1 = (bf16[272,1024]{1,0:T(8,128)(2,1)S(1)}, bf16[272,1024]{1,0:T(8,128)(2,1)S(1)}, u32[]{:S(2)}, u32[]{:S(2)}) collective-permute-start(bf16[272,1024]{1,0:T(8,128)(2,1)S(1)} %concatenate.41.refs_6_.refs_7_.refs_22_.refs_5_), channel_id=1, source_target_pairs={{0,4},{1,5},{2,6},{3,7},{4,0},{5,1},{6,2},{7,3},{8,12},{9,13},{10,... | collective-permute-start | bytes 1671176 | tf_op jit(solution)/shard_map/ppermute | solution.py:762
  15.4 14.7 %collective-permute-start = (bf16[272,1024]{1,0:T(8,128)(2,1)S(1)}, bf16[272,1024]{1,0:T(8,128)(2,1)S(1)}, u32[]{:S(2)}, u32[]{:S(2)}) collective-permute-start(bf16[272,1024]{1,0:T(8,128)(2,1)S(1)} %concatenate.41.refs_6_.refs_7_.refs_22_.refs_5_), channel_id=1, source_target_pairs={{0,2},{1,3},{2,0},{3,1},{4,6},{5,7},{6,4},{7,5},{8,10},{9,11},{10,... | collective-permute-start | bytes 1671176 | tf_op jit(solution)/shard_map/ppermute | solution.py:762
  30.1 8.3 %collective-permute-start.6 = (bf16[144,1024]{1,0:T(8,128)(2,1)S(1)}, bf16[144,1024]{1,0:T(8,128)(2,1)S(1)}, u32[]{:S(2)}, u32[]{:S(2)}) collective-permute-start(bf16[144,1024]{1,0:T(8,128)(2,1)S(1)} %slice.112), channel_id=1, source_target_pairs={{0,4},{1,5},{2,6},{3,7},{4,0},{5,1},{6,2},{7,3},{8,12},{9,13},{10,... | collective-permute-start | bytes 884744 | tf_op jit(solution)/shard_map/ppermute | solution.py:762
  30.5 7.7 %collective-permute-start.5 = (bf16[128,1024]{1,0:T(8,128)(2,1)S(1)}, bf16[128,1024]{1,0:T(8,128)(2,1)S(1)}, u32[]{:S(2)}, u32[]{:S(2)}) collective-permute-start(bf16[128,1024]{1,0:T(8,128)(2,1)S(1)} %slice.111), channel_id=1, source_target_pairs={{0,2},{1,3},{2,0},{3,1},{4,6},{5,7},{6,4},{7,5},{8,10},{9,11},{10,... | collective-permute-start | bytes 786440 | tf_op jit(solution)/shard_map/ppermute | solution.py:762
  38.4 37.7 %collective-permute-start.11 = (bf16[704,1024]{1,0:T(8,128)(2,1)}, bf16[704,1024]{1,0:T(8,128)(2,1)}, u32[]{:S(2)}, u32[]{:S(2)}) collective-permute-start(bf16[704,1024]{1,0:T(8,128)(2,1)} %get-tuple-element.157.refs_5_.refs_4_.refs_9_), channel_id=1, source_target_pairs={{0,1},{1,0},{2,3},{3,2},{4,5},{5,4},{6,7},{7,6},{8,9},{9,8},{10,11... | collective-permute-start | bytes 4325384 | tf_op jit(solution)/shard_map/ppermute | solution.py:762
  38.5 37.6 %collective-permute-start.10 = (bf16[704,1024]{1,0:T(8,128)(2,1)}, bf16[704,1024]{1,0:T(8,128)(2,1)S(1)}, u32[]{:S(2)}, u32[]{:S(2)}) collective-permute-start(bf16[704,1024]{1,0:T(8,128)(2,1)} %get-tuple-element.157.refs_5_.refs_4_.refs_9_), channel_id=1, source_target_pairs={{0,4},{1,5},{2,6},{3,7},{4,0},{5,1},{6,2},{7,3},{8,12},{9,13},{10,... | collective-permute-start | bytes 4325384 | tf_op jit(solution)/shard_map/ppermute | solution.py:762
  39.7 36.4 %collective-permute-start.9 = (bf16[704,1024]{1,0:T(8,128)(2,1)}, bf16[704,1024]{1,0:T(8,128)(2,1)S(1)}, u32[]{:S(2)}, u32[]{:S(2)}) collective-permute-start(bf16[704,1024]{1,0:T(8,128)(2,1)} %get-tuple-element.157.refs_5_.refs_4_.refs_9_), channel_id=1, source_target_pairs={{0,2},{1,3},{2,0},{3,1},{4,6},{5,7},{6,4},{7,5},{8,10},{9,11},{10,... | collective-permute-start | bytes 4325384 | tf_op jit(solution)/shard_map/ppermute | solution.py:762
  41.2 3.0 collective-permute-start.3
  41.2 2.3 collective-permute-start.7
  43.6 2.3 collective-permute-start.4
  76.2 21.8 %collective-permute-start.15 = (bf16[704,1024]{1,0:T(8,128)(2,1)S(1)}, bf16[704,1024]{1,0:T(8,128)(2,1)}, u32[]{:S(2)}, u32[]{:S(2)}) collective-permute-start(bf16[704,1024]{1,0:T(8,128)(2,1)S(1)} %collective-permute-done.10.refs_9_.refs_8_.refs_13_), channel_id=1, source_target_pairs={{0,1},{1,0},{2,3},{3,2},{4,5},{5,4},{6,7},{7,6},{8,9},{9,8},{10,11... | collective-permute-start | bytes 4325384 | tf_op jit(solution)/shard_map/ppermute | solution.py:762
  76.4 21.6 %collective-permute-start.14 = (bf16[704,1024]{1,0:T(8,128)(2,1)S(1)}, bf16[704,1024]{1,0:T(8,128)(2,1)}, u32[]{:S(2)}, u32[]{:S(2)}) collective-permute-start(bf16[704,1024]{1,0:T(8,128)(2,1)S(1)} %collective-permute-done.9.refs_7_.refs_6_.refs_11_), channel_id=1, source_target_pairs={{0,1},{1,0},{2,3},{3,2},{4,5},{5,4},{6,7},{7,6},{8,9},{9,8},{10,11... | collective-permute-start | bytes 4325384 | tf_op jit(solution)/shard_map/ppermute | solution.py:762
  78.8 18.4 %collective-permute-start.13 = (bf16[704,512]{1,0:T(8,128)(2,1)}, bf16[704,512]{1,0:T(8,128)(2,1)S(1)}, u32[]{:S(2)}, u32[]{:S(2)}) collective-permute-start(bf16[704,512]{1,0:T(8,128)(2,1)} %slice.114), channel_id=1, source_target_pairs={{0,4},{1,5},{2,6},{3,7},{4,0},{5,1},{6,2},{7,3},{8,12},{9,13},{10,... | collective-permute-start | bytes 2162696 | tf_op jit(solution)/shard_map/ppermute | solution.py:762
  79.7 18.2 %collective-permute-start.12 = (bf16[704,512]{1,0:T(8,128)(2,1)}, bf16[704,512]{1,0:T(8,128)(2,1)}, u32[]{:S(2)}, u32[]{:S(2)}) collective-permute-start(bf16[704,512]{1,0:T(8,128)(2,1)} %slice.113), channel_id=1, source_target_pairs={{0,2},{1,3},{2,0},{3,1},{4,6},{5,7},{6,4},{7,5},{8,10},{9,11},{10,... | collective-permute-start | bytes 2162696 | tf_op jit(solution)/shard_map/ppermute | solution.py:762
  97.9 3.6 collective-permute-start.16
  97.9 58.8 %collective-permute-start.21 = (bf16[576,1024]{1,0:T(8,128)(2,1)}, bf16[576,1024]{1,0:T(8,128)(2,1)S(1)}, u32[]{:S(2)}, u32[]{:S(2)}) collective-permute-start(bf16[576,1024]{1,0:T(8,128)(2,1)} %get-tuple-element.179.refs_4_), channel_id=1, source_target_pairs={{0,6},{1,7},{2,4},{3,5},{4,2},{5,3},{6,0},{7,1},{8,14},{9,15},{10,... | collective-permute-start | bytes 3538952 | tf_op jit(solution)/shard_map/ppermute | solution.py:762
  99.4 57.4 %collective-permute-start.20 = (bf16[576,1024]{1,0:T(8,128)(2,1)}, bf16[576,1024]{1,0:T(8,128)(2,1)}, u32[]{:S(2)}, u32[]{:S(2)}) collective-permute-start(bf16[576,1024]{1,0:T(8,128)(2,1)} %get-tuple-element.179.refs_4_), channel_id=1, source_target_pairs={{0,4},{1,5},{2,6},{3,7},{4,0},{5,1},{6,2},{7,3},{8,12},{9,13},{10,... | collective-permute-start | bytes 3538952 | tf_op jit(solution)/shard_map/ppermute | solution.py:762
  100.6 56.2 %collective-permute-start.19 = (bf16[576,1024]{1,0:T(8,128)(2,1)}, bf16[576,1024]{1,0:T(8,128)(2,1)}, u32[]{:S(2)}, u32[]{:S(2)}) collective-permute-start(bf16[576,1024]{1,0:T(8,128)(2,1)} %get-tuple-element.179.refs_4_), channel_id=1, source_target_pairs={{0,2},{1,3},{2,0},{3,1},{4,6},{5,7},{6,4},{7,5},{8,10},{9,11},{10,... | collective-permute-start | bytes 3538952 | tf_op jit(solution)/shard_map/ppermute | solution.py:762
  101.5 55.3 %collective-permute-start.18 = (bf16[576,1024]{1,0:T(8,128)(2,1)}, bf16[576,1024]{1,0:T(8,128)(2,1)}, u32[]{:S(2)}, u32[]{:S(2)}) collective-permute-start(bf16[576,1024]{1,0:T(8,128)(2,1)} %get-tuple-element.179.refs_4_), channel_id=1, source_target_pairs={{0,1},{1,0},{2,3},{3,2},{4,5},{5,4},{6,7},{7,6},{8,9},{9,8},{10,11... | collective-permute-start | bytes 3538952 | tf_op jit(solution)/shard_map/ppermute | solution.py:762
  101.5 3.9 collective-permute-start.17
  156.8 272.3 %reduce-scatter.5.cloned.1.call-start = ((), (), s32[]{:S(2)}) async-start(), calls=%async_computation.3 | async-start | bytes 10616832 | tf_op jit(solution)/shard_map/reduce_scatter | solution.py:770
  156.9 4.2 collective-permute-start.22
  157.1 6.3 %collective-permute-start.23 = (bf16[576,1024]{1,0:T(8,128)(2,1)}, bf16[576,1024]{1,0:T(8,128)(2,1)S(1)}, u32[]{:S(2)}, u32[]{:S(2)}) collective-permute-start(bf16[576,1024]{1,0:T(8,128)(2,1)} %collective-permute-done.20.refs_8_), channel_id=1, source_target_pairs={{0,1},{1,0},{2,3},{3,2},{4,5},{5,4},{6,7},{7,6},{8,9},{9,8},{10,11... | collective-permute-start | bytes 3538952 | tf_op jit(solution)/shard_map/ppermute | solution.py:762
  157.8 6.6 %collective-permute-start.24 = (bf16[576,1024]{1,0:T(8,128)(2,1)S(1)}, bf16[576,1024]{1,0:T(8,128)(2,1)}, u32[]{:S(2)}, u32[]{:S(2)}) collective-permute-start(bf16[576,1024]{1,0:T(8,128)(2,1)S(1)} %collective-permute-done.21.refs_10_), channel_id=1, source_target_pairs={{0,1},{1,0},{2,3},{3,2},{4,5},{5,4},{6,7},{7,6},{8,9},{9,8},{10,11... | collective-permute-start | bytes 3538952 | tf_op jit(solution)/shard_map/ppermute | solution.py:762
  158.5 50.0 %collective-permute-start.28 = (bf16[576,1024]{1,0:T(8,128)(2,1)S(1)}, bf16[576,1024]{1,0:T(8,128)(2,1)}, u32[]{:S(2)}, u32[]{:S(2)}) collective-permute-start(bf16[576,1024]{1,0:T(8,128)(2,1)S(1)} %copy-done.21), channel_id=1, source_target_pairs={{0,6},{1,7},{2,4},{3,5},{4,2},{5,3},{6,0},{7,1},{8,14},{9,15},{10,... | collective-permute-start | bytes 3538952 | tf_op jit(solution)/shard_map/ppermute | solution.py:762
  159.9 78.1 %collective-permute-start.27 = (bf16[576,1024]{1,0:T(8,128)(2,1)S(1)}, bf16[576,1024]{1,0:T(8,128)(2,1)}, u32[]{:S(2)}, u32[]{:S(2)}) collective-permute-start(bf16[576,1024]{1,0:T(8,128)(2,1)S(1)} %copy-done.21), channel_id=1, source_target_pairs={{0,4},{1,5},{2,6},{3,7},{4,0},{5,1},{6,2},{7,3},{8,12},{9,13},{10,... | collective-permute-start | bytes 3538952 | tf_op jit(solution)/shard_map/ppermute | solution.py:762
  161.1 77.0 %collective-permute-start.26 = (bf16[576,1024]{1,0:T(8,128)(2,1)S(1)}, bf16[576,1024]{1,0:T(8,128)(2,1)}, u32[]{:S(2)}, u32[]{:S(2)}) collective-permute-start(bf16[576,1024]{1,0:T(8,128)(2,1)S(1)} %copy-done.21), channel_id=1, source_target_pairs={{0,2},{1,3},{2,0},{3,1},{4,6},{5,7},{6,4},{7,5},{8,10},{9,11},{10,... | collective-permute-start | bytes 3538952 | tf_op jit(solution)/shard_map/ppermute | solution.py:762
  163.4 74.7 %collective-permute-start.25 = (bf16[576,1024]{1,0:T(8,128)(2,1)S(1)}, bf16[576,1024]{1,0:T(8,128)(2,1)}, u32[]{:S(2)}, u32[]{:S(2)}) collective-permute-start(bf16[576,1024]{1,0:T(8,128)(2,1)S(1)} %copy-done.21), channel_id=1, source_target_pairs={{0,1},{1,0},{2,3},{3,2},{4,5},{5,4},{6,7},{7,6},{8,9},{9,8},{10,11... | collective-permute-start | bytes 3538952 | tf_op jit(solution)/shard_map/ppermute | solution.py:762
  238.0 3.1 collective-permute-start.29
  238.1 4.7 collective-permute-start.30
  238.6 5.9 collective-permute-start.31
  288.2 279.1 %all-reduce.2.cloned.1.call-start = ((), (), s32[]{:S(2)}) async-start(), calls=%async_computation.4 | async-start | bytes 4718592 | tf_op jit(solution)/shard_map/psum | solution.py:1025
  288.2 15.1 %collective-permute-start.32 = (bf16[4,576,1024]{2,1,0:T(8,128)(2,1)}, bf16[4,576,1024]{2,1,0:T(8,128)(2,1)}, u32[]{:S(2)}, u32[]{:S(2)}) collective-permute-start(bf16[4,576,1024]{2,1,0:T(8,128)(2,1)} %get-tuple-element.205), channel_id=1, source_target_pairs={{0,1},{1,0},{2,3},{3,2},{4,5},{5,4},{6,7},{7,6},{8,9},{9,8},{10,11... | collective-permute-start | bytes 14155784 | tf_op jit(solution)/shard_map/ppermute | solution.py:762
  307.9 47.8 %collective-permute-start.33 = (bf16[576,1024]{1,0:T(8,128)(2,1)S(1)}, bf16[576,1024]{1,0:T(8,128)(2,1)}, u32[]{:S(2)}, u32[]{:S(2)}) collective-permute-start(bf16[576,1024]{1,0:T(8,128)(2,1)S(1)} %get-tuple-element.276), channel_id=1, source_target_pairs={{0,4},{1,5},{2,6},{3,7},{4,0},{5,1},{6,2},{7,3},{8,12},{9,13},{10,... | collective-permute-start | bytes 3538952 | tf_op jit(solution)/shard_map/ppermute | solution.py:762
  309.2 87.5 %collective-permute-start.35 = (bf16[576,1024]{1,0:T(8,128)(2,1)S(1)}, bf16[576,1024]{1,0:T(8,128)(2,1)S(1)}, u32[]{:S(2)}, u32[]{:S(2)}) collective-permute-start(bf16[576,1024]{1,0:T(8,128)(2,1)S(1)} %get-tuple-element.275), channel_id=1, source_target_pairs={{0,4},{1,5},{2,6},{3,7},{4,0},{5,1},{6,2},{7,3},{8,12},{9,13},{10,... | collective-permute-start | bytes 3538952 | tf_op jit(solution)/shard_map/ppermute | solution.py:762
  359.5 37.8 %collective-permute-start.34 = (bf16[576,1024]{1,0:T(8,128)(2,1)}, bf16[576,1024]{1,0:T(8,128)(2,1)S(1)}, u32[]{:S(2)}, u32[]{:S(2)}) collective-permute-start(bf16[576,1024]{1,0:T(8,128)(2,1)} %fusion.1), channel_id=1, source_target_pairs={{0,2},{1,3},{2,0},{3,1},{4,6},{5,7},{6,4},{7,5},{8,10},{9,11},{10,... | collective-permute-start | bytes 3538952 | tf_op jit(solution)/shard_map/ppermute | solution.py:762
  401.3 27.8 %collective-permute-start.36 = (bf16[576,1024]{1,0:T(8,128)(2,1)}, bf16[576,1024]{1,0:T(8,128)(2,1)S(1)}, u32[]{:S(2)}, u32[]{:S(2)}) collective-permute-start(bf16[576,1024]{1,0:T(8,128)(2,1)} %fusion.12), channel_id=1, source_target_pairs={{0,8},{24,16},{1,9},{25,17},{2,10},{26,18},{3,11},{27,19},{4,12},{... | collective-permute-start | bytes 3538952 | tf_op jit(solution)/shard_map/ppermute | solution.py:788
  429.1 6.9 %collective-permute-start.37 = (bf16[4,400,1024]{2,1,0:T(8,128)(2,1)}, bf16[4,400,1024]{2,1,0:T(8,128)(2,1)}, u32[]{:S(2)}, u32[]{:S(2)}) collective-permute-start(bf16[4,400,1024]{2,1,0:T(8,128)(2,1)} %get-tuple-element.236), channel_id=1, source_target_pairs={{0,1},{1,0},{2,3},{3,2},{4,5},{5,4},{6,7},{7,6},{8,9},{9,8},{10,11... | collective-permute-start | bytes 9830408 | tf_op jit(solution)/shard_map/ppermute | solution.py:762
  437.3 44.5 %collective-permute-start.38 = (bf16[576,1024]{1,0:T(8,128)(2,1)}, bf16[576,1024]{1,0:T(8,128)(2,1)S(1)}, u32[]{:S(2)}, u32[]{:S(2)}) collective-permute-start(bf16[576,1024]{1,0:T(8,128)(2,1)} %convert_element_type.241), channel_id=1, source_target_pairs={{8,16},{16,8},{9,17},{17,9},{10,18},{18,10},{11,19},{19,11},{12,20... | collective-permute-start | bytes 3538952 | tf_op jit(solution)/shard_map/ppermute | solution.py:788
  442.3 21.4 %collective-permute-start.39 = (bf16[400,1024]{1,0:T(8,128)(2,1)}, bf16[400,1024]{1,0:T(8,128)(2,1)}, u32[]{:S(2)}, u32[]{:S(2)}) collective-permute-start(bf16[400,1024]{1,0:T(8,128)(2,1)} %get-tuple-element.243), channel_id=1, source_target_pairs={{0,2},{1,3},{2,0},{3,1},{4,6},{5,7},{6,4},{7,5},{8,10},{9,11},{10,... | collective-permute-start | bytes 2457608 | tf_op jit(solution)/shard_map/ppermute | solution.py:762
  443.2 36.8 %collective-permute-start.40 = (bf16[400,1024]{1,0:T(8,128)(2,1)}, bf16[400,1024]{1,0:T(8,128)(2,1)}, u32[]{:S(2)}, u32[]{:S(2)}) collective-permute-start(bf16[400,1024]{1,0:T(8,128)(2,1)} %get-tuple-element.244), channel_id=1, source_target_pairs={{0,4},{1,5},{2,6},{3,7},{4,0},{5,1},{6,2},{7,3},{8,12},{9,13},{10,... | collective-permute-start | bytes 2457608 | tf_op jit(solution)/shard_map/ppermute | solution.py:762
  444.6 37.1 %collective-permute-start.41 = (bf16[400,1024]{1,0:T(8,128)(2,1)}, bf16[400,1024]{1,0:T(8,128)(2,1)}, u32[]{:S(2)}, u32[]{:S(2)}) collective-permute-start(bf16[400,1024]{1,0:T(8,128)(2,1)} %get-tuple-element.245), channel_id=1, source_target_pairs={{0,6},{1,7},{2,4},{3,5},{4,2},{5,3},{6,0},{7,1},{8,14},{9,15},{10,... | collective-permute-start | bytes 2457608 | tf_op jit(solution)/shard_map/ppermute | solution.py:762
  484.9 47.9 %collective-permute-start.42 = (bf16[400,1024]{1,0:T(8,128)(2,1)S(1)}, bf16[400,1024]{1,0:T(8,128)(2,1)S(1)}, u32[]{:S(2)}, u32[]{:S(2)}) collective-permute-start(bf16[400,1024]{1,0:T(8,128)(2,1)S(1)} %convert_element_type.249), channel_id=1, source_target_pairs={{0,8},{24,16},{1,9},{25,17},{2,10},{26,18},{3,11},{27,19},{4,12},{... | collective-permute-start | bytes 2457608 | tf_op jit(solution)/shard_map/ppermute | solution.py:788
  533.1 3.4 collective-permute-start.43
  535.3 48.4 %collective-permute-start.44 = (bf16[576,1024]{1,0:T(8,128)(2,1)}, bf16[576,1024]{1,0:T(8,128)(2,1)}, u32[]{:S(2)}, u32[]{:S(2)}) collective-permute-start(bf16[576,1024]{1,0:T(8,128)(2,1)} %fusion.4), channel_id=1, source_target_pairs={{8,0},{16,24},{9,1},{17,25},{10,2},{18,26},{11,3},{19,27},{12,4},{... | collective-permute-start | bytes 3538952 | tf_op jit(solution)/shard_map/ppermute | solution.py:788
  569.7 27.9 %collective-permute-start.45 = (bf16[400,1024]{1,0:T(8,128)(2,1)}, bf16[400,1024]{1,0:T(8,128)(2,1)}, u32[]{:S(2)}, u32[]{:S(2)}) collective-permute-start(bf16[400,1024]{1,0:T(8,128)(2,1)} %convert_element_type.257), channel_id=1, source_target_pairs={{8,0},{16,24},{9,1},{17,25},{10,2},{18,26},{11,3},{19,27},{12,4},{... | collective-permute-start | bytes 2457608 | tf_op jit(solution)/shard_map/ppermute | solution.py:788
  (39 other events, 249.8 us)
Sparse Core Ops, SparseCore 0:
  157.0 104.3 reduce-scatter.2
  288.3 112.6 reduce-scatter.4
  445.9 121.3 all-reduce.1

commit v4 on v3

--- a/solution.py
+++ b/solution.py
@@ -711,15 +711,17 @@
     )(w_output, w_gate, w_up, w_down)
 
 
-def unpack_kernel(*refs):
+def unpack_kernel(flag_ref, *refs):
     *in_refs, gate_ref, up_ref, down_ref = refs
     low = lanes(128) < 64
+    outer = flag_ref[0] > 0
 
     def rows_of(at, size, columns):
-        for ref in in_refs:
-            if at < ref.shape[0]:
-                return ref[at : at + size, columns].astype(F32)
-            at -= ref.shape[0]
+        for inside, outside in zip(in_refs[::2], in_refs[1::2]):
+            if at < inside.shape[0]:
+                one = inside[at : at + size, columns].astype(F32)
+                return jnp.where(outer, outside[at : at + size, columns].astype(F32), one)
+            at -= inside.shape[0]
 
     def segment(side, s, half):
         d = s // 9
@@ -736,9 +738,11 @@
         down_ref[t * 64 : t * 64 + 64, :] = rows_of(t * 192 + 128, 64, slice(None))
 
 
-def unpack_rows(*totals):
+def unpack_rows(flag, *totals):
+    whole = pl.BlockSpec(memory_space=pltpu.VMEM)
     return pl.pallas_call(
         unpack_kernel,
+        in_specs=[SMALL] + [whole] * len(totals),
         out_shape=[
             jax.ShapeDtypeStruct((128, 4608), F32),
             jax.ShapeDtypeStruct((128, 4608), F32),
@@ -747,7 +751,7 @@
         compiler_params=params(),
         cost_estimate=cost(0, 14),
         name="unpack_rows",
-    )(*totals)
+    )(flag, *totals)
 
 
 def tie(*values):
@@ -777,11 +781,38 @@
     return Pieces(groups)
 
 
-def add_parts(k, own, other, *more):
-    total = own[k].astype(F32) + other[k].astype(F32)
-    for term in more:
-        total = total + term.astype(F32)
-    return total
+def combine(*outputs, half=None):
+    terms = [term if isinstance(term, tuple) else (term, None) for out in outputs for term in out]
+    rows, width = terms[0][0].shape[-2:]
+    wide = width if half is None else width // 2
+    step = rows // (5 if rows % 64 else 4)
+
+    def spec(array, k):
+        column = half if half is not None and array.shape[-1] == width else 0
+        if k is None:
+            return pl.BlockSpec((step, wide), lambda i: (i, column))
+        return pl.BlockSpec((pl.Squeezed(), step, wide), lambda i: (k, i, column))
+
+    def kernel(*refs):
+        at = 0
+        for out, out_ref in zip(outputs, refs[len(terms) :]):
+            total = refs[at][...].astype(F32)
+            for ref in refs[at + 1 : at + len(out)]:
+                total = total + ref[...].astype(F32)
+            at += len(out)
+            out_ref[...] = total.astype(BF16)
+
+    found = pl.pallas_call(
+        kernel,
+        grid=(rows // step,),
+        in_specs=[spec(*term) for term in terms],
+        out_specs=[pl.BlockSpec((step, wide), lambda i: (i, 0))] * len(outputs),
+        out_shape=[jax.ShapeDtypeStruct((rows, wide), BF16)] * len(outputs),
+        compiler_params=params(),
+        cost_estimate=cost(0, 4),
+        name="combine",
+    )(*[array for array, _ in terms])
+    return found[0] if len(outputs) == 1 else found
 
 
 def rep_hop(array, pairs):
@@ -986,67 +1017,117 @@
     def feed_step(pieces, begin, n, paired):
         return feed(pieces, place, begin, n, normed_two, normed_two_t, back_out, paired)
 
-    (out_0, back_0, stack_0, normed_two), waiting = fence(
-        [*feed_step(early, rows, chunks[0], False), normed_two], *waiting
-    )
-    grads_0 = scatter_all(stack_0)
+    (out_0, back_0, own_0, sib_0, normed_two), waiting = fence(
+        [*feed_step(early, rows, chunks[0], True), normed_two], *waiting
+    )
     later = finish(packs[1], *waiting)
     waiting = [hop(packs[2], bit) for bit in (1, 2, 4, 6)]
-    (out_1, back_1, stack_1, normed_two), waiting = fence(
-        [*feed_step(later, 0, chunks[1], False), normed_two], *waiting
+    other_0 = hop(after(sib_0, *later.arrays), 1)
+    (out_1, back_1, own_1, sib_1, normed_two), (other_0, *waiting) = fence(
+        [*feed_step(later, 0, chunks[1], True), normed_two], other_0, *waiting
     )
     last = finish(packs[2], *waiting)
-    (out_2, back_2, own_2, sib_2), (grads_0,) = fence(
-        feed_step(last, 0, chunks[2], True), grads_0
-    )
-    grads_1 = scatter_all(after(stack_1, grads_0))
+    other_1 = hop(sib_1, 1)
+    moved_0 = hop(combine([(own_0, 3), (other_0, 3)]), 2)
+    normed_two, other_1 = tie(normed_two, other_1)
+    term = combine([(own_1, 3), (other_1, 3)])
+    normed_two, term = tie(normed_two, term)
+    moved_1 = hop(term, 4)
+    (out_2, back_2, own_2, sib_2), (moved_0, moved_1) = fence(
+        feed_step(last, 0, chunks[2], True), moved_0, moved_1
+    )
     other_2 = hop(sib_2, 1)
+    one, two = combine([(own_0, 1), (other_0, 1)], [(own_0, 2), (other_0, 2), moved_0])
+    first_0, second_0 = hop(one, 2), hop(two, 4)
+    three, four = combine([(own_1, 1), (other_1, 1), moved_1], [(own_1, 2), (other_1, 2)])
+    back_2, one, two, three, four = tie(back_2, one, two, three, four)
+    first_1, second_1 = hop(after(three, one), 2), hop(after(four, two), 4)
     middles = middle(
         early, place, first_sum, back_out, attended, gains, [back_0, back_1, back_2]
     )
     (back_first, back_attended, grad_out), (other_2,) = fence(middles, other_2)
-    moved_2 = hop(add_parts(3, own_2, other_2).astype(BF16), 4)
+    term = combine([(own_2, 3), (other_2, 3)])
+    back_attended, term = tie(back_attended, term)
+    moved_2 = hop(term, 2)
     halves = attend_back(q_back_0, k_aug, v_aug, attended_0, back_attended, 0, 4)
-    (dq_0, dkv_0, back_attended), (moved_2,) = fence([*halves, back_attended], moved_2)
-    first_2 = hop(add_parts(1, own_2, other_2, moved_2).astype(BF16), 2)
-    second_2 = hop(add_parts(2, own_2, other_2).astype(BF16), 4)
+    (dq_0, dkv_0, back_attended), (first_0, second_0, first_1, second_1) = fence(
+        [*halves, back_attended], first_0, second_0, first_1, second_1
+    )
+    grads_0, grads_1 = combine(
+        [(own_0, 0), (other_0, 0), first_0, second_0], [(own_1, 0), (other_1, 0), first_1, second_1]
+    )
+    back_attended, grads_0, grads_1 = tie(back_attended, grads_0, grads_1)
+    inward_0 = rep_hop(grads_0, INWARD)
+    inward_1 = rep_hop(grads_1, INWARD)
     halves = attend_back(q_back_1, k_aug, v_aug, attended_1, back_attended, 4, 4)
-    (dq_1, dkv_1), (first_2, second_2) = fence(halves, first_2, second_2)
-    grads_2 = add_parts(0, own_2, other_2, first_2, second_2)
-    inward_2 = rep_hop(grads_2, INWARD)
+    (dq_1, dkv_1), (moved_2, inward_0) = fence(halves, moved_2, inward_0)
+    one, two = combine([(own_2, 1), (other_2, 1)], [(own_2, 2), (other_2, 2), moved_2])
+    half_0 = combine([grads_0, inward_0])
+    dq_1, one, two, half_0 = tie(dq_1, one, two, half_0)
+    first_2, second_2 = hop(one, 2), hop(two, 4)
+    across_0 = rep_hop(half_0, ACROSS)
     result = raw_back(
         8, place, (dq_0, dq_1, dkv_0, dkv_1), units, normed_one, tables[0], tables[1], gains,
         grad_out,
     )
-    (back_raw, own, sib), (inward_2, grads_1) = fence(result, inward_2, grads_1)
+    (back_raw, own, sib), (first_2, second_2, inward_1, across_0) = fence(
+        result, first_2, second_2, inward_1, across_0
+    )
     other = hop(sib, 1)
-    both = jnp.concatenate([grads_0, grads_1])
-    back_raw, both = tie(back_raw, both)
-    total_01 = lax.psum(both, "rep")
-    half_2 = grads_2 + inward_2.astype(F32)
-    back_raw, other, half_2 = tie(back_raw, other, half_2)
-    terms = [add_parts(k, own, other).astype(BF16) for k in (1, 2, 3)]
-    back_raw, *terms = tie(back_raw, *terms)
-    steps = [hop(term, 2 * k) for k, term in zip((1, 2, 3), terms)]
-    across_2 = rep_hop(half_2, ACROSS)
+    half_1, total_0 = combine([grads_1, inward_1], [half_0, across_0])
+    grads_2 = combine([(own_2, 0), (other_2, 0), first_2, second_2])
+    back_raw, other, half_1, total_0, grads_2 = tie(back_raw, other, half_1, total_0, grads_2)
+    terms = [
+        combine(*[[(own, k), (other, k)] for k in (1, 2, 3)], half=side) for side in (0, 1)
+    ]
+    back_raw, *flat = tie(back_raw, *terms[0], *terms[1])
+    steps = [hop(term, 2 * k) for k, term in zip((1, 2, 3), flat[:3])]
+    inward_2 = rep_hop(grads_2, INWARD)
+    outward_0 = rep_hop(total_0, OUTWARD)
     input_grad = input_back(pairs, place, back_raw, x, back_first, gains)
-    (input_grad,), (across_2, *steps) = fence([input_grad], across_2, *steps)
-    grads = add_parts(0, own, other, *steps)
-    grads, across_2, first_sum = tie(grads, across_2, first_sum)
-    inward = rep_hop(grads, INWARD)
-    total_2 = half_2 + across_2.astype(F32)
-    outward_2 = rep_hop(total_2, OUTWARD)
+    (input_grad, half_1, *flat), (outward_0, *steps) = fence(
+        [input_grad, half_1, *flat[3:]], outward_0, *steps
+    )
+    across_1 = rep_hop(half_1, ACROSS)
+    more = [hop(term, 2 * k) for k, term in zip((1, 2, 3), flat)]
+    part_a = combine([(own, 0), (other, 0), *steps], half=0)
+    inward_a = rep_hop(part_a, INWARD)
+    first_sum, _ = tie(first_sum, part_a)
     outs = out_0.astype(F32) + out_1.astype(F32) + out_2.astype(F32)
     block_output = (first_sum + outs).astype(BF16)
-    (block_output,), (inward,) = fence([block_output], inward)
-    half = grads + inward.astype(F32)
-    across = rep_hop(half, ACROSS)
-    total = half + across.astype(F32)
-    total, total_01 = tie(total, total_01)
-    outward = rep_hop(total, OUTWARD)
-    feed_grads = unpack_rows(total_01, at_end(total_2, outward_2))
-    (*feed_grads,), (outward,) = fence(feed_grads, outward)
-    return block_output, input_grad, at_end(total, outward), feed_grads
+    (block_output,), (inward_2,) = fence([block_output], inward_2)
+    half_2 = combine([grads_2, inward_2])
+    across_2 = rep_hop(half_2, ACROSS)
+    *more, _ = tie(*more, half_2)
+    part_b = combine([(own, 0), (other, 0), *more], half=1)
+    inward_b = rep_hop(part_b, INWARD)
+    across_1, _ = tie(across_1, part_b)
+    total_1 = combine([half_1, across_1])
+    outward_1 = rep_hop(total_1, OUTWARD)
+    inward_a, _ = tie(inward_a, total_1)
+    half_a = combine([part_a, inward_a])
+    across_a = rep_hop(half_a, ACROSS)
+    inward_b, _ = tie(inward_b, half_a)
+    half_b = combine([part_b, inward_b])
+    across_b = rep_hop(half_b, ACROSS)
+    across_2, _ = tie(across_2, half_b)
+    total_2 = combine([half_2, across_2])
+    outward_2 = rep_hop(total_2, OUTWARD)
+    across_a, outward_1, _ = tie(across_a, outward_1, total_2)
+    total_a = combine([half_a, across_a])
+    outward_a = rep_hop(total_a, OUTWARD)
+    across_b, _ = tie(across_b, total_a)
+    total_b = combine([half_b, across_b])
+    outward_b = rep_hop(total_b, OUTWARD)
+    spot = lax.axis_index("rep")
+    flag = ((spot == 0) | (spot == 3)).astype(jnp.int32).reshape(1)
+    outward_2, _ = tie(outward_2, total_b)
+    feed_grads = unpack_rows(flag, total_0, outward_0, total_1, outward_1, total_2, outward_2)
+    (*feed_grads,), (outward_a, outward_b) = fence(feed_grads, outward_a, outward_b)
+    attn_grad = jnp.concatenate(
+        [at_end(total_a.astype(F32), outward_a), at_end(total_b.astype(F32), outward_b)], axis=1
+    )
+    return block_output, input_grad, attn_grad, feed_grads
 
 
 def solution(mesh):

time: 623 us -> 594 us (0.953)
  Pallas kernels: 285 us -> 380 us
  waiting for transfers between devices: 184 us -> 95.8 us
  other arithmetic: 54.4 us -> 17.7 us
  between operations: 14.7 us -> 1.62 us
  starting transfers between devices: 59.7 us -> 69.9 us
    pallas_call x1 -> x22, Pallas kernels: 6.25 us -> 93.8 us  [the longest x21 86.3 us: combine(): pl.pallas_call(kernel, grid=(rows // step,), in_specs=[spec(*term) for te...]
    ppermute x40 -> x51, waiting for transfers between devices: 114 us -> 62.3 us  [hop(): return lax.ppermute(array, 'shard', [(i, i ^ bit) for i in range(8)])]
    psum x1 -> x0, waiting for transfers between devices: 29.1 us -> none  [block_paired(): total_01 = lax.psum(both, 'rep')]
    convert_element_type x9 -> x0, other arithmetic: 21.7 us -> none  [the longest x6 9.54 us: rep_hop(): return lax.ppermute(array.astype(BF16), 'rep', pairs)]
    ppermute x40 -> x51, starting transfers between devices: 28.6 us -> 39.4 us  [hop(): return lax.ppermute(array, 'shard', [(i, i ^ bit) for i in range(8)])]
    pallas_call x2, Pallas kernels: 27.4 us -> 37.6 us  [attend(): pl.pallas_call(attend_kernel, grid=(groups,), in_specs=[pl.BlockSpec((2,...]
    add x3 -> x0, other arithmetic: 8.29 us -> none  [the longest x1 3.6 us: block_paired(): half_2 = grads_2 + inward_2.astype(F32)]
    ppermute x6 -> x15, waiting for transfers between devices: 40.7 us -> 33.5 us  [rep_hop(): return lax.ppermute(array.astype(BF16), 'rep', pairs)]
  transfers between devices with their start and end apart: 49 -> 66, of which waited for: 26 -> 23; matrix products, arithmetic and copies ran while one was open for 8% -> 3% of each run, Pallas kernels for 46% -> 64%
where the time goes in v4:
time: 594 us; the launch traced here: 586 us
  Pallas kernels  380 us (64%)
  waiting for transfers between devices  95.8 us (16%)
  starting transfers between devices  69.9 us (12%)
  local copies, waits for them, and re-layouts  20.5 us (3%)
  other arithmetic  17.7 us (3%)
    pallas_call x3, Pallas kernels, feed(): pl.pallas_call(lambda *refs: feed_kernel(pieces.layout, paired, *refs), g...  127 us
    pallas_call x21, Pallas kernels, combine(): pl.pallas_call(kernel, grid=(rows // step,), in_specs=[spec(*term) for te...  86.3 us
    ppermute x51, waiting for transfers between devices, hop(): return lax.ppermute(array, 'shard', [(i, i ^ bit) for i in range(8)])  62.3 us
    pallas_call x2, Pallas kernels, attend_back(): pl.pallas_call(attend_back_kernel, grid=(groups,), in_specs=[pl.BlockSpec...  47.7 us
    ppermute x51, starting transfers between devices, hop(): return lax.ppermute(array, 'shard', [(i, i ^ bit) for i in range(8)])  39.4 us
    pallas_call x2, Pallas kernels, attend(): pl.pallas_call(attend_kernel, grid=(groups,), in_specs=[pl.BlockSpec((2,...  37.6 us
    ppermute x15, waiting for transfers between devices, rep_hop(): return lax.ppermute(array.astype(BF16), 'rep', pairs)  33.5 us
    ppermute x15, starting transfers between devices, rep_hop(): return lax.ppermute(array.astype(BF16), 'rep', pairs)  30.5 us
  transfers between devices with their start and end apart: 66, of which 23 were waited for; matrix products, arithmetic and copies ran while one was open for 3% of the time, Pallas kernels for 64%

profile of v4, /device:TPU:0, one launch (start us, length us, event | category | flops | bytes accessed | tf_op | source)
XLA Modules:
  0.0 586.0 jit_solution(8492223012495424443)
XLA Ops:
  15.0 4.4 pack_rows.1
  25.1 6.0 %collective-permute-done.5.refs_18_.refs_17_ = bf16[128,1024]{1,0:T(8,128)(2,1)S(1)} collective-permute-done((bf16[128,1024]{1,0:T(8,128)(2,1)S(1)}, bf16[128,1024]{1,0:T(8,128)(2,1)S(1)}, u32[]{:S(2)}, u32[]{:S(2)}) %collective-permute-start.5) | collective-permute-done | bytes 262176 | tf_op jit(solution)/shard_map/ppermute | solution.py:766
  33.1 3.5 collective-permute-done.7.refs_20_.refs_19_
  39.7 15.9 %project.1 = (bf16[1024,1024]{1,0:T(8,128)(2,1)}, bf16[1024,1536]{1,0:T(8,128)(2,1)}, bf16[1024,1536]{1,0:T(8,128)(2,1)}, bf16[16,1024,128]{2,1,0:T(8,128)(2,1)}...) custom-call(s32[1]{0:T(128)} %bitcast.refs_0_, bf16[1024,1024]{1,0:T(8,128)(2,1)} %bitcast.33, ...), custom_call_target="tpu_custom_call" | custom-call | flops 8000000 | bytes 25000 | tf_op jit(solution)/shard_map/project/pallas_call | solution.py:203
  55.7 13.5 %attend.2 = (bf16[1024,512]{1,0:T(8,128)(2,1)}, bf16[8,1024,128]{2,1,0:T(8,128)(2,1)}) custom-call(bf16[16,1024,128]{2,1,0:T(8,128)(2,1)} %get-tuple-element.209.q_ref, bf16[8,1024,128]{2,1,0:T(8,128)(2,1)} %get-tuple-element.217.k_ref, bf16[8,1024,128]{2,1,0:T(8,128)(2,1)} %get-tuple-element.211.v_ref), custom_call_target="tpu_custom_call" | custom-call | flops 10000000 | bytes 8000 | tf_op jit(solution)/shard_map/attend/pallas_call | solution.py:264
  74.5 24.1 %attend.3 = (bf16[1024,512]{1,0:T(8,128)(2,1)}, bf16[8,1024,128]{2,1,0:T(8,128)(2,1)}) custom-call(bf16[16,1024,128]{2,1,0:T(8,128)(2,1)} %get-tuple-element.209.q_ref, bf16[8,1024,128]{2,1,0:T(8,128)(2,1)} %get-tuple-element.217.k_ref, bf16[8,1024,128]{2,1,0:T(8,128)(2,1)} %get-tuple-element.211.v_ref), custom_call_target="tpu_custom_call" | custom-call | flops 10000000 | bytes 8000 | tf_op jit(solution)/shard_map/attend/pallas_call | solution.py:264
  106.0 8.3 %output_rows.1 = (f32[1024,1024]{1,0:T(8,128)}, bf16[1024,1024]{1,0:T(8,128)(2,1)}, bf16[1024,1024]{1,0:T(8,128)(2,1)}) custom-call(s32[1]{0:T(128)} %bitcast.refs_0_, bf16[1024,512]{1,0:T(8,128)(2,1)} %get-tuple-element.216.refs_1_.refs_3_.o_ref, bf16[1024,512]{1,0:T(8,128)(2,1)} %get-tuple-element.222.refs_2_.refs_4_.o_ref, bf16[1024,1024]{1,0:T(8,128)(2,1)} %bitcast.34, ...), custom_call_target="tpu_custom_call" | custom-call | flops 5000000 | bytes 15000 | tf_op jit(solution)/shard_map/output_rows/pallas_call | solution.py:381
  114.4 42.3 %feed.3 = (bf16[1024,1024]{1,0:T(8,128)(2,1)}, bf16[1024,1024]{1,0:T(8,128)(2,1)}, bf16[4,576,1024]{2,1,0:T(8,128)(2,1)}, bf16[4,576,1024]{2,1,0:T(8,128)(2,1)}) custom-call(s32[1]{0:T(128)} %bitcast.refs_0_, bf16[1024,1024]{1,0:T(8,128)(2,1)} %get-tuple-element.258.refs_1_, bf16[1024,1024]{1,0:T(8,128)(2,1)} %get-tuple-element.232.refs_2_, ...), custom_call_target="tpu_custom_call" | custom-call | flops 37500000 | bytes 38000 | tf_op jit(solution)/shard_map/feed/pallas_call | solution.py:466
  167.3 42.6 %feed.4 = (bf16[1024,1024]{1,0:T(8,128)(2,1)}, bf16[1024,1024]{1,0:T(8,128)(2,1)}, bf16[4,576,1024]{2,1,0:T(8,128)(2,1)}, bf16[4,576,1024]{2,1,0:T(8,128)(2,1)}) custom-call(s32[1]{0:T(128)} %bitcast.refs_0_, bf16[1024,1024]{1,0:T(8,128)(2,1)} %get-tuple-element.258.refs_1_, bf16[1024,1024]{1,0:T(8,128)(2,1)} %get-tuple-element.232.refs_2_, ...), custom_call_target="tpu_custom_call" | custom-call | flops 37500000 | bytes 38000 | tf_op jit(solution)/shard_map/feed/pallas_call | solution.py:466
  209.9 7.6 %collective-permute-done.29.refs_10_ = bf16[576,1024]{1,0:T(8,128)(2,1)} collective-permute-done((bf16[576,1024]{1,0:T(8,128)(2,1)S(1)}, bf16[576,1024]{1,0:T(8,128)(2,1)}, u32[]{:S(2)}, u32[]{:S(2)}) %collective-permute-start.29) | collective-permute-done | bytes 1179680 | tf_op jit(solution)/shard_map/ppermute | solution.py:766
  218.5 3.7 combine.22
  223.6 3.8 collective-permute-done.30.refs_1_.refs_4_.refs_5_
  227.4 3.7 combine.21
  233.3 42.3 %feed.5 = (bf16[1024,1024]{1,0:T(8,128)(2,1)}, bf16[1024,1024]{1,0:T(8,128)(2,1)}, bf16[4,576,1024]{2,1,0:T(8,128)(2,1)}, bf16[4,576,1024]{2,1,0:T(8,128)(2,1)}) custom-call(s32[1]{0:T(128)} %bitcast.refs_0_, bf16[1024,1024]{1,0:T(8,128)(2,1)} %get-tuple-element.258.refs_1_, bf16[1024,1024]{1,0:T(8,128)(2,1)} %get-tuple-element.232.refs_2_, ...), custom_call_target="tpu_custom_call" | custom-call | flops 37500000 | bytes 38000 | tf_op jit(solution)/shard_map/feed/pallas_call | solution.py:466
  276.6 4.6 combine.23
  281.2 4.7 combine.24
  289.9 14.6 %middle.1 = (f32[1024,1024]{1,0:T(8,128)}, bf16[1024,1024]{1,0:T(8,128)(2,1)}, bf16[1024,1024]{1,0:T(8,128)(2,1)}) custom-call(s32[1]{0:T(128)} %bitcast.refs_0_, f32[1024,1024]{1,0:T(8,128)} %get-tuple-element.353.refs_1_, bf16[1024,1024]{1,0:T(8,128)(2,1)} %bitcast.32, bf16[1024,512]{1,0:T(8,128)(2,1)} %get-tuple-element.216.refs_1_.refs_3_.o_ref, ...), custom_call_target="tpu_custom_call" | custom-call | flops 9000000 | bytes 32000 | tf_op jit(solution)/shard_map/middle/pallas_call | solution.py:535
  304.5 3.7 combine.25
  308.2 23.6 %attend_back.2 = (f32[1024,512]{1,0:T(8,128)}, f32[1024,512]{1,0:T(8,128)}) custom-call(bf16[8,1024,128]{2,1,0:T(8,128)(2,1)} %get-tuple-element.230.q_ref, bf16[8,1024,128]{2,1,0:T(8,128)(2,1)} %get-tuple-element.217.k_ref, bf16[8,1024,128]{2,1,0:T(8,128)(2,1)} %get-tuple-element.211.v_ref, bf16[1024,512]{1,0:T(8,128)(2,1)} %get-tuple-element.216.refs_1_.refs_3_.o_ref, ...), custom_call_target="tpu_custom_call" | custom-call | flops 20000000 | bytes 12000 | tf_op jit(solution)/shard_map/attend_back/pallas_call | solution.py:336
  331.9 7.2 %collective-permute-done.39.refs_6_ = bf16[576,1024]{1,0:T(8,128)(2,1)S(1)} collective-permute-done((bf16[576,1024]{1,0:T(8,128)(2,1)}, bf16[576,1024]{1,0:T(8,128)(2,1)S(1)}, u32[]{:S(2)}, u32[]{:S(2)}) %collective-permute-start.39) | collective-permute-done | bytes 1179680 | tf_op jit(solution)/shard_map/ppermute | solution.py:766
  340.1 5.7 combine.26
  346.9 3.5 collective-permute-start.42
  351.8 24.0 %attend_back.3 = (f32[1024,512]{1,0:T(8,128)}, f32[1024,512]{1,0:T(8,128)}) custom-call(bf16[8,1024,128]{2,1,0:T(8,128)(2,1)} %get-tuple-element.291.q_ref, bf16[8,1024,128]{2,1,0:T(8,128)(2,1)} %get-tuple-element.217.k_ref, bf16[8,1024,128]{2,1,0:T(8,128)(2,1)} %get-tuple-element.211.v_ref, bf16[1024,512]{1,0:T(8,128)(2,1)} %get-tuple-element.222.refs_2_.refs_4_.o_ref, ...), custom_call_target="tpu_custom_call" | custom-call | flops 20000000 | bytes 12000 | tf_op jit(solution)/shard_map/attend_back/pallas_call | solution.py:336
  377.1 5.0 combine.27
  382.1 3.7 combine.28.refs_2_
  389.7 19.8 %raw_back.1 = (bf16[1024,2048]{1,0:T(8,128)(2,1)}, bf16[4,400,1024]{2,1,0:T(8,128)(2,1)}, bf16[4,400,1024]{2,1,0:T(8,128)(2,1)}) custom-call(s32[1]{0:T(128)} %bitcast.refs_0_, f32[1024,512]{1,0:T(8,128)} %get-tuple-element.290.refs_1_, f32[1024,512]{1,0:T(8,128)} %get-tuple-element.309.refs_2_, f32[1024,512]{1,0:T(8,128)} %get-tuple-element.310.refs_3_, ...), custom_call_target="tpu_custom_call" | custom-call | flops 10000000 | bytes 30000 | tf_op jit(solution)/shard_map/raw_back/pallas_call | solution.py:621
  413.4 4.3 combine.29
  417.7 4.3 combine.30.refs_0_
  423.3 6.6 %collective-permute-start.52 = (bf16[576,1024]{1,0:T(8,128)(2,1)}, bf16[576,1024]{1,0:T(8,128)(2,1)}, u32[]{:S(2)}, u32[]{:S(2)}) collective-permute-start(bf16[576,1024]{1,0:T(8,128)(2,1)} %combine.30.refs_0_), channel_id=1, source_target_pairs={{0,8},{24,16},{1,9},{25,17},{2,10},{26,18},{3,11},{27,19},{4,12},{... | collective-permute-start | bytes 3538952 | tf_op jit(solution)/shard_map/ppermute | solution.py:819
  429.9 4.4 combine.31
  434.3 4.3 combine.32
  442.1 11.2 %input_back.1 = f32[1024,1024]{1,0:T(8,128)} custom-call(s32[1]{0:T(128)} %bitcast.refs_0_, bf16[1024,2048]{1,0:T(8,128)(2,1)} %get-tuple-element.340.refs_1_, bf16[1024,1024]{1,0:T(8,128)(2,1)} %bitcast.35, f32[1024,1024]{1,0:T(8,128)} %get-tuple-element.341.refs_3_, f32[16,1024]{1,0:T(8,128)} %get-tuple-element.223.refs_4_.refs_5_.refs_10_, ...), custom_call_target="tpu_custom_call" | custom-call | flops 6000000 | bytes 18000 | tf_op jit(solution)/shard_map/input_back/pallas_call | solution.py:651
  453.4 6.4 %collective-permute-done.50.refs_3_ = bf16[400,512]{1,0:T(8,128)(2,1)S(1)} collective-permute-done((bf16[400,512]{1,0:T(8,128)(2,1)}, bf16[400,512]{1,0:T(8,128)(2,1)S(1)}, u32[]{:S(2)}, u32[]{:S(2)}) %collective-permute-start.50) | collective-permute-done | bytes 409632 | tf_op jit(solution)/shard_map/ppermute | solution.py:766
  460.5 4.1 combine.33.refs_0_
  466.3 6.4 %add_convert_fusion = bf16[1024,1024]{1,0:T(8,128)(2,1)} fusion(f32[1024,1024]{1,0:T(8,128)} %get-tuple-element.353.refs_1_, bf16[1024,1024]{1,0:T(8,128)(2,1)} %get-tuple-element.356, bf16[1024,1024]{1,0:T(8,128)(2,1)} %get-tuple-element.355, bf16[1024,1024]{1,0:T(8,128)(2,1)S(1)} %copy-done.17), kind=kLoop, calls=%fused_computation | loop fusion | flops 7340032 | bytes 12582912 | tf_op jit(solution)/shard_map/convert_element_type | solution.py:1097
  472.7 3.8 combine.34.refs_0_
  481.7 8.9 %collective-permute-done.54.refs_2_ = bf16[400,512]{1,0:T(8,128)(2,1)S(1)} collective-permute-done((bf16[400,512]{1,0:T(8,128)(2,1)S(1)}, bf16[400,512]{1,0:T(8,128)(2,1)S(1)}, u32[]{:S(2)}, u32[]{:S(2)}) %collective-permute-start.54) | collective-permute-done | bytes 409632 | tf_op jit(solution)/shard_map/ppermute | solution.py:766
  493.8 3.7 collective-permute-done.55.refs_3_
  499.0 4.1 combine.35.refs_0_
  506.1 3.7 combine.36.refs_2_
  511.8 3.6 combine.37.refs_0_
  516.2 3.6 combine.38.refs_0_
  519.8 3.8 combine.39.refs_4_
  526.4 14.4 %collective-permute-done.59.refs_3_ = bf16[576,1024]{1,0:T(8,128)(2,1)S(1)} collective-permute-done((bf16[576,1024]{1,0:T(8,128)(2,1)}, bf16[576,1024]{1,0:T(8,128)(2,1)S(1)}, u32[]{:S(2)}, u32[]{:S(2)}) %collective-permute-start.59) | collective-permute-done | bytes 1179680 | tf_op jit(solution)/shard_map/ppermute | solution.py:819
  540.8 3.8 combine.40
  546.6 3.6 combine.41
  551.5 14.5 %collective-permute-done.62.refs_5_ = bf16[576,1024]{1,0:T(8,128)(2,1)S(1)} collective-permute-done((bf16[576,1024]{1,0:T(8,128)(2,1)}, bf16[576,1024]{1,0:T(8,128)(2,1)S(1)}, u32[]{:S(2)}, u32[]{:S(2)}) %collective-permute-start.62) | collective-permute-done | bytes 1179680 | tf_op jit(solution)/shard_map/ppermute | solution.py:819
  567.1 7.5 %unpack_rows.1 = (f32[128,4608]{1,0:T(8,128)}, f32[128,4608]{1,0:T(8,128)}, f32[576,1024]{1,0:T(8,128)}) custom-call(s32[1]{0:T(128)} %bitcast.8.flag_ref, bf16[576,1024]{1,0:T(8,128)(2,1)} %get-tuple-element.346.refs_0_, bf16[576,1024]{1,0:T(8,128)(2,1)} %collective-permute-done.48.refs_1_, bf16[576,1024]{1,0:T(8,128)(2,1)} %combine.36.refs_2_, ...), custom_call_target="tpu_custom_call" | custom-call | bytes 14000 | tf_op jit(solution)/shard_map/unpack_rows/pallas_call | solution.py:743
  (292 shorter events, 111.3 us)
Async XLA Ops:
  5.7 15.6 %collective-permute-start = (bf16[272,1024]{1,0:T(8,128)(2,1)S(1)}, bf16[272,1024]{1,0:T(8,128)(2,1)S(1)}, u32[]{:S(2)}, u32[]{:S(2)}) collective-permute-start(bf16[272,1024]{1,0:T(8,128)(2,1)S(1)} %concatenate.41.refs_6_.refs_7_.refs_22_.refs_5_), channel_id=1, source_target_pairs={{0,2},{1,3},{2,0},{3,1},{4,6},{5,7},{6,4},{7,5},{8,10},{9,11},{10,... | collective-permute-start | bytes 1671176 | tf_op jit(solution)/shard_map/ppermute | solution.py:766
  31.1 38.1 %collective-permute-start.9 = (bf16[704,1024]{1,0:T(8,128)(2,1)}, bf16[704,1024]{1,0:T(8,128)(2,1)S(1)}, u32[]{:S(2)}, u32[]{:S(2)}) collective-permute-start(bf16[704,1024]{1,0:T(8,128)(2,1)} %get-tuple-element.215.refs_5_.refs_4_.refs_9_), channel_id=1, source_target_pairs={{0,2},{1,3},{2,0},{3,1},{4,6},{5,7},{6,4},{7,5},{8,10},{9,11},{10,... | collective-permute-start | bytes 4325384 | tf_op jit(solution)/shard_map/ppermute | solution.py:766
  31.8 37.4 %collective-permute-start.10 = (bf16[704,1024]{1,0:T(8,128)(2,1)}, bf16[704,1024]{1,0:T(8,128)(2,1)S(1)}, u32[]{:S(2)}, u32[]{:S(2)}) collective-permute-start(bf16[704,1024]{1,0:T(8,128)(2,1)} %get-tuple-element.215.refs_5_.refs_4_.refs_9_), channel_id=1, source_target_pairs={{0,4},{1,5},{2,6},{3,7},{4,0},{5,1},{6,2},{7,3},{8,12},{9,13},{10,... | collective-permute-start | bytes 4325384 | tf_op jit(solution)/shard_map/ppermute | solution.py:766
  32.6 36.6 %collective-permute-start.11 = (bf16[704,1024]{1,0:T(8,128)(2,1)}, bf16[704,1024]{1,0:T(8,128)(2,1)}, u32[]{:S(2)}, u32[]{:S(2)}) collective-permute-start(bf16[704,1024]{1,0:T(8,128)(2,1)} %get-tuple-element.215.refs_5_.refs_4_.refs_9_), channel_id=1, source_target_pairs={{0,1},{1,0},{2,3},{3,2},{4,5},{5,4},{6,7},{7,6},{8,9},{9,8},{10,11... | collective-permute-start | bytes 4325384 | tf_op jit(solution)/shard_map/ppermute | solution.py:766
  69.2 29.5 %collective-permute-start.14 = (bf16[704,1024]{1,0:T(8,128)(2,1)S(1)}, bf16[704,1024]{1,0:T(8,128)(2,1)}, u32[]{:S(2)}, u32[]{:S(2)}) collective-permute-start(bf16[704,1024]{1,0:T(8,128)(2,1)S(1)} %collective-permute-done.9.refs_7_.refs_6_.refs_11_), channel_id=1, source_target_pairs={{0,1},{1,0},{2,3},{3,2},{4,5},{5,4},{6,7},{7,6},{8,9},{9,8},{10,11... | collective-permute-start | bytes 4325384 | tf_op jit(solution)/shard_map/ppermute | solution.py:766
  69.7 29.0 %collective-permute-start.15 = (bf16[704,1024]{1,0:T(8,128)(2,1)S(1)}, bf16[704,1024]{1,0:T(8,128)(2,1)}, u32[]{:S(2)}, u32[]{:S(2)}) collective-permute-start(bf16[704,1024]{1,0:T(8,128)(2,1)S(1)} %collective-permute-done.10.refs_9_.refs_8_.refs_13_), channel_id=1, source_target_pairs={{0,1},{1,0},{2,3},{3,2},{4,5},{5,4},{6,7},{7,6},{8,9},{9,8},{10,11... | collective-permute-start | bytes 4325384 | tf_op jit(solution)/shard_map/ppermute | solution.py:766
  71.9 26.8 %collective-permute-start.12 = (bf16[704,512]{1,0:T(8,128)(2,1)}, bf16[704,512]{1,0:T(8,128)(2,1)S(1)}, u32[]{:S(2)}, u32[]{:S(2)}) collective-permute-start(bf16[704,512]{1,0:T(8,128)(2,1)} %slice.65), channel_id=1, source_target_pairs={{0,2},{1,3},{2,0},{3,1},{4,6},{5,7},{6,4},{7,5},{8,10},{9,11},{10,... | collective-permute-start | bytes 2162696 | tf_op jit(solution)/shard_map/ppermute | solution.py:766
  73.3 25.3 %collective-permute-start.13 = (bf16[704,512]{1,0:T(8,128)(2,1)}, bf16[704,512]{1,0:T(8,128)(2,1)}, u32[]{:S(2)}, u32[]{:S(2)}) collective-permute-start(bf16[704,512]{1,0:T(8,128)(2,1)} %slice.66), channel_id=1, source_target_pairs={{0,4},{1,5},{2,6},{3,7},{4,0},{5,1},{6,2},{7,3},{8,12},{9,13},{10,... | collective-permute-start | bytes 2162696 | tf_op jit(solution)/shard_map/ppermute | solution.py:766
  98.8 57.9 %collective-permute-start.18 = (bf16[576,1024]{1,0:T(8,128)(2,1)}, bf16[576,1024]{1,0:T(8,128)(2,1)S(1)}, u32[]{:S(2)}, u32[]{:S(2)}) collective-permute-start(bf16[576,1024]{1,0:T(8,128)(2,1)} %get-tuple-element.238.refs_4_), channel_id=1, source_target_pairs={{0,1},{1,0},{2,3},{3,2},{4,5},{5,4},{6,7},{7,6},{8,9},{9,8},{10,11... | collective-permute-start | bytes 3538952 | tf_op jit(solution)/shard_map/ppermute | solution.py:766
  99.3 57.4 %collective-permute-start.19 = (bf16[576,1024]{1,0:T(8,128)(2,1)}, bf16[576,1024]{1,0:T(8,128)(2,1)}, u32[]{:S(2)}, u32[]{:S(2)}) collective-permute-start(bf16[576,1024]{1,0:T(8,128)(2,1)} %get-tuple-element.238.refs_4_), channel_id=1, source_target_pairs={{0,2},{1,3},{2,0},{3,1},{4,6},{5,7},{6,4},{7,5},{8,10},{9,11},{10,... | collective-permute-start | bytes 3538952 | tf_op jit(solution)/shard_map/ppermute | solution.py:766
  99.9 56.8 %collective-permute-start.20 = (bf16[576,1024]{1,0:T(8,128)(2,1)}, bf16[576,1024]{1,0:T(8,128)(2,1)}, u32[]{:S(2)}, u32[]{:S(2)}) collective-permute-start(bf16[576,1024]{1,0:T(8,128)(2,1)} %get-tuple-element.238.refs_4_), channel_id=1, source_target_pairs={{0,4},{1,5},{2,6},{3,7},{4,0},{5,1},{6,2},{7,3},{8,12},{9,13},{10,... | collective-permute-start | bytes 3538952 | tf_op jit(solution)/shard_map/ppermute | solution.py:766
  100.7 56.0 %collective-permute-start.21 = (bf16[576,1024]{1,0:T(8,128)(2,1)}, bf16[576,1024]{1,0:T(8,128)(2,1)}, u32[]{:S(2)}, u32[]{:S(2)}) collective-permute-start(bf16[576,1024]{1,0:T(8,128)(2,1)} %get-tuple-element.238.refs_4_), channel_id=1, source_target_pairs={{0,6},{1,7},{2,4},{3,5},{4,2},{5,3},{6,0},{7,1},{8,14},{9,15},{10,... | collective-permute-start | bytes 3538952 | tf_op jit(solution)/shard_map/ppermute | solution.py:766
  163.2 54.3 %collective-permute-start.25 = (bf16[4,576,1024]{2,1,0:T(8,128)(2,1)}, bf16[4,576,1024]{2,1,0:T(8,128)(2,1)}, u32[]{:S(2)}, u32[]{:S(2)}) collective-permute-start(bf16[4,576,1024]{2,1,0:T(8,128)(2,1)} %get-tuple-element.250), channel_id=1, source_target_pairs={{0,1},{1,0},{2,3},{3,2},{4,5},{5,4},{6,7},{7,6},{8,9},{9,8},{10,11... | collective-permute-start | bytes 14155784 | tf_op jit(solution)/shard_map/ppermute | solution.py:766
  163.4 46.5 %collective-permute-start.26 = (bf16[576,1024]{1,0:T(8,128)(2,1)S(1)}, bf16[576,1024]{1,0:T(8,128)(2,1)}, u32[]{:S(2)}, u32[]{:S(2)}) collective-permute-start(bf16[576,1024]{1,0:T(8,128)(2,1)S(1)} %copy-done.23), channel_id=1, source_target_pairs={{0,1},{1,0},{2,3},{3,2},{4,5},{5,4},{6,7},{7,6},{8,9},{9,8},{10,11... | collective-permute-start | bytes 3538952 | tf_op jit(solution)/shard_map/ppermute | solution.py:766
  163.8 46.1 %collective-permute-start.27 = (bf16[576,1024]{1,0:T(8,128)(2,1)S(1)}, bf16[576,1024]{1,0:T(8,128)(2,1)}, u32[]{:S(2)}, u32[]{:S(2)}) collective-permute-start(bf16[576,1024]{1,0:T(8,128)(2,1)S(1)} %copy-done.23), channel_id=1, source_target_pairs={{0,2},{1,3},{2,0},{3,1},{4,6},{5,7},{6,4},{7,5},{8,10},{9,11},{10,... | collective-permute-start | bytes 3538952 | tf_op jit(solution)/shard_map/ppermute | solution.py:766
  164.4 45.5 %collective-permute-start.28 = (bf16[576,1024]{1,0:T(8,128)(2,1)S(1)}, bf16[576,1024]{1,0:T(8,128)(2,1)}, u32[]{:S(2)}, u32[]{:S(2)}) collective-permute-start(bf16[576,1024]{1,0:T(8,128)(2,1)S(1)} %copy-done.23), channel_id=1, source_target_pairs={{0,4},{1,5},{2,6},{3,7},{4,0},{5,1},{6,2},{7,3},{8,12},{9,13},{10,... | collective-permute-start | bytes 3538952 | tf_op jit(solution)/shard_map/ppermute | solution.py:766
  165.2 52.3 %collective-permute-start.29 = (bf16[576,1024]{1,0:T(8,128)(2,1)S(1)}, bf16[576,1024]{1,0:T(8,128)(2,1)}, u32[]{:S(2)}, u32[]{:S(2)}) collective-permute-start(bf16[576,1024]{1,0:T(8,128)(2,1)S(1)} %copy-done.23), channel_id=1, source_target_pairs={{0,6},{1,7},{2,4},{3,5},{4,2},{5,3},{6,0},{7,1},{8,14},{9,15},{10,... | collective-permute-start | bytes 3538952 | tf_op jit(solution)/shard_map/ppermute | solution.py:766
  217.5 14.8 %collective-permute-start.31 = (bf16[576,1024]{1,0:T(8,128)(2,1)}, bf16[576,1024]{1,0:T(8,128)(2,1)S(1)}, u32[]{:S(2)}, u32[]{:S(2)}) collective-permute-start(bf16[576,1024]{1,0:T(8,128)(2,1)} %collective-permute-done.27.refs_6_), channel_id=1, source_target_pairs={{0,1},{1,0},{2,3},{3,2},{4,5},{5,4},{6,7},{7,6},{8,9},{9,8},{10,11... | collective-permute-start | bytes 3538952 | tf_op jit(solution)/shard_map/ppermute | solution.py:766
  218.0 14.3 %collective-permute-start.32 = (bf16[576,1024]{1,0:T(8,128)(2,1)}, bf16[576,1024]{1,0:T(8,128)(2,1)}, u32[]{:S(2)}, u32[]{:S(2)}) collective-permute-start(bf16[576,1024]{1,0:T(8,128)(2,1)} %collective-permute-done.28.refs_8_), channel_id=1, source_target_pairs={{0,1},{1,0},{2,3},{3,2},{4,5},{5,4},{6,7},{7,6},{8,9},{9,8},{10,11... | collective-permute-start | bytes 3538952 | tf_op jit(solution)/shard_map/ppermute | solution.py:766
  218.0 14.3 %collective-permute-start.33 = (bf16[576,1024]{1,0:T(8,128)(2,1)}, bf16[576,1024]{1,0:T(8,128)(2,1)}, u32[]{:S(2)}, u32[]{:S(2)}) collective-permute-start(bf16[576,1024]{1,0:T(8,128)(2,1)} %collective-permute-done.29.refs_10_), channel_id=1, source_target_pairs={{0,1},{1,0},{2,3},{3,2},{4,5},{5,4},{6,7},{7,6},{8,9},{9,8},{10,11... | collective-permute-start | bytes 3538952 | tf_op jit(solution)/shard_map/ppermute | solution.py:766
  222.2 53.3 %collective-permute-start.34 = (bf16[576,1024]{1,0:T(8,128)(2,1)}, bf16[576,1024]{1,0:T(8,128)(2,1)S(1)}, u32[]{:S(2)}, u32[]{:S(2)}) collective-permute-start(bf16[576,1024]{1,0:T(8,128)(2,1)} %combine.22), channel_id=1, source_target_pairs={{0,2},{1,3},{2,0},{3,1},{4,6},{5,7},{6,4},{7,5},{8,10},{9,11},{10,... | collective-permute-start | bytes 3538952 | tf_op jit(solution)/shard_map/ppermute | solution.py:766
  231.1 44.5 %collective-permute-start.35 = (bf16[576,1024]{1,0:T(8,128)(2,1)}, bf16[576,1024]{1,0:T(8,128)(2,1)S(1)}, u32[]{:S(2)}, u32[]{:S(2)}) collective-permute-start(bf16[576,1024]{1,0:T(8,128)(2,1)} %combine.21), channel_id=1, source_target_pairs={{0,4},{1,5},{2,6},{3,7},{4,0},{5,1},{6,2},{7,3},{8,12},{9,13},{10,... | collective-permute-start | bytes 3538952 | tf_op jit(solution)/shard_map/ppermute | solution.py:766
  275.6 28.8 %collective-permute-start.36 = (bf16[4,576,1024]{2,1,0:T(8,128)(2,1)}, bf16[4,576,1024]{2,1,0:T(8,128)(2,1)}, u32[]{:S(2)}, u32[]{:S(2)}) collective-permute-start(bf16[4,576,1024]{2,1,0:T(8,128)(2,1)} %get-tuple-element.281), channel_id=1, source_target_pairs={{0,1},{1,0},{2,3},{3,2},{4,5},{5,4},{6,7},{7,6},{8,9},{9,8},{10,11... | collective-permute-start | bytes 14155784 | tf_op jit(solution)/shard_map/ppermute | solution.py:766
  285.8 46.0 %collective-permute-start.37 = (bf16[576,1024]{1,0:T(8,128)(2,1)}, bf16[576,1024]{1,0:T(8,128)(2,1)S(1)}, u32[]{:S(2)}, u32[]{:S(2)}) collective-permute-start(bf16[576,1024]{1,0:T(8,128)(2,1)} %get-tuple-element.272), channel_id=1, source_target_pairs={{0,2},{1,3},{2,0},{3,1},{4,6},{5,7},{6,4},{7,5},{8,10},{9,11},{10,... | collective-permute-start | bytes 3538952 | tf_op jit(solution)/shard_map/ppermute | solution.py:766
  286.9 44.9 %collective-permute-start.38 = (bf16[576,1024]{1,0:T(8,128)(2,1)}, bf16[576,1024]{1,0:T(8,128)(2,1)S(1)}, u32[]{:S(2)}, u32[]{:S(2)}) collective-permute-start(bf16[576,1024]{1,0:T(8,128)(2,1)} %get-tuple-element.273), channel_id=1, source_target_pairs={{0,4},{1,5},{2,6},{3,7},{4,0},{5,1},{6,2},{7,3},{8,12},{9,13},{10,... | collective-permute-start | bytes 3538952 | tf_op jit(solution)/shard_map/ppermute | solution.py:766
  288.2 50.9 %collective-permute-start.39 = (bf16[576,1024]{1,0:T(8,128)(2,1)}, bf16[576,1024]{1,0:T(8,128)(2,1)S(1)}, u32[]{:S(2)}, u32[]{:S(2)}) collective-permute-start(bf16[576,1024]{1,0:T(8,128)(2,1)} %get-tuple-element.288), channel_id=1, source_target_pairs={{0,2},{1,3},{2,0},{3,1},{4,6},{5,7},{6,4},{7,5},{8,10},{9,11},{10,... | collective-permute-start | bytes 3538952 | tf_op jit(solution)/shard_map/ppermute | solution.py:766
  288.8 51.2 %collective-permute-start.40 = (bf16[576,1024]{1,0:T(8,128)(2,1)}, bf16[576,1024]{1,0:T(8,128)(2,1)}, u32[]{:S(2)}, u32[]{:S(2)}) collective-permute-start(bf16[576,1024]{1,0:T(8,128)(2,1)} %get-tuple-element.289), channel_id=1, source_target_pairs={{0,4},{1,5},{2,6},{3,7},{4,0},{5,1},{6,2},{7,3},{8,12},{9,13},{10,... | collective-permute-start | bytes 3538952 | tf_op jit(solution)/shard_map/ppermute | solution.py:766
  345.8 30.1 %collective-permute-start.41 = (bf16[576,1024]{1,0:T(8,128)(2,1)}, bf16[576,1024]{1,0:T(8,128)(2,1)S(1)}, u32[]{:S(2)}, u32[]{:S(2)}) collective-permute-start(bf16[576,1024]{1,0:T(8,128)(2,1)} %combine.25), channel_id=1, source_target_pairs={{0,2},{1,3},{2,0},{3,1},{4,6},{5,7},{6,4},{7,5},{8,10},{9,11},{10,... | collective-permute-start | bytes 3538952 | tf_op jit(solution)/shard_map/ppermute | solution.py:766
  346.9 30.2 %collective-permute-start.42 = (bf16[576,1024]{1,0:T(8,128)(2,1)}, bf16[576,1024]{1,0:T(8,128)(2,1)S(1)}, u32[]{:S(2)}, u32[]{:S(2)}) collective-permute-start(bf16[576,1024]{1,0:T(8,128)(2,1)} %get-tuple-element.303.refs_0_), channel_id=1, source_target_pairs={{0,8},{24,16},{1,9},{25,17},{2,10},{26,18},{3,11},{27,19},{4,12},{... | collective-permute-start | bytes 3538952 | tf_op jit(solution)/shard_map/ppermute | solution.py:819
  350.4 59.1 %collective-permute-start.45 = (bf16[576,1024]{1,0:T(8,128)(2,1)}, bf16[576,1024]{1,0:T(8,128)(2,1)S(1)}, u32[]{:S(2)}, u32[]{:S(2)}) collective-permute-start(bf16[576,1024]{1,0:T(8,128)(2,1)} %get-tuple-element.321.refs_0_), channel_id=1, source_target_pairs={{0,8},{24,16},{1,9},{25,17},{2,10},{26,18},{3,11},{27,19},{4,12},{... | collective-permute-start | bytes 3538952 | tf_op jit(solution)/shard_map/ppermute | solution.py:819
  385.8 25.9 %collective-permute-start.43 = (bf16[576,1024]{1,0:T(8,128)(2,1)}, bf16[576,1024]{1,0:T(8,128)(2,1)S(1)}, u32[]{:S(2)}, u32[]{:S(2)}) collective-permute-start(bf16[576,1024]{1,0:T(8,128)(2,1)} %get-tuple-element.319), channel_id=1, source_target_pairs={{0,2},{1,3},{2,0},{3,1},{4,6},{5,7},{6,4},{7,5},{8,10},{9,11},{10,... | collective-permute-start | bytes 3538952 | tf_op jit(solution)/shard_map/ppermute | solution.py:766
  386.8 25.7 %collective-permute-start.44 = (bf16[576,1024]{1,0:T(8,128)(2,1)}, bf16[576,1024]{1,0:T(8,128)(2,1)S(1)}, u32[]{:S(2)}, u32[]{:S(2)}) collective-permute-start(bf16[576,1024]{1,0:T(8,128)(2,1)} %get-tuple-element.320), channel_id=1, source_target_pairs={{0,4},{1,5},{2,6},{3,7},{4,0},{5,1},{6,2},{7,3},{8,12},{9,13},{10,... | collective-permute-start | bytes 3538952 | tf_op jit(solution)/shard_map/ppermute | solution.py:766
  387.9 24.5 %collective-permute-start.46 = (bf16[576,1024]{1,0:T(8,128)(2,1)}, bf16[576,1024]{1,0:T(8,128)(2,1)}, u32[]{:S(2)}, u32[]{:S(2)}) collective-permute-start(bf16[576,1024]{1,0:T(8,128)(2,1)} %combine.28.refs_2_), channel_id=1, source_target_pairs={{8,16},{16,8},{9,17},{17,9},{10,18},{18,10},{11,19},{19,11},{12,20... | collective-permute-start | bytes 3538952 | tf_op jit(solution)/shard_map/ppermute | solution.py:819
  422.0 37.8 %collective-permute-start.48 = (bf16[576,1024]{1,0:T(8,128)(2,1)}, bf16[576,1024]{1,0:T(8,128)(2,1)}, u32[]{:S(2)}, u32[]{:S(2)}) collective-permute-start(bf16[576,1024]{1,0:T(8,128)(2,1)} %get-tuple-element.346.refs_0_), channel_id=1, source_target_pairs={{8,0},{16,24},{9,1},{17,25},{10,2},{18,26},{11,3},{19,27},{12,4},{... | collective-permute-start | bytes 3538952 | tf_op jit(solution)/shard_map/ppermute | solution.py:819
  423.3 49.4 %collective-permute-start.52 = (bf16[576,1024]{1,0:T(8,128)(2,1)}, bf16[576,1024]{1,0:T(8,128)(2,1)}, u32[]{:S(2)}, u32[]{:S(2)}) collective-permute-start(bf16[576,1024]{1,0:T(8,128)(2,1)} %combine.30.refs_0_), channel_id=1, source_target_pairs={{0,8},{24,16},{1,9},{25,17},{2,10},{26,18},{3,11},{27,19},{4,12},{... | collective-permute-start | bytes 3538952 | tf_op jit(solution)/shard_map/ppermute | solution.py:819
  438.6 14.7 %collective-permute-start.49 = (bf16[400,512]{1,0:T(8,128)(2,1)}, bf16[400,512]{1,0:T(8,128)(2,1)S(1)}, u32[]{:S(2)}, u32[]{:S(2)}) collective-permute-start(bf16[400,512]{1,0:T(8,128)(2,1)} %get-tuple-element.347), channel_id=1, source_target_pairs={{0,2},{1,3},{2,0},{3,1},{4,6},{5,7},{6,4},{7,5},{8,10},{9,11},{10,... | collective-permute-start | bytes 1228808 | tf_op jit(solution)/shard_map/ppermute | solution.py:766
  439.8 20.0 %collective-permute-start.50 = (bf16[400,512]{1,0:T(8,128)(2,1)}, bf16[400,512]{1,0:T(8,128)(2,1)S(1)}, u32[]{:S(2)}, u32[]{:S(2)}) collective-permute-start(bf16[400,512]{1,0:T(8,128)(2,1)} %get-tuple-element.348), channel_id=1, source_target_pairs={{0,4},{1,5},{2,6},{3,7},{4,0},{5,1},{6,2},{7,3},{8,12},{9,13},{10,... | collective-permute-start | bytes 1228808 | tf_op jit(solution)/shard_map/ppermute | solution.py:766
  441.0 18.8 %collective-permute-start.51 = (bf16[400,512]{1,0:T(8,128)(2,1)}, bf16[400,512]{1,0:T(8,128)(2,1)}, u32[]{:S(2)}, u32[]{:S(2)}) collective-permute-start(bf16[400,512]{1,0:T(8,128)(2,1)} %get-tuple-element.349), channel_id=1, source_target_pairs={{0,6},{1,7},{2,4},{3,5},{4,2},{5,3},{6,0},{7,1},{8,14},{9,15},{10,... | collective-permute-start | bytes 1228808 | tf_op jit(solution)/shard_map/ppermute | solution.py:766
  464.6 41.4 %collective-permute-start.53 = (bf16[576,1024]{1,0:T(8,128)(2,1)S(1)}, bf16[576,1024]{1,0:T(8,128)(2,1)}, u32[]{:S(2)}, u32[]{:S(2)}) collective-permute-start(bf16[576,1024]{1,0:T(8,128)(2,1)S(1)} %copy-done.37), channel_id=1, source_target_pairs={{8,16},{16,8},{9,17},{17,9},{10,18},{18,10},{11,19},{19,11},{12,20... | collective-permute-start | bytes 3538952 | tf_op jit(solution)/shard_map/ppermute | solution.py:819
  476.6 43.3 %collective-permute-start.60 = (bf16[576,1024]{1,0:T(8,128)(2,1)}, bf16[576,1024]{1,0:T(8,128)(2,1)}, u32[]{:S(2)}, u32[]{:S(2)}) collective-permute-start(bf16[576,1024]{1,0:T(8,128)(2,1)} %combine.34.refs_0_), channel_id=1, source_target_pairs={{8,16},{16,8},{9,17},{17,9},{10,18},{18,10},{11,19},{19,11},{12,20... | collective-permute-start | bytes 3538952 | tf_op jit(solution)/shard_map/ppermute | solution.py:819
  478.5 19.0 %collective-permute-start.55 = (bf16[400,512]{1,0:T(8,128)(2,1)S(1)}, bf16[400,512]{1,0:T(8,128)(2,1)S(1)}, u32[]{:S(2)}, u32[]{:S(2)}) collective-permute-start(bf16[400,512]{1,0:T(8,128)(2,1)S(1)} %copy-done.60), channel_id=1, source_target_pairs={{0,4},{1,5},{2,6},{3,7},{4,0},{5,1},{6,2},{7,3},{8,12},{9,13},{10,... | collective-permute-start | bytes 1228808 | tf_op jit(solution)/shard_map/ppermute | solution.py:766
  480.1 17.4 %collective-permute-start.56 = (bf16[400,512]{1,0:T(8,128)(2,1)S(1)}, bf16[400,512]{1,0:T(8,128)(2,1)S(1)}, u32[]{:S(2)}, u32[]{:S(2)}) collective-permute-start(bf16[400,512]{1,0:T(8,128)(2,1)S(1)} %copy-done.59), channel_id=1, source_target_pairs={{0,6},{1,7},{2,4},{3,5},{4,2},{5,3},{6,0},{7,1},{8,14},{9,15},{10,... | collective-permute-start | bytes 1228808 | tf_op jit(solution)/shard_map/ppermute | solution.py:766
  490.7 20.4 %collective-permute-start.57 = (bf16[400,512]{1,0:T(8,128)(2,1)S(1)}, bf16[400,512]{1,0:T(8,128)(2,1)S(1)}, u32[]{:S(2)}, u32[]{:S(2)}) collective-permute-start(bf16[400,512]{1,0:T(8,128)(2,1)S(1)} %copy-done.22), channel_id=1, source_target_pairs={{0,8},{24,16},{1,9},{25,17},{2,10},{26,18},{3,11},{27,19},{4,12},{... | collective-permute-start | bytes 1228808 | tf_op jit(solution)/shard_map/ppermute | solution.py:819
  509.8 31.0 %collective-permute-start.59 = (bf16[576,1024]{1,0:T(8,128)(2,1)}, bf16[576,1024]{1,0:T(8,128)(2,1)S(1)}, u32[]{:S(2)}, u32[]{:S(2)}) collective-permute-start(bf16[576,1024]{1,0:T(8,128)(2,1)} %combine.36.refs_2_), channel_id=1, source_target_pairs={{8,0},{16,24},{9,1},{17,25},{10,2},{18,26},{11,3},{19,27},{12,4},{... | collective-permute-start | bytes 3538952 | tf_op jit(solution)/shard_map/ppermute | solution.py:819
  523.6 42.4 %collective-permute-start.62 = (bf16[576,1024]{1,0:T(8,128)(2,1)}, bf16[576,1024]{1,0:T(8,128)(2,1)S(1)}, u32[]{:S(2)}, u32[]{:S(2)}) collective-permute-start(bf16[576,1024]{1,0:T(8,128)(2,1)} %combine.39.refs_4_), channel_id=1, source_target_pairs={{8,0},{16,24},{9,1},{17,25},{10,2},{18,26},{11,3},{19,27},{12,4},{... | collective-permute-start | bytes 3538952 | tf_op jit(solution)/shard_map/ppermute | solution.py:819
  525.6 20.2 %collective-permute-start.63 = (bf16[400,512]{1,0:T(8,128)(2,1)S(1)}, bf16[400,512]{1,0:T(8,128)(2,1)S(1)}, u32[]{:S(2)}, u32[]{:S(2)}) collective-permute-start(bf16[400,512]{1,0:T(8,128)(2,1)S(1)} %copy-done.20), channel_id=1, source_target_pairs={{8,16},{16,8},{9,17},{17,9},{10,18},{18,10},{11,19},{19,11},{12,20... | collective-permute-start | bytes 1228808 | tf_op jit(solution)/shard_map/ppermute | solution.py:819
  544.6 30.0 %collective-permute-start.64 = (bf16[400,512]{1,0:T(8,128)(2,1)}, bf16[400,512]{1,0:T(8,128)(2,1)S(1)}, u32[]{:S(2)}, u32[]{:S(2)}) collective-permute-start(bf16[400,512]{1,0:T(8,128)(2,1)} %combine.40), channel_id=1, source_target_pairs={{8,0},{16,24},{9,1},{17,25},{10,2},{18,26},{11,3},{19,27},{12,4},{... | collective-permute-start | bytes 1228808 | tf_op jit(solution)/shard_map/ppermute | solution.py:819
  550.2 27.6 %collective-permute-start.65 = (bf16[400,512]{1,0:T(8,128)(2,1)}, bf16[400,512]{1,0:T(8,128)(2,1)S(1)}, u32[]{:S(2)}, u32[]{:S(2)}) collective-permute-start(bf16[400,512]{1,0:T(8,128)(2,1)} %combine.41), channel_id=1, source_target_pairs={{8,0},{16,24},{9,1},{17,25},{10,2},{18,26},{11,3},{19,27},{12,4},{... | collective-permute-start | bytes 1228808 | tf_op jit(solution)/shard_map/ppermute | solution.py:819
  (80 other events, 491.0 us)

commit v5 on v4

--- a/solution.py
+++ b/solution.py
@@ -610,13 +610,13 @@
                 ref[q ^ half, :rows, :] = block[:, :1024]
                 ref[q ^ half, rows : 2 * rows, :] = block[:, 1024:]
                 ref[q ^ half, 2 * rows : 3 * rows, :] = wo_ref[source, :]
-                ref[q ^ half, 3 * rows :, :] = jnp.zeros((16, 1024), BF16)
+                ref[q ^ half, 3 * rows :, :] = jnp.zeros((32, 1024), BF16)
                 ref[q ^ half, 3 * rows :, :128] = more
 
 
 def raw_back(parts, me, halves, units, normed, cosine, sine, gains, grad_out):
     length, width = normed.shape
-    rows = 3 * (width // parts) + 16
+    rows = 3 * (width // parts) + 32
     grads = fixed((parts // 2, rows, 1024))
     return pl.pallas_call(
         lambda *refs: raw_back_kernel(parts, *refs),
@@ -627,7 +627,7 @@
         out_specs=[by_rows(2048), grads, grads],
         out_shape=[jax.ShapeDtypeStruct((length, 2048), BF16)]
         + [jax.ShapeDtypeStruct((parts // 2, rows, 1024), BF16)] * 2,
-        scratch_shapes=[pltpu.VMEM((width, 2048), F32), pltpu.VMEM((16, 128), F32)],
+        scratch_shapes=[pltpu.VMEM((width, 2048), F32), pltpu.VMEM((32, 128), F32)],
         compiler_params=params(),
         cost_estimate=cost(10, 30),
         name="raw_back",
@@ -781,17 +781,15 @@
     return Pieces(groups)
 
 
-def combine(*outputs, half=None):
+def combine(*outputs):
     terms = [term if isinstance(term, tuple) else (term, None) for out in outputs for term in out]
     rows, width = terms[0][0].shape[-2:]
-    wide = width if half is None else width // 2
-    step = rows // (5 if rows % 64 else 4)
-
-    def spec(array, k):
-        column = half if half is not None and array.shape[-1] == width else 0
+    step = rows // 2
+
+    def spec(k):
         if k is None:
-            return pl.BlockSpec((step, wide), lambda i: (i, column))
-        return pl.BlockSpec((pl.Squeezed(), step, wide), lambda i: (k, i, column))
+            return pl.BlockSpec((step, width), lambda i: (i, 0))
+        return pl.BlockSpec((pl.Squeezed(), step, width), lambda i: (k, i, 0))
 
     def kernel(*refs):
         at = 0
@@ -805,9 +803,9 @@
     found = pl.pallas_call(
         kernel,
         grid=(rows // step,),
-        in_specs=[spec(*term) for term in terms],
-        out_specs=[pl.BlockSpec((step, wide), lambda i: (i, 0))] * len(outputs),
-        out_shape=[jax.ShapeDtypeStruct((rows, wide), BF16)] * len(outputs),
+        in_specs=[spec(k) for _, k in terms],
+        out_specs=[pl.BlockSpec((step, width), lambda i: (i, 0))] * len(outputs),
+        out_shape=[jax.ShapeDtypeStruct((rows, width), BF16)] * len(outputs),
         compiler_params=params(),
         cost_estimate=cost(0, 4),
         name="combine",
@@ -1037,11 +1035,15 @@
         feed_step(last, 0, chunks[2], True), moved_0, moved_1
     )
     other_2 = hop(sib_2, 1)
-    one, two = combine([(own_0, 1), (other_0, 1)], [(own_0, 2), (other_0, 2), moved_0])
+    one, two, three, four = combine(
+        [(own_0, 1), (other_0, 1)],
+        [(own_0, 2), (other_0, 2), moved_0],
+        [(own_1, 1), (other_1, 1), moved_1],
+        [(own_1, 2), (other_1, 2)],
+    )
+    back_2, one, two, three, four = tie(back_2, one, two, three, four)
     first_0, second_0 = hop(one, 2), hop(two, 4)
-    three, four = combine([(own_1, 1), (other_1, 1), moved_1], [(own_1, 2), (other_1, 2)])
-    back_2, one, two, three, four = tie(back_2, one, two, three, four)
-    first_1, second_1 = hop(after(three, one), 2), hop(after(four, two), 4)
+    first_1, second_1 = hop(three, 2), hop(four, 4)
     middles = middle(
         early, place, first_sum, back_out, attended, gains, [back_0, back_1, back_2]
     )
@@ -1050,21 +1052,25 @@
     back_attended, term = tie(back_attended, term)
     moved_2 = hop(term, 2)
     halves = attend_back(q_back_0, k_aug, v_aug, attended_0, back_attended, 0, 4)
-    (dq_0, dkv_0, back_attended), (first_0, second_0, first_1, second_1) = fence(
-        [*halves, back_attended], first_0, second_0, first_1, second_1
-    )
-    grads_0, grads_1 = combine(
-        [(own_0, 0), (other_0, 0), first_0, second_0], [(own_1, 0), (other_1, 0), first_1, second_1]
-    )
-    back_attended, grads_0, grads_1 = tie(back_attended, grads_0, grads_1)
+    (dq_0, dkv_0, back_attended), (first_0, second_0) = fence(
+        [*halves, back_attended], first_0, second_0
+    )
+    grads_0 = combine([(own_0, 0), (other_0, 0), first_0, second_0])
+    back_attended, grads_0 = tie(back_attended, grads_0)
     inward_0 = rep_hop(grads_0, INWARD)
+    halves = attend_back(q_back_1, k_aug, v_aug, attended_1, back_attended, 4, 4)
+    (dq_1, dkv_1), (moved_2, inward_0, first_1, second_1) = fence(
+        halves, moved_2, inward_0, first_1, second_1
+    )
+    one, two, grads_1, half_0 = combine(
+        [(own_2, 1), (other_2, 1)],
+        [(own_2, 2), (other_2, 2), moved_2],
+        [(own_1, 0), (other_1, 0), first_1, second_1],
+        [grads_0, inward_0],
+    )
+    dq_1, one, two, grads_1, half_0 = tie(dq_1, one, two, grads_1, half_0)
+    first_2, second_2 = hop(one, 2), hop(two, 4)
     inward_1 = rep_hop(grads_1, INWARD)
-    halves = attend_back(q_back_1, k_aug, v_aug, attended_1, back_attended, 4, 4)
-    (dq_1, dkv_1), (moved_2, inward_0) = fence(halves, moved_2, inward_0)
-    one, two = combine([(own_2, 1), (other_2, 1)], [(own_2, 2), (other_2, 2), moved_2])
-    half_0 = combine([grads_0, inward_0])
-    dq_1, one, two, half_0 = tie(dq_1, one, two, half_0)
-    first_2, second_2 = hop(one, 2), hop(two, 4)
     across_0 = rep_hop(half_0, ACROSS)
     result = raw_back(
         8, place, (dq_0, dq_1, dkv_0, dkv_1), units, normed_one, tables[0], tables[1], gains,
@@ -1074,60 +1080,45 @@
         result, first_2, second_2, inward_1, across_0
     )
     other = hop(sib, 1)
-    half_1, total_0 = combine([grads_1, inward_1], [half_0, across_0])
-    grads_2 = combine([(own_2, 0), (other_2, 0), first_2, second_2])
+    half_1, total_0, grads_2 = combine(
+        [grads_1, inward_1], [half_0, across_0], [(own_2, 0), (other_2, 0), first_2, second_2]
+    )
     back_raw, other, half_1, total_0, grads_2 = tie(back_raw, other, half_1, total_0, grads_2)
-    terms = [
-        combine(*[[(own, k), (other, k)] for k in (1, 2, 3)], half=side) for side in (0, 1)
-    ]
-    back_raw, *flat = tie(back_raw, *terms[0], *terms[1])
-    steps = [hop(term, 2 * k) for k, term in zip((1, 2, 3), flat[:3])]
+    term = combine([(own, 3), (other, 3)])
+    back_raw, term = tie(back_raw, term)
+    moved = hop(term, 4)
+    outward_0 = rep_hop(total_0, OUTWARD)
+    across_1 = rep_hop(half_1, ACROSS)
     inward_2 = rep_hop(grads_2, INWARD)
-    outward_0 = rep_hop(total_0, OUTWARD)
     input_grad = input_back(pairs, place, back_raw, x, back_first, gains)
-    (input_grad, half_1, *flat), (outward_0, *steps) = fence(
-        [input_grad, half_1, *flat[3:]], outward_0, *steps
-    )
-    across_1 = rep_hop(half_1, ACROSS)
-    more = [hop(term, 2 * k) for k, term in zip((1, 2, 3), flat)]
-    part_a = combine([(own, 0), (other, 0), *steps], half=0)
-    inward_a = rep_hop(part_a, INWARD)
-    first_sum, _ = tie(first_sum, part_a)
+    (input_grad,), (moved,) = fence([input_grad], moved)
+    one, two = combine([(own, 1), (other, 1), moved], [(own, 2), (other, 2)])
+    one, two, across_1, inward_2, first_sum = tie(one, two, across_1, inward_2, first_sum)
+    first, second = hop(one, 2), hop(two, 4)
+    total_1, half_2 = combine([half_1, across_1], [grads_2, inward_2])
+    first_sum, total_1, half_2, outward_0 = tie(first_sum, total_1, half_2, outward_0)
+    outward_1 = rep_hop(total_1, OUTWARD)
+    across_2 = rep_hop(half_2, ACROSS)
     outs = out_0.astype(F32) + out_1.astype(F32) + out_2.astype(F32)
     block_output = (first_sum + outs).astype(BF16)
-    (block_output,), (inward_2,) = fence([block_output], inward_2)
-    half_2 = combine([grads_2, inward_2])
-    across_2 = rep_hop(half_2, ACROSS)
-    *more, _ = tie(*more, half_2)
-    part_b = combine([(own, 0), (other, 0), *more], half=1)
-    inward_b = rep_hop(part_b, INWARD)
-    across_1, _ = tie(across_1, part_b)
-    total_1 = combine([half_1, across_1])
-    outward_1 = rep_hop(total_1, OUTWARD)
-    inward_a, _ = tie(inward_a, total_1)
-    half_a = combine([part_a, inward_a])
-    across_a = rep_hop(half_a, ACROSS)
-    inward_b, _ = tie(inward_b, half_a)
-    half_b = combine([part_b, inward_b])
-    across_b = rep_hop(half_b, ACROSS)
-    across_2, _ = tie(across_2, half_b)
+    (block_output,), (first, second) = fence([block_output], first, second)
+    grads = combine([(own, 0), (other, 0), first, second])
+    inward = rep_hop(grads, INWARD)
+    across_2, _ = tie(across_2, grads)
     total_2 = combine([half_2, across_2])
     outward_2 = rep_hop(total_2, OUTWARD)
-    across_a, outward_1, _ = tie(across_a, outward_1, total_2)
-    total_a = combine([half_a, across_a])
-    outward_a = rep_hop(total_a, OUTWARD)
-    across_b, _ = tie(across_b, total_a)
-    total_b = combine([half_b, across_b])
-    outward_b = rep_hop(total_b, OUTWARD)
+    inward, outward_1, _ = tie(inward, outward_1, total_2)
+    half = combine([grads, inward])
+    across = rep_hop(half, ACROSS)
+    outward_2, across, _ = tie(outward_2, across, half)
+    total = combine([half, across])
+    outward = rep_hop(total, OUTWARD)
+    total, outward_2 = tie(total, outward_2)
     spot = lax.axis_index("rep")
     flag = ((spot == 0) | (spot == 3)).astype(jnp.int32).reshape(1)
-    outward_2, _ = tie(outward_2, total_b)
     feed_grads = unpack_rows(flag, total_0, outward_0, total_1, outward_1, total_2, outward_2)
-    (*feed_grads,), (outward_a, outward_b) = fence(feed_grads, outward_a, outward_b)
-    attn_grad = jnp.concatenate(
-        [at_end(total_a.astype(F32), outward_a), at_end(total_b.astype(F32), outward_b)], axis=1
-    )
-    return block_output, input_grad, attn_grad, feed_grads
+    (*feed_grads,), (outward,) = fence(feed_grads, outward)
+    return block_output, input_grad, at_end(total.astype(F32), outward), feed_grads
 
 
 def solution(mesh):

time: 594 us -> 549 us (0.924)
  Pallas kernels: 380 us -> 345 us
    pallas_call x21 -> x14, Pallas kernels: 86.3 us -> 50 us  [combine(): pl.pallas_call(kernel, grid=(rows // step,), in_specs=[spec(k) for _, k i...]
    ppermute x51 -> x48, waiting for transfers between devices: 62.3 us -> 49.1 us  [hop(): return lax.ppermute(array, 'shard', [(i, i ^ bit) for i in range(8)])]
    ppermute x15 -> x12, waiting for transfers between devices: 33.5 us -> 43.1 us  [rep_hop(): return lax.ppermute(array.astype(BF16), 'rep', pairs)]
    ppermute x51 -> x48, starting transfers between devices: 39.4 us -> 34.9 us  [hop(): return lax.ppermute(array, 'shard', [(i, i ^ bit) for i in range(8)])]
    unnamed x126 -> x98, local copies, waits for them, and re-layouts: 14.1 us -> 15.3 us
    ppermute x15 -> x12, starting transfers between devices: 30.5 us -> 30.9 us  [rep_hop(): return lax.ppermute(array.astype(BF16), 'rep', pairs)]
  transfers between devices with their start and end apart: 66 -> 60, of which waited for: 23 -> 22; matrix products, arithmetic and copies ran while one was open for 3% -> 3% of each run, Pallas kernels for 64% -> 62%
where the time goes in v5:
time: 549 us; the launch traced here: 543 us
  Pallas kernels  345 us (63%)
  waiting for transfers between devices  92.2 us (17%)
  starting transfers between devices  65.7 us (12%)
  local copies, waits for them, and re-layouts  21.8 us (4%)
  other arithmetic  17.2 us (3%)
    pallas_call x3, Pallas kernels, feed(): pl.pallas_call(lambda *refs: feed_kernel(pieces.layout, paired, *refs), g...  127 us
    pallas_call x14, Pallas kernels, combine(): pl.pallas_call(kernel, grid=(rows // step,), in_specs=[spec(k) for _, k i...  50 us
    ppermute x48, waiting for transfers between devices, hop(): return lax.ppermute(array, 'shard', [(i, i ^ bit) for i in range(8)])  49.1 us
    pallas_call x2, Pallas kernels, attend_back(): pl.pallas_call(attend_back_kernel, grid=(groups,), in_specs=[pl.BlockSpec...  47.7 us
    ppermute x12, waiting for transfers between devices, rep_hop(): return lax.ppermute(array.astype(BF16), 'rep', pairs)  43.1 us
    pallas_call x2, Pallas kernels, attend(): pl.pallas_call(attend_kernel, grid=(groups,), in_specs=[pl.BlockSpec((2,...  37.6 us
    ppermute x48, starting transfers between devices, hop(): return lax.ppermute(array, 'shard', [(i, i ^ bit) for i in range(8)])  34.9 us
    ppermute x12, starting transfers between devices, rep_hop(): return lax.ppermute(array.astype(BF16), 'rep', pairs)  30.9 us
  transfers between devices with their start and end apart: 60, of which 22 were waited for; matrix products, arithmetic and copies ran while one was open for 3% of the time, Pallas kernels for 62%

profile of v5, /device:TPU:0, one launch (start us, length us, event | category | flops | bytes accessed | tf_op | source)
XLA Modules:
  0.0 542.9 jit_solution(13061302537040062239)
XLA Ops:
  5.7 3.0 collective-permute-start
  15.0 4.4 pack_rows.1
  25.1 6.0 %collective-permute-done.5.refs_18_.refs_17_ = bf16[128,1024]{1,0:T(8,128)(2,1)S(1)} collective-permute-done((bf16[128,1024]{1,0:T(8,128)(2,1)S(1)}, bf16[128,1024]{1,0:T(8,128)(2,1)S(1)}, u32[]{:S(2)}, u32[]{:S(2)}) %collective-permute-start.5) | collective-permute-done | bytes 262176 | tf_op jit(solution)/shard_map/ppermute | solution.py:766
  33.1 3.5 collective-permute-done.7.refs_20_.refs_19_
  39.8 15.9 %project.1 = (bf16[1024,1024]{1,0:T(8,128)(2,1)}, bf16[1024,1536]{1,0:T(8,128)(2,1)}, bf16[1024,1536]{1,0:T(8,128)(2,1)}, bf16[16,1024,128]{2,1,0:T(8,128)(2,1)}...) custom-call(s32[1]{0:T(128)} %bitcast.refs_0_, bf16[1024,1024]{1,0:T(8,128)(2,1)} %bitcast.33, ...), custom_call_target="tpu_custom_call" | custom-call | flops 8000000 | bytes 25000 | tf_op jit(solution)/shard_map/project/pallas_call | solution.py:203
  55.7 13.5 %attend.2 = (bf16[1024,512]{1,0:T(8,128)(2,1)}, bf16[8,1024,128]{2,1,0:T(8,128)(2,1)}) custom-call(bf16[16,1024,128]{2,1,0:T(8,128)(2,1)} %get-tuple-element.202.q_ref, bf16[8,1024,128]{2,1,0:T(8,128)(2,1)} %get-tuple-element.210.k_ref, bf16[8,1024,128]{2,1,0:T(8,128)(2,1)} %get-tuple-element.204.v_ref), custom_call_target="tpu_custom_call" | custom-call | flops 10000000 | bytes 8000 | tf_op jit(solution)/shard_map/attend/pallas_call | solution.py:264
  74.6 24.1 %attend.3 = (bf16[1024,512]{1,0:T(8,128)(2,1)}, bf16[8,1024,128]{2,1,0:T(8,128)(2,1)}) custom-call(bf16[16,1024,128]{2,1,0:T(8,128)(2,1)} %get-tuple-element.202.q_ref, bf16[8,1024,128]{2,1,0:T(8,128)(2,1)} %get-tuple-element.210.k_ref, bf16[8,1024,128]{2,1,0:T(8,128)(2,1)} %get-tuple-element.204.v_ref), custom_call_target="tpu_custom_call" | custom-call | flops 10000000 | bytes 8000 | tf_op jit(solution)/shard_map/attend/pallas_call | solution.py:264
  102.9 2.4 collective-permute-done.17.refs_14_.refs_13_.refs_18_
  106.1 8.3 %output_rows.1 = (f32[1024,1024]{1,0:T(8,128)}, bf16[1024,1024]{1,0:T(8,128)(2,1)}, bf16[1024,1024]{1,0:T(8,128)(2,1)}) custom-call(s32[1]{0:T(128)} %bitcast.refs_0_, bf16[1024,512]{1,0:T(8,128)(2,1)} %get-tuple-element.211.refs_1_.refs_3_.o_ref, bf16[1024,512]{1,0:T(8,128)(2,1)} %get-tuple-element.216.refs_2_.refs_4_.o_ref, bf16[1024,1024]{1,0:T(8,128)(2,1)} %bitcast.34, ...), custom_call_target="tpu_custom_call" | custom-call | flops 5000000 | bytes 15000 | tf_op jit(solution)/shard_map/output_rows/pallas_call | solution.py:381
  114.4 42.3 %feed.3 = (bf16[1024,1024]{1,0:T(8,128)(2,1)}, bf16[1024,1024]{1,0:T(8,128)(2,1)}, bf16[4,576,1024]{2,1,0:T(8,128)(2,1)}, bf16[4,576,1024]{2,1,0:T(8,128)(2,1)}) custom-call(s32[1]{0:T(128)} %bitcast.refs_0_, bf16[1024,1024]{1,0:T(8,128)(2,1)} %get-tuple-element.251.refs_1_, bf16[1024,1024]{1,0:T(8,128)(2,1)} %get-tuple-element.225.refs_2_, ...), custom_call_target="tpu_custom_call" | custom-call | flops 37500000 | bytes 38000 | tf_op jit(solution)/shard_map/feed/pallas_call | solution.py:466
  157.5 2.4 collective-permute-done.22.refs_7_
  165.3 2.1 collective-permute-start.29
  167.3 42.6 %feed.4 = (bf16[1024,1024]{1,0:T(8,128)(2,1)}, bf16[1024,1024]{1,0:T(8,128)(2,1)}, bf16[4,576,1024]{2,1,0:T(8,128)(2,1)}, bf16[4,576,1024]{2,1,0:T(8,128)(2,1)}) custom-call(s32[1]{0:T(128)} %bitcast.refs_0_, bf16[1024,1024]{1,0:T(8,128)(2,1)} %get-tuple-element.251.refs_1_, bf16[1024,1024]{1,0:T(8,128)(2,1)} %get-tuple-element.225.refs_2_, ...), custom_call_target="tpu_custom_call" | custom-call | flops 37500000 | bytes 38000 | tf_op jit(solution)/shard_map/feed/pallas_call | solution.py:466
  210.0 7.6 %collective-permute-done.29.refs_10_ = bf16[576,1024]{1,0:T(8,128)(2,1)} collective-permute-done((bf16[576,1024]{1,0:T(8,128)(2,1)S(1)}, bf16[576,1024]{1,0:T(8,128)(2,1)}, u32[]{:S(2)}, u32[]{:S(2)}) %collective-permute-start.29) | collective-permute-done | bytes 1179680 | tf_op jit(solution)/shard_map/ppermute | solution.py:766
  218.6 2.6 combine.15
  222.6 4.9 collective-permute-done.30.refs_1_.refs_6_.refs_9_
  227.5 2.5 combine.14
  232.2 42.4 %feed.5 = (bf16[1024,1024]{1,0:T(8,128)(2,1)}, bf16[1024,1024]{1,0:T(8,128)(2,1)}, bf16[4,576,1024]{2,1,0:T(8,128)(2,1)}, bf16[4,576,1024]{2,1,0:T(8,128)(2,1)}) custom-call(s32[1]{0:T(128)} %bitcast.refs_0_, bf16[1024,1024]{1,0:T(8,128)(2,1)} %get-tuple-element.251.refs_1_, bf16[1024,1024]{1,0:T(8,128)(2,1)} %get-tuple-element.225.refs_2_, ...), custom_call_target="tpu_custom_call" | custom-call | flops 37500000 | bytes 38000 | tf_op jit(solution)/shard_map/feed/pallas_call | solution.py:466
  276.1 6.8 %combine.16 = (bf16[576,1024]{1,0:T(8,128)(2,1)}, bf16[576,1024]{1,0:T(8,128)(2,1)}, bf16[576,1024]{1,0:T(8,128)(2,1)}, bf16[576,1024]{1,0:T(8,128)(2,1)}) custom-call(bf16[4,576,1024]{2,1,0:T(8,128)(2,1)} %get-tuple-element.260.refs_0_.refs_2_, bf16[4,576,1024]{2,1,0:T(8,128)(2,1)} %collective-permute-done.25.refs_1_.refs_3_, ...), custom_call_target="tpu_custom_call" | custom-call | bytes 4000 | tf_op jit(solution)/shard_map/combine/pallas_call | solution.py:803
  287.1 14.6 %middle.1 = (f32[1024,1024]{1,0:T(8,128)}, bf16[1024,1024]{1,0:T(8,128)(2,1)}, bf16[1024,1024]{1,0:T(8,128)(2,1)}) custom-call(s32[1]{0:T(128)} %bitcast.refs_0_, f32[1024,1024]{1,0:T(8,128)} %get-tuple-element.344.refs_1_, bf16[1024,1024]{1,0:T(8,128)(2,1)} %bitcast.32, bf16[1024,512]{1,0:T(8,128)(2,1)} %get-tuple-element.211.refs_1_.refs_3_.o_ref, ...), custom_call_target="tpu_custom_call" | custom-call | flops 9000000 | bytes 32000 | tf_op jit(solution)/shard_map/middle/pallas_call | solution.py:535
  301.7 2.6 combine.17
  304.3 23.7 %attend_back.2 = (f32[1024,512]{1,0:T(8,128)}, f32[1024,512]{1,0:T(8,128)}) custom-call(bf16[8,1024,128]{2,1,0:T(8,128)(2,1)} %get-tuple-element.209.q_ref, bf16[8,1024,128]{2,1,0:T(8,128)(2,1)} %get-tuple-element.210.k_ref, bf16[8,1024,128]{2,1,0:T(8,128)(2,1)} %get-tuple-element.204.v_ref, bf16[1024,512]{1,0:T(8,128)(2,1)} %get-tuple-element.211.refs_1_.refs_3_.o_ref, ...), custom_call_target="tpu_custom_call" | custom-call | flops 20000000 | bytes 12000 | tf_op jit(solution)/shard_map/attend_back/pallas_call | solution.py:336
  329.0 3.4 combine.18.refs_9_
  333.5 4.5 collective-permute-start.40
  338.0 24.0 %attend_back.3 = (f32[1024,512]{1,0:T(8,128)}, f32[1024,512]{1,0:T(8,128)}) custom-call(bf16[8,1024,128]{2,1,0:T(8,128)(2,1)} %get-tuple-element.284.q_ref, bf16[8,1024,128]{2,1,0:T(8,128)(2,1)} %get-tuple-element.210.k_ref, bf16[8,1024,128]{2,1,0:T(8,128)(2,1)} %get-tuple-element.204.v_ref, bf16[1024,512]{1,0:T(8,128)(2,1)} %get-tuple-element.216.refs_2_.refs_4_.o_ref, ...), custom_call_target="tpu_custom_call" | custom-call | flops 20000000 | bytes 12000 | tf_op jit(solution)/shard_map/attend_back/pallas_call | solution.py:336
  363.8 7.5 %combine.19 = (bf16[576,1024]{1,0:T(8,128)(2,1)}, bf16[576,1024]{1,0:T(8,128)(2,1)}, bf16[576,1024]{1,0:T(8,128)(2,1)}, bf16[576,1024]{1,0:T(8,128)(2,1)}) custom-call(bf16[4,576,1024]{2,1,0:T(8,128)(2,1)} %get-tuple-element.276.refs_0_.refs_2_.refs_4_, bf16[4,576,1024]{2,1,0:T(8,128)(2,1)} %collective-permute-done.36.refs_1_.refs_3_.refs_5_, ...), custom_call_target="tpu_custom_call" | custom-call | bytes 4000 | tf_op jit(solution)/shard_map/combine/pallas_call | solution.py:803
  373.2 2.8 collective-permute-start.45
  377.7 19.9 %raw_back.1 = (bf16[1024,2048]{1,0:T(8,128)(2,1)}, bf16[4,416,1024]{2,1,0:T(8,128)(2,1)}, bf16[4,416,1024]{2,1,0:T(8,128)(2,1)}) custom-call(s32[1]{0:T(128)} %bitcast.refs_0_, f32[1024,512]{1,0:T(8,128)} %get-tuple-element.283.refs_1_, f32[1024,512]{1,0:T(8,128)} %get-tuple-element.304.refs_2_, f32[1024,512]{1,0:T(8,128)} %get-tuple-element.305.refs_3_, ...), custom_call_target="tpu_custom_call" | custom-call | flops 10000000 | bytes 30000 | tf_op jit(solution)/shard_map/raw_back/pallas_call | solution.py:621
  401.1 5.4 combine.20
  407.4 2.1 collective-permute-start.49
  409.5 7.2 %collective-permute-start.50 = (bf16[576,1024]{1,0:T(8,128)(2,1)}, bf16[576,1024]{1,0:T(8,128)(2,1)}, u32[]{:S(2)}, u32[]{:S(2)}) collective-permute-start(bf16[576,1024]{1,0:T(8,128)(2,1)} %get-tuple-element.337.refs_2_), channel_id=1, source_target_pairs={{0,8},{24,16},{1,9},{25,17},{2,10},{26,18},{3,11},{27,19},{4,12},{... | collective-permute-start | bytes 3538952 | tf_op jit(solution)/shard_map/ppermute | solution.py:817
  417.9 2.4 combine.21
  421.2 11.2 %input_back.1 = f32[1024,1024]{1,0:T(8,128)} custom-call(s32[1]{0:T(128)} %bitcast.refs_0_, bf16[1024,2048]{1,0:T(8,128)(2,1)} %get-tuple-element.330.refs_1_, bf16[1024,1024]{1,0:T(8,128)(2,1)} %bitcast.35, f32[1024,1024]{1,0:T(8,128)} %get-tuple-element.331.refs_3_, f32[16,1024]{1,0:T(8,128)} %get-tuple-element.217.refs_4_.refs_5_.refs_10_, ...), custom_call_target="tpu_custom_call" | custom-call | flops 6000000 | bytes 18000 | tf_op jit(solution)/shard_map/input_back/pallas_call | solution.py:651
  432.4 8.7 %collective-permute-done.48.refs_2_ = bf16[416,1024]{1,0:T(8,128)(2,1)S(1)} collective-permute-done((bf16[416,1024]{1,0:T(8,128)(2,1)}, bf16[416,1024]{1,0:T(8,128)(2,1)S(1)}, u32[]{:S(2)}, u32[]{:S(2)}) %collective-permute-start.48) | collective-permute-done | bytes 852000 | tf_op jit(solution)/shard_map/ppermute | solution.py:766
  441.9 3.2 combine.22
  447.0 3.5 combine.23
  453.5 6.4 %add_convert_fusion = bf16[1024,1024]{1,0:T(8,128)(2,1)} fusion(f32[1024,1024]{1,0:T(8,128)} %get-tuple-element.344.refs_1_, bf16[1024,1024]{1,0:T(8,128)(2,1)} %get-tuple-element.347, bf16[1024,1024]{1,0:T(8,128)(2,1)} %get-tuple-element.346, bf16[1024,1024]{1,0:T(8,128)(2,1)S(1)} %copy-done.18), kind=kLoop, calls=%fused_computation | loop fusion | flops 7340032 | bytes 12582912 | tf_op jit(solution)/shard_map/convert_element_type | solution.py:1103
  459.9 5.2 collective-permute-done.52.refs_2_
  466.0 2.9 combine.24.refs_0_
  468.8 5.0 collective-permute-start.54
  473.9 2.6 combine.25.refs_4_
  477.8 3.7 collective-permute-done.55.refs_3_
  481.5 8.7 %collective-permute-done.54.refs_1_ = bf16[416,1024]{1,0:T(8,128)(2,1)S(1)} collective-permute-done((bf16[416,1024]{1,0:T(8,128)(2,1)}, bf16[416,1024]{1,0:T(8,128)(2,1)S(1)}, u32[]{:S(2)}, u32[]{:S(2)}) %collective-permute-start.54) | collective-permute-done | bytes 852000 | tf_op jit(solution)/shard_map/ppermute | solution.py:817
  491.1 2.2 combine.26.refs_0_
  494.0 15.0 %collective-permute-done.57.refs_5_ = bf16[576,1024]{1,0:T(8,128)(2,1)S(1)} collective-permute-done((bf16[576,1024]{1,0:T(8,128)(2,1)}, bf16[576,1024]{1,0:T(8,128)(2,1)S(1)}, u32[]{:S(2)}, u32[]{:S(2)}) %collective-permute-start.57) | collective-permute-done | bytes 1179680 | tf_op jit(solution)/shard_map/ppermute | solution.py:817
  510.0 2.3 combine.27
  513.6 7.5 %unpack_rows.1 = (f32[128,4608]{1,0:T(8,128)}, f32[128,4608]{1,0:T(8,128)}, f32[576,1024]{1,0:T(8,128)}) custom-call(s32[1]{0:T(128)} %bitcast.8.flag_ref, bf16[576,1024]{1,0:T(8,128)(2,1)} %get-tuple-element.343.refs_0_, bf16[576,1024]{1,0:T(8,128)(2,1)} %collective-permute-done.51.refs_1_, bf16[576,1024]{1,0:T(8,128)(2,1)} %get-tuple-element.353.refs_2_, ...), custom_call_target="tpu_custom_call" | custom-call | bytes 14000 | tf_op jit(solution)/shard_map/unpack_rows/pallas_call | solution.py:743
  521.1 13.9 %collective-permute-done.59 = bf16[416,1024]{1,0:T(8,128)(2,1)S(1)} collective-permute-done((bf16[416,1024]{1,0:T(8,128)(2,1)}, bf16[416,1024]{1,0:T(8,128)(2,1)S(1)}, u32[]{:S(2)}, u32[]{:S(2)}) %collective-permute-start.59) | collective-permute-done | bytes 852000 | tf_op jit(solution)/shard_map/ppermute | solution.py:817
  (243 shorter events, 81.9 us)
Async XLA Ops:
  5.7 15.6 %collective-permute-start = (bf16[272,1024]{1,0:T(8,128)(2,1)S(1)}, bf16[272,1024]{1,0:T(8,128)(2,1)S(1)}, u32[]{:S(2)}, u32[]{:S(2)}) collective-permute-start(bf16[272,1024]{1,0:T(8,128)(2,1)S(1)} %concatenate.38.refs_6_.refs_7_.refs_22_.refs_5_), channel_id=1, source_target_pairs={{0,2},{1,3},{2,0},{3,1},{4,6},{5,7},{6,4},{7,5},{8,10},{9,11},{10,... | collective-permute-start | bytes 1671176 | tf_op jit(solution)/shard_map/ppermute | solution.py:766
  8.7 14.1 %collective-permute-start.1 = (bf16[272,1024]{1,0:T(8,128)(2,1)S(1)}, bf16[272,1024]{1,0:T(8,128)(2,1)S(1)}, u32[]{:S(2)}, u32[]{:S(2)}) collective-permute-start(bf16[272,1024]{1,0:T(8,128)(2,1)S(1)} %concatenate.38.refs_6_.refs_7_.refs_22_.refs_5_), channel_id=1, source_target_pairs={{0,4},{1,5},{2,6},{3,7},{4,0},{5,1},{6,2},{7,3},{8,12},{9,13},{10,... | collective-permute-start | bytes 1671176 | tf_op jit(solution)/shard_map/ppermute | solution.py:766
  10.2 12.6 %collective-permute-start.2 = (bf16[272,1024]{1,0:T(8,128)(2,1)S(1)}, bf16[272,1024]{1,0:T(8,128)(2,1)S(1)}, u32[]{:S(2)}, u32[]{:S(2)}) collective-permute-start(bf16[272,1024]{1,0:T(8,128)(2,1)S(1)} %concatenate.38.refs_6_.refs_7_.refs_22_.refs_5_), channel_id=1, source_target_pairs={{0,1},{1,0},{2,3},{3,2},{4,5},{5,4},{6,7},{7,6},{8,9},{9,8},{10,11... | collective-permute-start | bytes 1671176 | tf_op jit(solution)/shard_map/ppermute | solution.py:766
  31.1 38.1 %collective-permute-start.9 = (bf16[704,1024]{1,0:T(8,128)(2,1)}, bf16[704,1024]{1,0:T(8,128)(2,1)S(1)}, u32[]{:S(2)}, u32[]{:S(2)}) collective-permute-start(bf16[704,1024]{1,0:T(8,128)(2,1)} %get-tuple-element.208.refs_5_.refs_4_.refs_9_), channel_id=1, source_target_pairs={{0,2},{1,3},{2,0},{3,1},{4,6},{5,7},{6,4},{7,5},{8,10},{9,11},{10,... | collective-permute-start | bytes 4325384 | tf_op jit(solution)/shard_map/ppermute | solution.py:766
  31.8 37.4 %collective-permute-start.10 = (bf16[704,1024]{1,0:T(8,128)(2,1)}, bf16[704,1024]{1,0:T(8,128)(2,1)S(1)}, u32[]{:S(2)}, u32[]{:S(2)}) collective-permute-start(bf16[704,1024]{1,0:T(8,128)(2,1)} %get-tuple-element.208.refs_5_.refs_4_.refs_9_), channel_id=1, source_target_pairs={{0,4},{1,5},{2,6},{3,7},{4,0},{5,1},{6,2},{7,3},{8,12},{9,13},{10,... | collective-permute-start | bytes 4325384 | tf_op jit(solution)/shard_map/ppermute | solution.py:766
  32.6 36.6 %collective-permute-start.11 = (bf16[704,1024]{1,0:T(8,128)(2,1)}, bf16[704,1024]{1,0:T(8,128)(2,1)}, u32[]{:S(2)}, u32[]{:S(2)}) collective-permute-start(bf16[704,1024]{1,0:T(8,128)(2,1)} %get-tuple-element.208.refs_5_.refs_4_.refs_9_), channel_id=1, source_target_pairs={{0,1},{1,0},{2,3},{3,2},{4,5},{5,4},{6,7},{7,6},{8,9},{9,8},{10,11... | collective-permute-start | bytes 4325384 | tf_op jit(solution)/shard_map/ppermute | solution.py:766
  69.2 29.6 %collective-permute-start.14 = (bf16[704,1024]{1,0:T(8,128)(2,1)S(1)}, bf16[704,1024]{1,0:T(8,128)(2,1)}, u32[]{:S(2)}, u32[]{:S(2)}) collective-permute-start(bf16[704,1024]{1,0:T(8,128)(2,1)S(1)} %collective-permute-done.9.refs_7_.refs_6_.refs_11_), channel_id=1, source_target_pairs={{0,1},{1,0},{2,3},{3,2},{4,5},{5,4},{6,7},{7,6},{8,9},{9,8},{10,11... | collective-permute-start | bytes 4325384 | tf_op jit(solution)/shard_map/ppermute | solution.py:766
  69.7 29.1 %collective-permute-start.15 = (bf16[704,1024]{1,0:T(8,128)(2,1)S(1)}, bf16[704,1024]{1,0:T(8,128)(2,1)}, u32[]{:S(2)}, u32[]{:S(2)}) collective-permute-start(bf16[704,1024]{1,0:T(8,128)(2,1)S(1)} %collective-permute-done.10.refs_9_.refs_8_.refs_13_), channel_id=1, source_target_pairs={{0,1},{1,0},{2,3},{3,2},{4,5},{5,4},{6,7},{7,6},{8,9},{9,8},{10,11... | collective-permute-start | bytes 4325384 | tf_op jit(solution)/shard_map/ppermute | solution.py:766
  72.0 26.8 %collective-permute-start.12 = (bf16[704,512]{1,0:T(8,128)(2,1)}, bf16[704,512]{1,0:T(8,128)(2,1)S(1)}, u32[]{:S(2)}, u32[]{:S(2)}) collective-permute-start(bf16[704,512]{1,0:T(8,128)(2,1)} %slice.65), channel_id=1, source_target_pairs={{0,2},{1,3},{2,0},{3,1},{4,6},{5,7},{6,4},{7,5},{8,10},{9,11},{10,... | collective-permute-start | bytes 2162696 | tf_op jit(solution)/shard_map/ppermute | solution.py:766
  73.4 25.4 %collective-permute-start.13 = (bf16[704,512]{1,0:T(8,128)(2,1)}, bf16[704,512]{1,0:T(8,128)(2,1)}, u32[]{:S(2)}, u32[]{:S(2)}) collective-permute-start(bf16[704,512]{1,0:T(8,128)(2,1)} %slice.66), channel_id=1, source_target_pairs={{0,4},{1,5},{2,6},{3,7},{4,0},{5,1},{6,2},{7,3},{8,12},{9,13},{10,... | collective-permute-start | bytes 2162696 | tf_op jit(solution)/shard_map/ppermute | solution.py:766
  98.9 57.9 %collective-permute-start.18 = (bf16[576,1024]{1,0:T(8,128)(2,1)}, bf16[576,1024]{1,0:T(8,128)(2,1)S(1)}, u32[]{:S(2)}, u32[]{:S(2)}) collective-permute-start(bf16[576,1024]{1,0:T(8,128)(2,1)} %get-tuple-element.231.refs_4_), channel_id=1, source_target_pairs={{0,1},{1,0},{2,3},{3,2},{4,5},{5,4},{6,7},{7,6},{8,9},{9,8},{10,11... | collective-permute-start | bytes 3538952 | tf_op jit(solution)/shard_map/ppermute | solution.py:766
  99.4 57.4 %collective-permute-start.19 = (bf16[576,1024]{1,0:T(8,128)(2,1)}, bf16[576,1024]{1,0:T(8,128)(2,1)}, u32[]{:S(2)}, u32[]{:S(2)}) collective-permute-start(bf16[576,1024]{1,0:T(8,128)(2,1)} %get-tuple-element.231.refs_4_), channel_id=1, source_target_pairs={{0,2},{1,3},{2,0},{3,1},{4,6},{5,7},{6,4},{7,5},{8,10},{9,11},{10,... | collective-permute-start | bytes 3538952 | tf_op jit(solution)/shard_map/ppermute | solution.py:766
  100.0 56.8 %collective-permute-start.20 = (bf16[576,1024]{1,0:T(8,128)(2,1)}, bf16[576,1024]{1,0:T(8,128)(2,1)}, u32[]{:S(2)}, u32[]{:S(2)}) collective-permute-start(bf16[576,1024]{1,0:T(8,128)(2,1)} %get-tuple-element.231.refs_4_), channel_id=1, source_target_pairs={{0,4},{1,5},{2,6},{3,7},{4,0},{5,1},{6,2},{7,3},{8,12},{9,13},{10,... | collective-permute-start | bytes 3538952 | tf_op jit(solution)/shard_map/ppermute | solution.py:766
  100.8 56.0 %collective-permute-start.21 = (bf16[576,1024]{1,0:T(8,128)(2,1)}, bf16[576,1024]{1,0:T(8,128)(2,1)}, u32[]{:S(2)}, u32[]{:S(2)}) collective-permute-start(bf16[576,1024]{1,0:T(8,128)(2,1)} %get-tuple-element.231.refs_4_), channel_id=1, source_target_pairs={{0,6},{1,7},{2,4},{3,5},{4,2},{5,3},{6,0},{7,1},{8,14},{9,15},{10,... | collective-permute-start | bytes 3538952 | tf_op jit(solution)/shard_map/ppermute | solution.py:766
  163.3 54.3 %collective-permute-start.25 = (bf16[4,576,1024]{2,1,0:T(8,128)(2,1)}, bf16[4,576,1024]{2,1,0:T(8,128)(2,1)}, u32[]{:S(2)}, u32[]{:S(2)}) collective-permute-start(bf16[4,576,1024]{2,1,0:T(8,128)(2,1)} %get-tuple-element.243), channel_id=1, source_target_pairs={{0,1},{1,0},{2,3},{3,2},{4,5},{5,4},{6,7},{7,6},{8,9},{9,8},{10,11... | collective-permute-start | bytes 14155784 | tf_op jit(solution)/shard_map/ppermute | solution.py:766
  163.5 46.5 %collective-permute-start.26 = (bf16[576,1024]{1,0:T(8,128)(2,1)S(1)}, bf16[576,1024]{1,0:T(8,128)(2,1)}, u32[]{:S(2)}, u32[]{:S(2)}) collective-permute-start(bf16[576,1024]{1,0:T(8,128)(2,1)S(1)} %copy-done.19), channel_id=1, source_target_pairs={{0,1},{1,0},{2,3},{3,2},{4,5},{5,4},{6,7},{7,6},{8,9},{9,8},{10,11... | collective-permute-start | bytes 3538952 | tf_op jit(solution)/shard_map/ppermute | solution.py:766
  163.8 46.2 %collective-permute-start.27 = (bf16[576,1024]{1,0:T(8,128)(2,1)S(1)}, bf16[576,1024]{1,0:T(8,128)(2,1)}, u32[]{:S(2)}, u32[]{:S(2)}) collective-permute-start(bf16[576,1024]{1,0:T(8,128)(2,1)S(1)} %copy-done.19), channel_id=1, source_target_pairs={{0,2},{1,3},{2,0},{3,1},{4,6},{5,7},{6,4},{7,5},{8,10},{9,11},{10,... | collective-permute-start | bytes 3538952 | tf_op jit(solution)/shard_map/ppermute | solution.py:766
  164.5 45.6 %collective-permute-start.28 = (bf16[576,1024]{1,0:T(8,128)(2,1)S(1)}, bf16[576,1024]{1,0:T(8,128)(2,1)}, u32[]{:S(2)}, u32[]{:S(2)}) collective-permute-start(bf16[576,1024]{1,0:T(8,128)(2,1)S(1)} %copy-done.19), channel_id=1, source_target_pairs={{0,4},{1,5},{2,6},{3,7},{4,0},{5,1},{6,2},{7,3},{8,12},{9,13},{10,... | collective-permute-start | bytes 3538952 | tf_op jit(solution)/shard_map/ppermute | solution.py:766
  165.3 52.3 %collective-permute-start.29 = (bf16[576,1024]{1,0:T(8,128)(2,1)S(1)}, bf16[576,1024]{1,0:T(8,128)(2,1)}, u32[]{:S(2)}, u32[]{:S(2)}) collective-permute-start(bf16[576,1024]{1,0:T(8,128)(2,1)S(1)} %copy-done.19), channel_id=1, source_target_pairs={{0,6},{1,7},{2,4},{3,5},{4,2},{5,3},{6,0},{7,1},{8,14},{9,15},{10,... | collective-permute-start | bytes 3538952 | tf_op jit(solution)/shard_map/ppermute | solution.py:766
  217.6 9.9 %collective-permute-start.30 = (bf16[4,576,1024]{2,1,0:T(8,128)(2,1)}, bf16[4,576,1024]{2,1,0:T(8,128)(2,1)}, u32[]{:S(2)}, u32[]{:S(2)}) collective-permute-start(bf16[4,576,1024]{2,1,0:T(8,128)(2,1)} %get-tuple-element.247), channel_id=1, source_target_pairs={{0,1},{1,0},{2,3},{3,2},{4,5},{5,4},{6,7},{7,6},{8,9},{9,8},{10,11... | collective-permute-start | bytes 14155784 | tf_op jit(solution)/shard_map/ppermute | solution.py:766
  217.6 13.6 %collective-permute-start.31 = (bf16[576,1024]{1,0:T(8,128)(2,1)}, bf16[576,1024]{1,0:T(8,128)(2,1)S(1)}, u32[]{:S(2)}, u32[]{:S(2)}) collective-permute-start(bf16[576,1024]{1,0:T(8,128)(2,1)} %collective-permute-done.27.refs_6_), channel_id=1, source_target_pairs={{0,1},{1,0},{2,3},{3,2},{4,5},{5,4},{6,7},{7,6},{8,9},{9,8},{10,11... | collective-permute-start | bytes 3538952 | tf_op jit(solution)/shard_map/ppermute | solution.py:766
  218.1 13.1 %collective-permute-start.32 = (bf16[576,1024]{1,0:T(8,128)(2,1)}, bf16[576,1024]{1,0:T(8,128)(2,1)}, u32[]{:S(2)}, u32[]{:S(2)}) collective-permute-start(bf16[576,1024]{1,0:T(8,128)(2,1)} %collective-permute-done.28.refs_8_), channel_id=1, source_target_pairs={{0,1},{1,0},{2,3},{3,2},{4,5},{5,4},{6,7},{7,6},{8,9},{9,8},{10,11... | collective-permute-start | bytes 3538952 | tf_op jit(solution)/shard_map/ppermute | solution.py:766
  218.1 13.1 %collective-permute-start.33 = (bf16[576,1024]{1,0:T(8,128)(2,1)}, bf16[576,1024]{1,0:T(8,128)(2,1)}, u32[]{:S(2)}, u32[]{:S(2)}) collective-permute-start(bf16[576,1024]{1,0:T(8,128)(2,1)} %collective-permute-done.29.refs_10_), channel_id=1, source_target_pairs={{0,1},{1,0},{2,3},{3,2},{4,5},{5,4},{6,7},{7,6},{8,9},{9,8},{10,11... | collective-permute-start | bytes 3538952 | tf_op jit(solution)/shard_map/ppermute | solution.py:766
  221.2 53.5 %collective-permute-start.34 = (bf16[576,1024]{1,0:T(8,128)(2,1)}, bf16[576,1024]{1,0:T(8,128)(2,1)S(1)}, u32[]{:S(2)}, u32[]{:S(2)}) collective-permute-start(bf16[576,1024]{1,0:T(8,128)(2,1)} %combine.15), channel_id=1, source_target_pairs={{0,2},{1,3},{2,0},{3,1},{4,6},{5,7},{6,4},{7,5},{8,10},{9,11},{10,... | collective-permute-start | bytes 3538952 | tf_op jit(solution)/shard_map/ppermute | solution.py:766
  230.1 44.6 %collective-permute-start.35 = (bf16[576,1024]{1,0:T(8,128)(2,1)}, bf16[576,1024]{1,0:T(8,128)(2,1)S(1)}, u32[]{:S(2)}, u32[]{:S(2)}) collective-permute-start(bf16[576,1024]{1,0:T(8,128)(2,1)} %combine.14), channel_id=1, source_target_pairs={{0,4},{1,5},{2,6},{3,7},{4,0},{5,1},{6,2},{7,3},{8,12},{9,13},{10,... | collective-permute-start | bytes 3538952 | tf_op jit(solution)/shard_map/ppermute | solution.py:766
  274.7 27.0 %collective-permute-start.36 = (bf16[4,576,1024]{2,1,0:T(8,128)(2,1)}, bf16[4,576,1024]{2,1,0:T(8,128)(2,1)}, u32[]{:S(2)}, u32[]{:S(2)}) collective-permute-start(bf16[4,576,1024]{2,1,0:T(8,128)(2,1)} %get-tuple-element.274), channel_id=1, source_target_pairs={{0,1},{1,0},{2,3},{3,2},{4,5},{5,4},{6,7},{7,6},{8,9},{9,8},{10,11... | collective-permute-start | bytes 14155784 | tf_op jit(solution)/shard_map/ppermute | solution.py:766
  283.0 45.0 %collective-permute-start.37 = (bf16[576,1024]{1,0:T(8,128)(2,1)}, bf16[576,1024]{1,0:T(8,128)(2,1)S(1)}, u32[]{:S(2)}, u32[]{:S(2)}) collective-permute-start(bf16[576,1024]{1,0:T(8,128)(2,1)} %get-tuple-element.281), channel_id=1, source_target_pairs={{0,2},{1,3},{2,0},{3,1},{4,6},{5,7},{6,4},{7,5},{8,10},{9,11},{10,... | collective-permute-start | bytes 3538952 | tf_op jit(solution)/shard_map/ppermute | solution.py:766
  284.1 43.8 %collective-permute-start.38 = (bf16[576,1024]{1,0:T(8,128)(2,1)}, bf16[576,1024]{1,0:T(8,128)(2,1)}, u32[]{:S(2)}, u32[]{:S(2)}) collective-permute-start(bf16[576,1024]{1,0:T(8,128)(2,1)} %get-tuple-element.282), channel_id=1, source_target_pairs={{0,4},{1,5},{2,6},{3,7},{4,0},{5,1},{6,2},{7,3},{8,12},{9,13},{10,... | collective-permute-start | bytes 3538952 | tf_op jit(solution)/shard_map/ppermute | solution.py:766
  285.3 76.6 %collective-permute-start.41 = (bf16[576,1024]{1,0:T(8,128)(2,1)}, bf16[576,1024]{1,0:T(8,128)(2,1)S(1)}, u32[]{:S(2)}, u32[]{:S(2)}) collective-permute-start(bf16[576,1024]{1,0:T(8,128)(2,1)} %get-tuple-element.293), channel_id=1, source_target_pairs={{0,2},{1,3},{2,0},{3,1},{4,6},{5,7},{6,4},{7,5},{8,10},{9,11},{10,... | collective-permute-start | bytes 3538952 | tf_op jit(solution)/shard_map/ppermute | solution.py:766
  285.9 76.1 %collective-permute-start.42 = (bf16[576,1024]{1,0:T(8,128)(2,1)}, bf16[576,1024]{1,0:T(8,128)(2,1)S(1)}, u32[]{:S(2)}, u32[]{:S(2)}) collective-permute-start(bf16[576,1024]{1,0:T(8,128)(2,1)} %get-tuple-element.294), channel_id=1, source_target_pairs={{0,4},{1,5},{2,6},{3,7},{4,0},{5,1},{6,2},{7,3},{8,12},{9,13},{10,... | collective-permute-start | bytes 3538952 | tf_op jit(solution)/shard_map/ppermute | solution.py:766
  332.4 29.6 %collective-permute-start.39 = (bf16[576,1024]{1,0:T(8,128)(2,1)}, bf16[576,1024]{1,0:T(8,128)(2,1)S(1)}, u32[]{:S(2)}, u32[]{:S(2)}) collective-permute-start(bf16[576,1024]{1,0:T(8,128)(2,1)} %combine.17), channel_id=1, source_target_pairs={{0,2},{1,3},{2,0},{3,1},{4,6},{5,7},{6,4},{7,5},{8,10},{9,11},{10,... | collective-permute-start | bytes 3538952 | tf_op jit(solution)/shard_map/ppermute | solution.py:766
  333.5 28.5 %collective-permute-start.40 = (bf16[576,1024]{1,0:T(8,128)(2,1)}, bf16[576,1024]{1,0:T(8,128)(2,1)}, u32[]{:S(2)}, u32[]{:S(2)}) collective-permute-start(bf16[576,1024]{1,0:T(8,128)(2,1)} %combine.18.refs_9_), channel_id=1, source_target_pairs={{0,8},{24,16},{1,9},{25,17},{2,10},{26,18},{3,11},{27,19},{4,12},{... | collective-permute-start | bytes 3538952 | tf_op jit(solution)/shard_map/ppermute | solution.py:817
  371.3 26.3 %collective-permute-start.43 = (bf16[576,1024]{1,0:T(8,128)(2,1)}, bf16[576,1024]{1,0:T(8,128)(2,1)S(1)}, u32[]{:S(2)}, u32[]{:S(2)}) collective-permute-start(bf16[576,1024]{1,0:T(8,128)(2,1)} %get-tuple-element.314), channel_id=1, source_target_pairs={{0,2},{1,3},{2,0},{3,1},{4,6},{5,7},{6,4},{7,5},{8,10},{9,11},{10,... | collective-permute-start | bytes 3538952 | tf_op jit(solution)/shard_map/ppermute | solution.py:766
  372.3 26.0 %collective-permute-start.44 = (bf16[576,1024]{1,0:T(8,128)(2,1)}, bf16[576,1024]{1,0:T(8,128)(2,1)S(1)}, u32[]{:S(2)}, u32[]{:S(2)}) collective-permute-start(bf16[576,1024]{1,0:T(8,128)(2,1)} %get-tuple-element.315), channel_id=1, source_target_pairs={{0,4},{1,5},{2,6},{3,7},{4,0},{5,1},{6,2},{7,3},{8,12},{9,13},{10,... | collective-permute-start | bytes 3538952 | tf_op jit(solution)/shard_map/ppermute | solution.py:766
  373.2 26.9 %collective-permute-start.45 = (bf16[576,1024]{1,0:T(8,128)(2,1)}, bf16[576,1024]{1,0:T(8,128)(2,1)S(1)}, u32[]{:S(2)}, u32[]{:S(2)}) collective-permute-start(bf16[576,1024]{1,0:T(8,128)(2,1)} %get-tuple-element.316.refs_0_), channel_id=1, source_target_pairs={{0,8},{24,16},{1,9},{25,17},{2,10},{26,18},{3,11},{27,19},{4,12},{... | collective-permute-start | bytes 3538952 | tf_op jit(solution)/shard_map/ppermute | solution.py:817
  376.0 24.1 %collective-permute-start.46 = (bf16[576,1024]{1,0:T(8,128)(2,1)}, bf16[576,1024]{1,0:T(8,128)(2,1)}, u32[]{:S(2)}, u32[]{:S(2)}) collective-permute-start(bf16[576,1024]{1,0:T(8,128)(2,1)} %get-tuple-element.317.refs_2_), channel_id=1, source_target_pairs={{8,16},{16,8},{9,17},{17,9},{10,18},{18,10},{11,19},{19,11},{12,20... | collective-permute-start | bytes 3538952 | tf_op jit(solution)/shard_map/ppermute | solution.py:817
  407.4 37.8 %collective-permute-start.49 = (bf16[576,1024]{1,0:T(8,128)(2,1)}, bf16[576,1024]{1,0:T(8,128)(2,1)}, u32[]{:S(2)}, u32[]{:S(2)}) collective-permute-start(bf16[576,1024]{1,0:T(8,128)(2,1)} %get-tuple-element.336.refs_0_), channel_id=1, source_target_pairs={{8,16},{16,8},{9,17},{17,9},{10,18},{18,10},{11,19},{19,11},{12,20... | collective-permute-start | bytes 3538952 | tf_op jit(solution)/shard_map/ppermute | solution.py:817
  409.5 35.7 %collective-permute-start.50 = (bf16[576,1024]{1,0:T(8,128)(2,1)}, bf16[576,1024]{1,0:T(8,128)(2,1)}, u32[]{:S(2)}, u32[]{:S(2)}) collective-permute-start(bf16[576,1024]{1,0:T(8,128)(2,1)} %get-tuple-element.337.refs_2_), channel_id=1, source_target_pairs={{0,8},{24,16},{1,9},{25,17},{2,10},{26,18},{3,11},{27,19},{4,12},{... | collective-permute-start | bytes 3538952 | tf_op jit(solution)/shard_map/ppermute | solution.py:817
  416.6 33.8 %collective-permute-start.51 = (bf16[576,1024]{1,0:T(8,128)(2,1)}, bf16[576,1024]{1,0:T(8,128)(2,1)}, u32[]{:S(2)}, u32[]{:S(2)}) collective-permute-start(bf16[576,1024]{1,0:T(8,128)(2,1)} %get-tuple-element.343.refs_0_), channel_id=1, source_target_pairs={{8,0},{16,24},{9,1},{17,25},{10,2},{18,26},{11,3},{19,27},{12,4},{... | collective-permute-start | bytes 3538952 | tf_op jit(solution)/shard_map/ppermute | solution.py:817
  420.4 20.6 %collective-permute-start.48 = (bf16[416,1024]{1,0:T(8,128)(2,1)}, bf16[416,1024]{1,0:T(8,128)(2,1)S(1)}, u32[]{:S(2)}, u32[]{:S(2)}) collective-permute-start(bf16[416,1024]{1,0:T(8,128)(2,1)} %combine.21), channel_id=1, source_target_pairs={{0,4},{1,5},{2,6},{3,7},{4,0},{5,1},{6,2},{7,3},{8,12},{9,13},{10,... | collective-permute-start | bytes 2555912 | tf_op jit(solution)/shard_map/ppermute | solution.py:766
  445.2 19.9 %collective-permute-start.52 = (bf16[416,1024]{1,0:T(8,128)(2,1)}, bf16[416,1024]{1,0:T(8,128)(2,1)S(1)}, u32[]{:S(2)}, u32[]{:S(2)}) collective-permute-start(bf16[416,1024]{1,0:T(8,128)(2,1)} %get-tuple-element.348), channel_id=1, source_target_pairs={{0,2},{1,3},{2,0},{3,1},{4,6},{5,7},{6,4},{7,5},{8,10},{9,11},{10,... | collective-permute-start | bytes 2555912 | tf_op jit(solution)/shard_map/ppermute | solution.py:766
  445.9 19.7 %collective-permute-start.53 = (bf16[416,1024]{1,0:T(8,128)(2,1)}, bf16[416,1024]{1,0:T(8,128)(2,1)}, u32[]{:S(2)}, u32[]{:S(2)}) collective-permute-start(bf16[416,1024]{1,0:T(8,128)(2,1)} %get-tuple-element.349), channel_id=1, source_target_pairs={{0,4},{1,5},{2,6},{3,7},{4,0},{5,1},{6,2},{7,3},{8,12},{9,13},{10,... | collective-permute-start | bytes 2555912 | tf_op jit(solution)/shard_map/ppermute | solution.py:766
  450.5 23.4 %collective-permute-start.56 = (bf16[576,1024]{1,0:T(8,128)(2,1)}, bf16[576,1024]{1,0:T(8,128)(2,1)}, u32[]{:S(2)}, u32[]{:S(2)}) collective-permute-start(bf16[576,1024]{1,0:T(8,128)(2,1)} %get-tuple-element.356.refs_0_), channel_id=1, source_target_pairs={{8,16},{16,8},{9,17},{17,9},{10,18},{18,10},{11,19},{19,11},{12,20... | collective-permute-start | bytes 3538952 | tf_op jit(solution)/shard_map/ppermute | solution.py:817
  452.2 29.3 %collective-permute-start.55 = (bf16[576,1024]{1,0:T(8,128)(2,1)}, bf16[576,1024]{1,0:T(8,128)(2,1)S(1)}, u32[]{:S(2)}, u32[]{:S(2)}) collective-permute-start(bf16[576,1024]{1,0:T(8,128)(2,1)} %get-tuple-element.353.refs_2_), channel_id=1, source_target_pairs={{8,0},{16,24},{9,1},{17,25},{10,2},{18,26},{11,3},{19,27},{12,4},{... | collective-permute-start | bytes 3538952 | tf_op jit(solution)/shard_map/ppermute | solution.py:817
  468.8 21.3 %collective-permute-start.54 = (bf16[416,1024]{1,0:T(8,128)(2,1)}, bf16[416,1024]{1,0:T(8,128)(2,1)S(1)}, u32[]{:S(2)}, u32[]{:S(2)}) collective-permute-start(bf16[416,1024]{1,0:T(8,128)(2,1)} %combine.24.refs_0_), channel_id=1, source_target_pairs={{0,8},{24,16},{1,9},{25,17},{2,10},{26,18},{3,11},{27,19},{4,12},{... | collective-permute-start | bytes 2555912 | tf_op jit(solution)/shard_map/ppermute | solution.py:817
  476.5 32.6 %collective-permute-start.57 = (bf16[576,1024]{1,0:T(8,128)(2,1)}, bf16[576,1024]{1,0:T(8,128)(2,1)S(1)}, u32[]{:S(2)}, u32[]{:S(2)}) collective-permute-start(bf16[576,1024]{1,0:T(8,128)(2,1)} %combine.25.refs_4_), channel_id=1, source_target_pairs={{8,0},{16,24},{9,1},{17,25},{10,2},{18,26},{11,3},{19,27},{12,4},{... | collective-permute-start | bytes 3538952 | tf_op jit(solution)/shard_map/ppermute | solution.py:817
  493.3 15.7 %collective-permute-start.58 = (bf16[416,1024]{1,0:T(8,128)(2,1)}, bf16[416,1024]{1,0:T(8,128)(2,1)S(1)}, u32[]{:S(2)}, u32[]{:S(2)}) collective-permute-start(bf16[416,1024]{1,0:T(8,128)(2,1)} %combine.26.refs_0_), channel_id=1, source_target_pairs={{8,16},{16,8},{9,17},{17,9},{10,18},{18,10},{11,19},{19,11},{12,20... | collective-permute-start | bytes 2555912 | tf_op jit(solution)/shard_map/ppermute | solution.py:817
  512.2 22.7 %collective-permute-start.59 = (bf16[416,1024]{1,0:T(8,128)(2,1)}, bf16[416,1024]{1,0:T(8,128)(2,1)S(1)}, u32[]{:S(2)}, u32[]{:S(2)}) collective-permute-start(bf16[416,1024]{1,0:T(8,128)(2,1)} %combine.27), channel_id=1, source_target_pairs={{8,0},{16,24},{9,1},{17,25},{10,2},{18,26},{11,3},{19,27},{12,4},{... | collective-permute-start | bytes 2555912 | tf_op jit(solution)/shard_map/ppermute | solution.py:817
  (60 other events, 369.9 us)

commit v6 on v5

--- a/solution.py
+++ b/solution.py
@@ -237,17 +237,15 @@
     lane = lax.broadcasted_iota(jnp.int32, (TILE, 128), 1)
     for i in range(tiles):
         rows = slice(i * TILE, (i + 1) * TILE)
+        before = slice(0, i * TILE)
         halves = []
         for h in range(2):
             q = q_ref[h, rows, :]
-            out = None
-            for j in range(i + 1):
-                cols = slice(j * TILE, (j + 1) * TILE)
-                weights = jnp.exp(dot(q, k_ref[0, cols, :], NT))
-                if j == i:
-                    weights = jnp.where(keep, weights, 0.0)
-                part = dot(weights.astype(BF16), v_ref[0, cols, :])
-                out = part if out is None else out + part
+            weights = jnp.where(keep, jnp.exp(dot(q, k_ref[0, rows, :], NT)), 0.0)
+            out = dot(weights.astype(BF16), v_ref[0, rows, :])
+            if i:
+                weights = jnp.exp(dot(q, k_ref[0, before, :], NT)).astype(BF16)
+                out = out + dot(weights, v_ref[0, before, :])
             total = out[:, 64:65]
             halves.append(out / total)
             high, middle, low = split3(-jnp.log(total))
@@ -305,10 +303,12 @@
         cols = slice(j * TILE, (j + 1) * TILE)
         k = k_ref[0, cols, :]
         v = v_ref[0, cols, :]
-        dk = None
-        dv = None
-        for i in range(j, tiles):
-            rows = slice(i * TILE, (i + 1) * TILE)
+        dk = 0.0
+        dv = 0.0
+        for i, stop in ((j, j + 1), (j + 1, tiles)):
+            if i == tiles:
+                continue
+            rows = slice(i * TILE, stop * TILE)
             for h in range(2):
                 q = q_ref[h, rows, :]
                 do = do_aug[h, rows, :]
@@ -316,10 +316,8 @@
                 if i == j:
                     probs = jnp.where(keep, probs, 0.0)
                 scores = (probs * dot(v, do, NT)).astype(BF16)
-                to_v = dot(probs.astype(BF16), do)
-                to_k = dot(scores, q)
-                dv = to_v if dv is None else dv + to_v
-                dk = to_k if dk is None else dk + to_k
+                dv = dv + dot(probs.astype(BF16), do)
+                dk = dk + dot(scores, q)
                 to_q = dot(k_t[:, cols], scores)
                 if j == 0:
                     dq_t[h * 64 : (h + 1) * 64, rows] = to_q
@@ -407,39 +405,34 @@
 
 def feed_kernel(layout, paired, me_ref, n_ref, nt_ref, c_ref, *refs):
     parts = len(layout)
-    f_ref, b_ref, *grad_refs = refs[sum(layout) : -7]
-    w_all, d_all, back, w_grad, d_grad, f_sum, b_sum = refs[-7:]
+    f_ref, b_ref, *grad_refs = refs[sum(layout) : -8]
+    w_all, d_all, back, hidden, w_grad, d_grad, f_sum, b_sum = refs[-8:]
     me = me_ref[0]
     rows = w_all.shape[0] // parts
     seg = SLAB // parts
     for k, group in enumerate(grouped(refs, layout)):
         fill(w_all, aligned(me ^ k, rows), group, slice(0, rows))
         fill(d_all, aligned(me ^ k, seg), group, slice(rows, rows + seg))
+    step = pl.program_id(0)
+
+    @pl.when(step == 0)
+    def _():
+        f_sum[...] = jnp.zeros_like(f_sum)
+        b_sum[...] = jnp.zeros_like(b_sum)
+
     both = dot(n_ref[...], w_all[...])
     gate = both[:, :SLAB]
     up = both[:, SLAB:]
     sig = 1.0 / (1.0 + jnp.exp(-gate))
     swish = gate * sig
-    hidden = (swish * up).astype(BF16)
+    hidden[...] = (swish * up).astype(BF16)
     back_hidden = dot(c_ref[...], d_all[...], NT)
     back[:, SLAB:] = (back_hidden * swish).astype(BF16)
     back[:, :SLAB] = (back_hidden * up * sig * (1.0 + gate * (1.0 - sig))).astype(BF16)
-    out = dot(hidden, d_all[...])
+    f_sum[...] += dot(hidden[...], d_all[...])
+    b_sum[...] += dot(back[...], w_all[...], NT)
     w_grad[...] = dot(nt_ref[...], back[...]).astype(BF16)
-    d_grad[...] = dot(hidden, c_ref[...], TN).astype(BF16)
-    back_in = dot(back[...], w_all[...], NT)
-
-    step = pl.program_id(0)
-
-    @pl.when(step == 0)
-    def _():
-        f_sum[...] = out
-        b_sum[...] = back_in
-
-    @pl.when(step > 0)
-    def _():
-        f_sum[...] += out
-        b_sum[...] += back_in
+    d_grad[...] = dot(hidden[...], c_ref[...], TN).astype(BF16)
 
     @pl.when(step == pl.num_programs(0) - 1)
     def _():
@@ -478,6 +471,7 @@
             pltpu.VMEM((width, 2 * SLAB), BF16),
             pltpu.VMEM((SLAB, width), BF16),
             pltpu.VMEM((length, 2 * SLAB), BF16),
+            pltpu.VMEM((length, SLAB), BF16),
             pltpu.VMEM((width, 2 * SLAB), BF16),
             pltpu.VMEM((SLAB, width), BF16),
             pltpu.VMEM((length, width), F32),
@@ -987,7 +981,7 @@
         pairs += [(near[k], near[k], 1), (far[k], far[k], 1)]
     pairs += [(near[3], near[4], 0), (far[3], far[4], 0)]
 
-    pack = after(packs[0], corner_a, corner_b)
+    pack = after(packs[0], corner_a, corner_b, far[1], far[2])
     first, second, twin = hop(pack, 2), hop(pack, 4), hop(pack, 1)
     normed_one, *units, q_aug, k_aug, v_aug, gains = project(pairs, place, x, tables)
     (attended_0, q_back_0, k_aug), (first, second, twin) = fence(
@@ -1025,25 +1019,20 @@
         [*feed_step(later, 0, chunks[1], True), normed_two], other_0, *waiting
     )
     last = finish(packs[2], *waiting)
-    other_1 = hop(sib_1, 1)
     moved_0 = hop(combine([(own_0, 3), (other_0, 3)]), 2)
-    normed_two, other_1 = tie(normed_two, other_1)
-    term = combine([(own_1, 3), (other_1, 3)])
-    normed_two, term = tie(normed_two, term)
-    moved_1 = hop(term, 4)
-    (out_2, back_2, own_2, sib_2), (moved_0, moved_1) = fence(
-        feed_step(last, 0, chunks[2], True), moved_0, moved_1
+    other_1 = hop(after(sib_1, *last.arrays), 1)
+    (out_2, back_2, own_2, sib_2), (moved_0, other_1) = fence(
+        feed_step(last, 0, chunks[2], True), moved_0, other_1
     )
     other_2 = hop(sib_2, 1)
-    one, two, three, four = combine(
+    term, one, two = combine(
+        [(own_1, 3), (other_1, 3)],
         [(own_0, 1), (other_0, 1)],
         [(own_0, 2), (other_0, 2), moved_0],
-        [(own_1, 1), (other_1, 1), moved_1],
-        [(own_1, 2), (other_1, 2)],
-    )
-    back_2, one, two, three, four = tie(back_2, one, two, three, four)
+    )
+    back_2, term, one, two = tie(back_2, term, one, two)
+    moved_1 = hop(term, 4)
     first_0, second_0 = hop(one, 2), hop(two, 4)
-    first_1, second_1 = hop(three, 2), hop(four, 4)
     middles = middle(
         early, place, first_sum, back_out, attended, gains, [back_0, back_1, back_2]
     )
@@ -1052,11 +1041,16 @@
     back_attended, term = tie(back_attended, term)
     moved_2 = hop(term, 2)
     halves = attend_back(q_back_0, k_aug, v_aug, attended_0, back_attended, 0, 4)
-    (dq_0, dkv_0, back_attended), (first_0, second_0) = fence(
-        [*halves, back_attended], first_0, second_0
-    )
-    grads_0 = combine([(own_0, 0), (other_0, 0), first_0, second_0])
-    back_attended, grads_0 = tie(back_attended, grads_0)
+    (dq_0, dkv_0, back_attended), (first_0, second_0, moved_1) = fence(
+        [*halves, back_attended], first_0, second_0, moved_1
+    )
+    grads_0, three, four = combine(
+        [(own_0, 0), (other_0, 0), first_0, second_0],
+        [(own_1, 1), (other_1, 1), moved_1],
+        [(own_1, 2), (other_1, 2)],
+    )
+    back_attended, grads_0, three, four = tie(back_attended, grads_0, three, four)
+    first_1, second_1 = hop(three, 2), hop(four, 4)
     inward_0 = rep_hop(grads_0, INWARD)
     halves = attend_back(q_back_1, k_aug, v_aug, attended_1, back_attended, 4, 4)
     (dq_1, dkv_1), (moved_2, inward_0, first_1, second_1) = fence(
@@ -1085,7 +1079,7 @@
     )
     back_raw, other, half_1, total_0, grads_2 = tie(back_raw, other, half_1, total_0, grads_2)
     term = combine([(own, 3), (other, 3)])
-    back_raw, term = tie(back_raw, term)
+    back_raw, total_0, half_1, grads_2, term = tie(back_raw, total_0, half_1, grads_2, term)
     moved = hop(term, 4)
     outward_0 = rep_hop(total_0, OUTWARD)
     across_1 = rep_hop(half_1, ACROSS)
@@ -1110,7 +1104,6 @@
     inward, outward_1, _ = tie(inward, outward_1, total_2)
     half = combine([grads, inward])
     across = rep_hop(half, ACROSS)
-    outward_2, across, _ = tie(outward_2, across, half)
     total = combine([half, across])
     outward = rep_hop(total, OUTWARD)
     total, outward_2 = tie(total, outward_2)

time: 549 us -> 575 us (1.047)
  waiting for transfers between devices: 92.2 us -> 145 us
  Pallas kernels: 345 us -> 315 us
    ppermute x48, waiting for transfers between devices: 49.1 us -> 97.3 us  [hop(): return lax.ppermute(array, 'shard', [(i, i ^ bit) for i in range(8)])]
    pallas_call x2, Pallas kernels: 37.6 us -> 23 us  [attend(): pl.pallas_call(attend_kernel, grid=(groups,), in_specs=[pl.BlockSpec((2,...]
    pallas_call x2, Pallas kernels: 47.7 us -> 39.6 us  [attend_back(): pl.pallas_call(attend_back_kernel, grid=(groups,), in_specs=[pl.BlockSpec...]
    pallas_call x14 -> x13, Pallas kernels: 50 us -> 48.2 us  [combine(): pl.pallas_call(kernel, grid=(rows // step,), in_specs=[spec(k) for _, k i...]
    unnamed x98 -> x108, local copies, waits for them, and re-layouts: 15.3 us -> 16.7 us
  transfers between devices with their start and end apart: 60 -> 60, of which waited for: 22 -> 27; matrix products, arithmetic and copies ran while one was open for 3% -> 3% of each run, Pallas kernels for 62% -> 52%
where the time goes in v6:
time: 575 us; the launch traced here: 566 us
  Pallas kernels  315 us (55%)
  waiting for transfers between devices  145 us (25%)
  starting transfers between devices  63.7 us (11%)
  local copies, waits for them, and re-layouts  23.1 us (4%)
  other arithmetic  17.4 us (3%)
    pallas_call x3, Pallas kernels, feed(): pl.pallas_call(lambda *refs: feed_kernel(pieces.layout, paired, *refs), g...  122 us
    ppermute x48, waiting for transfers between devices, hop(): return lax.ppermute(array, 'shard', [(i, i ^ bit) for i in range(8)])  97.3 us
    pallas_call x13, Pallas kernels, combine(): pl.pallas_call(kernel, grid=(rows // step,), in_specs=[spec(k) for _, k i...  48.2 us
    ppermute x12, waiting for transfers between devices, rep_hop(): return lax.ppermute(array.astype(BF16), 'rep', pairs)  47.6 us
    pallas_call x2, Pallas kernels, attend_back(): pl.pallas_call(attend_back_kernel, grid=(groups,), in_specs=[pl.BlockSpec...  39.6 us
    ppermute x48, starting transfers between devices, hop(): return lax.ppermute(array, 'shard', [(i, i ^ bit) for i in range(8)])  34 us
    ppermute x12, starting transfers between devices, rep_hop(): return lax.ppermute(array.astype(BF16), 'rep', pairs)  29.7 us
    pallas_call x2, Pallas kernels, attend(): pl.pallas_call(attend_kernel, grid=(groups,), in_specs=[pl.BlockSpec((2,...  23 us
  transfers between devices with their start and end apart: 60, of which 27 were waited for; matrix products, arithmetic and copies ran while one was open for 3% of the time, Pallas kernels for 52%

profile of v6, /device:TPU:0, one launch (start us, length us, event | category | flops | bytes accessed | tf_op | source)
XLA Modules:
  0.0 566.0 jit_solution(10239572214575448111)
XLA Ops:
  5.7 3.0 collective-permute-start
  15.0 4.5 pack_rows.1
  25.6 7.5 %collective-permute-done.5.refs_18_.refs_17_ = bf16[128,1024]{1,0:T(8,128)(2,1)S(1)} collective-permute-done((bf16[128,1024]{1,0:T(8,128)(2,1)S(1)}, bf16[128,1024]{1,0:T(8,128)(2,1)S(1)}, u32[]{:S(2)}, u32[]{:S(2)}) %collective-permute-start.5) | collective-permute-done | bytes 262176 | tf_op jit(solution)/shard_map/ppermute | solution.py:760
  36.0 3.1 collective-permute-done.7.refs_20_.refs_19_
  40.0 16.0 %project.1 = (bf16[1024,1024]{1,0:T(8,128)(2,1)}, bf16[1024,1536]{1,0:T(8,128)(2,1)}, bf16[1024,1536]{1,0:T(8,128)(2,1)}, bf16[16,1024,128]{2,1,0:T(8,128)(2,1)}...) custom-call(s32[1]{0:T(128)} %bitcast.refs_0_, bf16[1024,1024]{1,0:T(8,128)(2,1)} %bitcast.33, ...), custom_call_target="tpu_custom_call" | custom-call | flops 8000000 | bytes 25000 | tf_op jit(solution)/shard_map/project/pallas_call | solution.py:203
  56.0 11.4 %attend.2 = (bf16[1024,512]{1,0:T(8,128)(2,1)}, bf16[8,1024,128]{2,1,0:T(8,128)(2,1)}) custom-call(bf16[16,1024,128]{2,1,0:T(8,128)(2,1)} %get-tuple-element.204.q_ref, bf16[8,1024,128]{2,1,0:T(8,128)(2,1)} %get-tuple-element.212.k_ref, bf16[8,1024,128]{2,1,0:T(8,128)(2,1)} %get-tuple-element.206.v_ref), custom_call_target="tpu_custom_call" | custom-call | flops 10000000 | bytes 8000 | tf_op jit(solution)/shard_map/attend/pallas_call | solution.py:262
  72.7 11.6 %attend.3 = (bf16[1024,512]{1,0:T(8,128)(2,1)}, bf16[8,1024,128]{2,1,0:T(8,128)(2,1)}) custom-call(bf16[16,1024,128]{2,1,0:T(8,128)(2,1)} %get-tuple-element.204.q_ref, bf16[8,1024,128]{2,1,0:T(8,128)(2,1)} %get-tuple-element.212.k_ref, bf16[8,1024,128]{2,1,0:T(8,128)(2,1)} %get-tuple-element.206.v_ref), custom_call_target="tpu_custom_call" | custom-call | flops 10000000 | bytes 8000 | tf_op jit(solution)/shard_map/attend/pallas_call | solution.py:262
  84.3 4.4 collective-permute-done.12.refs_11_.refs_10_.refs_15_
  94.0 2.4 collective-permute-done.17.refs_14_.refs_13_.refs_18_
  97.3 8.3 %output_rows.1 = (f32[1024,1024]{1,0:T(8,128)}, bf16[1024,1024]{1,0:T(8,128)(2,1)}, bf16[1024,1024]{1,0:T(8,128)(2,1)}) custom-call(s32[1]{0:T(128)} %bitcast.refs_0_, bf16[1024,512]{1,0:T(8,128)(2,1)} %get-tuple-element.213.refs_1_.refs_3_.o_ref, bf16[1024,512]{1,0:T(8,128)(2,1)} %get-tuple-element.218.refs_2_.refs_4_.o_ref, bf16[1024,1024]{1,0:T(8,128)(2,1)} %bitcast.34, ...), custom_call_target="tpu_custom_call" | custom-call | flops 5000000 | bytes 15000 | tf_op jit(solution)/shard_map/output_rows/pallas_call | solution.py:379
  105.6 40.7 %feed.3 = (bf16[1024,1024]{1,0:T(8,128)(2,1)}, bf16[1024,1024]{1,0:T(8,128)(2,1)}, bf16[4,576,1024]{2,1,0:T(8,128)(2,1)}, bf16[4,576,1024]{2,1,0:T(8,128)(2,1)}) custom-call(s32[1]{0:T(128)} %bitcast.refs_0_, bf16[1024,1024]{1,0:T(8,128)(2,1)} %get-tuple-element.248.refs_1_, bf16[1024,1024]{1,0:T(8,128)(2,1)} %get-tuple-element.227.refs_2_, ...), custom_call_target="tpu_custom_call" | custom-call | flops 37500000 | bytes 38000 | tf_op jit(solution)/shard_map/feed/pallas_call | solution.py:459
  147.1 2.4 collective-permute-done.22.refs_7_
  156.9 40.6 %feed.4 = (bf16[1024,1024]{1,0:T(8,128)(2,1)}, bf16[1024,1024]{1,0:T(8,128)(2,1)}, bf16[4,576,1024]{2,1,0:T(8,128)(2,1)}, bf16[4,576,1024]{2,1,0:T(8,128)(2,1)}) custom-call(s32[1]{0:T(128)} %bitcast.refs_0_, bf16[1024,1024]{1,0:T(8,128)(2,1)} %get-tuple-element.248.refs_1_, bf16[1024,1024]{1,0:T(8,128)(2,1)} %get-tuple-element.227.refs_2_, ...), custom_call_target="tpu_custom_call" | custom-call | flops 37500000 | bytes 38000 | tf_op jit(solution)/shard_map/feed/pallas_call | solution.py:459
  197.6 9.8 %collective-permute-done.29.refs_10_ = bf16[576,1024]{1,0:T(8,128)(2,1)} collective-permute-done((bf16[576,1024]{1,0:T(8,128)(2,1)S(1)}, bf16[576,1024]{1,0:T(8,128)(2,1)}, u32[]{:S(2)}, u32[]{:S(2)}) %collective-permute-start.29) | collective-permute-done | bytes 1179680 | tf_op jit(solution)/shard_map/ppermute | solution.py:760
  207.9 2.5 collective-permute-done.30.refs_7_
  210.4 3.4 collective-permute-done.31.refs_9_
  214.1 2.7 combine.13
  218.0 40.8 %feed.5 = (bf16[1024,1024]{1,0:T(8,128)(2,1)}, bf16[1024,1024]{1,0:T(8,128)(2,1)}, bf16[4,576,1024]{2,1,0:T(8,128)(2,1)}, bf16[4,576,1024]{2,1,0:T(8,128)(2,1)}) custom-call(s32[1]{0:T(128)} %bitcast.refs_0_, bf16[1024,1024]{1,0:T(8,128)(2,1)} %get-tuple-element.248.refs_1_, bf16[1024,1024]{1,0:T(8,128)(2,1)} %get-tuple-element.227.refs_2_, ...), custom_call_target="tpu_custom_call" | custom-call | flops 37500000 | bytes 38000 | tf_op jit(solution)/shard_map/feed/pallas_call | solution.py:459
  259.0 5.0 combine.14
  266.8 14.5 %middle.1 = (f32[1024,1024]{1,0:T(8,128)}, bf16[1024,1024]{1,0:T(8,128)(2,1)}, bf16[1024,1024]{1,0:T(8,128)(2,1)}) custom-call(s32[1]{0:T(128)} %bitcast.refs_0_, f32[1024,1024]{1,0:T(8,128)} %get-tuple-element.350.refs_1_, bf16[1024,1024]{1,0:T(8,128)(2,1)} %bitcast.32, bf16[1024,512]{1,0:T(8,128)(2,1)} %get-tuple-element.213.refs_1_.refs_3_.o_ref, ...), custom_call_target="tpu_custom_call" | custom-call | flops 9000000 | bytes 32000 | tf_op jit(solution)/shard_map/middle/pallas_call | solution.py:529
  281.4 2.6 combine.15
  283.9 19.7 %attend_back.2 = (f32[1024,512]{1,0:T(8,128)}, f32[1024,512]{1,0:T(8,128)}) custom-call(bf16[8,1024,128]{2,1,0:T(8,128)(2,1)} %get-tuple-element.211.q_ref, bf16[8,1024,128]{2,1,0:T(8,128)(2,1)} %get-tuple-element.212.k_ref, bf16[8,1024,128]{2,1,0:T(8,128)(2,1)} %get-tuple-element.206.v_ref, bf16[1024,512]{1,0:T(8,128)(2,1)} %get-tuple-element.213.refs_1_.refs_3_.o_ref, ...), custom_call_target="tpu_custom_call" | custom-call | flops 20000000 | bytes 12000 | tf_op jit(solution)/shard_map/attend_back/pallas_call | solution.py:334
  303.7 14.6 %collective-permute-done.38.refs_6_ = bf16[576,1024]{1,0:T(8,128)(2,1)S(1)} collective-permute-done((bf16[576,1024]{1,0:T(8,128)(2,1)}, bf16[576,1024]{1,0:T(8,128)(2,1)S(1)}, u32[]{:S(2)}, u32[]{:S(2)}) %collective-permute-start.38) | collective-permute-done | bytes 1179680 | tf_op jit(solution)/shard_map/ppermute | solution.py:760
  319.3 6.1 %combine.16 = (bf16[576,1024]{1,0:T(8,128)(2,1)}, bf16[576,1024]{1,0:T(8,128)(2,1)}, bf16[576,1024]{1,0:T(8,128)(2,1)}) custom-call(bf16[4,576,1024]{2,1,0:T(8,128)(2,1)} %get-tuple-element.257.refs_0_.refs_2_.refs_4_, bf16[4,576,1024]{2,1,0:T(8,128)(2,1)} %collective-permute-done.25.refs_1_.refs_3_.refs_5_, bf16[576,1024]{1,0:T(8,128)(2,1)} %copy-done.24, ...), custom_call_target="tpu_custom_call" | custom-call | bytes 4000 | tf_op jit(solution)/shard_map/combine/pallas_call | solution.py:797
  326.6 3.5 collective-permute-start.40
  331.9 19.9 %attend_back.3 = (f32[1024,512]{1,0:T(8,128)}, f32[1024,512]{1,0:T(8,128)}) custom-call(bf16[8,1024,128]{2,1,0:T(8,128)(2,1)} %get-tuple-element.283.q_ref, bf16[8,1024,128]{2,1,0:T(8,128)(2,1)} %get-tuple-element.212.k_ref, bf16[8,1024,128]{2,1,0:T(8,128)(2,1)} %get-tuple-element.206.v_ref, bf16[1024,512]{1,0:T(8,128)(2,1)} %get-tuple-element.218.refs_2_.refs_4_.o_ref, ...), custom_call_target="tpu_custom_call" | custom-call | flops 20000000 | bytes 12000 | tf_op jit(solution)/shard_map/attend_back/pallas_call | solution.py:334
  351.8 2.7 collective-permute-done.39.refs_4_
  354.8 23.3 %collective-permute-done.41.refs_7_ = bf16[576,1024]{1,0:T(8,128)(2,1)S(1)} collective-permute-done((bf16[576,1024]{1,0:T(8,128)(2,1)}, bf16[576,1024]{1,0:T(8,128)(2,1)S(1)}, u32[]{:S(2)}, u32[]{:S(2)}) %collective-permute-start.41) | collective-permute-done | bytes 1179680 | tf_op jit(solution)/shard_map/ppermute | solution.py:760
  379.2 7.5 %combine.17 = (bf16[576,1024]{1,0:T(8,128)(2,1)}, bf16[576,1024]{1,0:T(8,128)(2,1)}, bf16[576,1024]{1,0:T(8,128)(2,1)}, bf16[576,1024]{1,0:T(8,128)(2,1)}) custom-call(bf16[4,576,1024]{2,1,0:T(8,128)(2,1)} %get-tuple-element.274.refs_0_.refs_2_.refs_4_, bf16[4,576,1024]{2,1,0:T(8,128)(2,1)} %collective-permute-done.35.refs_1_.refs_3_.refs_5_, ...), custom_call_target="tpu_custom_call" | custom-call | bytes 4000 | tf_op jit(solution)/shard_map/combine/pallas_call | solution.py:797
  389.0 3.5 collective-permute-start.45
  394.3 19.9 %raw_back.1 = (bf16[1024,2048]{1,0:T(8,128)(2,1)}, bf16[4,416,1024]{2,1,0:T(8,128)(2,1)}, bf16[4,416,1024]{2,1,0:T(8,128)(2,1)}) custom-call(s32[1]{0:T(128)} %bitcast.refs_0_, f32[1024,512]{1,0:T(8,128)} %get-tuple-element.282.refs_1_, f32[1024,512]{1,0:T(8,128)} %get-tuple-element.307.refs_2_, f32[1024,512]{1,0:T(8,128)} %get-tuple-element.308.refs_3_, ...), custom_call_target="tpu_custom_call" | custom-call | flops 10000000 | bytes 30000 | tf_op jit(solution)/shard_map/raw_back/pallas_call | solution.py:615
  417.1 5.4 combine.18
  428.1 8.5 %collective-permute-start.50 = (bf16[576,1024]{1,0:T(8,128)(2,1)}, bf16[576,1024]{1,0:T(8,128)(2,1)}, u32[]{:S(2)}, u32[]{:S(2)}) collective-permute-start(bf16[576,1024]{1,0:T(8,128)(2,1)} %get-tuple-element.343.refs_2_), channel_id=1, source_target_pairs={{0,8},{24,16},{1,9},{25,17},{2,10},{26,18},{3,11},{27,19},{4,12},{... | collective-permute-start | bytes 3538952 | tf_op jit(solution)/shard_map/ppermute | solution.py:811
  438.9 11.4 %input_back.1 = f32[1024,1024]{1,0:T(8,128)} custom-call(s32[1]{0:T(128)} %bitcast.refs_0_, bf16[1024,2048]{1,0:T(8,128)(2,1)} %get-tuple-element.336.refs_1_, bf16[1024,1024]{1,0:T(8,128)(2,1)} %bitcast.35, f32[1024,1024]{1,0:T(8,128)} %get-tuple-element.337.refs_3_, f32[16,1024]{1,0:T(8,128)} %get-tuple-element.219.refs_4_.refs_5_.refs_10_, ...), custom_call_target="tpu_custom_call" | custom-call | flops 6000000 | bytes 18000 | tf_op jit(solution)/shard_map/input_back/pallas_call | solution.py:645
  450.3 8.3 %collective-permute-done.48.refs_2_ = bf16[416,1024]{1,0:T(8,128)(2,1)S(1)} collective-permute-done((bf16[416,1024]{1,0:T(8,128)(2,1)}, bf16[416,1024]{1,0:T(8,128)(2,1)S(1)}, u32[]{:S(2)}, u32[]{:S(2)}) %collective-permute-start.48) | collective-permute-done | bytes 852000 | tf_op jit(solution)/shard_map/ppermute | solution.py:760
  459.5 3.2 combine.20
  465.5 3.5 combine.21
  472.0 6.6 %add_convert_fusion = bf16[1024,1024]{1,0:T(8,128)(2,1)} fusion(f32[1024,1024]{1,0:T(8,128)} %get-tuple-element.350.refs_1_, bf16[1024,1024]{1,0:T(8,128)(2,1)} %get-tuple-element.353, bf16[1024,1024]{1,0:T(8,128)(2,1)} %get-tuple-element.352, bf16[1024,1024]{1,0:T(8,128)(2,1)S(1)} %copy-done.20), kind=kLoop, calls=%fused_computation | loop fusion | flops 7340032 | bytes 12582912 | tf_op jit(solution)/shard_map/convert_element_type | solution.py:1097
  478.6 4.9 collective-permute-done.52.refs_2_
  484.4 2.9 combine.22.refs_0_
  487.3 4.2 collective-permute-start.54
  491.5 2.6 combine.23.refs_4_
  494.0 3.2 collective-permute-done.55.refs_3_
  497.2 10.5 %collective-permute-done.54.refs_1_ = bf16[416,1024]{1,0:T(8,128)(2,1)S(1)} collective-permute-done((bf16[416,1024]{1,0:T(8,128)(2,1)}, bf16[416,1024]{1,0:T(8,128)(2,1)S(1)}, u32[]{:S(2)}, u32[]{:S(2)}) %collective-permute-start.54) | collective-permute-done | bytes 852000 | tf_op jit(solution)/shard_map/ppermute | solution.py:811
  513.8 2.3 combine.25
  517.4 26.4 %collective-permute-done.58.refs_5_ = bf16[576,1024]{1,0:T(8,128)(2,1)S(1)} collective-permute-done((bf16[576,1024]{1,0:T(8,128)(2,1)S(1)}, bf16[576,1024]{1,0:T(8,128)(2,1)S(1)}, u32[]{:S(2)}, u32[]{:S(2)}) %collective-permute-start.58) | collective-permute-done | bytes 1179680 | tf_op jit(solution)/shard_map/ppermute | solution.py:811
  544.9 7.5 %unpack_rows.1 = (f32[128,4608]{1,0:T(8,128)}, f32[128,4608]{1,0:T(8,128)}, f32[576,1024]{1,0:T(8,128)}) custom-call(s32[1]{0:T(128)} %bitcast.8.flag_ref, bf16[576,1024]{1,0:T(8,128)(2,1)} %get-tuple-element.349.refs_0_, bf16[576,1024]{1,0:T(8,128)(2,1)} %copy-done.38, bf16[576,1024]{1,0:T(8,128)(2,1)} %get-tuple-element.359.refs_2_, ...), custom_call_target="tpu_custom_call" | custom-call | bytes 14000 | tf_op jit(solution)/shard_map/unpack_rows/pallas_call | solution.py:737
  552.3 5.4 collective-permute-done.59
  (252 shorter events, 89.5 us)
Async XLA Ops:
  5.7 15.6 %collective-permute-start = (bf16[272,1024]{1,0:T(8,128)(2,1)S(1)}, bf16[272,1024]{1,0:T(8,128)(2,1)S(1)}, u32[]{:S(2)}, u32[]{:S(2)}) collective-permute-start(bf16[272,1024]{1,0:T(8,128)(2,1)S(1)} %concatenate.38.refs_6_.refs_7_.refs_22_.refs_5_), channel_id=1, source_target_pairs={{0,2},{1,3},{2,0},{3,1},{4,6},{5,7},{6,4},{7,5},{8,10},{9,11},{10,... | collective-permute-start | bytes 1671176 | tf_op jit(solution)/shard_map/ppermute | solution.py:760
  8.7 14.1 %collective-permute-start.1 = (bf16[272,1024]{1,0:T(8,128)(2,1)S(1)}, bf16[272,1024]{1,0:T(8,128)(2,1)S(1)}, u32[]{:S(2)}, u32[]{:S(2)}) collective-permute-start(bf16[272,1024]{1,0:T(8,128)(2,1)S(1)} %concatenate.38.refs_6_.refs_7_.refs_22_.refs_5_), channel_id=1, source_target_pairs={{0,4},{1,5},{2,6},{3,7},{4,0},{5,1},{6,2},{7,3},{8,12},{9,13},{10,... | collective-permute-start | bytes 1671176 | tf_op jit(solution)/shard_map/ppermute | solution.py:760
  10.2 12.6 %collective-permute-start.2 = (bf16[272,1024]{1,0:T(8,128)(2,1)S(1)}, bf16[272,1024]{1,0:T(8,128)(2,1)S(1)}, u32[]{:S(2)}, u32[]{:S(2)}) collective-permute-start(bf16[272,1024]{1,0:T(8,128)(2,1)S(1)} %concatenate.38.refs_6_.refs_7_.refs_22_.refs_5_), channel_id=1, source_target_pairs={{0,1},{1,0},{2,3},{3,2},{4,5},{5,4},{6,7},{7,6},{8,9},{9,8},{10,11... | collective-permute-start | bytes 1671176 | tf_op jit(solution)/shard_map/ppermute | solution.py:760
  22.8 10.3 %collective-permute-start.3 = (bf16[272,1024]{1,0:T(8,128)(2,1)S(1)}, bf16[272,1024]{1,0:T(8,128)(2,1)S(1)}, u32[]{:S(2)}, u32[]{:S(2)}) collective-permute-start(bf16[272,1024]{1,0:T(8,128)(2,1)S(1)} %collective-permute-done.refs_10_.refs_11_.refs_24_.refs_9_), channel_id=1, source_target_pairs={{0,1},{1,0},{2,3},{3,2},{4,5},{5,4},{6,7},{7,6},{8,9},{9,8},{10,11... | collective-permute-start | bytes 1671176 | tf_op jit(solution)/shard_map/ppermute | solution.py:760
  22.9 10.2 %collective-permute-start.4 = (bf16[272,1024]{1,0:T(8,128)(2,1)S(1)}, bf16[272,1024]{1,0:T(8,128)(2,1)S(1)}, u32[]{:S(2)}, u32[]{:S(2)}) collective-permute-start(bf16[272,1024]{1,0:T(8,128)(2,1)S(1)} %collective-permute-done.1.refs_14_.refs_15_.refs_26_.refs_13_), channel_id=1, source_target_pairs={{0,1},{1,0},{2,3},{3,2},{4,5},{5,4},{6,7},{7,6},{8,9},{9,8},{10,11... | collective-permute-start | bytes 1671176 | tf_op jit(solution)/shard_map/ppermute | solution.py:760
  23.4 9.7 %collective-permute-start.6 = (bf16[144,1024]{1,0:T(8,128)(2,1)S(1)}, bf16[144,1024]{1,0:T(8,128)(2,1)S(1)}, u32[]{:S(2)}, u32[]{:S(2)}) collective-permute-start(bf16[144,1024]{1,0:T(8,128)(2,1)S(1)} %slice.64), channel_id=1, source_target_pairs={{0,4},{1,5},{2,6},{3,7},{4,0},{5,1},{6,2},{7,3},{8,12},{9,13},{10,... | collective-permute-start | bytes 884744 | tf_op jit(solution)/shard_map/ppermute | solution.py:760
  25.0 8.1 %collective-permute-start.5 = (bf16[128,1024]{1,0:T(8,128)(2,1)S(1)}, bf16[128,1024]{1,0:T(8,128)(2,1)S(1)}, u32[]{:S(2)}, u32[]{:S(2)}) collective-permute-start(bf16[128,1024]{1,0:T(8,128)(2,1)S(1)} %slice.63), channel_id=1, source_target_pairs={{0,2},{1,3},{2,0},{3,1},{4,6},{5,7},{6,4},{7,5},{8,10},{9,11},{10,... | collective-permute-start | bytes 786440 | tf_op jit(solution)/shard_map/ppermute | solution.py:760
  34.1 33.3 %collective-permute-start.9 = (bf16[704,1024]{1,0:T(8,128)(2,1)}, bf16[704,1024]{1,0:T(8,128)(2,1)S(1)}, u32[]{:S(2)}, u32[]{:S(2)}) collective-permute-start(bf16[704,1024]{1,0:T(8,128)(2,1)} %get-tuple-element.210.refs_5_.refs_4_.refs_9_), channel_id=1, source_target_pairs={{0,2},{1,3},{2,0},{3,1},{4,6},{5,7},{6,4},{7,5},{8,10},{9,11},{10,... | collective-permute-start | bytes 4325384 | tf_op jit(solution)/shard_map/ppermute | solution.py:760
  34.6 32.7 %collective-permute-start.10 = (bf16[704,1024]{1,0:T(8,128)(2,1)}, bf16[704,1024]{1,0:T(8,128)(2,1)S(1)}, u32[]{:S(2)}, u32[]{:S(2)}) collective-permute-start(bf16[704,1024]{1,0:T(8,128)(2,1)} %get-tuple-element.210.refs_5_.refs_4_.refs_9_), channel_id=1, source_target_pairs={{0,4},{1,5},{2,6},{3,7},{4,0},{5,1},{6,2},{7,3},{8,12},{9,13},{10,... | collective-permute-start | bytes 4325384 | tf_op jit(solution)/shard_map/ppermute | solution.py:760
  35.5 31.9 %collective-permute-start.11 = (bf16[704,1024]{1,0:T(8,128)(2,1)}, bf16[704,1024]{1,0:T(8,128)(2,1)}, u32[]{:S(2)}, u32[]{:S(2)}) collective-permute-start(bf16[704,1024]{1,0:T(8,128)(2,1)} %get-tuple-element.210.refs_5_.refs_4_.refs_9_), channel_id=1, source_target_pairs={{0,1},{1,0},{2,3},{3,2},{4,5},{5,4},{6,7},{7,6},{8,9},{9,8},{10,11... | collective-permute-start | bytes 4325384 | tf_op jit(solution)/shard_map/ppermute | solution.py:760
  67.4 22.6 %collective-permute-start.14 = (bf16[704,1024]{1,0:T(8,128)(2,1)S(1)}, bf16[704,1024]{1,0:T(8,128)(2,1)}, u32[]{:S(2)}, u32[]{:S(2)}) collective-permute-start(bf16[704,1024]{1,0:T(8,128)(2,1)S(1)} %collective-permute-done.9.refs_7_.refs_6_.refs_11_), channel_id=1, source_target_pairs={{0,1},{1,0},{2,3},{3,2},{4,5},{5,4},{6,7},{7,6},{8,9},{9,8},{10,11... | collective-permute-start | bytes 4325384 | tf_op jit(solution)/shard_map/ppermute | solution.py:760
  67.8 22.2 %collective-permute-start.15 = (bf16[704,1024]{1,0:T(8,128)(2,1)S(1)}, bf16[704,1024]{1,0:T(8,128)(2,1)}, u32[]{:S(2)}, u32[]{:S(2)}) collective-permute-start(bf16[704,1024]{1,0:T(8,128)(2,1)S(1)} %collective-permute-done.10.refs_9_.refs_8_.refs_13_), channel_id=1, source_target_pairs={{0,1},{1,0},{2,3},{3,2},{4,5},{5,4},{6,7},{7,6},{8,9},{9,8},{10,11... | collective-permute-start | bytes 4325384 | tf_op jit(solution)/shard_map/ppermute | solution.py:760
  70.1 18.6 %collective-permute-start.12 = (bf16[704,512]{1,0:T(8,128)(2,1)}, bf16[704,512]{1,0:T(8,128)(2,1)S(1)}, u32[]{:S(2)}, u32[]{:S(2)}) collective-permute-start(bf16[704,512]{1,0:T(8,128)(2,1)} %slice.65), channel_id=1, source_target_pairs={{0,2},{1,3},{2,0},{3,1},{4,6},{5,7},{6,4},{7,5},{8,10},{9,11},{10,... | collective-permute-start | bytes 2162696 | tf_op jit(solution)/shard_map/ppermute | solution.py:760
  71.6 18.4 %collective-permute-start.13 = (bf16[704,512]{1,0:T(8,128)(2,1)}, bf16[704,512]{1,0:T(8,128)(2,1)}, u32[]{:S(2)}, u32[]{:S(2)}) collective-permute-start(bf16[704,512]{1,0:T(8,128)(2,1)} %slice.66), channel_id=1, source_target_pairs={{0,4},{1,5},{2,6},{3,7},{4,0},{5,1},{6,2},{7,3},{8,12},{9,13},{10,... | collective-permute-start | bytes 2162696 | tf_op jit(solution)/shard_map/ppermute | solution.py:760
  90.0 56.3 %collective-permute-start.18 = (bf16[576,1024]{1,0:T(8,128)(2,1)}, bf16[576,1024]{1,0:T(8,128)(2,1)S(1)}, u32[]{:S(2)}, u32[]{:S(2)}) collective-permute-start(bf16[576,1024]{1,0:T(8,128)(2,1)} %get-tuple-element.233.refs_4_), channel_id=1, source_target_pairs={{0,1},{1,0},{2,3},{3,2},{4,5},{5,4},{6,7},{7,6},{8,9},{9,8},{10,11... | collective-permute-start | bytes 3538952 | tf_op jit(solution)/shard_map/ppermute | solution.py:760
  90.5 55.8 %collective-permute-start.19 = (bf16[576,1024]{1,0:T(8,128)(2,1)}, bf16[576,1024]{1,0:T(8,128)(2,1)}, u32[]{:S(2)}, u32[]{:S(2)}) collective-permute-start(bf16[576,1024]{1,0:T(8,128)(2,1)} %get-tuple-element.233.refs_4_), channel_id=1, source_target_pairs={{0,2},{1,3},{2,0},{3,1},{4,6},{5,7},{6,4},{7,5},{8,10},{9,11},{10,... | collective-permute-start | bytes 3538952 | tf_op jit(solution)/shard_map/ppermute | solution.py:760
  91.1 55.3 %collective-permute-start.20 = (bf16[576,1024]{1,0:T(8,128)(2,1)}, bf16[576,1024]{1,0:T(8,128)(2,1)}, u32[]{:S(2)}, u32[]{:S(2)}) collective-permute-start(bf16[576,1024]{1,0:T(8,128)(2,1)} %get-tuple-element.233.refs_4_), channel_id=1, source_target_pairs={{0,4},{1,5},{2,6},{3,7},{4,0},{5,1},{6,2},{7,3},{8,12},{9,13},{10,... | collective-permute-start | bytes 3538952 | tf_op jit(solution)/shard_map/ppermute | solution.py:760
  92.2 54.2 %collective-permute-start.21 = (bf16[576,1024]{1,0:T(8,128)(2,1)}, bf16[576,1024]{1,0:T(8,128)(2,1)}, u32[]{:S(2)}, u32[]{:S(2)}) collective-permute-start(bf16[576,1024]{1,0:T(8,128)(2,1)} %get-tuple-element.233.refs_4_), channel_id=1, source_target_pairs={{0,6},{1,7},{2,4},{3,5},{4,2},{5,3},{6,0},{7,1},{8,14},{9,15},{10,... | collective-permute-start | bytes 3538952 | tf_op jit(solution)/shard_map/ppermute | solution.py:760
  152.9 54.5 %collective-permute-start.25 = (bf16[4,576,1024]{2,1,0:T(8,128)(2,1)}, bf16[4,576,1024]{2,1,0:T(8,128)(2,1)}, u32[]{:S(2)}, u32[]{:S(2)}) collective-permute-start(bf16[4,576,1024]{2,1,0:T(8,128)(2,1)} %get-tuple-element.245), channel_id=1, source_target_pairs={{0,1},{1,0},{2,3},{3,2},{4,5},{5,4},{6,7},{7,6},{8,9},{9,8},{10,11... | collective-permute-start | bytes 14155784 | tf_op jit(solution)/shard_map/ppermute | solution.py:760
  153.0 44.5 %collective-permute-start.26 = (bf16[576,1024]{1,0:T(8,128)(2,1)S(1)}, bf16[576,1024]{1,0:T(8,128)(2,1)S(1)}, u32[]{:S(2)}, u32[]{:S(2)}) collective-permute-start(bf16[576,1024]{1,0:T(8,128)(2,1)S(1)} %copy-done.21), channel_id=1, source_target_pairs={{0,1},{1,0},{2,3},{3,2},{4,5},{5,4},{6,7},{7,6},{8,9},{9,8},{10,11... | collective-permute-start | bytes 3538952 | tf_op jit(solution)/shard_map/ppermute | solution.py:760
  153.4 44.1 %collective-permute-start.27 = (bf16[576,1024]{1,0:T(8,128)(2,1)S(1)}, bf16[576,1024]{1,0:T(8,128)(2,1)}, u32[]{:S(2)}, u32[]{:S(2)}) collective-permute-start(bf16[576,1024]{1,0:T(8,128)(2,1)S(1)} %copy-done.21), channel_id=1, source_target_pairs={{0,2},{1,3},{2,0},{3,1},{4,6},{5,7},{6,4},{7,5},{8,10},{9,11},{10,... | collective-permute-start | bytes 3538952 | tf_op jit(solution)/shard_map/ppermute | solution.py:760
  153.9 43.6 %collective-permute-start.28 = (bf16[576,1024]{1,0:T(8,128)(2,1)S(1)}, bf16[576,1024]{1,0:T(8,128)(2,1)}, u32[]{:S(2)}, u32[]{:S(2)}) collective-permute-start(bf16[576,1024]{1,0:T(8,128)(2,1)S(1)} %copy-done.21), channel_id=1, source_target_pairs={{0,4},{1,5},{2,6},{3,7},{4,0},{5,1},{6,2},{7,3},{8,12},{9,13},{10,... | collective-permute-start | bytes 3538952 | tf_op jit(solution)/shard_map/ppermute | solution.py:760
  155.1 52.3 %collective-permute-start.29 = (bf16[576,1024]{1,0:T(8,128)(2,1)S(1)}, bf16[576,1024]{1,0:T(8,128)(2,1)}, u32[]{:S(2)}, u32[]{:S(2)}) collective-permute-start(bf16[576,1024]{1,0:T(8,128)(2,1)S(1)} %copy-done.21), channel_id=1, source_target_pairs={{0,6},{1,7},{2,4},{3,5},{4,2},{5,3},{6,0},{7,1},{8,14},{9,15},{10,... | collective-permute-start | bytes 3538952 | tf_op jit(solution)/shard_map/ppermute | solution.py:760
  213.9 44.9 %collective-permute-start.34 = (bf16[4,576,1024]{2,1,0:T(8,128)(2,1)}, bf16[4,576,1024]{2,1,0:T(8,128)(2,1)}, u32[]{:S(2)}, u32[]{:S(2)}) collective-permute-start(bf16[4,576,1024]{2,1,0:T(8,128)(2,1)} %get-tuple-element.260), channel_id=1, source_target_pairs={{0,1},{1,0},{2,3},{3,2},{4,5},{5,4},{6,7},{7,6},{8,9},{9,8},{10,11... | collective-permute-start | bytes 14155784 | tf_op jit(solution)/shard_map/ppermute | solution.py:760
  216.8 42.1 %collective-permute-start.33 = (bf16[576,1024]{1,0:T(8,128)(2,1)}, bf16[576,1024]{1,0:T(8,128)(2,1)}, u32[]{:S(2)}, u32[]{:S(2)}) collective-permute-start(bf16[576,1024]{1,0:T(8,128)(2,1)} %combine.13), channel_id=1, source_target_pairs={{0,2},{1,3},{2,0},{3,1},{4,6},{5,7},{6,4},{7,5},{8,10},{9,11},{10,... | collective-permute-start | bytes 3538952 | tf_op jit(solution)/shard_map/ppermute | solution.py:760
  258.9 22.5 %collective-permute-start.35 = (bf16[4,576,1024]{2,1,0:T(8,128)(2,1)}, bf16[4,576,1024]{2,1,0:T(8,128)(2,1)}, u32[]{:S(2)}, u32[]{:S(2)}) collective-permute-start(bf16[4,576,1024]{2,1,0:T(8,128)(2,1)} %get-tuple-element.272), channel_id=1, source_target_pairs={{0,1},{1,0},{2,3},{3,2},{4,5},{5,4},{6,7},{7,6},{8,9},{9,8},{10,11... | collective-permute-start | bytes 14155784 | tf_op jit(solution)/shard_map/ppermute | solution.py:760
  263.9 39.8 %collective-permute-start.36 = (bf16[576,1024]{1,0:T(8,128)(2,1)}, bf16[576,1024]{1,0:T(8,128)(2,1)S(1)}, u32[]{:S(2)}, u32[]{:S(2)}) collective-permute-start(bf16[576,1024]{1,0:T(8,128)(2,1)} %get-tuple-element.279), channel_id=1, source_target_pairs={{0,2},{1,3},{2,0},{3,1},{4,6},{5,7},{6,4},{7,5},{8,10},{9,11},{10,... | collective-permute-start | bytes 3538952 | tf_op jit(solution)/shard_map/ppermute | solution.py:760
  264.8 38.9 %collective-permute-start.37 = (bf16[576,1024]{1,0:T(8,128)(2,1)}, bf16[576,1024]{1,0:T(8,128)(2,1)S(1)}, u32[]{:S(2)}, u32[]{:S(2)}) collective-permute-start(bf16[576,1024]{1,0:T(8,128)(2,1)} %get-tuple-element.280), channel_id=1, source_target_pairs={{0,4},{1,5},{2,6},{3,7},{4,0},{5,1},{6,2},{7,3},{8,12},{9,13},{10,... | collective-permute-start | bytes 3538952 | tf_op jit(solution)/shard_map/ppermute | solution.py:760
  265.6 52.7 %collective-permute-start.38 = (bf16[576,1024]{1,0:T(8,128)(2,1)}, bf16[576,1024]{1,0:T(8,128)(2,1)S(1)}, u32[]{:S(2)}, u32[]{:S(2)}) collective-permute-start(bf16[576,1024]{1,0:T(8,128)(2,1)} %get-tuple-element.281), channel_id=1, source_target_pairs={{0,4},{1,5},{2,6},{3,7},{4,0},{5,1},{6,2},{7,3},{8,12},{9,13},{10,... | collective-permute-start | bytes 3538952 | tf_op jit(solution)/shard_map/ppermute | solution.py:760
  325.4 29.1 %collective-permute-start.39 = (bf16[576,1024]{1,0:T(8,128)(2,1)}, bf16[576,1024]{1,0:T(8,128)(2,1)S(1)}, u32[]{:S(2)}, u32[]{:S(2)}) collective-permute-start(bf16[576,1024]{1,0:T(8,128)(2,1)} %combine.15), channel_id=1, source_target_pairs={{0,2},{1,3},{2,0},{3,1},{4,6},{5,7},{6,4},{7,5},{8,10},{9,11},{10,... | collective-permute-start | bytes 3538952 | tf_op jit(solution)/shard_map/ppermute | solution.py:760
  326.6 28.3 %collective-permute-start.40 = (bf16[576,1024]{1,0:T(8,128)(2,1)}, bf16[576,1024]{1,0:T(8,128)(2,1)S(1)}, u32[]{:S(2)}, u32[]{:S(2)}) collective-permute-start(bf16[576,1024]{1,0:T(8,128)(2,1)} %get-tuple-element.295.refs_9_), channel_id=1, source_target_pairs={{0,8},{24,16},{1,9},{25,17},{2,10},{26,18},{3,11},{27,19},{4,12},{... | collective-permute-start | bytes 3538952 | tf_op jit(solution)/shard_map/ppermute | solution.py:811
  330.1 48.0 %collective-permute-start.41 = (bf16[576,1024]{1,0:T(8,128)(2,1)}, bf16[576,1024]{1,0:T(8,128)(2,1)S(1)}, u32[]{:S(2)}, u32[]{:S(2)}) collective-permute-start(bf16[576,1024]{1,0:T(8,128)(2,1)} %get-tuple-element.296), channel_id=1, source_target_pairs={{0,2},{1,3},{2,0},{3,1},{4,6},{5,7},{6,4},{7,5},{8,10},{9,11},{10,... | collective-permute-start | bytes 3538952 | tf_op jit(solution)/shard_map/ppermute | solution.py:760
  331.0 47.1 %collective-permute-start.42 = (bf16[576,1024]{1,0:T(8,128)(2,1)}, bf16[576,1024]{1,0:T(8,128)(2,1)}, u32[]{:S(2)}, u32[]{:S(2)}) collective-permute-start(bf16[576,1024]{1,0:T(8,128)(2,1)} %get-tuple-element.297), channel_id=1, source_target_pairs={{0,4},{1,5},{2,6},{3,7},{4,0},{5,1},{6,2},{7,3},{8,12},{9,13},{10,... | collective-permute-start | bytes 3538952 | tf_op jit(solution)/shard_map/ppermute | solution.py:760
  386.7 27.6 %collective-permute-start.43 = (bf16[576,1024]{1,0:T(8,128)(2,1)}, bf16[576,1024]{1,0:T(8,128)(2,1)S(1)}, u32[]{:S(2)}, u32[]{:S(2)}) collective-permute-start(bf16[576,1024]{1,0:T(8,128)(2,1)} %get-tuple-element.317), channel_id=1, source_target_pairs={{0,2},{1,3},{2,0},{3,1},{4,6},{5,7},{6,4},{7,5},{8,10},{9,11},{10,... | collective-permute-start | bytes 3538952 | tf_op jit(solution)/shard_map/ppermute | solution.py:760
  387.9 26.4 %collective-permute-start.44 = (bf16[576,1024]{1,0:T(8,128)(2,1)}, bf16[576,1024]{1,0:T(8,128)(2,1)S(1)}, u32[]{:S(2)}, u32[]{:S(2)}) collective-permute-start(bf16[576,1024]{1,0:T(8,128)(2,1)} %get-tuple-element.318), channel_id=1, source_target_pairs={{0,4},{1,5},{2,6},{3,7},{4,0},{5,1},{6,2},{7,3},{8,12},{9,13},{10,... | collective-permute-start | bytes 3538952 | tf_op jit(solution)/shard_map/ppermute | solution.py:760
  389.0 27.1 %collective-permute-start.45 = (bf16[576,1024]{1,0:T(8,128)(2,1)}, bf16[576,1024]{1,0:T(8,128)(2,1)S(1)}, u32[]{:S(2)}, u32[]{:S(2)}) collective-permute-start(bf16[576,1024]{1,0:T(8,128)(2,1)} %get-tuple-element.319.refs_0_), channel_id=1, source_target_pairs={{0,8},{24,16},{1,9},{25,17},{2,10},{26,18},{3,11},{27,19},{4,12},{... | collective-permute-start | bytes 3538952 | tf_op jit(solution)/shard_map/ppermute | solution.py:811
  392.6 23.5 %collective-permute-start.46 = (bf16[576,1024]{1,0:T(8,128)(2,1)}, bf16[576,1024]{1,0:T(8,128)(2,1)}, u32[]{:S(2)}, u32[]{:S(2)}) collective-permute-start(bf16[576,1024]{1,0:T(8,128)(2,1)} %get-tuple-element.320.refs_2_), channel_id=1, source_target_pairs={{8,16},{16,8},{9,17},{17,9},{10,18},{18,10},{11,19},{19,11},{12,20... | collective-permute-start | bytes 3538952 | tf_op jit(solution)/shard_map/ppermute | solution.py:811
  427.4 35.4 %collective-permute-start.49 = (bf16[576,1024]{1,0:T(8,128)(2,1)}, bf16[576,1024]{1,0:T(8,128)(2,1)S(1)}, u32[]{:S(2)}, u32[]{:S(2)}) collective-permute-start(bf16[576,1024]{1,0:T(8,128)(2,1)} %get-tuple-element.342.refs_0_), channel_id=1, source_target_pairs={{8,16},{16,8},{9,17},{17,9},{10,18},{18,10},{11,19},{19,11},{12,20... | collective-permute-start | bytes 3538952 | tf_op jit(solution)/shard_map/ppermute | solution.py:811
  428.1 34.6 %collective-permute-start.50 = (bf16[576,1024]{1,0:T(8,128)(2,1)}, bf16[576,1024]{1,0:T(8,128)(2,1)}, u32[]{:S(2)}, u32[]{:S(2)}) collective-permute-start(bf16[576,1024]{1,0:T(8,128)(2,1)} %get-tuple-element.343.refs_2_), channel_id=1, source_target_pairs={{0,8},{24,16},{1,9},{25,17},{2,10},{26,18},{3,11},{27,19},{4,12},{... | collective-permute-start | bytes 3538952 | tf_op jit(solution)/shard_map/ppermute | solution.py:811
  436.6 32.4 %collective-permute-start.51 = (bf16[576,1024]{1,0:T(8,128)(2,1)}, bf16[576,1024]{1,0:T(8,128)(2,1)S(1)}, u32[]{:S(2)}, u32[]{:S(2)}) collective-permute-start(bf16[576,1024]{1,0:T(8,128)(2,1)} %get-tuple-element.349.refs_0_), channel_id=1, source_target_pairs={{8,0},{16,24},{9,1},{17,25},{10,2},{18,26},{11,3},{19,27},{12,4},{... | collective-permute-start | bytes 3538952 | tf_op jit(solution)/shard_map/ppermute | solution.py:811
  437.9 20.7 %collective-permute-start.48 = (bf16[416,1024]{1,0:T(8,128)(2,1)}, bf16[416,1024]{1,0:T(8,128)(2,1)S(1)}, u32[]{:S(2)}, u32[]{:S(2)}) collective-permute-start(bf16[416,1024]{1,0:T(8,128)(2,1)} %combine.19), channel_id=1, source_target_pairs={{0,4},{1,5},{2,6},{3,7},{4,0},{5,1},{6,2},{7,3},{8,12},{9,13},{10,... | collective-permute-start | bytes 2555912 | tf_op jit(solution)/shard_map/ppermute | solution.py:760
  463.8 19.7 %collective-permute-start.52 = (bf16[416,1024]{1,0:T(8,128)(2,1)}, bf16[416,1024]{1,0:T(8,128)(2,1)S(1)}, u32[]{:S(2)}, u32[]{:S(2)}) collective-permute-start(bf16[416,1024]{1,0:T(8,128)(2,1)} %get-tuple-element.354), channel_id=1, source_target_pairs={{0,2},{1,3},{2,0},{3,1},{4,6},{5,7},{6,4},{7,5},{8,10},{9,11},{10,... | collective-permute-start | bytes 2555912 | tf_op jit(solution)/shard_map/ppermute | solution.py:760
  464.4 19.5 %collective-permute-start.53 = (bf16[416,1024]{1,0:T(8,128)(2,1)}, bf16[416,1024]{1,0:T(8,128)(2,1)}, u32[]{:S(2)}, u32[]{:S(2)}) collective-permute-start(bf16[416,1024]{1,0:T(8,128)(2,1)} %get-tuple-element.355), channel_id=1, source_target_pairs={{0,4},{1,5},{2,6},{3,7},{4,0},{5,1},{6,2},{7,3},{8,12},{9,13},{10,... | collective-permute-start | bytes 2555912 | tf_op jit(solution)/shard_map/ppermute | solution.py:760
  469.0 28.2 %collective-permute-start.55 = (bf16[576,1024]{1,0:T(8,128)(2,1)}, bf16[576,1024]{1,0:T(8,128)(2,1)}, u32[]{:S(2)}, u32[]{:S(2)}) collective-permute-start(bf16[576,1024]{1,0:T(8,128)(2,1)} %get-tuple-element.359.refs_2_), channel_id=1, source_target_pairs={{8,0},{16,24},{9,1},{17,25},{10,2},{18,26},{11,3},{19,27},{12,4},{... | collective-permute-start | bytes 3538952 | tf_op jit(solution)/shard_map/ppermute | solution.py:811
  470.3 21.1 %collective-permute-start.56 = (bf16[576,1024]{1,0:T(8,128)(2,1)}, bf16[576,1024]{1,0:T(8,128)(2,1)}, u32[]{:S(2)}, u32[]{:S(2)}) collective-permute-start(bf16[576,1024]{1,0:T(8,128)(2,1)} %get-tuple-element.362.refs_0_), channel_id=1, source_target_pairs={{8,16},{16,8},{9,17},{17,9},{10,18},{18,10},{11,19},{19,11},{12,20... | collective-permute-start | bytes 3538952 | tf_op jit(solution)/shard_map/ppermute | solution.py:811
  487.3 20.5 %collective-permute-start.54 = (bf16[416,1024]{1,0:T(8,128)(2,1)}, bf16[416,1024]{1,0:T(8,128)(2,1)S(1)}, u32[]{:S(2)}, u32[]{:S(2)}) collective-permute-start(bf16[416,1024]{1,0:T(8,128)(2,1)} %combine.22.refs_0_), channel_id=1, source_target_pairs={{0,8},{24,16},{1,9},{25,17},{2,10},{26,18},{3,11},{27,19},{4,12},{... | collective-permute-start | bytes 2555912 | tf_op jit(solution)/shard_map/ppermute | solution.py:811
  511.6 32.2 %collective-permute-start.58 = (bf16[576,1024]{1,0:T(8,128)(2,1)S(1)}, bf16[576,1024]{1,0:T(8,128)(2,1)S(1)}, u32[]{:S(2)}, u32[]{:S(2)}) collective-permute-start(bf16[576,1024]{1,0:T(8,128)(2,1)S(1)} %copy-done.12), channel_id=1, source_target_pairs={{8,0},{16,24},{9,1},{17,25},{10,2},{18,26},{11,3},{19,27},{12,4},{... | collective-permute-start | bytes 3538952 | tf_op jit(solution)/shard_map/ppermute | solution.py:811
  516.1 41.7 %collective-permute-start.59 = (bf16[416,1024]{1,0:T(8,128)(2,1)}, bf16[416,1024]{1,0:T(8,128)(2,1)S(1)}, u32[]{:S(2)}, u32[]{:S(2)}) collective-permute-start(bf16[416,1024]{1,0:T(8,128)(2,1)} %combine.25), channel_id=1, source_target_pairs={{8,0},{16,24},{9,1},{17,25},{10,2},{18,26},{11,3},{19,27},{12,4},{... | collective-permute-start | bytes 2555912 | tf_op jit(solution)/shard_map/ppermute | solution.py:811
  (65 other events, 420.6 us)

commit v7 on v6

--- a/solution.py
+++ b/solution.py
@@ -1019,20 +1019,25 @@
         [*feed_step(later, 0, chunks[1], True), normed_two], other_0, *waiting
     )
     last = finish(packs[2], *waiting)
+    other_1 = hop(sib_1, 1)
     moved_0 = hop(combine([(own_0, 3), (other_0, 3)]), 2)
-    other_1 = hop(after(sib_1, *last.arrays), 1)
-    (out_2, back_2, own_2, sib_2), (moved_0, other_1) = fence(
-        feed_step(last, 0, chunks[2], True), moved_0, other_1
+    normed_two, other_1 = tie(normed_two, other_1)
+    term = combine([(own_1, 3), (other_1, 3)])
+    normed_two, term = tie(normed_two, term)
+    moved_1 = hop(term, 4)
+    (out_2, back_2, own_2, sib_2), (moved_0, moved_1) = fence(
+        feed_step(last, 0, chunks[2], True), moved_0, moved_1
     )
     other_2 = hop(sib_2, 1)
-    term, one, two = combine(
-        [(own_1, 3), (other_1, 3)],
+    one, two, three, four = combine(
         [(own_0, 1), (other_0, 1)],
         [(own_0, 2), (other_0, 2), moved_0],
-    )
-    back_2, term, one, two = tie(back_2, term, one, two)
-    moved_1 = hop(term, 4)
+        [(own_1, 1), (other_1, 1), moved_1],
+        [(own_1, 2), (other_1, 2)],
+    )
+    back_2, one, two, three, four = tie(back_2, one, two, three, four)
     first_0, second_0 = hop(one, 2), hop(two, 4)
+    first_1, second_1 = hop(three, 2), hop(four, 4)
     middles = middle(
         early, place, first_sum, back_out, attended, gains, [back_0, back_1, back_2]
     )
@@ -1041,16 +1046,11 @@
     back_attended, term = tie(back_attended, term)
     moved_2 = hop(term, 2)
     halves = attend_back(q_back_0, k_aug, v_aug, attended_0, back_attended, 0, 4)
-    (dq_0, dkv_0, back_attended), (first_0, second_0, moved_1) = fence(
-        [*halves, back_attended], first_0, second_0, moved_1
-    )
-    grads_0, three, four = combine(
-        [(own_0, 0), (other_0, 0), first_0, second_0],
-        [(own_1, 1), (other_1, 1), moved_1],
-        [(own_1, 2), (other_1, 2)],
-    )
-    back_attended, grads_0, three, four = tie(back_attended, grads_0, three, four)
-    first_1, second_1 = hop(three, 2), hop(four, 4)
+    (dq_0, dkv_0, back_attended), (first_0, second_0) = fence(
+        [*halves, back_attended], first_0, second_0
+    )
+    grads_0 = combine([(own_0, 0), (other_0, 0), first_0, second_0])
+    back_attended, grads_0 = tie(back_attended, grads_0)
     inward_0 = rep_hop(grads_0, INWARD)
     halves = attend_back(q_back_1, k_aug, v_aug, attended_1, back_attended, 4, 4)
     (dq_1, dkv_1), (moved_2, inward_0, first_1, second_1) = fence(
@@ -1079,7 +1079,7 @@
     )
     back_raw, other, half_1, total_0, grads_2 = tie(back_raw, other, half_1, total_0, grads_2)
     term = combine([(own, 3), (other, 3)])
-    back_raw, total_0, half_1, grads_2, term = tie(back_raw, total_0, half_1, grads_2, term)
+    back_raw, term = tie(back_raw, term)
     moved = hop(term, 4)
     outward_0 = rep_hop(total_0, OUTWARD)
     across_1 = rep_hop(half_1, ACROSS)
@@ -1104,6 +1104,7 @@
     inward, outward_1, _ = tie(inward, outward_1, total_2)
     half = combine([grads, inward])
     across = rep_hop(half, ACROSS)
+    outward_2, across, _ = tie(outward_2, across, half)
     total = combine([half, across])
     outward = rep_hop(total, OUTWARD)
     total, outward_2 = tie(total, outward_2)

time: 575 us -> 540 us (0.939)
  waiting for transfers between devices: 145 us -> 107 us
    ppermute x48, waiting for transfers between devices: 97.3 us -> 63.9 us  [hop(): return lax.ppermute(array, 'shard', [(i, i ^ bit) for i in range(8)])]
    pallas_call x13 -> x14, Pallas kernels: 48.2 us -> 50.2 us  [combine(): pl.pallas_call(kernel, grid=(rows // step,), in_specs=[spec(k) for _, k i...]
    unnamed x108 -> x102, local copies, waits for them, and re-layouts: 16.7 us -> 14.9 us
  transfers between devices with their start and end apart: 60 -> 60, of which waited for: 27 -> 23; matrix products, arithmetic and copies ran while one was open for 3% -> 3% of each run, Pallas kernels for 52% -> 58%
where the time goes in v7:
time: 540 us; the launch traced here: 531 us
  Pallas kernels  317 us (59%)
  waiting for transfers between devices  107 us (20%)
  starting transfers between devices  66.7 us (12%)
  local copies, waits for them, and re-layouts  21.5 us (4%)
  other arithmetic  17.2 us (3%)
    pallas_call x3, Pallas kernels, feed(): pl.pallas_call(lambda *refs: feed_kernel(pieces.layout, paired, *refs), g...  122 us
    ppermute x48, waiting for transfers between devices, hop(): return lax.ppermute(array, 'shard', [(i, i ^ bit) for i in range(8)])  63.9 us
    pallas_call x14, Pallas kernels, combine(): pl.pallas_call(kernel, grid=(rows // step,), in_specs=[spec(k) for _, k i...  50.2 us
    ppermute x12, waiting for transfers between devices, rep_hop(): return lax.ppermute(array.astype(BF16), 'rep', pairs)  43 us
    pallas_call x2, Pallas kernels, attend_back(): pl.pallas_call(attend_back_kernel, grid=(groups,), in_specs=[pl.BlockSpec...  39.6 us
    ppermute x48, starting transfers between devices, hop(): return lax.ppermute(array, 'shard', [(i, i ^ bit) for i in range(8)])  35.2 us
    ppermute x12, starting transfers between devices, rep_hop(): return lax.ppermute(array.astype(BF16), 'rep', pairs)  31.6 us
    pallas_call x2, Pallas kernels, attend(): pl.pallas_call(attend_kernel, grid=(groups,), in_specs=[pl.BlockSpec((2,...  23.1 us
  transfers between devices with their start and end apart: 60, of which 23 were waited for; matrix products, arithmetic and copies ran while one was open for 3% of the time, Pallas kernels for 58%

profile of v7, /device:TPU:0, one launch (start us, length us, event | category | flops | bytes accessed | tf_op | source)
XLA Modules:
  0.0 530.6 jit_solution(14830279955323813653)
XLA Ops:
  5.7 3.0 collective-permute-start
  15.0 4.4 pack_rows.1
  25.6 7.5 %collective-permute-done.5.refs_18_.refs_17_ = bf16[128,1024]{1,0:T(8,128)(2,1)S(1)} collective-permute-done((bf16[128,1024]{1,0:T(8,128)(2,1)S(1)}, bf16[128,1024]{1,0:T(8,128)(2,1)S(1)}, u32[]{:S(2)}, u32[]{:S(2)}) %collective-permute-start.5) | collective-permute-done | bytes 262176 | tf_op jit(solution)/shard_map/ppermute | solution.py:760
  36.0 3.1 collective-permute-done.7.refs_20_.refs_19_
  39.9 16.0 %project.1 = (bf16[1024,1024]{1,0:T(8,128)(2,1)}, bf16[1024,1536]{1,0:T(8,128)(2,1)}, bf16[1024,1536]{1,0:T(8,128)(2,1)}, bf16[16,1024,128]{2,1,0:T(8,128)(2,1)}...) custom-call(s32[1]{0:T(128)} %bitcast.refs_0_, bf16[1024,1024]{1,0:T(8,128)(2,1)} %bitcast.33, ...), custom_call_target="tpu_custom_call" | custom-call | flops 8000000 | bytes 25000 | tf_op jit(solution)/shard_map/project/pallas_call | solution.py:203
  55.9 11.4 %attend.2 = (bf16[1024,512]{1,0:T(8,128)(2,1)}, bf16[8,1024,128]{2,1,0:T(8,128)(2,1)}) custom-call(bf16[16,1024,128]{2,1,0:T(8,128)(2,1)} %get-tuple-element.202.q_ref, bf16[8,1024,128]{2,1,0:T(8,128)(2,1)} %get-tuple-element.210.k_ref, bf16[8,1024,128]{2,1,0:T(8,128)(2,1)} %get-tuple-element.204.v_ref), custom_call_target="tpu_custom_call" | custom-call | flops 10000000 | bytes 8000 | tf_op jit(solution)/shard_map/attend/pallas_call | solution.py:262
  72.7 11.7 %attend.3 = (bf16[1024,512]{1,0:T(8,128)(2,1)}, bf16[8,1024,128]{2,1,0:T(8,128)(2,1)}) custom-call(bf16[16,1024,128]{2,1,0:T(8,128)(2,1)} %get-tuple-element.202.q_ref, bf16[8,1024,128]{2,1,0:T(8,128)(2,1)} %get-tuple-element.210.k_ref, bf16[8,1024,128]{2,1,0:T(8,128)(2,1)} %get-tuple-element.204.v_ref), custom_call_target="tpu_custom_call" | custom-call | flops 10000000 | bytes 8000 | tf_op jit(solution)/shard_map/attend/pallas_call | solution.py:262
  84.5 4.2 collective-permute-done.12.refs_11_.refs_10_.refs_15_
  94.0 2.4 collective-permute-done.17.refs_14_.refs_13_.refs_18_
  97.3 8.3 %output_rows.1 = (f32[1024,1024]{1,0:T(8,128)}, bf16[1024,1024]{1,0:T(8,128)(2,1)}, bf16[1024,1024]{1,0:T(8,128)(2,1)}) custom-call(s32[1]{0:T(128)} %bitcast.refs_0_, bf16[1024,512]{1,0:T(8,128)(2,1)} %get-tuple-element.211.refs_1_.refs_3_.o_ref, bf16[1024,512]{1,0:T(8,128)(2,1)} %get-tuple-element.216.refs_2_.refs_4_.o_ref, bf16[1024,1024]{1,0:T(8,128)(2,1)} %bitcast.34, ...), custom_call_target="tpu_custom_call" | custom-call | flops 5000000 | bytes 15000 | tf_op jit(solution)/shard_map/output_rows/pallas_call | solution.py:379
  105.6 40.5 %feed.3 = (bf16[1024,1024]{1,0:T(8,128)(2,1)}, bf16[1024,1024]{1,0:T(8,128)(2,1)}, bf16[4,576,1024]{2,1,0:T(8,128)(2,1)}, bf16[4,576,1024]{2,1,0:T(8,128)(2,1)}) custom-call(s32[1]{0:T(128)} %bitcast.refs_0_, bf16[1024,1024]{1,0:T(8,128)(2,1)} %get-tuple-element.251.refs_1_, bf16[1024,1024]{1,0:T(8,128)(2,1)} %get-tuple-element.225.refs_2_, ...), custom_call_target="tpu_custom_call" | custom-call | flops 37500000 | bytes 38000 | tf_op jit(solution)/shard_map/feed/pallas_call | solution.py:459
  146.9 2.4 collective-permute-done.22.refs_7_
  156.7 40.7 %feed.4 = (bf16[1024,1024]{1,0:T(8,128)(2,1)}, bf16[1024,1024]{1,0:T(8,128)(2,1)}, bf16[4,576,1024]{2,1,0:T(8,128)(2,1)}, bf16[4,576,1024]{2,1,0:T(8,128)(2,1)}) custom-call(s32[1]{0:T(128)} %bitcast.refs_0_, bf16[1024,1024]{1,0:T(8,128)(2,1)} %get-tuple-element.251.refs_1_, bf16[1024,1024]{1,0:T(8,128)(2,1)} %get-tuple-element.225.refs_2_, ...), custom_call_target="tpu_custom_call" | custom-call | flops 37500000 | bytes 38000 | tf_op jit(solution)/shard_map/feed/pallas_call | solution.py:459
  197.4 9.8 %collective-permute-done.29.refs_10_ = bf16[576,1024]{1,0:T(8,128)(2,1)} collective-permute-done((bf16[576,1024]{1,0:T(8,128)(2,1)S(1)}, bf16[576,1024]{1,0:T(8,128)(2,1)}, u32[]{:S(2)}, u32[]{:S(2)}) %collective-permute-start.29) | collective-permute-done | bytes 1179680 | tf_op jit(solution)/shard_map/ppermute | solution.py:760
  208.2 2.6 combine.15
  211.9 5.2 collective-permute-done.30.refs_1_.refs_6_.refs_9_
  217.1 2.6 combine.14
  221.6 40.7 %feed.5 = (bf16[1024,1024]{1,0:T(8,128)(2,1)}, bf16[1024,1024]{1,0:T(8,128)(2,1)}, bf16[4,576,1024]{2,1,0:T(8,128)(2,1)}, bf16[4,576,1024]{2,1,0:T(8,128)(2,1)}) custom-call(s32[1]{0:T(128)} %bitcast.refs_0_, bf16[1024,1024]{1,0:T(8,128)(2,1)} %get-tuple-element.251.refs_1_, bf16[1024,1024]{1,0:T(8,128)(2,1)} %get-tuple-element.225.refs_2_, ...), custom_call_target="tpu_custom_call" | custom-call | flops 37500000 | bytes 38000 | tf_op jit(solution)/shard_map/feed/pallas_call | solution.py:459
  263.8 6.9 %combine.16 = (bf16[576,1024]{1,0:T(8,128)(2,1)}, bf16[576,1024]{1,0:T(8,128)(2,1)}, bf16[576,1024]{1,0:T(8,128)(2,1)}, bf16[576,1024]{1,0:T(8,128)(2,1)}) custom-call(bf16[4,576,1024]{2,1,0:T(8,128)(2,1)} %get-tuple-element.260.refs_0_.refs_2_, bf16[4,576,1024]{2,1,0:T(8,128)(2,1)} %collective-permute-done.25.refs_1_.refs_3_, ...), custom_call_target="tpu_custom_call" | custom-call | bytes 4000 | tf_op jit(solution)/shard_map/combine/pallas_call | solution.py:797
  274.7 14.8 %middle.1 = (f32[1024,1024]{1,0:T(8,128)}, bf16[1024,1024]{1,0:T(8,128)(2,1)}, bf16[1024,1024]{1,0:T(8,128)(2,1)}) custom-call(s32[1]{0:T(128)} %bitcast.refs_0_, f32[1024,1024]{1,0:T(8,128)} %get-tuple-element.344.refs_1_, bf16[1024,1024]{1,0:T(8,128)(2,1)} %bitcast.32, bf16[1024,512]{1,0:T(8,128)(2,1)} %get-tuple-element.211.refs_1_.refs_3_.o_ref, ...), custom_call_target="tpu_custom_call" | custom-call | flops 9000000 | bytes 32000 | tf_op jit(solution)/shard_map/middle/pallas_call | solution.py:529
  289.5 2.6 combine.17
  292.1 19.8 %attend_back.2 = (f32[1024,512]{1,0:T(8,128)}, f32[1024,512]{1,0:T(8,128)}) custom-call(bf16[8,1024,128]{2,1,0:T(8,128)(2,1)} %get-tuple-element.209.q_ref, bf16[8,1024,128]{2,1,0:T(8,128)(2,1)} %get-tuple-element.210.k_ref, bf16[8,1024,128]{2,1,0:T(8,128)(2,1)} %get-tuple-element.204.v_ref, bf16[1024,512]{1,0:T(8,128)(2,1)} %get-tuple-element.211.refs_1_.refs_3_.o_ref, ...), custom_call_target="tpu_custom_call" | custom-call | flops 20000000 | bytes 12000 | tf_op jit(solution)/shard_map/attend_back/pallas_call | solution.py:334
  312.9 3.5 combine.18.refs_9_
  317.8 4.5 collective-permute-start.40
  322.3 19.9 %attend_back.3 = (f32[1024,512]{1,0:T(8,128)}, f32[1024,512]{1,0:T(8,128)}) custom-call(bf16[8,1024,128]{2,1,0:T(8,128)(2,1)} %get-tuple-element.284.q_ref, bf16[8,1024,128]{2,1,0:T(8,128)(2,1)} %get-tuple-element.210.k_ref, bf16[8,1024,128]{2,1,0:T(8,128)(2,1)} %get-tuple-element.204.v_ref, bf16[1024,512]{1,0:T(8,128)(2,1)} %get-tuple-element.216.refs_2_.refs_4_.o_ref, ...), custom_call_target="tpu_custom_call" | custom-call | flops 20000000 | bytes 12000 | tf_op jit(solution)/shard_map/attend_back/pallas_call | solution.py:334
  342.2 7.0 %collective-permute-done.39.refs_4_ = bf16[576,1024]{1,0:T(8,128)(2,1)S(1)} collective-permute-done((bf16[576,1024]{1,0:T(8,128)(2,1)}, bf16[576,1024]{1,0:T(8,128)(2,1)S(1)}, u32[]{:S(2)}, u32[]{:S(2)}) %collective-permute-start.39) | collective-permute-done | bytes 1179680 | tf_op jit(solution)/shard_map/ppermute | solution.py:760
  350.2 7.5 %combine.19 = (bf16[576,1024]{1,0:T(8,128)(2,1)}, bf16[576,1024]{1,0:T(8,128)(2,1)}, bf16[576,1024]{1,0:T(8,128)(2,1)}, bf16[576,1024]{1,0:T(8,128)(2,1)}) custom-call(bf16[4,576,1024]{2,1,0:T(8,128)(2,1)} %get-tuple-element.276.refs_0_.refs_2_.refs_4_, bf16[4,576,1024]{2,1,0:T(8,128)(2,1)} %collective-permute-done.36.refs_1_.refs_3_.refs_5_, ...), custom_call_target="tpu_custom_call" | custom-call | bytes 4000 | tf_op jit(solution)/shard_map/combine/pallas_call | solution.py:797
  360.1 3.5 collective-permute-start.45
  365.4 19.9 %raw_back.1 = (bf16[1024,2048]{1,0:T(8,128)(2,1)}, bf16[4,416,1024]{2,1,0:T(8,128)(2,1)}, bf16[4,416,1024]{2,1,0:T(8,128)(2,1)}) custom-call(s32[1]{0:T(128)} %bitcast.refs_0_, f32[1024,512]{1,0:T(8,128)} %get-tuple-element.283.refs_1_, f32[1024,512]{1,0:T(8,128)} %get-tuple-element.304.refs_2_, f32[1024,512]{1,0:T(8,128)} %get-tuple-element.305.refs_3_, ...), custom_call_target="tpu_custom_call" | custom-call | flops 10000000 | bytes 30000 | tf_op jit(solution)/shard_map/raw_back/pallas_call | solution.py:615
  388.7 5.5 %combine.20 = (bf16[576,1024]{1,0:T(8,128)(2,1)}, bf16[576,1024]{1,0:T(8,128)(2,1)}, bf16[576,1024]{1,0:T(8,128)(2,1)}) custom-call(bf16[576,1024]{1,0:T(8,128)(2,1)} %get-tuple-element.316.refs_0_, bf16[576,1024]{1,0:T(8,128)(2,1)} %copy-done.29, bf16[576,1024]{1,0:T(8,128)(2,1)} %get-tuple-element.317.refs_2_, ...), custom_call_target="tpu_custom_call" | custom-call | bytes 4000 | tf_op jit(solution)/shard_map/combine/pallas_call | solution.py:797
  397.1 7.2 %collective-permute-start.50 = (bf16[576,1024]{1,0:T(8,128)(2,1)}, bf16[576,1024]{1,0:T(8,128)(2,1)}, u32[]{:S(2)}, u32[]{:S(2)}) collective-permute-start(bf16[576,1024]{1,0:T(8,128)(2,1)} %get-tuple-element.337.refs_2_), channel_id=1, source_target_pairs={{0,8},{24,16},{1,9},{25,17},{2,10},{26,18},{3,11},{27,19},{4,12},{... | collective-permute-start | bytes 3538952 | tf_op jit(solution)/shard_map/ppermute | solution.py:811
  405.5 2.5 combine.21
  409.2 11.2 %input_back.1 = f32[1024,1024]{1,0:T(8,128)} custom-call(s32[1]{0:T(128)} %bitcast.refs_0_, bf16[1024,2048]{1,0:T(8,128)(2,1)} %get-tuple-element.330.refs_1_, bf16[1024,1024]{1,0:T(8,128)(2,1)} %bitcast.35, f32[1024,1024]{1,0:T(8,128)} %get-tuple-element.331.refs_3_, f32[16,1024]{1,0:T(8,128)} %get-tuple-element.217.refs_4_.refs_5_.refs_10_, ...), custom_call_target="tpu_custom_call" | custom-call | flops 6000000 | bytes 18000 | tf_op jit(solution)/shard_map/input_back/pallas_call | solution.py:645
  420.3 8.3 %collective-permute-done.48.refs_2_ = bf16[416,1024]{1,0:T(8,128)(2,1)S(1)} collective-permute-done((bf16[416,1024]{1,0:T(8,128)(2,1)}, bf16[416,1024]{1,0:T(8,128)(2,1)S(1)}, u32[]{:S(2)}, u32[]{:S(2)}) %collective-permute-start.48) | collective-permute-done | bytes 852000 | tf_op jit(solution)/shard_map/ppermute | solution.py:760
  429.6 3.2 combine.22
  434.6 3.5 combine.23
  441.1 6.4 %add_convert_fusion = bf16[1024,1024]{1,0:T(8,128)(2,1)} fusion(f32[1024,1024]{1,0:T(8,128)} %get-tuple-element.344.refs_1_, bf16[1024,1024]{1,0:T(8,128)(2,1)} %get-tuple-element.347, bf16[1024,1024]{1,0:T(8,128)(2,1)} %get-tuple-element.346, bf16[1024,1024]{1,0:T(8,128)(2,1)S(1)} %copy-done.19), kind=kLoop, calls=%fused_computation | loop fusion | flops 7340032 | bytes 12582912 | tf_op jit(solution)/shard_map/convert_element_type | solution.py:1097
  447.5 5.2 collective-permute-done.52.refs_2_
  453.6 2.9 combine.24.refs_0_
  456.5 5.0 collective-permute-start.54
  461.6 2.6 combine.25.refs_4_
  465.4 3.7 collective-permute-done.55.refs_3_
  469.1 8.7 %collective-permute-done.54.refs_1_ = bf16[416,1024]{1,0:T(8,128)(2,1)S(1)} collective-permute-done((bf16[416,1024]{1,0:T(8,128)(2,1)}, bf16[416,1024]{1,0:T(8,128)(2,1)S(1)}, u32[]{:S(2)}, u32[]{:S(2)}) %collective-permute-start.54) | collective-permute-done | bytes 852000 | tf_op jit(solution)/shard_map/ppermute | solution.py:811
  478.7 2.2 combine.26.refs_0_
  481.7 15.0 %collective-permute-done.57.refs_5_ = bf16[576,1024]{1,0:T(8,128)(2,1)S(1)} collective-permute-done((bf16[576,1024]{1,0:T(8,128)(2,1)}, bf16[576,1024]{1,0:T(8,128)(2,1)S(1)}, u32[]{:S(2)}, u32[]{:S(2)}) %collective-permute-start.57) | collective-permute-done | bytes 1179680 | tf_op jit(solution)/shard_map/ppermute | solution.py:811
  497.6 2.3 combine.27
  501.2 7.5 %unpack_rows.1 = (f32[128,4608]{1,0:T(8,128)}, f32[128,4608]{1,0:T(8,128)}, f32[576,1024]{1,0:T(8,128)}) custom-call(s32[1]{0:T(128)} %bitcast.8.flag_ref, bf16[576,1024]{1,0:T(8,128)(2,1)} %get-tuple-element.343.refs_0_, bf16[576,1024]{1,0:T(8,128)(2,1)} %collective-permute-done.51.refs_1_, bf16[576,1024]{1,0:T(8,128)(2,1)} %get-tuple-element.353.refs_2_, ...), custom_call_target="tpu_custom_call" | custom-call | bytes 14000 | tf_op jit(solution)/shard_map/unpack_rows/pallas_call | solution.py:737
  508.7 13.9 %collective-permute-done.59 = bf16[416,1024]{1,0:T(8,128)(2,1)S(1)} collective-permute-done((bf16[416,1024]{1,0:T(8,128)(2,1)}, bf16[416,1024]{1,0:T(8,128)(2,1)S(1)}, u32[]{:S(2)}, u32[]{:S(2)}) %collective-permute-start.59) | collective-permute-done | bytes 852000 | tf_op jit(solution)/shard_map/ppermute | solution.py:811
  (247 shorter events, 86.2 us)
Async XLA Ops:
  5.7 15.6 %collective-permute-start = (bf16[272,1024]{1,0:T(8,128)(2,1)S(1)}, bf16[272,1024]{1,0:T(8,128)(2,1)S(1)}, u32[]{:S(2)}, u32[]{:S(2)}) collective-permute-start(bf16[272,1024]{1,0:T(8,128)(2,1)S(1)} %concatenate.38.refs_6_.refs_7_.refs_22_.refs_5_), channel_id=1, source_target_pairs={{0,2},{1,3},{2,0},{3,1},{4,6},{5,7},{6,4},{7,5},{8,10},{9,11},{10,... | collective-permute-start | bytes 1671176 | tf_op jit(solution)/shard_map/ppermute | solution.py:760
  8.7 14.1 %collective-permute-start.1 = (bf16[272,1024]{1,0:T(8,128)(2,1)S(1)}, bf16[272,1024]{1,0:T(8,128)(2,1)S(1)}, u32[]{:S(2)}, u32[]{:S(2)}) collective-permute-start(bf16[272,1024]{1,0:T(8,128)(2,1)S(1)} %concatenate.38.refs_6_.refs_7_.refs_22_.refs_5_), channel_id=1, source_target_pairs={{0,4},{1,5},{2,6},{3,7},{4,0},{5,1},{6,2},{7,3},{8,12},{9,13},{10,... | collective-permute-start | bytes 1671176 | tf_op jit(solution)/shard_map/ppermute | solution.py:760
  10.2 12.6 %collective-permute-start.2 = (bf16[272,1024]{1,0:T(8,128)(2,1)S(1)}, bf16[272,1024]{1,0:T(8,128)(2,1)S(1)}, u32[]{:S(2)}, u32[]{:S(2)}) collective-permute-start(bf16[272,1024]{1,0:T(8,128)(2,1)S(1)} %concatenate.38.refs_6_.refs_7_.refs_22_.refs_5_), channel_id=1, source_target_pairs={{0,1},{1,0},{2,3},{3,2},{4,5},{5,4},{6,7},{7,6},{8,9},{9,8},{10,11... | collective-permute-start | bytes 1671176 | tf_op jit(solution)/shard_map/ppermute | solution.py:760
  22.8 10.3 %collective-permute-start.3 = (bf16[272,1024]{1,0:T(8,128)(2,1)S(1)}, bf16[272,1024]{1,0:T(8,128)(2,1)S(1)}, u32[]{:S(2)}, u32[]{:S(2)}) collective-permute-start(bf16[272,1024]{1,0:T(8,128)(2,1)S(1)} %collective-permute-done.refs_10_.refs_11_.refs_24_.refs_9_), channel_id=1, source_target_pairs={{0,1},{1,0},{2,3},{3,2},{4,5},{5,4},{6,7},{7,6},{8,9},{9,8},{10,11... | collective-permute-start | bytes 1671176 | tf_op jit(solution)/shard_map/ppermute | solution.py:760
  34.0 33.2 %collective-permute-start.9 = (bf16[704,1024]{1,0:T(8,128)(2,1)}, bf16[704,1024]{1,0:T(8,128)(2,1)S(1)}, u32[]{:S(2)}, u32[]{:S(2)}) collective-permute-start(bf16[704,1024]{1,0:T(8,128)(2,1)} %get-tuple-element.208.refs_5_.refs_4_.refs_9_), channel_id=1, source_target_pairs={{0,2},{1,3},{2,0},{3,1},{4,6},{5,7},{6,4},{7,5},{8,10},{9,11},{10,... | collective-permute-start | bytes 4325384 | tf_op jit(solution)/shard_map/ppermute | solution.py:760
  34.6 32.7 %collective-permute-start.10 = (bf16[704,1024]{1,0:T(8,128)(2,1)}, bf16[704,1024]{1,0:T(8,128)(2,1)S(1)}, u32[]{:S(2)}, u32[]{:S(2)}) collective-permute-start(bf16[704,1024]{1,0:T(8,128)(2,1)} %get-tuple-element.208.refs_5_.refs_4_.refs_9_), channel_id=1, source_target_pairs={{0,4},{1,5},{2,6},{3,7},{4,0},{5,1},{6,2},{7,3},{8,12},{9,13},{10,... | collective-permute-start | bytes 4325384 | tf_op jit(solution)/shard_map/ppermute | solution.py:760
  35.5 31.8 %collective-permute-start.11 = (bf16[704,1024]{1,0:T(8,128)(2,1)}, bf16[704,1024]{1,0:T(8,128)(2,1)}, u32[]{:S(2)}, u32[]{:S(2)}) collective-permute-start(bf16[704,1024]{1,0:T(8,128)(2,1)} %get-tuple-element.208.refs_5_.refs_4_.refs_9_), channel_id=1, source_target_pairs={{0,1},{1,0},{2,3},{3,2},{4,5},{5,4},{6,7},{7,6},{8,9},{9,8},{10,11... | collective-permute-start | bytes 4325384 | tf_op jit(solution)/shard_map/ppermute | solution.py:760
  67.3 22.7 %collective-permute-start.14 = (bf16[704,1024]{1,0:T(8,128)(2,1)S(1)}, bf16[704,1024]{1,0:T(8,128)(2,1)}, u32[]{:S(2)}, u32[]{:S(2)}) collective-permute-start(bf16[704,1024]{1,0:T(8,128)(2,1)S(1)} %collective-permute-done.9.refs_7_.refs_6_.refs_11_), channel_id=1, source_target_pairs={{0,1},{1,0},{2,3},{3,2},{4,5},{5,4},{6,7},{7,6},{8,9},{9,8},{10,11... | collective-permute-start | bytes 4325384 | tf_op jit(solution)/shard_map/ppermute | solution.py:760
  67.7 22.3 %collective-permute-start.15 = (bf16[704,1024]{1,0:T(8,128)(2,1)S(1)}, bf16[704,1024]{1,0:T(8,128)(2,1)}, u32[]{:S(2)}, u32[]{:S(2)}) collective-permute-start(bf16[704,1024]{1,0:T(8,128)(2,1)S(1)} %collective-permute-done.10.refs_9_.refs_8_.refs_13_), channel_id=1, source_target_pairs={{0,1},{1,0},{2,3},{3,2},{4,5},{5,4},{6,7},{7,6},{8,9},{9,8},{10,11... | collective-permute-start | bytes 4325384 | tf_op jit(solution)/shard_map/ppermute | solution.py:760
  70.1 18.6 %collective-permute-start.12 = (bf16[704,512]{1,0:T(8,128)(2,1)}, bf16[704,512]{1,0:T(8,128)(2,1)S(1)}, u32[]{:S(2)}, u32[]{:S(2)}) collective-permute-start(bf16[704,512]{1,0:T(8,128)(2,1)} %slice.65), channel_id=1, source_target_pairs={{0,2},{1,3},{2,0},{3,1},{4,6},{5,7},{6,4},{7,5},{8,10},{9,11},{10,... | collective-permute-start | bytes 2162696 | tf_op jit(solution)/shard_map/ppermute | solution.py:760
  71.6 18.4 %collective-permute-start.13 = (bf16[704,512]{1,0:T(8,128)(2,1)}, bf16[704,512]{1,0:T(8,128)(2,1)}, u32[]{:S(2)}, u32[]{:S(2)}) collective-permute-start(bf16[704,512]{1,0:T(8,128)(2,1)} %slice.66), channel_id=1, source_target_pairs={{0,4},{1,5},{2,6},{3,7},{4,0},{5,1},{6,2},{7,3},{8,12},{9,13},{10,... | collective-permute-start | bytes 2162696 | tf_op jit(solution)/shard_map/ppermute | solution.py:760
  90.0 56.1 %collective-permute-start.18 = (bf16[576,1024]{1,0:T(8,128)(2,1)}, bf16[576,1024]{1,0:T(8,128)(2,1)S(1)}, u32[]{:S(2)}, u32[]{:S(2)}) collective-permute-start(bf16[576,1024]{1,0:T(8,128)(2,1)} %get-tuple-element.231.refs_4_), channel_id=1, source_target_pairs={{0,1},{1,0},{2,3},{3,2},{4,5},{5,4},{6,7},{7,6},{8,9},{9,8},{10,11... | collective-permute-start | bytes 3538952 | tf_op jit(solution)/shard_map/ppermute | solution.py:760
  90.5 55.6 %collective-permute-start.19 = (bf16[576,1024]{1,0:T(8,128)(2,1)}, bf16[576,1024]{1,0:T(8,128)(2,1)}, u32[]{:S(2)}, u32[]{:S(2)}) collective-permute-start(bf16[576,1024]{1,0:T(8,128)(2,1)} %get-tuple-element.231.refs_4_), channel_id=1, source_target_pairs={{0,2},{1,3},{2,0},{3,1},{4,6},{5,7},{6,4},{7,5},{8,10},{9,11},{10,... | collective-permute-start | bytes 3538952 | tf_op jit(solution)/shard_map/ppermute | solution.py:760
  91.1 55.1 %collective-permute-start.20 = (bf16[576,1024]{1,0:T(8,128)(2,1)}, bf16[576,1024]{1,0:T(8,128)(2,1)}, u32[]{:S(2)}, u32[]{:S(2)}) collective-permute-start(bf16[576,1024]{1,0:T(8,128)(2,1)} %get-tuple-element.231.refs_4_), channel_id=1, source_target_pairs={{0,4},{1,5},{2,6},{3,7},{4,0},{5,1},{6,2},{7,3},{8,12},{9,13},{10,... | collective-permute-start | bytes 3538952 | tf_op jit(solution)/shard_map/ppermute | solution.py:760
  92.2 54.0 %collective-permute-start.21 = (bf16[576,1024]{1,0:T(8,128)(2,1)}, bf16[576,1024]{1,0:T(8,128)(2,1)}, u32[]{:S(2)}, u32[]{:S(2)}) collective-permute-start(bf16[576,1024]{1,0:T(8,128)(2,1)} %get-tuple-element.231.refs_4_), channel_id=1, source_target_pairs={{0,6},{1,7},{2,4},{3,5},{4,2},{5,3},{6,0},{7,1},{8,14},{9,15},{10,... | collective-permute-start | bytes 3538952 | tf_op jit(solution)/shard_map/ppermute | solution.py:760
  152.7 54.5 %collective-permute-start.25 = (bf16[4,576,1024]{2,1,0:T(8,128)(2,1)}, bf16[4,576,1024]{2,1,0:T(8,128)(2,1)}, u32[]{:S(2)}, u32[]{:S(2)}) collective-permute-start(bf16[4,576,1024]{2,1,0:T(8,128)(2,1)} %get-tuple-element.243), channel_id=1, source_target_pairs={{0,1},{1,0},{2,3},{3,2},{4,5},{5,4},{6,7},{7,6},{8,9},{9,8},{10,11... | collective-permute-start | bytes 14155784 | tf_op jit(solution)/shard_map/ppermute | solution.py:760
  152.8 44.6 %collective-permute-start.26 = (bf16[576,1024]{1,0:T(8,128)(2,1)S(1)}, bf16[576,1024]{1,0:T(8,128)(2,1)S(1)}, u32[]{:S(2)}, u32[]{:S(2)}) collective-permute-start(bf16[576,1024]{1,0:T(8,128)(2,1)S(1)} %copy-done.20), channel_id=1, source_target_pairs={{0,1},{1,0},{2,3},{3,2},{4,5},{5,4},{6,7},{7,6},{8,9},{9,8},{10,11... | collective-permute-start | bytes 3538952 | tf_op jit(solution)/shard_map/ppermute | solution.py:760
  153.2 44.2 %collective-permute-start.27 = (bf16[576,1024]{1,0:T(8,128)(2,1)S(1)}, bf16[576,1024]{1,0:T(8,128)(2,1)}, u32[]{:S(2)}, u32[]{:S(2)}) collective-permute-start(bf16[576,1024]{1,0:T(8,128)(2,1)S(1)} %copy-done.20), channel_id=1, source_target_pairs={{0,2},{1,3},{2,0},{3,1},{4,6},{5,7},{6,4},{7,5},{8,10},{9,11},{10,... | collective-permute-start | bytes 3538952 | tf_op jit(solution)/shard_map/ppermute | solution.py:760
  153.7 43.7 %collective-permute-start.28 = (bf16[576,1024]{1,0:T(8,128)(2,1)S(1)}, bf16[576,1024]{1,0:T(8,128)(2,1)}, u32[]{:S(2)}, u32[]{:S(2)}) collective-permute-start(bf16[576,1024]{1,0:T(8,128)(2,1)S(1)} %copy-done.20), channel_id=1, source_target_pairs={{0,4},{1,5},{2,6},{3,7},{4,0},{5,1},{6,2},{7,3},{8,12},{9,13},{10,... | collective-permute-start | bytes 3538952 | tf_op jit(solution)/shard_map/ppermute | solution.py:760
  154.9 52.3 %collective-permute-start.29 = (bf16[576,1024]{1,0:T(8,128)(2,1)S(1)}, bf16[576,1024]{1,0:T(8,128)(2,1)}, u32[]{:S(2)}, u32[]{:S(2)}) collective-permute-start(bf16[576,1024]{1,0:T(8,128)(2,1)S(1)} %copy-done.20), channel_id=1, source_target_pairs={{0,6},{1,7},{2,4},{3,5},{4,2},{5,3},{6,0},{7,1},{8,14},{9,15},{10,... | collective-permute-start | bytes 3538952 | tf_op jit(solution)/shard_map/ppermute | solution.py:760
  207.2 13.4 %collective-permute-start.31 = (bf16[576,1024]{1,0:T(8,128)(2,1)}, bf16[576,1024]{1,0:T(8,128)(2,1)S(1)}, u32[]{:S(2)}, u32[]{:S(2)}) collective-permute-start(bf16[576,1024]{1,0:T(8,128)(2,1)} %collective-permute-done.27.refs_6_), channel_id=1, source_target_pairs={{0,1},{1,0},{2,3},{3,2},{4,5},{5,4},{6,7},{7,6},{8,9},{9,8},{10,11... | collective-permute-start | bytes 3538952 | tf_op jit(solution)/shard_map/ppermute | solution.py:760
  207.7 12.9 %collective-permute-start.32 = (bf16[576,1024]{1,0:T(8,128)(2,1)}, bf16[576,1024]{1,0:T(8,128)(2,1)}, u32[]{:S(2)}, u32[]{:S(2)}) collective-permute-start(bf16[576,1024]{1,0:T(8,128)(2,1)} %collective-permute-done.28.refs_8_), channel_id=1, source_target_pairs={{0,1},{1,0},{2,3},{3,2},{4,5},{5,4},{6,7},{7,6},{8,9},{9,8},{10,11... | collective-permute-start | bytes 3538952 | tf_op jit(solution)/shard_map/ppermute | solution.py:760
  207.7 12.9 %collective-permute-start.33 = (bf16[576,1024]{1,0:T(8,128)(2,1)}, bf16[576,1024]{1,0:T(8,128)(2,1)}, u32[]{:S(2)}, u32[]{:S(2)}) collective-permute-start(bf16[576,1024]{1,0:T(8,128)(2,1)} %collective-permute-done.29.refs_10_), channel_id=1, source_target_pairs={{0,1},{1,0},{2,3},{3,2},{4,5},{5,4},{6,7},{7,6},{8,9},{9,8},{10,11... | collective-permute-start | bytes 3538952 | tf_op jit(solution)/shard_map/ppermute | solution.py:760
  210.8 51.5 %collective-permute-start.34 = (bf16[576,1024]{1,0:T(8,128)(2,1)}, bf16[576,1024]{1,0:T(8,128)(2,1)S(1)}, u32[]{:S(2)}, u32[]{:S(2)}) collective-permute-start(bf16[576,1024]{1,0:T(8,128)(2,1)} %combine.15), channel_id=1, source_target_pairs={{0,2},{1,3},{2,0},{3,1},{4,6},{5,7},{6,4},{7,5},{8,10},{9,11},{10,... | collective-permute-start | bytes 3538952 | tf_op jit(solution)/shard_map/ppermute | solution.py:760
  219.7 42.6 %collective-permute-start.35 = (bf16[576,1024]{1,0:T(8,128)(2,1)}, bf16[576,1024]{1,0:T(8,128)(2,1)S(1)}, u32[]{:S(2)}, u32[]{:S(2)}) collective-permute-start(bf16[576,1024]{1,0:T(8,128)(2,1)} %combine.14), channel_id=1, source_target_pairs={{0,4},{1,5},{2,6},{3,7},{4,0},{5,1},{6,2},{7,3},{8,12},{9,13},{10,... | collective-permute-start | bytes 3538952 | tf_op jit(solution)/shard_map/ppermute | solution.py:760
  262.3 27.2 %collective-permute-start.36 = (bf16[4,576,1024]{2,1,0:T(8,128)(2,1)}, bf16[4,576,1024]{2,1,0:T(8,128)(2,1)}, u32[]{:S(2)}, u32[]{:S(2)}) collective-permute-start(bf16[4,576,1024]{2,1,0:T(8,128)(2,1)} %get-tuple-element.274), channel_id=1, source_target_pairs={{0,1},{1,0},{2,3},{3,2},{4,5},{5,4},{6,7},{7,6},{8,9},{9,8},{10,11... | collective-permute-start | bytes 14155784 | tf_op jit(solution)/shard_map/ppermute | solution.py:760
  270.6 41.2 %collective-permute-start.37 = (bf16[576,1024]{1,0:T(8,128)(2,1)}, bf16[576,1024]{1,0:T(8,128)(2,1)S(1)}, u32[]{:S(2)}, u32[]{:S(2)}) collective-permute-start(bf16[576,1024]{1,0:T(8,128)(2,1)} %get-tuple-element.281), channel_id=1, source_target_pairs={{0,2},{1,3},{2,0},{3,1},{4,6},{5,7},{6,4},{7,5},{8,10},{9,11},{10,... | collective-permute-start | bytes 3538952 | tf_op jit(solution)/shard_map/ppermute | solution.py:760
  272.2 39.7 %collective-permute-start.38 = (bf16[576,1024]{1,0:T(8,128)(2,1)}, bf16[576,1024]{1,0:T(8,128)(2,1)}, u32[]{:S(2)}, u32[]{:S(2)}) collective-permute-start(bf16[576,1024]{1,0:T(8,128)(2,1)} %get-tuple-element.282), channel_id=1, source_target_pairs={{0,4},{1,5},{2,6},{3,7},{4,0},{5,1},{6,2},{7,3},{8,12},{9,13},{10,... | collective-permute-start | bytes 3538952 | tf_op jit(solution)/shard_map/ppermute | solution.py:760
  273.0 69.1 %collective-permute-start.41 = (bf16[576,1024]{1,0:T(8,128)(2,1)}, bf16[576,1024]{1,0:T(8,128)(2,1)S(1)}, u32[]{:S(2)}, u32[]{:S(2)}) collective-permute-start(bf16[576,1024]{1,0:T(8,128)(2,1)} %get-tuple-element.293), channel_id=1, source_target_pairs={{0,2},{1,3},{2,0},{3,1},{4,6},{5,7},{6,4},{7,5},{8,10},{9,11},{10,... | collective-permute-start | bytes 3538952 | tf_op jit(solution)/shard_map/ppermute | solution.py:760
  273.9 68.3 %collective-permute-start.42 = (bf16[576,1024]{1,0:T(8,128)(2,1)}, bf16[576,1024]{1,0:T(8,128)(2,1)S(1)}, u32[]{:S(2)}, u32[]{:S(2)}) collective-permute-start(bf16[576,1024]{1,0:T(8,128)(2,1)} %get-tuple-element.294), channel_id=1, source_target_pairs={{0,4},{1,5},{2,6},{3,7},{4,0},{5,1},{6,2},{7,3},{8,12},{9,13},{10,... | collective-permute-start | bytes 3538952 | tf_op jit(solution)/shard_map/ppermute | solution.py:760
  316.3 32.9 %collective-permute-start.39 = (bf16[576,1024]{1,0:T(8,128)(2,1)}, bf16[576,1024]{1,0:T(8,128)(2,1)S(1)}, u32[]{:S(2)}, u32[]{:S(2)}) collective-permute-start(bf16[576,1024]{1,0:T(8,128)(2,1)} %combine.17), channel_id=1, source_target_pairs={{0,2},{1,3},{2,0},{3,1},{4,6},{5,7},{6,4},{7,5},{8,10},{9,11},{10,... | collective-permute-start | bytes 3538952 | tf_op jit(solution)/shard_map/ppermute | solution.py:760
  317.8 31.4 %collective-permute-start.40 = (bf16[576,1024]{1,0:T(8,128)(2,1)}, bf16[576,1024]{1,0:T(8,128)(2,1)}, u32[]{:S(2)}, u32[]{:S(2)}) collective-permute-start(bf16[576,1024]{1,0:T(8,128)(2,1)} %combine.18.refs_9_), channel_id=1, source_target_pairs={{0,8},{24,16},{1,9},{25,17},{2,10},{26,18},{3,11},{27,19},{4,12},{... | collective-permute-start | bytes 3538952 | tf_op jit(solution)/shard_map/ppermute | solution.py:811
  357.7 27.6 %collective-permute-start.43 = (bf16[576,1024]{1,0:T(8,128)(2,1)}, bf16[576,1024]{1,0:T(8,128)(2,1)S(1)}, u32[]{:S(2)}, u32[]{:S(2)}) collective-permute-start(bf16[576,1024]{1,0:T(8,128)(2,1)} %get-tuple-element.314), channel_id=1, source_target_pairs={{0,2},{1,3},{2,0},{3,1},{4,6},{5,7},{6,4},{7,5},{8,10},{9,11},{10,... | collective-permute-start | bytes 3538952 | tf_op jit(solution)/shard_map/ppermute | solution.py:760
  359.2 26.8 %collective-permute-start.44 = (bf16[576,1024]{1,0:T(8,128)(2,1)}, bf16[576,1024]{1,0:T(8,128)(2,1)S(1)}, u32[]{:S(2)}, u32[]{:S(2)}) collective-permute-start(bf16[576,1024]{1,0:T(8,128)(2,1)} %get-tuple-element.315), channel_id=1, source_target_pairs={{0,4},{1,5},{2,6},{3,7},{4,0},{5,1},{6,2},{7,3},{8,12},{9,13},{10,... | collective-permute-start | bytes 3538952 | tf_op jit(solution)/shard_map/ppermute | solution.py:760
  360.1 27.6 %collective-permute-start.45 = (bf16[576,1024]{1,0:T(8,128)(2,1)}, bf16[576,1024]{1,0:T(8,128)(2,1)S(1)}, u32[]{:S(2)}, u32[]{:S(2)}) collective-permute-start(bf16[576,1024]{1,0:T(8,128)(2,1)} %get-tuple-element.316.refs_0_), channel_id=1, source_target_pairs={{0,8},{24,16},{1,9},{25,17},{2,10},{26,18},{3,11},{27,19},{4,12},{... | collective-permute-start | bytes 3538952 | tf_op jit(solution)/shard_map/ppermute | solution.py:811
  363.6 24.1 %collective-permute-start.46 = (bf16[576,1024]{1,0:T(8,128)(2,1)}, bf16[576,1024]{1,0:T(8,128)(2,1)}, u32[]{:S(2)}, u32[]{:S(2)}) collective-permute-start(bf16[576,1024]{1,0:T(8,128)(2,1)} %get-tuple-element.317.refs_2_), channel_id=1, source_target_pairs={{8,16},{16,8},{9,17},{17,9},{10,18},{18,10},{11,19},{19,11},{12,20... | collective-permute-start | bytes 3538952 | tf_op jit(solution)/shard_map/ppermute | solution.py:811
  395.0 37.8 %collective-permute-start.49 = (bf16[576,1024]{1,0:T(8,128)(2,1)}, bf16[576,1024]{1,0:T(8,128)(2,1)}, u32[]{:S(2)}, u32[]{:S(2)}) collective-permute-start(bf16[576,1024]{1,0:T(8,128)(2,1)} %get-tuple-element.336.refs_0_), channel_id=1, source_target_pairs={{8,16},{16,8},{9,17},{17,9},{10,18},{18,10},{11,19},{19,11},{12,20... | collective-permute-start | bytes 3538952 | tf_op jit(solution)/shard_map/ppermute | solution.py:811
  397.1 35.7 %collective-permute-start.50 = (bf16[576,1024]{1,0:T(8,128)(2,1)}, bf16[576,1024]{1,0:T(8,128)(2,1)}, u32[]{:S(2)}, u32[]{:S(2)}) collective-permute-start(bf16[576,1024]{1,0:T(8,128)(2,1)} %get-tuple-element.337.refs_2_), channel_id=1, source_target_pairs={{0,8},{24,16},{1,9},{25,17},{2,10},{26,18},{3,11},{27,19},{4,12},{... | collective-permute-start | bytes 3538952 | tf_op jit(solution)/shard_map/ppermute | solution.py:811
  404.2 33.9 %collective-permute-start.51 = (bf16[576,1024]{1,0:T(8,128)(2,1)}, bf16[576,1024]{1,0:T(8,128)(2,1)}, u32[]{:S(2)}, u32[]{:S(2)}) collective-permute-start(bf16[576,1024]{1,0:T(8,128)(2,1)} %get-tuple-element.343.refs_0_), channel_id=1, source_target_pairs={{8,0},{16,24},{9,1},{17,25},{10,2},{18,26},{11,3},{19,27},{12,4},{... | collective-permute-start | bytes 3538952 | tf_op jit(solution)/shard_map/ppermute | solution.py:811
  408.0 20.6 %collective-permute-start.48 = (bf16[416,1024]{1,0:T(8,128)(2,1)}, bf16[416,1024]{1,0:T(8,128)(2,1)S(1)}, u32[]{:S(2)}, u32[]{:S(2)}) collective-permute-start(bf16[416,1024]{1,0:T(8,128)(2,1)} %combine.21), channel_id=1, source_target_pairs={{0,4},{1,5},{2,6},{3,7},{4,0},{5,1},{6,2},{7,3},{8,12},{9,13},{10,... | collective-permute-start | bytes 2555912 | tf_op jit(solution)/shard_map/ppermute | solution.py:760
  432.8 19.9 %collective-permute-start.52 = (bf16[416,1024]{1,0:T(8,128)(2,1)}, bf16[416,1024]{1,0:T(8,128)(2,1)S(1)}, u32[]{:S(2)}, u32[]{:S(2)}) collective-permute-start(bf16[416,1024]{1,0:T(8,128)(2,1)} %get-tuple-element.348), channel_id=1, source_target_pairs={{0,2},{1,3},{2,0},{3,1},{4,6},{5,7},{6,4},{7,5},{8,10},{9,11},{10,... | collective-permute-start | bytes 2555912 | tf_op jit(solution)/shard_map/ppermute | solution.py:760
  433.7 19.7 %collective-permute-start.53 = (bf16[416,1024]{1,0:T(8,128)(2,1)}, bf16[416,1024]{1,0:T(8,128)(2,1)}, u32[]{:S(2)}, u32[]{:S(2)}) collective-permute-start(bf16[416,1024]{1,0:T(8,128)(2,1)} %get-tuple-element.349), channel_id=1, source_target_pairs={{0,4},{1,5},{2,6},{3,7},{4,0},{5,1},{6,2},{7,3},{8,12},{9,13},{10,... | collective-permute-start | bytes 2555912 | tf_op jit(solution)/shard_map/ppermute | solution.py:760
  438.1 23.4 %collective-permute-start.56 = (bf16[576,1024]{1,0:T(8,128)(2,1)}, bf16[576,1024]{1,0:T(8,128)(2,1)}, u32[]{:S(2)}, u32[]{:S(2)}) collective-permute-start(bf16[576,1024]{1,0:T(8,128)(2,1)} %get-tuple-element.356.refs_0_), channel_id=1, source_target_pairs={{8,16},{16,8},{9,17},{17,9},{10,18},{18,10},{11,19},{19,11},{12,20... | collective-permute-start | bytes 3538952 | tf_op jit(solution)/shard_map/ppermute | solution.py:811
  439.8 29.3 %collective-permute-start.55 = (bf16[576,1024]{1,0:T(8,128)(2,1)}, bf16[576,1024]{1,0:T(8,128)(2,1)S(1)}, u32[]{:S(2)}, u32[]{:S(2)}) collective-permute-start(bf16[576,1024]{1,0:T(8,128)(2,1)} %get-tuple-element.353.refs_2_), channel_id=1, source_target_pairs={{8,0},{16,24},{9,1},{17,25},{10,2},{18,26},{11,3},{19,27},{12,4},{... | collective-permute-start | bytes 3538952 | tf_op jit(solution)/shard_map/ppermute | solution.py:811
  456.5 21.3 %collective-permute-start.54 = (bf16[416,1024]{1,0:T(8,128)(2,1)}, bf16[416,1024]{1,0:T(8,128)(2,1)S(1)}, u32[]{:S(2)}, u32[]{:S(2)}) collective-permute-start(bf16[416,1024]{1,0:T(8,128)(2,1)} %combine.24.refs_0_), channel_id=1, source_target_pairs={{0,8},{24,16},{1,9},{25,17},{2,10},{26,18},{3,11},{27,19},{4,12},{... | collective-permute-start | bytes 2555912 | tf_op jit(solution)/shard_map/ppermute | solution.py:811
  464.1 32.6 %collective-permute-start.57 = (bf16[576,1024]{1,0:T(8,128)(2,1)}, bf16[576,1024]{1,0:T(8,128)(2,1)S(1)}, u32[]{:S(2)}, u32[]{:S(2)}) collective-permute-start(bf16[576,1024]{1,0:T(8,128)(2,1)} %combine.25.refs_4_), channel_id=1, source_target_pairs={{8,0},{16,24},{9,1},{17,25},{10,2},{18,26},{11,3},{19,27},{12,4},{... | collective-permute-start | bytes 3538952 | tf_op jit(solution)/shard_map/ppermute | solution.py:811
  481.0 15.8 %collective-permute-start.58 = (bf16[416,1024]{1,0:T(8,128)(2,1)}, bf16[416,1024]{1,0:T(8,128)(2,1)S(1)}, u32[]{:S(2)}, u32[]{:S(2)}) collective-permute-start(bf16[416,1024]{1,0:T(8,128)(2,1)} %combine.26.refs_0_), channel_id=1, source_target_pairs={{8,16},{16,8},{9,17},{17,9},{10,18},{18,10},{11,19},{19,11},{12,20... | collective-permute-start | bytes 2555912 | tf_op jit(solution)/shard_map/ppermute | solution.py:811
  499.9 22.7 %collective-permute-start.59 = (bf16[416,1024]{1,0:T(8,128)(2,1)}, bf16[416,1024]{1,0:T(8,128)(2,1)S(1)}, u32[]{:S(2)}, u32[]{:S(2)}) collective-permute-start(bf16[416,1024]{1,0:T(8,128)(2,1)} %combine.27), channel_id=1, source_target_pairs={{8,0},{16,24},{9,1},{17,25},{10,2},{18,26},{11,3},{19,27},{12,4},{... | collective-permute-start | bytes 2555912 | tf_op jit(solution)/shard_map/ppermute | solution.py:811
  (62 other events, 391.1 us)

commit v8 on v6

--- a/solution.py
+++ b/solution.py
@@ -1019,20 +1019,20 @@
         [*feed_step(later, 0, chunks[1], True), normed_two], other_0, *waiting
     )
     last = finish(packs[2], *waiting)
-    moved_0 = hop(combine([(own_0, 3), (other_0, 3)]), 2)
+    terms = combine(*[[(own_0, k), (other_0, k)] for k in (1, 2, 3)])
     other_1 = hop(after(sib_1, *last.arrays), 1)
-    (out_2, back_2, own_2, sib_2), (moved_0, other_1) = fence(
-        feed_step(last, 0, chunks[2], True), moved_0, other_1
+    normed_two, *terms = tie(normed_two, *terms)
+    steps = [hop(term, 2 * k) for k, term in zip((1, 2, 3), terms)]
+    (out_2, back_2, own_2, sib_2), (other_1, *steps) = fence(
+        feed(last, place, 0, chunks[2], normed_two, normed_two_t, back_out, True), other_1, *steps
     )
     other_2 = hop(sib_2, 1)
-    term, one, two = combine(
-        [(own_1, 3), (other_1, 3)],
-        [(own_0, 1), (other_0, 1)],
-        [(own_0, 2), (other_0, 2), moved_0],
-    )
-    back_2, term, one, two = tie(back_2, term, one, two)
+    grads_0, term = combine(
+        [(own_0, 0), (other_0, 0), *steps], [(own_1, 3), (other_1, 3)]
+    )
+    back_2, grads_0, term = tie(back_2, grads_0, term)
     moved_1 = hop(term, 4)
-    first_0, second_0 = hop(one, 2), hop(two, 4)
+    inward_0 = rep_hop(grads_0, INWARD)
     middles = middle(
         early, place, first_sum, back_out, attended, gains, [back_0, back_1, back_2]
     )
@@ -1041,47 +1041,45 @@
     back_attended, term = tie(back_attended, term)
     moved_2 = hop(term, 2)
     halves = attend_back(q_back_0, k_aug, v_aug, attended_0, back_attended, 0, 4)
-    (dq_0, dkv_0, back_attended), (first_0, second_0, moved_1) = fence(
-        [*halves, back_attended], first_0, second_0, moved_1
-    )
-    grads_0, three, four = combine(
-        [(own_0, 0), (other_0, 0), first_0, second_0],
+    (dq_0, dkv_0, back_attended), (moved_1, moved_2, inward_0) = fence(
+        [*halves, back_attended], moved_1, moved_2, inward_0
+    )
+    one, two, three, four, half_0 = combine(
         [(own_1, 1), (other_1, 1), moved_1],
         [(own_1, 2), (other_1, 2)],
-    )
-    back_attended, grads_0, three, four = tie(back_attended, grads_0, three, four)
-    first_1, second_1 = hop(three, 2), hop(four, 4)
-    inward_0 = rep_hop(grads_0, INWARD)
-    halves = attend_back(q_back_1, k_aug, v_aug, attended_1, back_attended, 4, 4)
-    (dq_1, dkv_1), (moved_2, inward_0, first_1, second_1) = fence(
-        halves, moved_2, inward_0, first_1, second_1
-    )
-    one, two, grads_1, half_0 = combine(
         [(own_2, 1), (other_2, 1)],
         [(own_2, 2), (other_2, 2), moved_2],
-        [(own_1, 0), (other_1, 0), first_1, second_1],
         [grads_0, inward_0],
     )
-    dq_1, one, two, grads_1, half_0 = tie(dq_1, one, two, grads_1, half_0)
-    first_2, second_2 = hop(one, 2), hop(two, 4)
+    back_attended, one, two, three, four, half_0 = tie(
+        back_attended, one, two, three, four, half_0
+    )
+    first_1, second_1 = hop(one, 2), hop(two, 4)
+    first_2, second_2 = hop(three, 2), hop(four, 4)
+    across_0 = rep_hop(half_0, ACROSS)
+    halves = attend_back(q_back_1, k_aug, v_aug, attended_1, back_attended, 4, 4)
+    (dq_1, dkv_1), (first_1, second_1, across_0) = fence(halves, first_1, second_1, across_0)
+    grads_1, total_0 = combine(
+        [(own_1, 0), (other_1, 0), first_1, second_1], [half_0, across_0]
+    )
+    dq_1, grads_1, total_0 = tie(dq_1, grads_1, total_0)
     inward_1 = rep_hop(grads_1, INWARD)
-    across_0 = rep_hop(half_0, ACROSS)
+    outward_0 = rep_hop(total_0, OUTWARD)
     result = raw_back(
         8, place, (dq_0, dq_1, dkv_0, dkv_1), units, normed_one, tables[0], tables[1], gains,
         grad_out,
     )
-    (back_raw, own, sib), (first_2, second_2, inward_1, across_0) = fence(
-        result, first_2, second_2, inward_1, across_0
+    (back_raw, own, sib), (first_2, second_2, inward_1, outward_0) = fence(
+        result, first_2, second_2, inward_1, outward_0
     )
     other = hop(sib, 1)
-    half_1, total_0, grads_2 = combine(
-        [grads_1, inward_1], [half_0, across_0], [(own_2, 0), (other_2, 0), first_2, second_2]
-    )
-    back_raw, other, half_1, total_0, grads_2 = tie(back_raw, other, half_1, total_0, grads_2)
+    half_1, grads_2 = combine(
+        [grads_1, inward_1], [(own_2, 0), (other_2, 0), first_2, second_2]
+    )
+    back_raw, other, half_1, grads_2 = tie(back_raw, other, half_1, grads_2)
     term = combine([(own, 3), (other, 3)])
-    back_raw, total_0, half_1, grads_2, term = tie(back_raw, total_0, half_1, grads_2, term)
+    back_raw, term = tie(back_raw, term)
     moved = hop(term, 4)
-    outward_0 = rep_hop(total_0, OUTWARD)
     across_1 = rep_hop(half_1, ACROSS)
     inward_2 = rep_hop(grads_2, INWARD)
     input_grad = input_back(pairs, place, back_raw, x, back_first, gains)
@@ -1090,7 +1088,7 @@
     one, two, across_1, inward_2, first_sum = tie(one, two, across_1, inward_2, first_sum)
     first, second = hop(one, 2), hop(two, 4)
     total_1, half_2 = combine([half_1, across_1], [grads_2, inward_2])
-    first_sum, total_1, half_2, outward_0 = tie(first_sum, total_1, half_2, outward_0)
+    first_sum, total_1, half_2 = tie(first_sum, total_1, half_2)
     outward_1 = rep_hop(total_1, OUTWARD)
     across_2 = rep_hop(half_2, ACROSS)
     outs = out_0.astype(F32) + out_1.astype(F32) + out_2.astype(F32)
@@ -1104,6 +1102,7 @@
     inward, outward_1, _ = tie(inward, outward_1, total_2)
     half = combine([grads, inward])
     across = rep_hop(half, ACROSS)
+    outward_2, across, _ = tie(outward_2, across, half)
     total = combine([half, across])
     outward = rep_hop(total, OUTWARD)
     total, outward_2 = tie(total, outward_2)

time: 575 us -> 546 us (0.950)
  waiting for transfers between devices: 145 us -> 127 us
  starting transfers between devices: 63.7 us -> 57.1 us
    ppermute x48, waiting for transfers between devices: 97.3 us -> 79.7 us  [hop(): return lax.ppermute(array, 'shard', [(i, i ^ bit) for i in range(8)])]
    ppermute x12, starting transfers between devices: 29.7 us -> 23.2 us  [rep_hop(): return lax.ppermute(array.astype(BF16), 'rep', pairs)]
    unnamed x108 -> x106, local copies, waits for them, and re-layouts: 16.7 us -> 12.1 us
  transfers between devices with their start and end apart: 60 -> 60, of which waited for: 27 -> 28; matrix products, arithmetic and copies ran while one was open for 3% -> 3% of each run, Pallas kernels for 52% -> 57%
where the time goes in v8:
time: 546 us; the launch traced here: 537 us
  Pallas kernels  315 us (58%)
  waiting for transfers between devices  127 us (23%)
  starting transfers between devices  57.1 us (10%)
  local copies, waits for them, and re-layouts  18.6 us (3%)
  other arithmetic  17.2 us (3%)
    pallas_call x3, Pallas kernels, feed(): pl.pallas_call(lambda *refs: feed_kernel(pieces.layout, paired, *refs), g...  122 us
    ppermute x48, waiting for transfers between devices, hop(): return lax.ppermute(array, 'shard', [(i, i ^ bit) for i in range(8)])  79.7 us
    pallas_call x13, Pallas kernels, combine(): pl.pallas_call(kernel, grid=(rows // step,), in_specs=[spec(k) for _, k i...  48.2 us
    ppermute x12, waiting for transfers between devices, rep_hop(): return lax.ppermute(array.astype(BF16), 'rep', pairs)  47.5 us
    pallas_call x2, Pallas kernels, attend_back(): pl.pallas_call(attend_back_kernel, grid=(groups,), in_specs=[pl.BlockSpec...  39.6 us
    ppermute x48, starting transfers between devices, hop(): return lax.ppermute(array, 'shard', [(i, i ^ bit) for i in range(8)])  34 us
    ppermute x12, starting transfers between devices, rep_hop(): return lax.ppermute(array.astype(BF16), 'rep', pairs)  23.2 us
    pallas_call x2, Pallas kernels, attend(): pl.pallas_call(attend_kernel, grid=(groups,), in_specs=[pl.BlockSpec((2,...  23.1 us
  transfers between devices with their start and end apart: 60, of which 28 were waited for; matrix products, arithmetic and copies ran while one was open for 3% of the time, Pallas kernels for 57%

profile of v8, /device:TPU:0, one launch (start us, length us, event | category | flops | bytes accessed | tf_op | source)
XLA Modules:
  0.0 536.6 jit_solution(3996586115920098541)
XLA Ops:
  5.7 3.0 collective-permute-start
  15.0 4.4 pack_rows.1
  25.6 7.5 %collective-permute-done.5.refs_18_.refs_17_ = bf16[128,1024]{1,0:T(8,128)(2,1)S(1)} collective-permute-done((bf16[128,1024]{1,0:T(8,128)(2,1)S(1)}, bf16[128,1024]{1,0:T(8,128)(2,1)S(1)}, u32[]{:S(2)}, u32[]{:S(2)}) %collective-permute-start.5) | collective-permute-done | bytes 262176 | tf_op jit(solution)/shard_map/ppermute | solution.py:760
  36.0 3.1 collective-permute-done.7.refs_20_.refs_19_
  39.9 16.0 %project.1 = (bf16[1024,1024]{1,0:T(8,128)(2,1)}, bf16[1024,1536]{1,0:T(8,128)(2,1)}, bf16[1024,1536]{1,0:T(8,128)(2,1)}, bf16[16,1024,128]{2,1,0:T(8,128)(2,1)}...) custom-call(s32[1]{0:T(128)} %bitcast.refs_0_, bf16[1024,1024]{1,0:T(8,128)(2,1)} %bitcast.33, ...), custom_call_target="tpu_custom_call" | custom-call | flops 8000000 | bytes 25000 | tf_op jit(solution)/shard_map/project/pallas_call | solution.py:203
  55.9 11.4 %attend.2 = (bf16[1024,512]{1,0:T(8,128)(2,1)}, bf16[8,1024,128]{2,1,0:T(8,128)(2,1)}) custom-call(bf16[16,1024,128]{2,1,0:T(8,128)(2,1)} %get-tuple-element.206.q_ref, bf16[8,1024,128]{2,1,0:T(8,128)(2,1)} %get-tuple-element.214.k_ref, bf16[8,1024,128]{2,1,0:T(8,128)(2,1)} %get-tuple-element.208.v_ref), custom_call_target="tpu_custom_call" | custom-call | flops 10000000 | bytes 8000 | tf_op jit(solution)/shard_map/attend/pallas_call | solution.py:262
  72.7 11.7 %attend.3 = (bf16[1024,512]{1,0:T(8,128)(2,1)}, bf16[8,1024,128]{2,1,0:T(8,128)(2,1)}) custom-call(bf16[16,1024,128]{2,1,0:T(8,128)(2,1)} %get-tuple-element.206.q_ref, bf16[8,1024,128]{2,1,0:T(8,128)(2,1)} %get-tuple-element.214.k_ref, bf16[8,1024,128]{2,1,0:T(8,128)(2,1)} %get-tuple-element.208.v_ref), custom_call_target="tpu_custom_call" | custom-call | flops 10000000 | bytes 8000 | tf_op jit(solution)/shard_map/attend/pallas_call | solution.py:262
  84.5 4.2 collective-permute-done.12.refs_11_.refs_10_.refs_15_
  94.0 2.4 collective-permute-done.17.refs_14_.refs_13_.refs_18_
  97.3 8.3 %output_rows.1 = (f32[1024,1024]{1,0:T(8,128)}, bf16[1024,1024]{1,0:T(8,128)(2,1)}, bf16[1024,1024]{1,0:T(8,128)(2,1)}) custom-call(s32[1]{0:T(128)} %bitcast.refs_0_, bf16[1024,512]{1,0:T(8,128)(2,1)} %get-tuple-element.215.refs_1_.refs_3_.o_ref, bf16[1024,512]{1,0:T(8,128)(2,1)} %get-tuple-element.220.refs_2_.refs_4_.o_ref, bf16[1024,1024]{1,0:T(8,128)(2,1)} %bitcast.34, ...), custom_call_target="tpu_custom_call" | custom-call | flops 5000000 | bytes 15000 | tf_op jit(solution)/shard_map/output_rows/pallas_call | solution.py:379
  105.6 40.7 %feed.3 = (bf16[1024,1024]{1,0:T(8,128)(2,1)}, bf16[1024,1024]{1,0:T(8,128)(2,1)}, bf16[4,576,1024]{2,1,0:T(8,128)(2,1)}, bf16[4,576,1024]{2,1,0:T(8,128)(2,1)}) custom-call(s32[1]{0:T(128)} %bitcast.refs_0_, bf16[1024,1024]{1,0:T(8,128)(2,1)} %get-tuple-element.256.refs_1_, bf16[1024,1024]{1,0:T(8,128)(2,1)} %get-tuple-element.229.refs_2_, ...), custom_call_target="tpu_custom_call" | custom-call | flops 37500000 | bytes 38000 | tf_op jit(solution)/shard_map/feed/pallas_call | solution.py:459
  147.1 2.4 collective-permute-done.22.refs_7_
  156.9 40.6 %feed.4 = (bf16[1024,1024]{1,0:T(8,128)(2,1)}, bf16[1024,1024]{1,0:T(8,128)(2,1)}, bf16[4,576,1024]{2,1,0:T(8,128)(2,1)}, bf16[4,576,1024]{2,1,0:T(8,128)(2,1)}) custom-call(s32[1]{0:T(128)} %bitcast.refs_0_, bf16[1024,1024]{1,0:T(8,128)(2,1)} %get-tuple-element.256.refs_1_, bf16[1024,1024]{1,0:T(8,128)(2,1)} %get-tuple-element.229.refs_2_, ...), custom_call_target="tpu_custom_call" | custom-call | flops 37500000 | bytes 38000 | tf_op jit(solution)/shard_map/feed/pallas_call | solution.py:459
  197.5 9.8 %collective-permute-done.29.refs_10_ = bf16[576,1024]{1,0:T(8,128)(2,1)} collective-permute-done((bf16[576,1024]{1,0:T(8,128)(2,1)S(1)}, bf16[576,1024]{1,0:T(8,128)(2,1)}, u32[]{:S(2)}, u32[]{:S(2)}) %collective-permute-start.29) | collective-permute-done | bytes 1179680 | tf_op jit(solution)/shard_map/ppermute | solution.py:760
  207.9 4.0 collective-permute-done.30.refs_7_
  214.1 4.6 combine.13
  222.2 40.7 %feed.5 = (bf16[1024,1024]{1,0:T(8,128)(2,1)}, bf16[1024,1024]{1,0:T(8,128)(2,1)}, bf16[4,576,1024]{2,1,0:T(8,128)(2,1)}, bf16[4,576,1024]{2,1,0:T(8,128)(2,1)}) custom-call(s32[1]{0:T(128)} %bitcast.refs_0_, bf16[1024,1024]{1,0:T(8,128)(2,1)} %get-tuple-element.256.refs_1_, bf16[1024,1024]{1,0:T(8,128)(2,1)} %get-tuple-element.229.refs_2_, ...), custom_call_target="tpu_custom_call" | custom-call | flops 37500000 | bytes 38000 | tf_op jit(solution)/shard_map/feed/pallas_call | solution.py:459
  262.9 10.5 %collective-permute-done.35.refs_3_ = bf16[576,1024]{1,0:T(8,128)(2,1)S(1)} collective-permute-done((bf16[576,1024]{1,0:T(8,128)(2,1)}, bf16[576,1024]{1,0:T(8,128)(2,1)S(1)}, u32[]{:S(2)}, u32[]{:S(2)}) %collective-permute-start.35) | collective-permute-done | bytes 1179680 | tf_op jit(solution)/shard_map/ppermute | solution.py:760
  274.8 4.9 combine.14
  280.8 3.5 collective-permute-start.40
  284.4 14.8 %middle.1 = (f32[1024,1024]{1,0:T(8,128)}, bf16[1024,1024]{1,0:T(8,128)(2,1)}, bf16[1024,1024]{1,0:T(8,128)(2,1)}) custom-call(s32[1]{0:T(128)} %bitcast.refs_0_, f32[1024,1024]{1,0:T(8,128)} %get-tuple-element.352.refs_1_, bf16[1024,1024]{1,0:T(8,128)(2,1)} %bitcast.32, bf16[1024,512]{1,0:T(8,128)(2,1)} %get-tuple-element.215.refs_1_.refs_3_.o_ref, ...), custom_call_target="tpu_custom_call" | custom-call | flops 9000000 | bytes 32000 | tf_op jit(solution)/shard_map/middle/pallas_call | solution.py:529
  299.2 2.6 combine.15
  302.0 19.7 %attend_back.2 = (f32[1024,512]{1,0:T(8,128)}, f32[1024,512]{1,0:T(8,128)}) custom-call(bf16[8,1024,128]{2,1,0:T(8,128)(2,1)} %get-tuple-element.213.q_ref, bf16[8,1024,128]{2,1,0:T(8,128)(2,1)} %get-tuple-element.214.k_ref, bf16[8,1024,128]{2,1,0:T(8,128)(2,1)} %get-tuple-element.208.v_ref, bf16[1024,512]{1,0:T(8,128)(2,1)} %get-tuple-element.215.refs_1_.refs_3_.o_ref, ...), custom_call_target="tpu_custom_call" | custom-call | flops 20000000 | bytes 12000 | tf_op jit(solution)/shard_map/attend_back/pallas_call | solution.py:334
  321.7 6.8 %collective-permute-done.39.refs_9_ = bf16[576,1024]{1,0:T(8,128)(2,1)S(1)} collective-permute-done((bf16[576,1024]{1,0:T(8,128)(2,1)}, bf16[576,1024]{1,0:T(8,128)(2,1)S(1)}, u32[]{:S(2)}, u32[]{:S(2)}) %collective-permute-start.39) | collective-permute-done | bytes 1179680 | tf_op jit(solution)/shard_map/ppermute | solution.py:760
  329.5 8.3 %combine.16 = (bf16[576,1024]{1,0:T(8,128)(2,1)}, bf16[576,1024]{1,0:T(8,128)(2,1)}, bf16[576,1024]{1,0:T(8,128)(2,1)}, bf16[576,1024]{1,0:T(8,128)(2,1)}, bf16[576,1024]{1,0:T(8,128)(2,1)}) custom-call(bf16[4,576,1024]{2,1,0:T(8,128)(2,1)} %get-tuple-element.274.refs_5_.refs_0_.refs_3_, ...), custom_call_target="tpu_custom_call" | custom-call | bytes 4000 | tf_op jit(solution)/shard_map/combine/pallas_call | solution.py:797
  343.6 19.9 %attend_back.3 = (f32[1024,512]{1,0:T(8,128)}, f32[1024,512]{1,0:T(8,128)}) custom-call(bf16[8,1024,128]{2,1,0:T(8,128)(2,1)} %get-tuple-element.293.q_ref, bf16[8,1024,128]{2,1,0:T(8,128)(2,1)} %get-tuple-element.214.k_ref, bf16[8,1024,128]{2,1,0:T(8,128)(2,1)} %get-tuple-element.208.v_ref, bf16[1024,512]{1,0:T(8,128)(2,1)} %get-tuple-element.220.refs_2_.refs_4_.o_ref, ...), custom_call_target="tpu_custom_call" | custom-call | flops 20000000 | bytes 12000 | tf_op jit(solution)/shard_map/attend_back/pallas_call | solution.py:334
  363.5 3.5 collective-permute-done.41.refs_2_
  368.0 4.4 combine.17
  375.2 19.9 %raw_back.1 = (bf16[1024,2048]{1,0:T(8,128)(2,1)}, bf16[4,416,1024]{2,1,0:T(8,128)(2,1)}, bf16[4,416,1024]{2,1,0:T(8,128)(2,1)}) custom-call(s32[1]{0:T(128)} %bitcast.refs_0_, f32[1024,512]{1,0:T(8,128)} %get-tuple-element.292.refs_1_, f32[1024,512]{1,0:T(8,128)} %get-tuple-element.315.refs_2_, f32[1024,512]{1,0:T(8,128)} %get-tuple-element.316.refs_3_, ...), custom_call_target="tpu_custom_call" | custom-call | flops 10000000 | bytes 30000 | tf_op jit(solution)/shard_map/raw_back/pallas_call | solution.py:615
  395.9 4.2 collective-permute-done.47.refs_1_
  400.2 4.4 combine.18
  408.5 4.8 collective-permute-start.51
  413.3 2.5 combine.19
  416.7 11.2 %input_back.1 = f32[1024,1024]{1,0:T(8,128)} custom-call(s32[1]{0:T(128)} %bitcast.refs_0_, bf16[1024,2048]{1,0:T(8,128)(2,1)} %get-tuple-element.339.refs_1_, bf16[1024,1024]{1,0:T(8,128)(2,1)} %bitcast.35, f32[1024,1024]{1,0:T(8,128)} %get-tuple-element.340.refs_3_, f32[16,1024]{1,0:T(8,128)} %get-tuple-element.221.refs_4_.refs_5_.refs_10_, ...), custom_call_target="tpu_custom_call" | custom-call | flops 6000000 | bytes 18000 | tf_op jit(solution)/shard_map/input_back/pallas_call | solution.py:645
  427.8 8.6 %collective-permute-done.49.refs_2_ = bf16[416,1024]{1,0:T(8,128)(2,1)S(1)} collective-permute-done((bf16[416,1024]{1,0:T(8,128)(2,1)}, bf16[416,1024]{1,0:T(8,128)(2,1)S(1)}, u32[]{:S(2)}, u32[]{:S(2)}) %collective-permute-start.49) | collective-permute-done | bytes 852000 | tf_op jit(solution)/shard_map/ppermute | solution.py:760
  437.3 3.2 combine.20
  442.6 3.5 combine.21
  449.1 6.4 %add_convert_fusion = bf16[1024,1024]{1,0:T(8,128)(2,1)} fusion(f32[1024,1024]{1,0:T(8,128)} %get-tuple-element.352.refs_1_, bf16[1024,1024]{1,0:T(8,128)(2,1)} %get-tuple-element.355, bf16[1024,1024]{1,0:T(8,128)(2,1)} %get-tuple-element.354, bf16[1024,1024]{1,0:T(8,128)(2,1)S(1)} %copy-done.19), kind=kLoop, calls=%fused_computation | loop fusion | flops 7340032 | bytes 12582912 | tf_op jit(solution)/shard_map/convert_element_type | solution.py:1095
  455.5 4.8 collective-permute-done.52.refs_2_
  461.3 2.9 combine.22.refs_0_
  466.1 2.6 combine.23.refs_4_
  470.0 5.9 %collective-permute-done.55.refs_3_ = bf16[576,1024]{1,0:T(8,128)(2,1)S(1)} collective-permute-done((bf16[576,1024]{1,0:T(8,128)(2,1)}, bf16[576,1024]{1,0:T(8,128)(2,1)S(1)}, u32[]{:S(2)}, u32[]{:S(2)}) %collective-permute-start.55) | collective-permute-done | bytes 1179680 | tf_op jit(solution)/shard_map/ppermute | solution.py:811
  475.9 6.9 %collective-permute-done.54.refs_1_ = bf16[416,1024]{1,0:T(8,128)(2,1)S(1)} collective-permute-done((bf16[416,1024]{1,0:T(8,128)(2,1)}, bf16[416,1024]{1,0:T(8,128)(2,1)S(1)}, u32[]{:S(2)}, u32[]{:S(2)}) %collective-permute-start.54) | collective-permute-done | bytes 852000 | tf_op jit(solution)/shard_map/ppermute | solution.py:811
  483.8 2.2 combine.24.refs_0_
  486.7 15.3 %collective-permute-done.57.refs_5_ = bf16[576,1024]{1,0:T(8,128)(2,1)S(1)} collective-permute-done((bf16[576,1024]{1,0:T(8,128)(2,1)}, bf16[576,1024]{1,0:T(8,128)(2,1)S(1)}, u32[]{:S(2)}, u32[]{:S(2)}) %collective-permute-start.57) | collective-permute-done | bytes 1179680 | tf_op jit(solution)/shard_map/ppermute | solution.py:811
  503.0 2.3 combine.25
  506.5 7.5 %unpack_rows.1 = (f32[128,4608]{1,0:T(8,128)}, f32[128,4608]{1,0:T(8,128)}, f32[576,1024]{1,0:T(8,128)}) custom-call(s32[1]{0:T(128)} %bitcast.8.flag_ref, bf16[576,1024]{1,0:T(8,128)(2,1)} %get-tuple-element.328.refs_0_, bf16[576,1024]{1,0:T(8,128)(2,1)} %collective-permute-done.47.refs_1_, bf16[576,1024]{1,0:T(8,128)(2,1)} %get-tuple-element.361.refs_2_, ...), custom_call_target="tpu_custom_call" | custom-call | bytes 14000 | tf_op jit(solution)/shard_map/unpack_rows/pallas_call | solution.py:737
  514.0 14.5 %collective-permute-done.59 = bf16[416,1024]{1,0:T(8,128)(2,1)S(1)} collective-permute-done((bf16[416,1024]{1,0:T(8,128)(2,1)}, bf16[416,1024]{1,0:T(8,128)(2,1)S(1)}, u32[]{:S(2)}, u32[]{:S(2)}) %collective-permute-start.59) | collective-permute-done | bytes 852000 | tf_op jit(solution)/shard_map/ppermute | solution.py:811
  (250 shorter events, 87.9 us)
Async XLA Ops:
  5.7 15.6 %collective-permute-start = (bf16[272,1024]{1,0:T(8,128)(2,1)S(1)}, bf16[272,1024]{1,0:T(8,128)(2,1)S(1)}, u32[]{:S(2)}, u32[]{:S(2)}) collective-permute-start(bf16[272,1024]{1,0:T(8,128)(2,1)S(1)} %concatenate.38.refs_6_.refs_7_.refs_22_.refs_5_), channel_id=1, source_target_pairs={{0,2},{1,3},{2,0},{3,1},{4,6},{5,7},{6,4},{7,5},{8,10},{9,11},{10,... | collective-permute-start | bytes 1671176 | tf_op jit(solution)/shard_map/ppermute | solution.py:760
  8.7 14.1 %collective-permute-start.1 = (bf16[272,1024]{1,0:T(8,128)(2,1)S(1)}, bf16[272,1024]{1,0:T(8,128)(2,1)S(1)}, u32[]{:S(2)}, u32[]{:S(2)}) collective-permute-start(bf16[272,1024]{1,0:T(8,128)(2,1)S(1)} %concatenate.38.refs_6_.refs_7_.refs_22_.refs_5_), channel_id=1, source_target_pairs={{0,4},{1,5},{2,6},{3,7},{4,0},{5,1},{6,2},{7,3},{8,12},{9,13},{10,... | collective-permute-start | bytes 1671176 | tf_op jit(solution)/shard_map/ppermute | solution.py:760
  10.2 12.6 %collective-permute-start.2 = (bf16[272,1024]{1,0:T(8,128)(2,1)S(1)}, bf16[272,1024]{1,0:T(8,128)(2,1)S(1)}, u32[]{:S(2)}, u32[]{:S(2)}) collective-permute-start(bf16[272,1024]{1,0:T(8,128)(2,1)S(1)} %concatenate.38.refs_6_.refs_7_.refs_22_.refs_5_), channel_id=1, source_target_pairs={{0,1},{1,0},{2,3},{3,2},{4,5},{5,4},{6,7},{7,6},{8,9},{9,8},{10,11... | collective-permute-start | bytes 1671176 | tf_op jit(solution)/shard_map/ppermute | solution.py:760
  22.8 10.3 %collective-permute-start.3 = (bf16[272,1024]{1,0:T(8,128)(2,1)S(1)}, bf16[272,1024]{1,0:T(8,128)(2,1)S(1)}, u32[]{:S(2)}, u32[]{:S(2)}) collective-permute-start(bf16[272,1024]{1,0:T(8,128)(2,1)S(1)} %collective-permute-done.refs_10_.refs_11_.refs_24_.refs_9_), channel_id=1, source_target_pairs={{0,1},{1,0},{2,3},{3,2},{4,5},{5,4},{6,7},{7,6},{8,9},{9,8},{10,11... | collective-permute-start | bytes 1671176 | tf_op jit(solution)/shard_map/ppermute | solution.py:760
  22.9 10.2 %collective-permute-start.4 = (bf16[272,1024]{1,0:T(8,128)(2,1)S(1)}, bf16[272,1024]{1,0:T(8,128)(2,1)S(1)}, u32[]{:S(2)}, u32[]{:S(2)}) collective-permute-start(bf16[272,1024]{1,0:T(8,128)(2,1)S(1)} %collective-permute-done.1.refs_14_.refs_15_.refs_26_.refs_13_), channel_id=1, source_target_pairs={{0,1},{1,0},{2,3},{3,2},{4,5},{5,4},{6,7},{7,6},{8,9},{9,8},{10,11... | collective-permute-start | bytes 1671176 | tf_op jit(solution)/shard_map/ppermute | solution.py:760
  23.4 9.7 %collective-permute-start.6 = (bf16[144,1024]{1,0:T(8,128)(2,1)S(1)}, bf16[144,1024]{1,0:T(8,128)(2,1)S(1)}, u32[]{:S(2)}, u32[]{:S(2)}) collective-permute-start(bf16[144,1024]{1,0:T(8,128)(2,1)S(1)} %slice.64), channel_id=1, source_target_pairs={{0,4},{1,5},{2,6},{3,7},{4,0},{5,1},{6,2},{7,3},{8,12},{9,13},{10,... | collective-permute-start | bytes 884744 | tf_op jit(solution)/shard_map/ppermute | solution.py:760
  34.1 33.3 %collective-permute-start.9 = (bf16[704,1024]{1,0:T(8,128)(2,1)}, bf16[704,1024]{1,0:T(8,128)(2,1)S(1)}, u32[]{:S(2)}, u32[]{:S(2)}) collective-permute-start(bf16[704,1024]{1,0:T(8,128)(2,1)} %get-tuple-element.212.refs_5_.refs_4_.refs_9_), channel_id=1, source_target_pairs={{0,2},{1,3},{2,0},{3,1},{4,6},{5,7},{6,4},{7,5},{8,10},{9,11},{10,... | collective-permute-start | bytes 4325384 | tf_op jit(solution)/shard_map/ppermute | solution.py:760
  34.6 32.7 %collective-permute-start.10 = (bf16[704,1024]{1,0:T(8,128)(2,1)}, bf16[704,1024]{1,0:T(8,128)(2,1)S(1)}, u32[]{:S(2)}, u32[]{:S(2)}) collective-permute-start(bf16[704,1024]{1,0:T(8,128)(2,1)} %get-tuple-element.212.refs_5_.refs_4_.refs_9_), channel_id=1, source_target_pairs={{0,4},{1,5},{2,6},{3,7},{4,0},{5,1},{6,2},{7,3},{8,12},{9,13},{10,... | collective-permute-start | bytes 4325384 | tf_op jit(solution)/shard_map/ppermute | solution.py:760
  35.5 31.9 %collective-permute-start.11 = (bf16[704,1024]{1,0:T(8,128)(2,1)}, bf16[704,1024]{1,0:T(8,128)(2,1)}, u32[]{:S(2)}, u32[]{:S(2)}) collective-permute-start(bf16[704,1024]{1,0:T(8,128)(2,1)} %get-tuple-element.212.refs_5_.refs_4_.refs_9_), channel_id=1, source_target_pairs={{0,1},{1,0},{2,3},{3,2},{4,5},{5,4},{6,7},{7,6},{8,9},{9,8},{10,11... | collective-permute-start | bytes 4325384 | tf_op jit(solution)/shard_map/ppermute | solution.py:760
  67.4 22.7 %collective-permute-start.14 = (bf16[704,1024]{1,0:T(8,128)(2,1)S(1)}, bf16[704,1024]{1,0:T(8,128)(2,1)}, u32[]{:S(2)}, u32[]{:S(2)}) collective-permute-start(bf16[704,1024]{1,0:T(8,128)(2,1)S(1)} %collective-permute-done.9.refs_7_.refs_6_.refs_11_), channel_id=1, source_target_pairs={{0,1},{1,0},{2,3},{3,2},{4,5},{5,4},{6,7},{7,6},{8,9},{9,8},{10,11... | collective-permute-start | bytes 4325384 | tf_op jit(solution)/shard_map/ppermute | solution.py:760
  67.8 22.2 %collective-permute-start.15 = (bf16[704,1024]{1,0:T(8,128)(2,1)S(1)}, bf16[704,1024]{1,0:T(8,128)(2,1)}, u32[]{:S(2)}, u32[]{:S(2)}) collective-permute-start(bf16[704,1024]{1,0:T(8,128)(2,1)S(1)} %collective-permute-done.10.refs_9_.refs_8_.refs_13_), channel_id=1, source_target_pairs={{0,1},{1,0},{2,3},{3,2},{4,5},{5,4},{6,7},{7,6},{8,9},{9,8},{10,11... | collective-permute-start | bytes 4325384 | tf_op jit(solution)/shard_map/ppermute | solution.py:760
  70.1 18.6 %collective-permute-start.12 = (bf16[704,512]{1,0:T(8,128)(2,1)}, bf16[704,512]{1,0:T(8,128)(2,1)S(1)}, u32[]{:S(2)}, u32[]{:S(2)}) collective-permute-start(bf16[704,512]{1,0:T(8,128)(2,1)} %slice.65), channel_id=1, source_target_pairs={{0,2},{1,3},{2,0},{3,1},{4,6},{5,7},{6,4},{7,5},{8,10},{9,11},{10,... | collective-permute-start | bytes 2162696 | tf_op jit(solution)/shard_map/ppermute | solution.py:760
  71.6 18.4 %collective-permute-start.13 = (bf16[704,512]{1,0:T(8,128)(2,1)}, bf16[704,512]{1,0:T(8,128)(2,1)}, u32[]{:S(2)}, u32[]{:S(2)}) collective-permute-start(bf16[704,512]{1,0:T(8,128)(2,1)} %slice.66), channel_id=1, source_target_pairs={{0,4},{1,5},{2,6},{3,7},{4,0},{5,1},{6,2},{7,3},{8,12},{9,13},{10,... | collective-permute-start | bytes 2162696 | tf_op jit(solution)/shard_map/ppermute | solution.py:760
  90.0 56.3 %collective-permute-start.18 = (bf16[576,1024]{1,0:T(8,128)(2,1)}, bf16[576,1024]{1,0:T(8,128)(2,1)S(1)}, u32[]{:S(2)}, u32[]{:S(2)}) collective-permute-start(bf16[576,1024]{1,0:T(8,128)(2,1)} %get-tuple-element.235.refs_4_), channel_id=1, source_target_pairs={{0,1},{1,0},{2,3},{3,2},{4,5},{5,4},{6,7},{7,6},{8,9},{9,8},{10,11... | collective-permute-start | bytes 3538952 | tf_op jit(solution)/shard_map/ppermute | solution.py:760
  90.5 55.8 %collective-permute-start.19 = (bf16[576,1024]{1,0:T(8,128)(2,1)}, bf16[576,1024]{1,0:T(8,128)(2,1)}, u32[]{:S(2)}, u32[]{:S(2)}) collective-permute-start(bf16[576,1024]{1,0:T(8,128)(2,1)} %get-tuple-element.235.refs_4_), channel_id=1, source_target_pairs={{0,2},{1,3},{2,0},{3,1},{4,6},{5,7},{6,4},{7,5},{8,10},{9,11},{10,... | collective-permute-start | bytes 3538952 | tf_op jit(solution)/shard_map/ppermute | solution.py:760
  91.1 55.3 %collective-permute-start.20 = (bf16[576,1024]{1,0:T(8,128)(2,1)}, bf16[576,1024]{1,0:T(8,128)(2,1)}, u32[]{:S(2)}, u32[]{:S(2)}) collective-permute-start(bf16[576,1024]{1,0:T(8,128)(2,1)} %get-tuple-element.235.refs_4_), channel_id=1, source_target_pairs={{0,4},{1,5},{2,6},{3,7},{4,0},{5,1},{6,2},{7,3},{8,12},{9,13},{10,... | collective-permute-start | bytes 3538952 | tf_op jit(solution)/shard_map/ppermute | solution.py:760
  92.2 54.2 %collective-permute-start.21 = (bf16[576,1024]{1,0:T(8,128)(2,1)}, bf16[576,1024]{1,0:T(8,128)(2,1)}, u32[]{:S(2)}, u32[]{:S(2)}) collective-permute-start(bf16[576,1024]{1,0:T(8,128)(2,1)} %get-tuple-element.235.refs_4_), channel_id=1, source_target_pairs={{0,6},{1,7},{2,4},{3,5},{4,2},{5,3},{6,0},{7,1},{8,14},{9,15},{10,... | collective-permute-start | bytes 3538952 | tf_op jit(solution)/shard_map/ppermute | solution.py:760
  152.9 54.5 %collective-permute-start.25 = (bf16[4,576,1024]{2,1,0:T(8,128)(2,1)}, bf16[4,576,1024]{2,1,0:T(8,128)(2,1)}, u32[]{:S(2)}, u32[]{:S(2)}) collective-permute-start(bf16[4,576,1024]{2,1,0:T(8,128)(2,1)} %get-tuple-element.247), channel_id=1, source_target_pairs={{0,1},{1,0},{2,3},{3,2},{4,5},{5,4},{6,7},{7,6},{8,9},{9,8},{10,11... | collective-permute-start | bytes 14155784 | tf_op jit(solution)/shard_map/ppermute | solution.py:760
  153.0 44.4 %collective-permute-start.26 = (bf16[576,1024]{1,0:T(8,128)(2,1)S(1)}, bf16[576,1024]{1,0:T(8,128)(2,1)S(1)}, u32[]{:S(2)}, u32[]{:S(2)}) collective-permute-start(bf16[576,1024]{1,0:T(8,128)(2,1)S(1)} %copy-done.20), channel_id=1, source_target_pairs={{0,1},{1,0},{2,3},{3,2},{4,5},{5,4},{6,7},{7,6},{8,9},{9,8},{10,11... | collective-permute-start | bytes 3538952 | tf_op jit(solution)/shard_map/ppermute | solution.py:760
  153.4 44.1 %collective-permute-start.27 = (bf16[576,1024]{1,0:T(8,128)(2,1)S(1)}, bf16[576,1024]{1,0:T(8,128)(2,1)S(1)}, u32[]{:S(2)}, u32[]{:S(2)}) collective-permute-start(bf16[576,1024]{1,0:T(8,128)(2,1)S(1)} %copy-done.20), channel_id=1, source_target_pairs={{0,2},{1,3},{2,0},{3,1},{4,6},{5,7},{6,4},{7,5},{8,10},{9,11},{10,... | collective-permute-start | bytes 3538952 | tf_op jit(solution)/shard_map/ppermute | solution.py:760
  153.9 43.6 %collective-permute-start.28 = (bf16[576,1024]{1,0:T(8,128)(2,1)S(1)}, bf16[576,1024]{1,0:T(8,128)(2,1)}, u32[]{:S(2)}, u32[]{:S(2)}) collective-permute-start(bf16[576,1024]{1,0:T(8,128)(2,1)S(1)} %copy-done.20), channel_id=1, source_target_pairs={{0,4},{1,5},{2,6},{3,7},{4,0},{5,1},{6,2},{7,3},{8,12},{9,13},{10,... | collective-permute-start | bytes 3538952 | tf_op jit(solution)/shard_map/ppermute | solution.py:760
  155.1 52.3 %collective-permute-start.29 = (bf16[576,1024]{1,0:T(8,128)(2,1)S(1)}, bf16[576,1024]{1,0:T(8,128)(2,1)}, u32[]{:S(2)}, u32[]{:S(2)}) collective-permute-start(bf16[576,1024]{1,0:T(8,128)(2,1)S(1)} %copy-done.20), channel_id=1, source_target_pairs={{0,6},{1,7},{2,4},{3,5},{4,2},{5,3},{6,0},{7,1},{8,14},{9,15},{10,... | collective-permute-start | bytes 3538952 | tf_op jit(solution)/shard_map/ppermute | solution.py:760
  213.9 59.5 %collective-permute-start.33 = (bf16[4,576,1024]{2,1,0:T(8,128)(2,1)}, bf16[4,576,1024]{2,1,0:T(8,128)(2,1)}, u32[]{:S(2)}, u32[]{:S(2)}) collective-permute-start(bf16[4,576,1024]{2,1,0:T(8,128)(2,1)} %get-tuple-element.266), channel_id=1, source_target_pairs={{0,1},{1,0},{2,3},{3,2},{4,5},{5,4},{6,7},{7,6},{8,9},{9,8},{10,11... | collective-permute-start | bytes 14155784 | tf_op jit(solution)/shard_map/ppermute | solution.py:760
  218.7 44.2 %collective-permute-start.34 = (bf16[576,1024]{1,0:T(8,128)(2,1)}, bf16[576,1024]{1,0:T(8,128)(2,1)S(1)}, u32[]{:S(2)}, u32[]{:S(2)}) collective-permute-start(bf16[576,1024]{1,0:T(8,128)(2,1)} %get-tuple-element.267), channel_id=1, source_target_pairs={{0,2},{1,3},{2,0},{3,1},{4,6},{5,7},{6,4},{7,5},{8,10},{9,11},{10,... | collective-permute-start | bytes 3538952 | tf_op jit(solution)/shard_map/ppermute | solution.py:760
  219.9 53.4 %collective-permute-start.35 = (bf16[576,1024]{1,0:T(8,128)(2,1)}, bf16[576,1024]{1,0:T(8,128)(2,1)S(1)}, u32[]{:S(2)}, u32[]{:S(2)}) collective-permute-start(bf16[576,1024]{1,0:T(8,128)(2,1)} %get-tuple-element.268), channel_id=1, source_target_pairs={{0,4},{1,5},{2,6},{3,7},{4,0},{5,1},{6,2},{7,3},{8,12},{9,13},{10,... | collective-permute-start | bytes 3538952 | tf_op jit(solution)/shard_map/ppermute | solution.py:760
  221.1 52.3 %collective-permute-start.36 = (bf16[576,1024]{1,0:T(8,128)(2,1)}, bf16[576,1024]{1,0:T(8,128)(2,1)S(1)}, u32[]{:S(2)}, u32[]{:S(2)}) collective-permute-start(bf16[576,1024]{1,0:T(8,128)(2,1)} %get-tuple-element.269), channel_id=1, source_target_pairs={{0,6},{1,7},{2,4},{3,5},{4,2},{5,3},{6,0},{7,1},{8,14},{9,15},{10,... | collective-permute-start | bytes 3538952 | tf_op jit(solution)/shard_map/ppermute | solution.py:760
  273.4 25.8 %collective-permute-start.37 = (bf16[4,576,1024]{2,1,0:T(8,128)(2,1)}, bf16[4,576,1024]{2,1,0:T(8,128)(2,1)}, u32[]{:S(2)}, u32[]{:S(2)}) collective-permute-start(bf16[4,576,1024]{2,1,0:T(8,128)(2,1)} %get-tuple-element.282), channel_id=1, source_target_pairs={{0,1},{1,0},{2,3},{3,2},{4,5},{5,4},{6,7},{7,6},{8,9},{9,8},{10,11... | collective-permute-start | bytes 14155784 | tf_op jit(solution)/shard_map/ppermute | solution.py:760
  279.7 42.0 %collective-permute-start.38 = (bf16[576,1024]{1,0:T(8,128)(2,1)}, bf16[576,1024]{1,0:T(8,128)(2,1)S(1)}, u32[]{:S(2)}, u32[]{:S(2)}) collective-permute-start(bf16[576,1024]{1,0:T(8,128)(2,1)} %get-tuple-element.289), channel_id=1, source_target_pairs={{0,4},{1,5},{2,6},{3,7},{4,0},{5,1},{6,2},{7,3},{8,12},{9,13},{10,... | collective-permute-start | bytes 3538952 | tf_op jit(solution)/shard_map/ppermute | solution.py:760
  280.8 40.9 %collective-permute-start.40 = (bf16[576,1024]{1,0:T(8,128)(2,1)}, bf16[576,1024]{1,0:T(8,128)(2,1)S(1)}, u32[]{:S(2)}, u32[]{:S(2)}) collective-permute-start(bf16[576,1024]{1,0:T(8,128)(2,1)} %get-tuple-element.291.refs_10_), channel_id=1, source_target_pairs={{0,8},{24,16},{1,9},{25,17},{2,10},{26,18},{3,11},{27,19},{4,12},{... | collective-permute-start | bytes 3538952 | tf_op jit(solution)/shard_map/ppermute | solution.py:811
  301.8 26.7 %collective-permute-start.39 = (bf16[576,1024]{1,0:T(8,128)(2,1)}, bf16[576,1024]{1,0:T(8,128)(2,1)S(1)}, u32[]{:S(2)}, u32[]{:S(2)}) collective-permute-start(bf16[576,1024]{1,0:T(8,128)(2,1)} %combine.15), channel_id=1, source_target_pairs={{0,2},{1,3},{2,0},{3,1},{4,6},{5,7},{6,4},{7,5},{8,10},{9,11},{10,... | collective-permute-start | bytes 3538952 | tf_op jit(solution)/shard_map/ppermute | solution.py:760
  337.8 29.2 %collective-permute-start.41 = (bf16[576,1024]{1,0:T(8,128)(2,1)}, bf16[576,1024]{1,0:T(8,128)(2,1)S(1)}, u32[]{:S(2)}, u32[]{:S(2)}) collective-permute-start(bf16[576,1024]{1,0:T(8,128)(2,1)} %get-tuple-element.306), channel_id=1, source_target_pairs={{0,2},{1,3},{2,0},{3,1},{4,6},{5,7},{6,4},{7,5},{8,10},{9,11},{10,... | collective-permute-start | bytes 3538952 | tf_op jit(solution)/shard_map/ppermute | solution.py:760
  338.4 29.2 %collective-permute-start.42 = (bf16[576,1024]{1,0:T(8,128)(2,1)}, bf16[576,1024]{1,0:T(8,128)(2,1)}, u32[]{:S(2)}, u32[]{:S(2)}) collective-permute-start(bf16[576,1024]{1,0:T(8,128)(2,1)} %get-tuple-element.307), channel_id=1, source_target_pairs={{0,4},{1,5},{2,6},{3,7},{4,0},{5,1},{6,2},{7,3},{8,12},{9,13},{10,... | collective-permute-start | bytes 3538952 | tf_op jit(solution)/shard_map/ppermute | solution.py:760
  339.6 28.1 %collective-permute-start.43 = (bf16[576,1024]{1,0:T(8,128)(2,1)}, bf16[576,1024]{1,0:T(8,128)(2,1)}, u32[]{:S(2)}, u32[]{:S(2)}) collective-permute-start(bf16[576,1024]{1,0:T(8,128)(2,1)} %get-tuple-element.308.refs_4_), channel_id=1, source_target_pairs={{8,16},{16,8},{9,17},{17,9},{10,18},{18,10},{11,19},{19,11},{12,20... | collective-permute-start | bytes 3538952 | tf_op jit(solution)/shard_map/ppermute | solution.py:811
  341.2 53.9 %collective-permute-start.44 = (bf16[576,1024]{1,0:T(8,128)(2,1)}, bf16[576,1024]{1,0:T(8,128)(2,1)S(1)}, u32[]{:S(2)}, u32[]{:S(2)}) collective-permute-start(bf16[576,1024]{1,0:T(8,128)(2,1)} %get-tuple-element.325), channel_id=1, source_target_pairs={{0,2},{1,3},{2,0},{3,1},{4,6},{5,7},{6,4},{7,5},{8,10},{9,11},{10,... | collective-permute-start | bytes 3538952 | tf_op jit(solution)/shard_map/ppermute | solution.py:760
  342.5 52.7 %collective-permute-start.45 = (bf16[576,1024]{1,0:T(8,128)(2,1)}, bf16[576,1024]{1,0:T(8,128)(2,1)S(1)}, u32[]{:S(2)}, u32[]{:S(2)}) collective-permute-start(bf16[576,1024]{1,0:T(8,128)(2,1)} %get-tuple-element.326), channel_id=1, source_target_pairs={{0,4},{1,5},{2,6},{3,7},{4,0},{5,1},{6,2},{7,3},{8,12},{9,13},{10,... | collective-permute-start | bytes 3538952 | tf_op jit(solution)/shard_map/ppermute | solution.py:760
  372.4 23.5 %collective-permute-start.46 = (bf16[576,1024]{1,0:T(8,128)(2,1)}, bf16[576,1024]{1,0:T(8,128)(2,1)S(1)}, u32[]{:S(2)}, u32[]{:S(2)}) collective-permute-start(bf16[576,1024]{1,0:T(8,128)(2,1)} %get-tuple-element.327.refs_0_), channel_id=1, source_target_pairs={{0,8},{24,16},{1,9},{25,17},{2,10},{26,18},{3,11},{27,19},{4,12},{... | collective-permute-start | bytes 3538952 | tf_op jit(solution)/shard_map/ppermute | solution.py:811
  373.9 26.1 %collective-permute-start.47 = (bf16[576,1024]{1,0:T(8,128)(2,1)}, bf16[576,1024]{1,0:T(8,128)(2,1)}, u32[]{:S(2)}, u32[]{:S(2)}) collective-permute-start(bf16[576,1024]{1,0:T(8,128)(2,1)} %get-tuple-element.328.refs_0_), channel_id=1, source_target_pairs={{8,0},{16,24},{9,1},{17,25},{10,2},{18,26},{11,3},{19,27},{12,4},{... | collective-permute-start | bytes 3538952 | tf_op jit(solution)/shard_map/ppermute | solution.py:811
  406.4 34.1 %collective-permute-start.50 = (bf16[576,1024]{1,0:T(8,128)(2,1)}, bf16[576,1024]{1,0:T(8,128)(2,1)}, u32[]{:S(2)}, u32[]{:S(2)}) collective-permute-start(bf16[576,1024]{1,0:T(8,128)(2,1)} %get-tuple-element.345.refs_0_), channel_id=1, source_target_pairs={{8,16},{16,8},{9,17},{17,9},{10,18},{18,10},{11,19},{19,11},{12,20... | collective-permute-start | bytes 3538952 | tf_op jit(solution)/shard_map/ppermute | solution.py:811
  408.5 32.0 %collective-permute-start.51 = (bf16[576,1024]{1,0:T(8,128)(2,1)}, bf16[576,1024]{1,0:T(8,128)(2,1)}, u32[]{:S(2)}, u32[]{:S(2)}) collective-permute-start(bf16[576,1024]{1,0:T(8,128)(2,1)} %get-tuple-element.346.refs_2_), channel_id=1, source_target_pairs={{0,8},{24,16},{1,9},{25,17},{2,10},{26,18},{3,11},{27,19},{4,12},{... | collective-permute-start | bytes 3538952 | tf_op jit(solution)/shard_map/ppermute | solution.py:811
  415.8 20.6 %collective-permute-start.49 = (bf16[416,1024]{1,0:T(8,128)(2,1)}, bf16[416,1024]{1,0:T(8,128)(2,1)S(1)}, u32[]{:S(2)}, u32[]{:S(2)}) collective-permute-start(bf16[416,1024]{1,0:T(8,128)(2,1)} %combine.19), channel_id=1, source_target_pairs={{0,4},{1,5},{2,6},{3,7},{4,0},{5,1},{6,2},{7,3},{8,12},{9,13},{10,... | collective-permute-start | bytes 2555912 | tf_op jit(solution)/shard_map/ppermute | solution.py:760
  440.5 19.8 %collective-permute-start.52 = (bf16[416,1024]{1,0:T(8,128)(2,1)}, bf16[416,1024]{1,0:T(8,128)(2,1)S(1)}, u32[]{:S(2)}, u32[]{:S(2)}) collective-permute-start(bf16[416,1024]{1,0:T(8,128)(2,1)} %get-tuple-element.356), channel_id=1, source_target_pairs={{0,2},{1,3},{2,0},{3,1},{4,6},{5,7},{6,4},{7,5},{8,10},{9,11},{10,... | collective-permute-start | bytes 2555912 | tf_op jit(solution)/shard_map/ppermute | solution.py:760
  441.7 19.5 %collective-permute-start.53 = (bf16[416,1024]{1,0:T(8,128)(2,1)}, bf16[416,1024]{1,0:T(8,128)(2,1)}, u32[]{:S(2)}, u32[]{:S(2)}) collective-permute-start(bf16[416,1024]{1,0:T(8,128)(2,1)} %get-tuple-element.357), channel_id=1, source_target_pairs={{0,4},{1,5},{2,6},{3,7},{4,0},{5,1},{6,2},{7,3},{8,12},{9,13},{10,... | collective-permute-start | bytes 2555912 | tf_op jit(solution)/shard_map/ppermute | solution.py:760
  446.2 20.0 %collective-permute-start.56 = (bf16[576,1024]{1,0:T(8,128)(2,1)}, bf16[576,1024]{1,0:T(8,128)(2,1)}, u32[]{:S(2)}, u32[]{:S(2)}) collective-permute-start(bf16[576,1024]{1,0:T(8,128)(2,1)} %get-tuple-element.364.refs_0_), channel_id=1, source_target_pairs={{8,16},{16,8},{9,17},{17,9},{10,18},{18,10},{11,19},{19,11},{12,20... | collective-permute-start | bytes 3538952 | tf_op jit(solution)/shard_map/ppermute | solution.py:811
  447.8 28.1 %collective-permute-start.55 = (bf16[576,1024]{1,0:T(8,128)(2,1)}, bf16[576,1024]{1,0:T(8,128)(2,1)S(1)}, u32[]{:S(2)}, u32[]{:S(2)}) collective-permute-start(bf16[576,1024]{1,0:T(8,128)(2,1)} %get-tuple-element.361.refs_2_), channel_id=1, source_target_pairs={{8,0},{16,24},{9,1},{17,25},{10,2},{18,26},{11,3},{19,27},{12,4},{... | collective-permute-start | bytes 3538952 | tf_op jit(solution)/shard_map/ppermute | solution.py:811
  464.2 18.7 %collective-permute-start.54 = (bf16[416,1024]{1,0:T(8,128)(2,1)}, bf16[416,1024]{1,0:T(8,128)(2,1)S(1)}, u32[]{:S(2)}, u32[]{:S(2)}) collective-permute-start(bf16[416,1024]{1,0:T(8,128)(2,1)} %combine.22.refs_0_), channel_id=1, source_target_pairs={{0,8},{24,16},{1,9},{25,17},{2,10},{26,18},{3,11},{27,19},{4,12},{... | collective-permute-start | bytes 2555912 | tf_op jit(solution)/shard_map/ppermute | solution.py:811
  468.7 33.3 %collective-permute-start.57 = (bf16[576,1024]{1,0:T(8,128)(2,1)}, bf16[576,1024]{1,0:T(8,128)(2,1)S(1)}, u32[]{:S(2)}, u32[]{:S(2)}) collective-permute-start(bf16[576,1024]{1,0:T(8,128)(2,1)} %combine.23.refs_4_), channel_id=1, source_target_pairs={{8,0},{16,24},{9,1},{17,25},{10,2},{18,26},{11,3},{19,27},{12,4},{... | collective-permute-start | bytes 3538952 | tf_op jit(solution)/shard_map/ppermute | solution.py:811
  486.0 16.0 %collective-permute-start.58 = (bf16[416,1024]{1,0:T(8,128)(2,1)}, bf16[416,1024]{1,0:T(8,128)(2,1)S(1)}, u32[]{:S(2)}, u32[]{:S(2)}) collective-permute-start(bf16[416,1024]{1,0:T(8,128)(2,1)} %combine.24.refs_0_), channel_id=1, source_target_pairs={{8,16},{16,8},{9,17},{17,9},{10,18},{18,10},{11,19},{19,11},{12,20... | collective-permute-start | bytes 2555912 | tf_op jit(solution)/shard_map/ppermute | solution.py:811
  505.2 23.3 %collective-permute-start.59 = (bf16[416,1024]{1,0:T(8,128)(2,1)}, bf16[416,1024]{1,0:T(8,128)(2,1)S(1)}, u32[]{:S(2)}, u32[]{:S(2)}) collective-permute-start(bf16[416,1024]{1,0:T(8,128)(2,1)} %combine.25), channel_id=1, source_target_pairs={{8,0},{16,24},{9,1},{17,25},{10,2},{18,26},{11,3},{19,27},{12,4},{... | collective-permute-start | bytes 2555912 | tf_op jit(solution)/shard_map/ppermute | solution.py:811
  (64 other events, 422.1 us)

commit v9 on v8

--- a/solution.py
+++ b/solution.py
@@ -1015,13 +1015,14 @@
     later = finish(packs[1], *waiting)
     waiting = [hop(packs[2], bit) for bit in (1, 2, 4, 6)]
     other_0 = hop(after(sib_0, *later.arrays), 1)
-    (out_1, back_1, own_1, sib_1, normed_two), (other_0, *waiting) = fence(
-        [*feed_step(later, 0, chunks[1], True), normed_two], other_0, *waiting
-    )
-    last = finish(packs[2], *waiting)
+    *early_rows, corner = waiting
+    (out_1, back_1, own_1, sib_1, normed_two), (other_0, *early_rows) = fence(
+        [*feed_step(later, 0, chunks[1], True), normed_two], other_0, *early_rows
+    )
     terms = combine(*[[(own_0, k), (other_0, k)] for k in (1, 2, 3)])
+    corner, *terms = tie(corner, *terms)
+    last = finish(packs[2], *early_rows, corner)
     other_1 = hop(after(sib_1, *last.arrays), 1)
-    normed_two, *terms = tie(normed_two, *terms)
     steps = [hop(term, 2 * k) for k, term in zip((1, 2, 3), terms)]
     (out_2, back_2, own_2, sib_2), (other_1, *steps) = fence(
         feed(last, place, 0, chunks[2], normed_two, normed_two_t, back_out, True), other_1, *steps
@@ -1077,24 +1078,21 @@
         [grads_1, inward_1], [(own_2, 0), (other_2, 0), first_2, second_2]
     )
     back_raw, other, half_1, grads_2 = tie(back_raw, other, half_1, grads_2)
-    term = combine([(own, 3), (other, 3)])
-    back_raw, term = tie(back_raw, term)
-    moved = hop(term, 4)
+    terms = combine(*[[(own, k), (other, k)] for k in (1, 2, 3)])
+    back_raw, *terms = tie(back_raw, *terms)
+    steps = [hop(term, 2 * k) for k, term in zip((1, 2, 3), terms)]
     across_1 = rep_hop(half_1, ACROSS)
     inward_2 = rep_hop(grads_2, INWARD)
     input_grad = input_back(pairs, place, back_raw, x, back_first, gains)
-    (input_grad,), (moved,) = fence([input_grad], moved)
-    one, two = combine([(own, 1), (other, 1), moved], [(own, 2), (other, 2)])
-    one, two, across_1, inward_2, first_sum = tie(one, two, across_1, inward_2, first_sum)
-    first, second = hop(one, 2), hop(two, 4)
+    (input_grad,), (across_1, inward_2) = fence([input_grad], across_1, inward_2)
     total_1, half_2 = combine([half_1, across_1], [grads_2, inward_2])
     first_sum, total_1, half_2 = tie(first_sum, total_1, half_2)
     outward_1 = rep_hop(total_1, OUTWARD)
     across_2 = rep_hop(half_2, ACROSS)
     outs = out_0.astype(F32) + out_1.astype(F32) + out_2.astype(F32)
     block_output = (first_sum + outs).astype(BF16)
-    (block_output,), (first, second) = fence([block_output], first, second)
-    grads = combine([(own, 0), (other, 0), first, second])
+    (block_output,), steps = fence([block_output], *steps)
+    grads = combine([(own, 0), (other, 0), *steps])
     inward = rep_hop(grads, INWARD)
     across_2, _ = tie(across_2, grads)
     total_2 = combine([half_2, across_2])

time: 546 us -> 540 us (0.989)
  waiting for transfers between devices: 127 us -> 118 us
  starting transfers between devices: 57.1 us -> 63 us
    ppermute x48, waiting for transfers between devices: 79.7 us -> 63 us  [hop(): return lax.ppermute(array, 'shard', [(i, i ^ bit) for i in range(8)])]
    ppermute x12, waiting for transfers between devices: 47.5 us -> 55.1 us  [rep_hop(): return lax.ppermute(array.astype(BF16), 'rep', pairs)]
    ppermute x48, starting transfers between devices: 34 us -> 40.3 us  [hop(): return lax.ppermute(array, 'shard', [(i, i ^ bit) for i in range(8)])]
    unnamed x106 -> x104, local copies, waits for them, and re-layouts: 12.1 us -> 9.97 us
    pallas_call x13 -> x12, Pallas kernels: 48.2 us -> 47.8 us  [combine(): pl.pallas_call(kernel, grid=(rows // step,), in_specs=[spec(k) for _, k i...]
  transfers between devices with their start and end apart: 60 -> 60, of which waited for: 28 -> 24; matrix products, arithmetic and copies ran while one was open for 3% -> 3% of each run, Pallas kernels for 57% -> 57%
where the time goes in v9:
time: 540 us; the launch traced here: 531 us
  Pallas kernels  314 us (58%)
  waiting for transfers between devices  118 us (22%)
  starting transfers between devices  63 us (12%)
  other arithmetic  17.2 us (3%)
  local copies, waits for them, and re-layouts  16.4 us (3%)
    pallas_call x3, Pallas kernels, feed(): pl.pallas_call(lambda *refs: feed_kernel(pieces.layout, paired, *refs), g...  122 us
    ppermute x48, waiting for transfers between devices, hop(): return lax.ppermute(array, 'shard', [(i, i ^ bit) for i in range(8)])  63 us
    ppermute x12, waiting for transfers between devices, rep_hop(): return lax.ppermute(array.astype(BF16), 'rep', pairs)  55.1 us
    pallas_call x12, Pallas kernels, combine(): pl.pallas_call(kernel, grid=(rows // step,), in_specs=[spec(k) for _, k i...  47.8 us
    ppermute x48, starting transfers between devices, hop(): return lax.ppermute(array, 'shard', [(i, i ^ bit) for i in range(8)])  40.3 us
    pallas_call x2, Pallas kernels, attend_back(): pl.pallas_call(attend_back_kernel, grid=(groups,), in_specs=[pl.BlockSpec...  39.6 us
    pallas_call x2, Pallas kernels, attend(): pl.pallas_call(attend_kernel, grid=(groups,), in_specs=[pl.BlockSpec((2,...  23.1 us
    ppermute x12, starting transfers between devices, rep_hop(): return lax.ppermute(array.astype(BF16), 'rep', pairs)  22.6 us
  transfers between devices with their start and end apart: 60, of which 24 were waited for; matrix products, arithmetic and copies ran while one was open for 3% of the time, Pallas kernels for 57%

profile of v9, /device:TPU:0, one launch (start us, length us, event | category | flops | bytes accessed | tf_op | source)
XLA Modules:
  0.0 530.7 jit_solution(7231943159508082660)
XLA Ops:
  5.7 3.0 collective-permute-start
  15.0 4.4 pack_rows.1
  25.6 7.5 %collective-permute-done.5.refs_18_.refs_17_ = bf16[128,1024]{1,0:T(8,128)(2,1)S(1)} collective-permute-done((bf16[128,1024]{1,0:T(8,128)(2,1)S(1)}, bf16[128,1024]{1,0:T(8,128)(2,1)S(1)}, u32[]{:S(2)}, u32[]{:S(2)}) %collective-permute-start.5) | collective-permute-done | bytes 262176 | tf_op jit(solution)/shard_map/ppermute | solution.py:760
  36.0 3.1 collective-permute-done.7.refs_20_.refs_19_
  39.9 15.9 %project.1 = (bf16[1024,1024]{1,0:T(8,128)(2,1)}, bf16[1024,1536]{1,0:T(8,128)(2,1)}, bf16[1024,1536]{1,0:T(8,128)(2,1)}, bf16[16,1024,128]{2,1,0:T(8,128)(2,1)}...) custom-call(s32[1]{0:T(128)} %bitcast.refs_0_, bf16[1024,1024]{1,0:T(8,128)(2,1)} %bitcast.33, ...), custom_call_target="tpu_custom_call" | custom-call | flops 8000000 | bytes 25000 | tf_op jit(solution)/shard_map/project/pallas_call | solution.py:203
  55.9 11.4 %attend.2 = (bf16[1024,512]{1,0:T(8,128)(2,1)}, bf16[8,1024,128]{2,1,0:T(8,128)(2,1)}) custom-call(bf16[16,1024,128]{2,1,0:T(8,128)(2,1)} %get-tuple-element.205.q_ref, bf16[8,1024,128]{2,1,0:T(8,128)(2,1)} %get-tuple-element.213.k_ref, bf16[8,1024,128]{2,1,0:T(8,128)(2,1)} %get-tuple-element.207.v_ref), custom_call_target="tpu_custom_call" | custom-call | flops 10000000 | bytes 8000 | tf_op jit(solution)/shard_map/attend/pallas_call | solution.py:262
  72.7 11.7 %attend.3 = (bf16[1024,512]{1,0:T(8,128)(2,1)}, bf16[8,1024,128]{2,1,0:T(8,128)(2,1)}) custom-call(bf16[16,1024,128]{2,1,0:T(8,128)(2,1)} %get-tuple-element.205.q_ref, bf16[8,1024,128]{2,1,0:T(8,128)(2,1)} %get-tuple-element.213.k_ref, bf16[8,1024,128]{2,1,0:T(8,128)(2,1)} %get-tuple-element.207.v_ref), custom_call_target="tpu_custom_call" | custom-call | flops 10000000 | bytes 8000 | tf_op jit(solution)/shard_map/attend/pallas_call | solution.py:262
  84.4 4.3 collective-permute-done.12.refs_11_.refs_10_.refs_15_
  94.0 2.4 collective-permute-done.17.refs_14_.refs_13_.refs_18_
  97.3 8.3 %output_rows.1 = (f32[1024,1024]{1,0:T(8,128)}, bf16[1024,1024]{1,0:T(8,128)(2,1)}, bf16[1024,1024]{1,0:T(8,128)(2,1)}) custom-call(s32[1]{0:T(128)} %bitcast.refs_0_, bf16[1024,512]{1,0:T(8,128)(2,1)} %get-tuple-element.212.refs_1_.refs_3_.o_ref, bf16[1024,512]{1,0:T(8,128)(2,1)} %get-tuple-element.218.refs_2_.refs_4_.o_ref, bf16[1024,1024]{1,0:T(8,128)(2,1)} %bitcast.34, ...), custom_call_target="tpu_custom_call" | custom-call | flops 5000000 | bytes 15000 | tf_op jit(solution)/shard_map/output_rows/pallas_call | solution.py:379
  105.6 40.6 %feed.3 = (bf16[1024,1024]{1,0:T(8,128)(2,1)}, bf16[1024,1024]{1,0:T(8,128)(2,1)}, bf16[4,576,1024]{2,1,0:T(8,128)(2,1)}, bf16[4,576,1024]{2,1,0:T(8,128)(2,1)}) custom-call(s32[1]{0:T(128)} %bitcast.refs_0_, bf16[1024,1024]{1,0:T(8,128)(2,1)} %get-tuple-element.249.refs_1_, bf16[1024,1024]{1,0:T(8,128)(2,1)} %get-tuple-element.228.refs_2_, ...), custom_call_target="tpu_custom_call" | custom-call | flops 37500000 | bytes 38000 | tf_op jit(solution)/shard_map/feed/pallas_call | solution.py:459
  147.0 2.4 collective-permute-done.22.refs_7_
  156.8 40.6 %feed.4 = (bf16[1024,1024]{1,0:T(8,128)(2,1)}, bf16[1024,1024]{1,0:T(8,128)(2,1)}, bf16[4,576,1024]{2,1,0:T(8,128)(2,1)}, bf16[4,576,1024]{2,1,0:T(8,128)(2,1)}) custom-call(s32[1]{0:T(128)} %bitcast.refs_0_, bf16[1024,1024]{1,0:T(8,128)(2,1)} %get-tuple-element.249.refs_1_, bf16[1024,1024]{1,0:T(8,128)(2,1)} %get-tuple-element.228.refs_2_, ...), custom_call_target="tpu_custom_call" | custom-call | flops 37500000 | bytes 38000 | tf_op jit(solution)/shard_map/feed/pallas_call | solution.py:459
  198.0 4.8 combine.12
  202.8 4.5 collective-permute-done.31.refs_10_
  207.3 3.0 collective-permute-done.32.refs_11_
  210.5 6.4 %collective-permute-start.34 = (bf16[576,1024]{1,0:T(8,128)(2,1)}, bf16[576,1024]{1,0:T(8,128)(2,1)S(1)}, u32[]{:S(2)}, u32[]{:S(2)}) collective-permute-start(bf16[576,1024]{1,0:T(8,128)(2,1)} %get-tuple-element.265), channel_id=1, source_target_pairs={{0,2},{1,3},{2,0},{3,1},{4,6},{5,7},{6,4},{7,5},{8,10},{9,11},{10,... | collective-permute-start | bytes 3538952 | tf_op jit(solution)/shard_map/ppermute | solution.py:760
  219.2 40.6 %feed.5 = (bf16[1024,1024]{1,0:T(8,128)(2,1)}, bf16[1024,1024]{1,0:T(8,128)(2,1)}, bf16[4,576,1024]{2,1,0:T(8,128)(2,1)}, bf16[4,576,1024]{2,1,0:T(8,128)(2,1)}) custom-call(s32[1]{0:T(128)} %bitcast.refs_0_, bf16[1024,1024]{1,0:T(8,128)(2,1)} %get-tuple-element.249.refs_1_, bf16[1024,1024]{1,0:T(8,128)(2,1)} %get-tuple-element.228.refs_2_, ...), custom_call_target="tpu_custom_call" | custom-call | flops 37500000 | bytes 38000 | tf_op jit(solution)/shard_map/feed/pallas_call | solution.py:459
  259.9 10.5 %collective-permute-done.35.refs_3_ = bf16[576,1024]{1,0:T(8,128)(2,1)S(1)} collective-permute-done((bf16[576,1024]{1,0:T(8,128)(2,1)}, bf16[576,1024]{1,0:T(8,128)(2,1)S(1)}, u32[]{:S(2)}, u32[]{:S(2)}) %collective-permute-start.35) | collective-permute-done | bytes 1179680 | tf_op jit(solution)/shard_map/ppermute | solution.py:760
  271.7 4.9 combine.13
  277.7 3.5 collective-permute-start.40
  281.3 14.8 %middle.1 = (f32[1024,1024]{1,0:T(8,128)}, bf16[1024,1024]{1,0:T(8,128)(2,1)}, bf16[1024,1024]{1,0:T(8,128)(2,1)}) custom-call(s32[1]{0:T(128)} %bitcast.refs_0_, f32[1024,1024]{1,0:T(8,128)} %get-tuple-element.348.refs_1_, bf16[1024,1024]{1,0:T(8,128)(2,1)} %bitcast.32, bf16[1024,512]{1,0:T(8,128)(2,1)} %get-tuple-element.212.refs_1_.refs_3_.o_ref, ...), custom_call_target="tpu_custom_call" | custom-call | flops 9000000 | bytes 32000 | tf_op jit(solution)/shard_map/middle/pallas_call | solution.py:529
  296.1 2.6 combine.14
  299.6 19.7 %attend_back.2 = (f32[1024,512]{1,0:T(8,128)}, f32[1024,512]{1,0:T(8,128)}) custom-call(bf16[8,1024,128]{2,1,0:T(8,128)(2,1)} %get-tuple-element.226.q_ref, bf16[8,1024,128]{2,1,0:T(8,128)(2,1)} %get-tuple-element.213.k_ref, bf16[8,1024,128]{2,1,0:T(8,128)(2,1)} %get-tuple-element.207.v_ref, bf16[1024,512]{1,0:T(8,128)(2,1)} %get-tuple-element.212.refs_1_.refs_3_.o_ref, ...), custom_call_target="tpu_custom_call" | custom-call | flops 20000000 | bytes 12000 | tf_op jit(solution)/shard_map/attend_back/pallas_call | solution.py:334
  319.4 6.1 %collective-permute-done.39.refs_9_ = bf16[576,1024]{1,0:T(8,128)(2,1)S(1)} collective-permute-done((bf16[576,1024]{1,0:T(8,128)(2,1)}, bf16[576,1024]{1,0:T(8,128)(2,1)S(1)}, u32[]{:S(2)}, u32[]{:S(2)}) %collective-permute-start.39) | collective-permute-done | bytes 1179680 | tf_op jit(solution)/shard_map/ppermute | solution.py:760
  326.5 8.3 %combine.15 = (bf16[576,1024]{1,0:T(8,128)(2,1)}, bf16[576,1024]{1,0:T(8,128)(2,1)}, bf16[576,1024]{1,0:T(8,128)(2,1)}, bf16[576,1024]{1,0:T(8,128)(2,1)}, bf16[576,1024]{1,0:T(8,128)(2,1)}) custom-call(bf16[4,576,1024]{2,1,0:T(8,128)(2,1)} %get-tuple-element.272.refs_5_.refs_0_.refs_3_, ...), custom_call_target="tpu_custom_call" | custom-call | bytes 4000 | tf_op jit(solution)/shard_map/combine/pallas_call | solution.py:797
  340.6 19.9 %attend_back.3 = (f32[1024,512]{1,0:T(8,128)}, f32[1024,512]{1,0:T(8,128)}) custom-call(bf16[8,1024,128]{2,1,0:T(8,128)(2,1)} %get-tuple-element.291.q_ref, bf16[8,1024,128]{2,1,0:T(8,128)(2,1)} %get-tuple-element.213.k_ref, bf16[8,1024,128]{2,1,0:T(8,128)(2,1)} %get-tuple-element.207.v_ref, bf16[1024,512]{1,0:T(8,128)(2,1)} %get-tuple-element.218.refs_2_.refs_4_.o_ref, ...), custom_call_target="tpu_custom_call" | custom-call | flops 20000000 | bytes 12000 | tf_op jit(solution)/shard_map/attend_back/pallas_call | solution.py:334
  360.4 3.5 collective-permute-done.41.refs_2_
  364.9 4.4 combine.16
  372.2 19.9 %raw_back.1 = (bf16[1024,2048]{1,0:T(8,128)(2,1)}, bf16[4,416,1024]{2,1,0:T(8,128)(2,1)}, bf16[4,416,1024]{2,1,0:T(8,128)(2,1)}) custom-call(s32[1]{0:T(128)} %bitcast.refs_0_, f32[1024,512]{1,0:T(8,128)} %get-tuple-element.290.refs_1_, f32[1024,512]{1,0:T(8,128)} %get-tuple-element.313.refs_2_, f32[1024,512]{1,0:T(8,128)} %get-tuple-element.314.refs_3_, ...), custom_call_target="tpu_custom_call" | custom-call | flops 10000000 | bytes 30000 | tf_op jit(solution)/shard_map/raw_back/pallas_call | solution.py:615
  392.7 4.2 collective-permute-done.47.refs_1_
  397.0 4.4 combine.17
  403.2 2.1 collective-permute-start.49
  405.4 4.9 collective-permute-start.50
  410.2 3.9 combine.18
  417.7 11.2 %input_back.1 = f32[1024,1024]{1,0:T(8,128)} custom-call(s32[1]{0:T(128)} %bitcast.refs_0_, bf16[1024,2048]{1,0:T(8,128)(2,1)} %get-tuple-element.341.refs_1_, bf16[1024,1024]{1,0:T(8,128)(2,1)} %bitcast.35, f32[1024,1024]{1,0:T(8,128)} %get-tuple-element.342.refs_3_, f32[16,1024]{1,0:T(8,128)} %get-tuple-element.219.refs_4_.refs_5_.refs_10_, ...), custom_call_target="tpu_custom_call" | custom-call | flops 6000000 | bytes 18000 | tf_op jit(solution)/shard_map/input_back/pallas_call | solution.py:645
  428.8 5.9 %collective-permute-done.50.refs_3_ = bf16[576,1024]{1,0:T(8,128)(2,1)} collective-permute-done((bf16[576,1024]{1,0:T(8,128)(2,1)}, bf16[576,1024]{1,0:T(8,128)(2,1)}, u32[]{:S(2)}, u32[]{:S(2)}) %collective-permute-start.50) | collective-permute-done | bytes 1179680 | tf_op jit(solution)/shard_map/ppermute | solution.py:811
  434.7 3.5 combine.19
  441.2 6.4 %add_convert_fusion = bf16[1024,1024]{1,0:T(8,128)(2,1)} fusion(f32[1024,1024]{1,0:T(8,128)} %get-tuple-element.348.refs_1_, bf16[1024,1024]{1,0:T(8,128)(2,1)} %get-tuple-element.351, bf16[1024,1024]{1,0:T(8,128)(2,1)} %get-tuple-element.350, bf16[1024,1024]{1,0:T(8,128)(2,1)S(1)} %copy-done.19), kind=kLoop, calls=%fused_computation | loop fusion | flops 7340032 | bytes 12582912 | tf_op jit(solution)/shard_map/convert_element_type | solution.py:1093
  447.7 6.4 %collective-permute-done.52.refs_3_ = bf16[416,1024]{1,0:T(8,128)(2,1)} collective-permute-done((bf16[416,1024]{1,0:T(8,128)(2,1)}, bf16[416,1024]{1,0:T(8,128)(2,1)}, u32[]{:S(2)}, u32[]{:S(2)}) %collective-permute-start.52) | collective-permute-done | bytes 852000 | tf_op jit(solution)/shard_map/ppermute | solution.py:760
  454.0 3.2 combine.20.refs_0_
  458.6 2.6 combine.21.refs_4_
  462.4 13.1 %collective-permute-done.54.refs_1_ = bf16[416,1024]{1,0:T(8,128)(2,1)S(1)} collective-permute-done((bf16[416,1024]{1,0:T(8,128)(2,1)}, bf16[416,1024]{1,0:T(8,128)(2,1)S(1)}, u32[]{:S(2)}, u32[]{:S(2)}) %collective-permute-start.54) | collective-permute-done | bytes 852000 | tf_op jit(solution)/shard_map/ppermute | solution.py:811
  476.5 2.7 combine.22.refs_0_
  479.9 18.1 %collective-permute-done.57.refs_5_ = bf16[576,1024]{1,0:T(8,128)(2,1)S(1)} collective-permute-done((bf16[576,1024]{1,0:T(8,128)(2,1)}, bf16[576,1024]{1,0:T(8,128)(2,1)S(1)}, u32[]{:S(2)}, u32[]{:S(2)}) %collective-permute-start.57) | collective-permute-done | bytes 1179680 | tf_op jit(solution)/shard_map/ppermute | solution.py:811
  498.0 2.7 combine.23
  502.1 7.5 %unpack_rows.1 = (f32[128,4608]{1,0:T(8,128)}, f32[128,4608]{1,0:T(8,128)}, f32[576,1024]{1,0:T(8,128)}) custom-call(s32[1]{0:T(128)} %bitcast.8.flag_ref, bf16[576,1024]{1,0:T(8,128)(2,1)} %get-tuple-element.326.refs_0_, bf16[576,1024]{1,0:T(8,128)(2,1)} %collective-permute-done.47.refs_1_, bf16[576,1024]{1,0:T(8,128)(2,1)} %get-tuple-element.358.refs_2_, ...), custom_call_target="tpu_custom_call" | custom-call | bytes 14000 | tf_op jit(solution)/shard_map/unpack_rows/pallas_call | solution.py:737
  509.5 13.1 %collective-permute-done.59 = bf16[416,1024]{1,0:T(8,128)(2,1)S(1)} collective-permute-done((bf16[416,1024]{1,0:T(8,128)(2,1)}, bf16[416,1024]{1,0:T(8,128)(2,1)S(1)}, u32[]{:S(2)}, u32[]{:S(2)}) %collective-permute-start.59) | collective-permute-done | bytes 852000 | tf_op jit(solution)/shard_map/ppermute | solution.py:811
  (247 shorter events, 80.2 us)
Async XLA Ops:
  5.7 15.6 %collective-permute-start = (bf16[272,1024]{1,0:T(8,128)(2,1)S(1)}, bf16[272,1024]{1,0:T(8,128)(2,1)S(1)}, u32[]{:S(2)}, u32[]{:S(2)}) collective-permute-start(bf16[272,1024]{1,0:T(8,128)(2,1)S(1)} %concatenate.38.refs_6_.refs_7_.refs_22_.refs_5_), channel_id=1, source_target_pairs={{0,2},{1,3},{2,0},{3,1},{4,6},{5,7},{6,4},{7,5},{8,10},{9,11},{10,... | collective-permute-start | bytes 1671176 | tf_op jit(solution)/shard_map/ppermute | solution.py:760
  8.7 14.1 %collective-permute-start.1 = (bf16[272,1024]{1,0:T(8,128)(2,1)S(1)}, bf16[272,1024]{1,0:T(8,128)(2,1)S(1)}, u32[]{:S(2)}, u32[]{:S(2)}) collective-permute-start(bf16[272,1024]{1,0:T(8,128)(2,1)S(1)} %concatenate.38.refs_6_.refs_7_.refs_22_.refs_5_), channel_id=1, source_target_pairs={{0,4},{1,5},{2,6},{3,7},{4,0},{5,1},{6,2},{7,3},{8,12},{9,13},{10,... | collective-permute-start | bytes 1671176 | tf_op jit(solution)/shard_map/ppermute | solution.py:760
  10.2 12.6 %collective-permute-start.2 = (bf16[272,1024]{1,0:T(8,128)(2,1)S(1)}, bf16[272,1024]{1,0:T(8,128)(2,1)S(1)}, u32[]{:S(2)}, u32[]{:S(2)}) collective-permute-start(bf16[272,1024]{1,0:T(8,128)(2,1)S(1)} %concatenate.38.refs_6_.refs_7_.refs_22_.refs_5_), channel_id=1, source_target_pairs={{0,1},{1,0},{2,3},{3,2},{4,5},{5,4},{6,7},{7,6},{8,9},{9,8},{10,11... | collective-permute-start | bytes 1671176 | tf_op jit(solution)/shard_map/ppermute | solution.py:760
  22.8 10.3 %collective-permute-start.3 = (bf16[272,1024]{1,0:T(8,128)(2,1)S(1)}, bf16[272,1024]{1,0:T(8,128)(2,1)S(1)}, u32[]{:S(2)}, u32[]{:S(2)}) collective-permute-start(bf16[272,1024]{1,0:T(8,128)(2,1)S(1)} %collective-permute-done.refs_10_.refs_11_.refs_24_.refs_9_), channel_id=1, source_target_pairs={{0,1},{1,0},{2,3},{3,2},{4,5},{5,4},{6,7},{7,6},{8,9},{9,8},{10,11... | collective-permute-start | bytes 1671176 | tf_op jit(solution)/shard_map/ppermute | solution.py:760
  22.9 10.2 %collective-permute-start.4 = (bf16[272,1024]{1,0:T(8,128)(2,1)S(1)}, bf16[272,1024]{1,0:T(8,128)(2,1)S(1)}, u32[]{:S(2)}, u32[]{:S(2)}) collective-permute-start(bf16[272,1024]{1,0:T(8,128)(2,1)S(1)} %collective-permute-done.1.refs_14_.refs_15_.refs_26_.refs_13_), channel_id=1, source_target_pairs={{0,1},{1,0},{2,3},{3,2},{4,5},{5,4},{6,7},{7,6},{8,9},{9,8},{10,11... | collective-permute-start | bytes 1671176 | tf_op jit(solution)/shard_map/ppermute | solution.py:760
  34.1 33.2 %collective-permute-start.9 = (bf16[704,1024]{1,0:T(8,128)(2,1)}, bf16[704,1024]{1,0:T(8,128)(2,1)S(1)}, u32[]{:S(2)}, u32[]{:S(2)}) collective-permute-start(bf16[704,1024]{1,0:T(8,128)(2,1)} %get-tuple-element.211.refs_5_.refs_4_.refs_9_), channel_id=1, source_target_pairs={{0,2},{1,3},{2,0},{3,1},{4,6},{5,7},{6,4},{7,5},{8,10},{9,11},{10,... | collective-permute-start | bytes 4325384 | tf_op jit(solution)/shard_map/ppermute | solution.py:760
  34.6 32.7 %collective-permute-start.10 = (bf16[704,1024]{1,0:T(8,128)(2,1)}, bf16[704,1024]{1,0:T(8,128)(2,1)S(1)}, u32[]{:S(2)}, u32[]{:S(2)}) collective-permute-start(bf16[704,1024]{1,0:T(8,128)(2,1)} %get-tuple-element.211.refs_5_.refs_4_.refs_9_), channel_id=1, source_target_pairs={{0,4},{1,5},{2,6},{3,7},{4,0},{5,1},{6,2},{7,3},{8,12},{9,13},{10,... | collective-permute-start | bytes 4325384 | tf_op jit(solution)/shard_map/ppermute | solution.py:760
  35.5 31.8 %collective-permute-start.11 = (bf16[704,1024]{1,0:T(8,128)(2,1)}, bf16[704,1024]{1,0:T(8,128)(2,1)}, u32[]{:S(2)}, u32[]{:S(2)}) collective-permute-start(bf16[704,1024]{1,0:T(8,128)(2,1)} %get-tuple-element.211.refs_5_.refs_4_.refs_9_), channel_id=1, source_target_pairs={{0,1},{1,0},{2,3},{3,2},{4,5},{5,4},{6,7},{7,6},{8,9},{9,8},{10,11... | collective-permute-start | bytes 4325384 | tf_op jit(solution)/shard_map/ppermute | solution.py:760
  67.3 22.7 %collective-permute-start.14 = (bf16[704,1024]{1,0:T(8,128)(2,1)S(1)}, bf16[704,1024]{1,0:T(8,128)(2,1)}, u32[]{:S(2)}, u32[]{:S(2)}) collective-permute-start(bf16[704,1024]{1,0:T(8,128)(2,1)S(1)} %collective-permute-done.9.refs_7_.refs_6_.refs_11_), channel_id=1, source_target_pairs={{0,1},{1,0},{2,3},{3,2},{4,5},{5,4},{6,7},{7,6},{8,9},{9,8},{10,11... | collective-permute-start | bytes 4325384 | tf_op jit(solution)/shard_map/ppermute | solution.py:760
  67.8 22.2 %collective-permute-start.15 = (bf16[704,1024]{1,0:T(8,128)(2,1)S(1)}, bf16[704,1024]{1,0:T(8,128)(2,1)}, u32[]{:S(2)}, u32[]{:S(2)}) collective-permute-start(bf16[704,1024]{1,0:T(8,128)(2,1)S(1)} %collective-permute-done.10.refs_9_.refs_8_.refs_13_), channel_id=1, source_target_pairs={{0,1},{1,0},{2,3},{3,2},{4,5},{5,4},{6,7},{7,6},{8,9},{9,8},{10,11... | collective-permute-start | bytes 4325384 | tf_op jit(solution)/shard_map/ppermute | solution.py:760
  70.1 18.6 %collective-permute-start.12 = (bf16[704,512]{1,0:T(8,128)(2,1)}, bf16[704,512]{1,0:T(8,128)(2,1)S(1)}, u32[]{:S(2)}, u32[]{:S(2)}) collective-permute-start(bf16[704,512]{1,0:T(8,128)(2,1)} %slice.65), channel_id=1, source_target_pairs={{0,2},{1,3},{2,0},{3,1},{4,6},{5,7},{6,4},{7,5},{8,10},{9,11},{10,... | collective-permute-start | bytes 2162696 | tf_op jit(solution)/shard_map/ppermute | solution.py:760
  71.6 18.4 %collective-permute-start.13 = (bf16[704,512]{1,0:T(8,128)(2,1)}, bf16[704,512]{1,0:T(8,128)(2,1)}, u32[]{:S(2)}, u32[]{:S(2)}) collective-permute-start(bf16[704,512]{1,0:T(8,128)(2,1)} %slice.66), channel_id=1, source_target_pairs={{0,4},{1,5},{2,6},{3,7},{4,0},{5,1},{6,2},{7,3},{8,12},{9,13},{10,... | collective-permute-start | bytes 2162696 | tf_op jit(solution)/shard_map/ppermute | solution.py:760
  90.0 56.2 %collective-permute-start.18 = (bf16[576,1024]{1,0:T(8,128)(2,1)}, bf16[576,1024]{1,0:T(8,128)(2,1)S(1)}, u32[]{:S(2)}, u32[]{:S(2)}) collective-permute-start(bf16[576,1024]{1,0:T(8,128)(2,1)} %get-tuple-element.234.refs_4_), channel_id=1, source_target_pairs={{0,1},{1,0},{2,3},{3,2},{4,5},{5,4},{6,7},{7,6},{8,9},{9,8},{10,11... | collective-permute-start | bytes 3538952 | tf_op jit(solution)/shard_map/ppermute | solution.py:760
  90.5 55.7 %collective-permute-start.19 = (bf16[576,1024]{1,0:T(8,128)(2,1)}, bf16[576,1024]{1,0:T(8,128)(2,1)}, u32[]{:S(2)}, u32[]{:S(2)}) collective-permute-start(bf16[576,1024]{1,0:T(8,128)(2,1)} %get-tuple-element.234.refs_4_), channel_id=1, source_target_pairs={{0,2},{1,3},{2,0},{3,1},{4,6},{5,7},{6,4},{7,5},{8,10},{9,11},{10,... | collective-permute-start | bytes 3538952 | tf_op jit(solution)/shard_map/ppermute | solution.py:760
  91.1 55.2 %collective-permute-start.20 = (bf16[576,1024]{1,0:T(8,128)(2,1)}, bf16[576,1024]{1,0:T(8,128)(2,1)}, u32[]{:S(2)}, u32[]{:S(2)}) collective-permute-start(bf16[576,1024]{1,0:T(8,128)(2,1)} %get-tuple-element.234.refs_4_), channel_id=1, source_target_pairs={{0,4},{1,5},{2,6},{3,7},{4,0},{5,1},{6,2},{7,3},{8,12},{9,13},{10,... | collective-permute-start | bytes 3538952 | tf_op jit(solution)/shard_map/ppermute | solution.py:760
  92.2 54.1 %collective-permute-start.21 = (bf16[576,1024]{1,0:T(8,128)(2,1)}, bf16[576,1024]{1,0:T(8,128)(2,1)}, u32[]{:S(2)}, u32[]{:S(2)}) collective-permute-start(bf16[576,1024]{1,0:T(8,128)(2,1)} %get-tuple-element.234.refs_4_), channel_id=1, source_target_pairs={{0,6},{1,7},{2,4},{3,5},{4,2},{5,3},{6,0},{7,1},{8,14},{9,15},{10,... | collective-permute-start | bytes 3538952 | tf_op jit(solution)/shard_map/ppermute | solution.py:760
  152.8 44.6 %collective-permute-start.25 = (bf16[4,576,1024]{2,1,0:T(8,128)(2,1)}, bf16[4,576,1024]{2,1,0:T(8,128)(2,1)}, u32[]{:S(2)}, u32[]{:S(2)}) collective-permute-start(bf16[4,576,1024]{2,1,0:T(8,128)(2,1)} %get-tuple-element.246), channel_id=1, source_target_pairs={{0,1},{1,0},{2,3},{3,2},{4,5},{5,4},{6,7},{7,6},{8,9},{9,8},{10,11... | collective-permute-start | bytes 14155784 | tf_op jit(solution)/shard_map/ppermute | solution.py:760
  152.9 44.4 %collective-permute-start.26 = (bf16[576,1024]{1,0:T(8,128)(2,1)S(1)}, bf16[576,1024]{1,0:T(8,128)(2,1)S(1)}, u32[]{:S(2)}, u32[]{:S(2)}) collective-permute-start(bf16[576,1024]{1,0:T(8,128)(2,1)S(1)} %copy-done.20), channel_id=1, source_target_pairs={{0,1},{1,0},{2,3},{3,2},{4,5},{5,4},{6,7},{7,6},{8,9},{9,8},{10,11... | collective-permute-start | bytes 3538952 | tf_op jit(solution)/shard_map/ppermute | solution.py:760
  153.3 44.1 %collective-permute-start.27 = (bf16[576,1024]{1,0:T(8,128)(2,1)S(1)}, bf16[576,1024]{1,0:T(8,128)(2,1)S(1)}, u32[]{:S(2)}, u32[]{:S(2)}) collective-permute-start(bf16[576,1024]{1,0:T(8,128)(2,1)S(1)} %copy-done.20), channel_id=1, source_target_pairs={{0,2},{1,3},{2,0},{3,1},{4,6},{5,7},{6,4},{7,5},{8,10},{9,11},{10,... | collective-permute-start | bytes 3538952 | tf_op jit(solution)/shard_map/ppermute | solution.py:760
  153.8 43.6 %collective-permute-start.28 = (bf16[576,1024]{1,0:T(8,128)(2,1)S(1)}, bf16[576,1024]{1,0:T(8,128)(2,1)}, u32[]{:S(2)}, u32[]{:S(2)}) collective-permute-start(bf16[576,1024]{1,0:T(8,128)(2,1)S(1)} %copy-done.20), channel_id=1, source_target_pairs={{0,4},{1,5},{2,6},{3,7},{4,0},{5,1},{6,2},{7,3},{8,12},{9,13},{10,... | collective-permute-start | bytes 3538952 | tf_op jit(solution)/shard_map/ppermute | solution.py:760
  155.0 52.3 %collective-permute-start.31 = (bf16[576,1024]{1,0:T(8,128)(2,1)S(1)}, bf16[576,1024]{1,0:T(8,128)(2,1)}, u32[]{:S(2)}, u32[]{:S(2)}) collective-permute-start(bf16[576,1024]{1,0:T(8,128)(2,1)S(1)} %copy-done.20), channel_id=1, source_target_pairs={{0,6},{1,7},{2,4},{3,5},{4,2},{5,3},{6,0},{7,1},{8,14},{9,15},{10,... | collective-permute-start | bytes 3538952 | tf_op jit(solution)/shard_map/ppermute | solution.py:760
  197.4 9.9 %collective-permute-start.29 = (bf16[576,1024]{1,0:T(8,128)(2,1)S(1)}, bf16[576,1024]{1,0:T(8,128)(2,1)}, u32[]{:S(2)}, u32[]{:S(2)}) collective-permute-start(bf16[576,1024]{1,0:T(8,128)(2,1)S(1)} %collective-permute-done.27.refs_6_), channel_id=1, source_target_pairs={{0,1},{1,0},{2,3},{3,2},{4,5},{5,4},{6,7},{7,6},{8,9},{9,8},{10,11... | collective-permute-start | bytes 3538952 | tf_op jit(solution)/shard_map/ppermute | solution.py:760
  197.5 9.8 %collective-permute-start.30 = (bf16[576,1024]{1,0:T(8,128)(2,1)}, bf16[576,1024]{1,0:T(8,128)(2,1)}, u32[]{:S(2)}, u32[]{:S(2)}) collective-permute-start(bf16[576,1024]{1,0:T(8,128)(2,1)} %collective-permute-done.28.refs_8_), channel_id=1, source_target_pairs={{0,1},{1,0},{2,3},{3,2},{4,5},{5,4},{6,7},{7,6},{8,9},{9,8},{10,11... | collective-permute-start | bytes 3538952 | tf_op jit(solution)/shard_map/ppermute | solution.py:760
  210.3 60.0 %collective-permute-start.33 = (bf16[4,576,1024]{2,1,0:T(8,128)(2,1)}, bf16[4,576,1024]{2,1,0:T(8,128)(2,1)}, u32[]{:S(2)}, u32[]{:S(2)}) collective-permute-start(bf16[4,576,1024]{2,1,0:T(8,128)(2,1)} %get-tuple-element.264), channel_id=1, source_target_pairs={{0,1},{1,0},{2,3},{3,2},{4,5},{5,4},{6,7},{7,6},{8,9},{9,8},{10,11... | collective-permute-start | bytes 14155784 | tf_op jit(solution)/shard_map/ppermute | solution.py:760
  210.5 49.4 %collective-permute-start.34 = (bf16[576,1024]{1,0:T(8,128)(2,1)}, bf16[576,1024]{1,0:T(8,128)(2,1)S(1)}, u32[]{:S(2)}, u32[]{:S(2)}) collective-permute-start(bf16[576,1024]{1,0:T(8,128)(2,1)} %get-tuple-element.265), channel_id=1, source_target_pairs={{0,2},{1,3},{2,0},{3,1},{4,6},{5,7},{6,4},{7,5},{8,10},{9,11},{10,... | collective-permute-start | bytes 3538952 | tf_op jit(solution)/shard_map/ppermute | solution.py:760
  216.9 53.4 %collective-permute-start.35 = (bf16[576,1024]{1,0:T(8,128)(2,1)}, bf16[576,1024]{1,0:T(8,128)(2,1)S(1)}, u32[]{:S(2)}, u32[]{:S(2)}) collective-permute-start(bf16[576,1024]{1,0:T(8,128)(2,1)} %get-tuple-element.266), channel_id=1, source_target_pairs={{0,4},{1,5},{2,6},{3,7},{4,0},{5,1},{6,2},{7,3},{8,12},{9,13},{10,... | collective-permute-start | bytes 3538952 | tf_op jit(solution)/shard_map/ppermute | solution.py:760
  218.0 52.3 %collective-permute-start.36 = (bf16[576,1024]{1,0:T(8,128)(2,1)}, bf16[576,1024]{1,0:T(8,128)(2,1)S(1)}, u32[]{:S(2)}, u32[]{:S(2)}) collective-permute-start(bf16[576,1024]{1,0:T(8,128)(2,1)} %get-tuple-element.267), channel_id=1, source_target_pairs={{0,6},{1,7},{2,4},{3,5},{4,2},{5,3},{6,0},{7,1},{8,14},{9,15},{10,... | collective-permute-start | bytes 3538952 | tf_op jit(solution)/shard_map/ppermute | solution.py:760
  270.3 25.8 %collective-permute-start.37 = (bf16[4,576,1024]{2,1,0:T(8,128)(2,1)}, bf16[4,576,1024]{2,1,0:T(8,128)(2,1)}, u32[]{:S(2)}, u32[]{:S(2)}) collective-permute-start(bf16[4,576,1024]{2,1,0:T(8,128)(2,1)} %get-tuple-element.280), channel_id=1, source_target_pairs={{0,1},{1,0},{2,3},{3,2},{4,5},{5,4},{6,7},{7,6},{8,9},{9,8},{10,11... | collective-permute-start | bytes 14155784 | tf_op jit(solution)/shard_map/ppermute | solution.py:760
  276.6 42.7 %collective-permute-start.38 = (bf16[576,1024]{1,0:T(8,128)(2,1)}, bf16[576,1024]{1,0:T(8,128)(2,1)S(1)}, u32[]{:S(2)}, u32[]{:S(2)}) collective-permute-start(bf16[576,1024]{1,0:T(8,128)(2,1)} %get-tuple-element.287), channel_id=1, source_target_pairs={{0,4},{1,5},{2,6},{3,7},{4,0},{5,1},{6,2},{7,3},{8,12},{9,13},{10,... | collective-permute-start | bytes 3538952 | tf_op jit(solution)/shard_map/ppermute | solution.py:760
  277.7 41.6 %collective-permute-start.40 = (bf16[576,1024]{1,0:T(8,128)(2,1)}, bf16[576,1024]{1,0:T(8,128)(2,1)S(1)}, u32[]{:S(2)}, u32[]{:S(2)}) collective-permute-start(bf16[576,1024]{1,0:T(8,128)(2,1)} %get-tuple-element.289.refs_10_), channel_id=1, source_target_pairs={{0,8},{24,16},{1,9},{25,17},{2,10},{26,18},{3,11},{27,19},{4,12},{... | collective-permute-start | bytes 3538952 | tf_op jit(solution)/shard_map/ppermute | solution.py:811
  298.7 26.8 %collective-permute-start.39 = (bf16[576,1024]{1,0:T(8,128)(2,1)}, bf16[576,1024]{1,0:T(8,128)(2,1)S(1)}, u32[]{:S(2)}, u32[]{:S(2)}) collective-permute-start(bf16[576,1024]{1,0:T(8,128)(2,1)} %combine.14), channel_id=1, source_target_pairs={{0,2},{1,3},{2,0},{3,1},{4,6},{5,7},{6,4},{7,5},{8,10},{9,11},{10,... | collective-permute-start | bytes 3538952 | tf_op jit(solution)/shard_map/ppermute | solution.py:760
  334.8 29.2 %collective-permute-start.41 = (bf16[576,1024]{1,0:T(8,128)(2,1)}, bf16[576,1024]{1,0:T(8,128)(2,1)S(1)}, u32[]{:S(2)}, u32[]{:S(2)}) collective-permute-start(bf16[576,1024]{1,0:T(8,128)(2,1)} %get-tuple-element.304), channel_id=1, source_target_pairs={{0,2},{1,3},{2,0},{3,1},{4,6},{5,7},{6,4},{7,5},{8,10},{9,11},{10,... | collective-permute-start | bytes 3538952 | tf_op jit(solution)/shard_map/ppermute | solution.py:760
  335.7 29.2 %collective-permute-start.42 = (bf16[576,1024]{1,0:T(8,128)(2,1)}, bf16[576,1024]{1,0:T(8,128)(2,1)}, u32[]{:S(2)}, u32[]{:S(2)}) collective-permute-start(bf16[576,1024]{1,0:T(8,128)(2,1)} %get-tuple-element.305), channel_id=1, source_target_pairs={{0,4},{1,5},{2,6},{3,7},{4,0},{5,1},{6,2},{7,3},{8,12},{9,13},{10,... | collective-permute-start | bytes 3538952 | tf_op jit(solution)/shard_map/ppermute | solution.py:760
  336.5 28.4 %collective-permute-start.43 = (bf16[576,1024]{1,0:T(8,128)(2,1)}, bf16[576,1024]{1,0:T(8,128)(2,1)}, u32[]{:S(2)}, u32[]{:S(2)}) collective-permute-start(bf16[576,1024]{1,0:T(8,128)(2,1)} %get-tuple-element.306.refs_4_), channel_id=1, source_target_pairs={{8,16},{16,8},{9,17},{17,9},{10,18},{18,10},{11,19},{19,11},{12,20... | collective-permute-start | bytes 3538952 | tf_op jit(solution)/shard_map/ppermute | solution.py:811
  338.2 53.9 %collective-permute-start.44 = (bf16[576,1024]{1,0:T(8,128)(2,1)}, bf16[576,1024]{1,0:T(8,128)(2,1)S(1)}, u32[]{:S(2)}, u32[]{:S(2)}) collective-permute-start(bf16[576,1024]{1,0:T(8,128)(2,1)} %get-tuple-element.323), channel_id=1, source_target_pairs={{0,2},{1,3},{2,0},{3,1},{4,6},{5,7},{6,4},{7,5},{8,10},{9,11},{10,... | collective-permute-start | bytes 3538952 | tf_op jit(solution)/shard_map/ppermute | solution.py:760
  339.4 52.8 %collective-permute-start.45 = (bf16[576,1024]{1,0:T(8,128)(2,1)}, bf16[576,1024]{1,0:T(8,128)(2,1)S(1)}, u32[]{:S(2)}, u32[]{:S(2)}) collective-permute-start(bf16[576,1024]{1,0:T(8,128)(2,1)} %get-tuple-element.324), channel_id=1, source_target_pairs={{0,4},{1,5},{2,6},{3,7},{4,0},{5,1},{6,2},{7,3},{8,12},{9,13},{10,... | collective-permute-start | bytes 3538952 | tf_op jit(solution)/shard_map/ppermute | solution.py:760
  369.3 23.4 %collective-permute-start.46 = (bf16[576,1024]{1,0:T(8,128)(2,1)}, bf16[576,1024]{1,0:T(8,128)(2,1)S(1)}, u32[]{:S(2)}, u32[]{:S(2)}) collective-permute-start(bf16[576,1024]{1,0:T(8,128)(2,1)} %get-tuple-element.325.refs_0_), channel_id=1, source_target_pairs={{0,8},{24,16},{1,9},{25,17},{2,10},{26,18},{3,11},{27,19},{4,12},{... | collective-permute-start | bytes 3538952 | tf_op jit(solution)/shard_map/ppermute | solution.py:811
  370.9 26.0 %collective-permute-start.47 = (bf16[576,1024]{1,0:T(8,128)(2,1)}, bf16[576,1024]{1,0:T(8,128)(2,1)}, u32[]{:S(2)}, u32[]{:S(2)}) collective-permute-start(bf16[576,1024]{1,0:T(8,128)(2,1)} %get-tuple-element.326.refs_0_), channel_id=1, source_target_pairs={{8,0},{16,24},{9,1},{17,25},{10,2},{18,26},{11,3},{19,27},{12,4},{... | collective-permute-start | bytes 3538952 | tf_op jit(solution)/shard_map/ppermute | solution.py:811
  403.2 25.6 %collective-permute-start.49 = (bf16[576,1024]{1,0:T(8,128)(2,1)}, bf16[576,1024]{1,0:T(8,128)(2,1)}, u32[]{:S(2)}, u32[]{:S(2)}) collective-permute-start(bf16[576,1024]{1,0:T(8,128)(2,1)} %get-tuple-element.334.refs_0_), channel_id=1, source_target_pairs={{8,16},{16,8},{9,17},{17,9},{10,18},{18,10},{11,19},{19,11},{12,20... | collective-permute-start | bytes 3538952 | tf_op jit(solution)/shard_map/ppermute | solution.py:811
  405.4 29.4 %collective-permute-start.50 = (bf16[576,1024]{1,0:T(8,128)(2,1)}, bf16[576,1024]{1,0:T(8,128)(2,1)}, u32[]{:S(2)}, u32[]{:S(2)}) collective-permute-start(bf16[576,1024]{1,0:T(8,128)(2,1)} %get-tuple-element.343.refs_2_), channel_id=1, source_target_pairs={{0,8},{24,16},{1,9},{25,17},{2,10},{26,18},{3,11},{27,19},{4,12},{... | collective-permute-start | bytes 3538952 | tf_op jit(solution)/shard_map/ppermute | solution.py:811
  414.2 33.5 %collective-permute-start.51 = (bf16[416,1024]{1,0:T(8,128)(2,1)}, bf16[416,1024]{1,0:T(8,128)(2,1)S(1)}, u32[]{:S(2)}, u32[]{:S(2)}) collective-permute-start(bf16[416,1024]{1,0:T(8,128)(2,1)} %get-tuple-element.352), channel_id=1, source_target_pairs={{0,2},{1,3},{2,0},{3,1},{4,6},{5,7},{6,4},{7,5},{8,10},{9,11},{10,... | collective-permute-start | bytes 2555912 | tf_op jit(solution)/shard_map/ppermute | solution.py:760
  415.3 38.7 %collective-permute-start.52 = (bf16[416,1024]{1,0:T(8,128)(2,1)}, bf16[416,1024]{1,0:T(8,128)(2,1)}, u32[]{:S(2)}, u32[]{:S(2)}) collective-permute-start(bf16[416,1024]{1,0:T(8,128)(2,1)} %get-tuple-element.353), channel_id=1, source_target_pairs={{0,4},{1,5},{2,6},{3,7},{4,0},{5,1},{6,2},{7,3},{8,12},{9,13},{10,... | collective-permute-start | bytes 2555912 | tf_op jit(solution)/shard_map/ppermute | solution.py:760
  416.1 37.9 %collective-permute-start.53 = (bf16[416,1024]{1,0:T(8,128)(2,1)}, bf16[416,1024]{1,0:T(8,128)(2,1)}, u32[]{:S(2)}, u32[]{:S(2)}) collective-permute-start(bf16[416,1024]{1,0:T(8,128)(2,1)} %get-tuple-element.354), channel_id=1, source_target_pairs={{0,6},{1,7},{2,4},{3,5},{4,2},{5,3},{6,0},{7,1},{8,14},{9,15},{10,... | collective-permute-start | bytes 2555912 | tf_op jit(solution)/shard_map/ppermute | solution.py:760
  438.3 20.3 %collective-permute-start.56 = (bf16[576,1024]{1,0:T(8,128)(2,1)}, bf16[576,1024]{1,0:T(8,128)(2,1)}, u32[]{:S(2)}, u32[]{:S(2)}) collective-permute-start(bf16[576,1024]{1,0:T(8,128)(2,1)} %get-tuple-element.362.refs_0_), channel_id=1, source_target_pairs={{8,16},{16,8},{9,17},{17,9},{10,18},{18,10},{11,19},{19,11},{12,20... | collective-permute-start | bytes 3538952 | tf_op jit(solution)/shard_map/ppermute | solution.py:811
  439.9 35.6 %collective-permute-start.55 = (bf16[576,1024]{1,0:T(8,128)(2,1)}, bf16[576,1024]{1,0:T(8,128)(2,1)S(1)}, u32[]{:S(2)}, u32[]{:S(2)}) collective-permute-start(bf16[576,1024]{1,0:T(8,128)(2,1)} %get-tuple-element.358.refs_2_), channel_id=1, source_target_pairs={{8,0},{16,24},{9,1},{17,25},{10,2},{18,26},{11,3},{19,27},{12,4},{... | collective-permute-start | bytes 3538952 | tf_op jit(solution)/shard_map/ppermute | solution.py:811
  457.2 18.4 %collective-permute-start.54 = (bf16[416,1024]{1,0:T(8,128)(2,1)}, bf16[416,1024]{1,0:T(8,128)(2,1)S(1)}, u32[]{:S(2)}, u32[]{:S(2)}) collective-permute-start(bf16[416,1024]{1,0:T(8,128)(2,1)} %combine.20.refs_0_), channel_id=1, source_target_pairs={{0,8},{24,16},{1,9},{25,17},{2,10},{26,18},{3,11},{27,19},{4,12},{... | collective-permute-start | bytes 2555912 | tf_op jit(solution)/shard_map/ppermute | solution.py:811
  461.2 36.9 %collective-permute-start.57 = (bf16[576,1024]{1,0:T(8,128)(2,1)}, bf16[576,1024]{1,0:T(8,128)(2,1)S(1)}, u32[]{:S(2)}, u32[]{:S(2)}) collective-permute-start(bf16[576,1024]{1,0:T(8,128)(2,1)} %combine.21.refs_4_), channel_id=1, source_target_pairs={{8,0},{16,24},{9,1},{17,25},{10,2},{18,26},{11,3},{19,27},{12,4},{... | collective-permute-start | bytes 3538952 | tf_op jit(solution)/shard_map/ppermute | solution.py:811
  500.7 21.9 %collective-permute-start.59 = (bf16[416,1024]{1,0:T(8,128)(2,1)}, bf16[416,1024]{1,0:T(8,128)(2,1)S(1)}, u32[]{:S(2)}, u32[]{:S(2)}) collective-permute-start(bf16[416,1024]{1,0:T(8,128)(2,1)} %combine.23), channel_id=1, source_target_pairs={{8,0},{16,24},{9,1},{17,25},{10,2},{18,26},{11,3},{19,27},{12,4},{... | collective-permute-start | bytes 2555912 | tf_op jit(solution)/shard_map/ppermute | solution.py:811
  (63 other events, 405.5 us)

commit v10 on v9

--- a/solution.py
+++ b/solution.py
@@ -13,7 +13,6 @@
 FAR = 32768.0
 TILE = 256
 SLAB = 512
-VMEM_LIMIT = 60 * 1024 * 1024
 NT = ((1,), (1,))
 NN = ((1,), (0,))
 TN = ((0,), (0,))
@@ -26,8 +25,8 @@
     return lax.dot_general(left, right, (dims, ((), ())), preferred_element_type=F32)
 
 
-def params():
-    return pltpu.CompilerParams(vmem_limit_bytes=VMEM_LIMIT)
+def params(mega_bytes=60):
+    return pltpu.CompilerParams(vmem_limit_bytes=mega_bytes * 1024 * 1024)
 
 
 def cost(giga_flops, mega_bytes, exps=0):
@@ -219,7 +218,7 @@
             jax.ShapeDtypeStruct((16, 1024), F32),
         ],
         scratch_shapes=[pltpu.VMEM((width, 2048), BF16)],
-        compiler_params=params(),
+        compiler_params=params(32),
         cost_estimate=cost(8, 25),
         name="project",
     )(me, x, *tables, *arrays, *[array for array, _ in gains])
@@ -275,7 +274,7 @@
             jax.ShapeDtypeStruct((length, groups * 128), BF16),
             jax.ShapeDtypeStruct((2 * groups, length, 128), BF16),
         ],
-        compiler_params=params(),
+        compiler_params=params(32),
         cost_estimate=cost(2.5 * groups, 2 * groups, groups * 2**20),
         name="attend",
     )(q_aug, k_aug, v_aug)
@@ -348,7 +347,7 @@
             pltpu.VMEM((64, length), BF16),
             pltpu.VMEM((128, length), F32),
         ],
-        compiler_params=params(),
+        compiler_params=params(36),
         cost_estimate=cost(5 * groups, 3 * groups, groups * 2**20),
         name="attend_back",
     )(q_back, k_aug, v_aug, attended, back_attended)
@@ -388,7 +387,7 @@
             jax.ShapeDtypeStruct((width, length), BF16),
         ],
         scratch_shapes=[pltpu.VMEM((1024, width), BF16)],
-        compiler_params=params(),
+        compiler_params=params(32),
         cost_estimate=cost(5, 15),
         name="output_rows",
     )(me, *attended, x, gain, *pieces.arrays)
@@ -539,7 +538,7 @@
             jax.ShapeDtypeStruct((1024, width), BF16),
         ],
         scratch_shapes=[pltpu.VMEM((1024, width), BF16), pltpu.VMEM((1024, width), F32)],
-        compiler_params=params(),
+        compiler_params=params(32),
         cost_estimate=cost(9, 32),
         name="middle",
     )(me, first_sum, cotangent, *attended, gain, *backs, *pieces.arrays)
@@ -622,7 +621,7 @@
         out_shape=[jax.ShapeDtypeStruct((length, 2048), BF16)]
         + [jax.ShapeDtypeStruct((parts // 2, rows, 1024), BF16)] * 2,
         scratch_shapes=[pltpu.VMEM((width, 2048), F32), pltpu.VMEM((32, 128), F32)],
-        compiler_params=params(),
+        compiler_params=params(44),
         cost_estimate=cost(10, 30),
         name="raw_back",
     )(me, *halves, *units, normed, cosine, sine, gains, grad_out)
@@ -649,7 +648,7 @@
         out_specs=by_rows(width),
         out_shape=jax.ShapeDtypeStruct((length, width), F32),
         scratch_shapes=[pltpu.VMEM((width, 2048), BF16)],
-        compiler_params=params(),
+        compiler_params=params(32),
         cost_estimate=cost(6, 18),
         name="input_back",
     )(me, back_raw, x, back_first, gain, *arrays)
@@ -699,7 +698,7 @@
             jax.ShapeDtypeStruct((n * 192 + (0 if c else 128), 1024), BF16)
             for c, n in enumerate(chunks)
         ],
-        compiler_params=params(),
+        compiler_params=params(32),
         cost_estimate=cost(0, 7),
         name="pack_rows",
     )(w_output, w_gate, w_up, w_down)
@@ -742,7 +741,7 @@
             jax.ShapeDtypeStruct((128, 4608), F32),
             jax.ShapeDtypeStruct((576, 1024), F32),
         ],
-        compiler_params=params(),
+        compiler_params=params(44),
         cost_estimate=cost(0, 14),
         name="unpack_rows",
     )(flag, *totals)
@@ -800,7 +799,7 @@
         in_specs=[spec(k) for _, k in terms],
         out_specs=[pl.BlockSpec((step, width), lambda i: (i, 0))] * len(outputs),
         out_shape=[jax.ShapeDtypeStruct((rows, width), BF16)] * len(outputs),
-        compiler_params=params(),
+        compiler_params=params(30),
         cost_estimate=cost(0, 4),
         name="combine",
     )(*[array for array, _ in terms])

time: 540 us -> 568 us (1.052)
  local copies, waits for them, and re-layouts: 16.4 us -> 88.9 us
  Pallas kernels: 314 us -> 267 us
    unnamed x104 -> x252, local copies, waits for them, and re-layouts: 9.97 us -> 84.4 us
    pallas_call x12, Pallas kernels: 47.8 us -> 24.4 us  [combine(): pl.pallas_call(kernel, grid=(rows // step,), in_specs=[spec(k) for _, k i...]
  transfers between devices with their start and end apart: 60 -> 60, of which waited for: 24 -> 21; matrix products, arithmetic and copies ran while one was open for 3% -> 2% of each run, Pallas kernels for 57% -> 47%
where the time goes in v10:
time: 568 us; the launch traced here: 558 us
  Pallas kernels  267 us (47%)
  waiting for transfers between devices  121 us (21%)
  local copies, waits for them, and re-layouts  88.9 us (16%)
  starting transfers between devices  63.9 us (11%)
  other arithmetic  15.3 us (3%)
    pallas_call x3, Pallas kernels, feed(): pl.pallas_call(lambda *refs: feed_kernel(pieces.layout, paired, *refs), g...  122 us
    unnamed x252, local copies, waits for them, and re-layouts  84.4 us
    ppermute x48, waiting for transfers between devices, hop(): return lax.ppermute(array, 'shard', [(i, i ^ bit) for i in range(8)])  61.1 us
    ppermute x12, waiting for transfers between devices, rep_hop(): return lax.ppermute(array.astype(BF16), 'rep', pairs)  59.7 us
    ppermute x48, starting transfers between devices, hop(): return lax.ppermute(array, 'shard', [(i, i ^ bit) for i in range(8)])  40.7 us
    pallas_call x2, Pallas kernels, attend_back(): pl.pallas_call(attend_back_kernel, grid=(groups,), in_specs=[pl.BlockSpec...  36.5 us
    pallas_call x12, Pallas kernels, combine(): pl.pallas_call(kernel, grid=(rows // step,), in_specs=[spec(k) for _, k i...  24.4 us
    ppermute x12, starting transfers between devices, rep_hop(): return lax.ppermute(array.astype(BF16), 'rep', pairs)  23.2 us
  transfers between devices with their start and end apart: 60, of which 21 were waited for; matrix products, arithmetic and copies ran while one was open for 2% of the time, Pallas kernels for 47%

profile of v10, /device:TPU:0, one launch (start us, length us, event | category | flops | bytes accessed | tf_op | source)
XLA Modules:
  0.0 558.3 jit_solution(4224939795848562709)
XLA Ops:
  5.7 3.0 collective-permute-start
  14.6 2.1 pack_rows.1
  17.3 4.1 collective-permute-done.refs_10_.refs_11_.refs_24_.refs_9_
  25.6 7.5 %collective-permute-done.5.refs_18_.refs_17_ = bf16[128,1024]{1,0:T(8,128)(2,1)S(1)} collective-permute-done((bf16[128,1024]{1,0:T(8,128)(2,1)S(1)}, bf16[128,1024]{1,0:T(8,128)(2,1)S(1)}, u32[]{:S(2)}, u32[]{:S(2)}) %collective-permute-start.5) | collective-permute-done | bytes 262176 | tf_op jit(solution)/shard_map/ppermute | solution.py:759
  35.1 3.1 collective-permute-done.7.refs_20_.refs_19_
  38.3 12.8 %project.1 = (bf16[1024,1024]{1,0:T(8,128)(2,1)S(1)}, bf16[1024,1536]{1,0:T(8,128)(2,1)S(1)}, bf16[1024,1536]{1,0:T(8,128)(2,1)S(1)}, bf16[16,1024,128]{2,1,0:T(...) custom-call(s32[1]{0:T(128)} %bitcast.refs_0_, ...), custom_call_target="tpu_custom_call" | custom-call | flops 8000000 | bytes 25000 | tf_op jit(solution)/shard_map/project/pallas_call | solution.py:202
  54.2 4.8 copy-done.20
  59.0 9.4 %attend.2 = (bf16[1024,512]{1,0:T(8,128)(2,1)S(1)}, bf16[8,1024,128]{2,1,0:T(8,128)(2,1)S(1)}) custom-call(bf16[16,1024,128]{2,1,0:T(8,128)(2,1)S(1)} %copy-done.20, bf16[8,1024,128]{2,1,0:T(8,128)(2,1)S(1)} %get-tuple-element.213.k_ref, bf16[8,1024,128]{2,1,0:T(8,128)(2,1)S(1)} %get-tuple-element.207.v_ref), custom_call_target="tpu_custom_call" | custom-call | flops 10000000 | bytes 8000 | tf_op jit(solution)/shard_map/attend/pallas_call | solution.py:261
  73.2 9.7 %attend.3 = (bf16[1024,512]{1,0:T(8,128)(2,1)S(1)}, bf16[8,1024,128]{2,1,0:T(8,128)(2,1)S(1)}) custom-call(bf16[16,1024,128]{2,1,0:T(8,128)(2,1)S(1)} %copy-done.20, bf16[8,1024,128]{2,1,0:T(8,128)(2,1)S(1)} %get-tuple-element.213.k_ref, bf16[8,1024,128]{2,1,0:T(8,128)(2,1)S(1)} %get-tuple-element.207.v_ref), custom_call_target="tpu_custom_call" | custom-call | flops 10000000 | bytes 8000 | tf_op jit(solution)/shard_map/attend/pallas_call | solution.py:261
  84.3 4.7 collective-permute-done.12.refs_11_.refs_10_.refs_15_
  95.3 2.2 collective-permute-done.17.refs_14_.refs_13_.refs_18_
  100.5 6.1 %output_rows.1 = (f32[1024,1024]{1,0:T(8,128)}, bf16[1024,1024]{1,0:T(8,128)(2,1)S(1)}, bf16[1024,1024]{1,0:T(8,128)(2,1)S(1)}) custom-call(s32[1]{0:T(128)} %bitcast.refs_0_, bf16[1024,512]{1,0:T(8,128)(2,1)S(1)} %get-tuple-element.212.refs_1_.refs_3_.o_ref, bf16[1024,512]{1,0:T(8,128)(2,1)S(1)} %get-tuple-element.218.refs_2_.refs_4_.o_ref, ...), custom_call_target="tpu_custom_call" | custom-call | flops 5000000 | bytes 15000 | tf_op jit(solution)/shard_map/output_rows/pallas_call | solution.py:378
  112.0 40.6 %feed.3 = (bf16[1024,1024]{1,0:T(8,128)(2,1)}, bf16[1024,1024]{1,0:T(8,128)(2,1)}, bf16[4,576,1024]{2,1,0:T(8,128)(2,1)}, bf16[4,576,1024]{2,1,0:T(8,128)(2,1)}) custom-call(s32[1]{0:T(128)} %bitcast.refs_0_, bf16[1024,1024]{1,0:T(8,128)(2,1)} %copy-done.14, bf16[1024,1024]{1,0:T(8,128)(2,1)} %copy-done.15, bf16[1024,1024]{1,0:T(8,128)(2,1)} %bitcast.35, ...), custom_call_target="tpu_custom_call" | custom-call | flops 37500000 | bytes 38000 | tf_op jit(solution)/shard_map/feed/pallas_call | solution.py:458
  153.4 2.4 collective-permute-done.22.refs_7_
  163.2 40.6 %feed.4 = (bf16[1024,1024]{1,0:T(8,128)(2,1)}, bf16[1024,1024]{1,0:T(8,128)(2,1)}, bf16[4,576,1024]{2,1,0:T(8,128)(2,1)}, bf16[4,576,1024]{2,1,0:T(8,128)(2,1)}) custom-call(s32[1]{0:T(128)} %bitcast.refs_0_, bf16[1024,1024]{1,0:T(8,128)(2,1)} %copy-done.14, bf16[1024,1024]{1,0:T(8,128)(2,1)} %copy-done.15, bf16[1024,1024]{1,0:T(8,128)(2,1)} %bitcast.36, ...), custom_call_target="tpu_custom_call" | custom-call | flops 37500000 | bytes 38000 | tf_op jit(solution)/shard_map/feed/pallas_call | solution.py:458
  204.4 2.3 copy-done
  206.7 3.7 combine.12
  210.4 3.3 collective-permute-done.31.refs_10_
  213.7 3.0 collective-permute-done.32.refs_11_
  216.9 7.8 %collective-permute-start.34 = (bf16[576,1024]{1,0:T(8,128)(2,1)}, bf16[576,1024]{1,0:T(8,128)(2,1)S(1)}, u32[]{:S(2)}, u32[]{:S(2)}) collective-permute-start(bf16[576,1024]{1,0:T(8,128)(2,1)} %get-tuple-element.265), channel_id=1, source_target_pairs={{0,2},{1,3},{2,0},{3,1},{4,6},{5,7},{6,4},{7,5},{8,10},{9,11},{10,... | collective-permute-start | bytes 3538952 | tf_op jit(solution)/shard_map/ppermute | solution.py:759
  226.2 40.7 %feed.5 = (bf16[1024,1024]{1,0:T(8,128)(2,1)}, bf16[1024,1024]{1,0:T(8,128)(2,1)}, bf16[4,576,1024]{2,1,0:T(8,128)(2,1)}, bf16[4,576,1024]{2,1,0:T(8,128)(2,1)}) custom-call(s32[1]{0:T(128)} %bitcast.refs_0_, bf16[1024,1024]{1,0:T(8,128)(2,1)} %copy-done.14, bf16[1024,1024]{1,0:T(8,128)(2,1)} %copy-done.15, bf16[1024,1024]{1,0:T(8,128)(2,1)} %bitcast.37, ...), custom_call_target="tpu_custom_call" | custom-call | flops 37500000 | bytes 38000 | tf_op jit(solution)/shard_map/feed/pallas_call | solution.py:458
  266.9 11.2 %collective-permute-done.35.refs_3_ = bf16[576,1024]{1,0:T(8,128)(2,1)S(1)} collective-permute-done((bf16[576,1024]{1,0:T(8,128)(2,1)}, bf16[576,1024]{1,0:T(8,128)(2,1)S(1)}, u32[]{:S(2)}, u32[]{:S(2)}) %collective-permute-start.35) | collective-permute-done | bytes 1179680 | tf_op jit(solution)/shard_map/ppermute | solution.py:759
  278.1 2.3 copy-done.1
  280.4 2.3 copy-done.2
  282.8 3.5 combine.13
  287.4 4.5 collective-permute-start.40
  309.9 12.6 %middle.1 = (f32[1024,1024]{1,0:T(8,128)}, bf16[1024,1024]{1,0:T(8,128)(2,1)S(1)}, bf16[1024,1024]{1,0:T(8,128)(2,1)S(1)}) custom-call(s32[1]{0:T(128)} %bitcast.refs_0_, f32[1024,1024]{1,0:T(8,128)} %get-tuple-element.348.refs_1_, bf16[1024,1024]{1,0:T(8,128)(2,1)S(1)} %bitcast.38, bf16[1024,512]{1,0:T(8,128)(2,1)S(1)} %copy-done.41, ...), custom_call_target="tpu_custom_call" | custom-call | flops 9000000 | bytes 32000 | tf_op jit(solution)/shard_map/middle/pallas_call | solution.py:528
  325.1 2.1 copy-done.3
  327.2 2.5 copy-done.4
  335.6 18.2 %attend_back.2 = (f32[1024,512]{1,0:T(8,128)S(1)}, f32[1024,512]{1,0:T(8,128)S(1)}) custom-call(bf16[8,1024,128]{2,1,0:T(8,128)(2,1)S(1)} %copy-done.80, bf16[8,1024,128]{2,1,0:T(8,128)(2,1)S(1)} %copy-done.8, bf16[8,1024,128]{2,1,0:T(8,128)(2,1)S(1)} %copy-done.10, bf16[1024,512]{1,0:T(8,128)(2,1)S(1)} %copy-done.42, bf16[1024,1024]{1,0:T(8,128)(2,1)S(1)} %copy-done.44), custom_call_target="tpu_custom_call" | custom-call | flops 20000000 | bytes 12000 | tf_op jit(solution)/shard_map/attend_back/pallas_call | solution.py:333
  360.3 5.7 %combine.15 = (bf16[576,1024]{1,0:T(8,128)(2,1)}, bf16[576,1024]{1,0:T(8,128)(2,1)}, bf16[576,1024]{1,0:T(8,128)(2,1)}, bf16[576,1024]{1,0:T(8,128)(2,1)}, bf16[576,1024]{1,0:T(8,128)(2,1)}) custom-call(bf16[4,576,1024]{2,1,0:T(8,128)(2,1)S(1)} %bitcast.30, bf16[4,576,1024]{2,1,0:T(8,128)(2,1)} %collective-permute-done.33.refs_6_.refs_1_.refs_4_, ...), custom_call_target="tpu_custom_call" | custom-call | bytes 4000 | tf_op jit(solution)/shard_map/combine/pallas_call | solution.py:796
  377.7 18.3 %attend_back.3 = (f32[1024,512]{1,0:T(8,128)S(1)}, f32[1024,512]{1,0:T(8,128)S(1)}) custom-call(bf16[8,1024,128]{2,1,0:T(8,128)(2,1)S(1)} %copy-done.78, bf16[8,1024,128]{2,1,0:T(8,128)(2,1)S(1)} %copy-done.8, bf16[8,1024,128]{2,1,0:T(8,128)(2,1)S(1)} %copy-done.11, bf16[1024,512]{1,0:T(8,128)(2,1)S(1)} %copy-done.39, bf16[1024,1024]{1,0:T(8,128)(2,1)S(1)} %copy-done.45), custom_call_target="tpu_custom_call" | custom-call | flops 20000000 | bytes 12000 | tf_op jit(solution)/shard_map/attend_back/pallas_call | solution.py:333
  398.4 3.5 combine.16
  401.8 3.5 collective-permute-start.46
  411.5 18.6 %raw_back.1 = (bf16[1024,2048]{1,0:T(8,128)(2,1)}, bf16[4,416,1024]{2,1,0:T(8,128)(2,1)}, bf16[4,416,1024]{2,1,0:T(8,128)(2,1)}) custom-call(s32[1]{0:T(128)} %bitcast.refs_0_, f32[1024,512]{1,0:T(8,128)S(1)} %copy-done.74, f32[1024,512]{1,0:T(8,128)S(1)} %get-tuple-element.313.refs_2_, f32[1024,512]{1,0:T(8,128)S(1)} %copy-done.76, ...), custom_call_target="tpu_custom_call" | custom-call | flops 10000000 | bytes 30000 | tf_op jit(solution)/shard_map/raw_back/pallas_call | solution.py:614
  430.2 3.0 collective-permute-done.47.refs_1_
  433.2 2.9 combine.17
  436.1 3.3 collective-permute-done.48.refs_1_.refs_3_.refs_5_
  440.3 4.5 collective-permute-start.50
  444.9 1.9 combine.18
  450.4 7.4 %input_back.1 = f32[1024,1024]{1,0:T(8,128)} custom-call(s32[1]{0:T(128)} %bitcast.refs_0_, bf16[1024,2048]{1,0:T(8,128)(2,1)S(1)} %copy-done.63, bf16[1024,1024]{1,0:T(8,128)(2,1)S(1)} %bitcast.41, f32[1024,1024]{1,0:T(8,128)S(1)} %copy-done.62, f32[16,1024]{1,0:T(8,128)S(1)} %copy-done.97, ...), custom_call_target="tpu_custom_call" | custom-call | flops 6000000 | bytes 18000 | tf_op jit(solution)/shard_map/input_back/pallas_call | solution.py:644
  457.8 12.2 %collective-permute-done.50.refs_3_ = bf16[576,1024]{1,0:T(8,128)(2,1)S(1)} collective-permute-done((bf16[576,1024]{1,0:T(8,128)(2,1)S(1)}, bf16[576,1024]{1,0:T(8,128)(2,1)S(1)}, u32[]{:S(2)}, u32[]{:S(2)}) %collective-permute-start.50) | collective-permute-done | bytes 1179680 | tf_op jit(solution)/shard_map/ppermute | solution.py:810
  472.6 5.2 add_convert_fusion
  477.8 8.7 %collective-permute-done.52.refs_3_ = bf16[416,1024]{1,0:T(8,128)(2,1)S(1)} collective-permute-done((bf16[416,1024]{1,0:T(8,128)(2,1)}, bf16[416,1024]{1,0:T(8,128)(2,1)S(1)}, u32[]{:S(2)}, u32[]{:S(2)}) %collective-permute-start.52) | collective-permute-done | bytes 852000 | tf_op jit(solution)/shard_map/ppermute | solution.py:759
  493.3 14.4 %collective-permute-done.54.refs_1_ = bf16[416,1024]{1,0:T(8,128)(2,1)S(1)} collective-permute-done((bf16[416,1024]{1,0:T(8,128)(2,1)S(1)}, bf16[416,1024]{1,0:T(8,128)(2,1)S(1)}, u32[]{:S(2)}, u32[]{:S(2)}) %collective-permute-start.54) | collective-permute-done | bytes 852000 | tf_op jit(solution)/shard_map/ppermute | solution.py:810
  508.7 19.3 %collective-permute-done.57.refs_5_ = bf16[576,1024]{1,0:T(8,128)(2,1)S(1)} collective-permute-done((bf16[576,1024]{1,0:T(8,128)(2,1)S(1)}, bf16[576,1024]{1,0:T(8,128)(2,1)S(1)}, u32[]{:S(2)}, u32[]{:S(2)}) %collective-permute-start.57) | collective-permute-done | bytes 1179680 | tf_op jit(solution)/shard_map/ppermute | solution.py:810
  532.9 6.0 %unpack_rows.1 = (f32[128,4608]{1,0:T(8,128)}, f32[128,4608]{1,0:T(8,128)}, f32[576,1024]{1,0:T(8,128)}) custom-call(s32[1]{0:T(128)} %bitcast.8.flag_ref, bf16[576,1024]{1,0:T(8,128)(2,1)} %get-tuple-element.326.refs_0_, bf16[576,1024]{1,0:T(8,128)(2,1)} %collective-permute-done.47.refs_1_, bf16[576,1024]{1,0:T(8,128)(2,1)S(1)} %get-tuple-element.358.refs_2_, ...), custom_call_target="tpu_custom_call" | custom-call | bytes 14000 | tf_op jit(solution)/shard_map/unpack_rows/pallas_call | solution.py:736
  538.9 10.8 %collective-permute-done.59 = bf16[416,1024]{1,0:T(8,128)(2,1)} collective-permute-done((bf16[416,1024]{1,0:T(8,128)(2,1)S(1)}, bf16[416,1024]{1,0:T(8,128)(2,1)}, u32[]{:S(2)}, u32[]{:S(2)}) %collective-permute-start.59) | collective-permute-done | bytes 852000 | tf_op jit(solution)/shard_map/ppermute | solution.py:810
  (398 shorter events, 134.1 us)
Async XLA Ops:
  5.7 15.6 %collective-permute-start = (bf16[272,1024]{1,0:T(8,128)(2,1)S(1)}, bf16[272,1024]{1,0:T(8,128)(2,1)S(1)}, u32[]{:S(2)}, u32[]{:S(2)}) collective-permute-start(bf16[272,1024]{1,0:T(8,128)(2,1)S(1)} %concatenate.38.refs_6_.refs_7_.refs_22_.refs_5_), channel_id=1, source_target_pairs={{0,2},{1,3},{2,0},{3,1},{4,6},{5,7},{6,4},{7,5},{8,10},{9,11},{10,... | collective-permute-start | bytes 1671176 | tf_op jit(solution)/shard_map/ppermute | solution.py:759
  8.7 14.1 %collective-permute-start.1 = (bf16[272,1024]{1,0:T(8,128)(2,1)S(1)}, bf16[272,1024]{1,0:T(8,128)(2,1)S(1)}, u32[]{:S(2)}, u32[]{:S(2)}) collective-permute-start(bf16[272,1024]{1,0:T(8,128)(2,1)S(1)} %concatenate.38.refs_6_.refs_7_.refs_22_.refs_5_), channel_id=1, source_target_pairs={{0,4},{1,5},{2,6},{3,7},{4,0},{5,1},{6,2},{7,3},{8,12},{9,13},{10,... | collective-permute-start | bytes 1671176 | tf_op jit(solution)/shard_map/ppermute | solution.py:759
  10.2 12.6 %collective-permute-start.2 = (bf16[272,1024]{1,0:T(8,128)(2,1)S(1)}, bf16[272,1024]{1,0:T(8,128)(2,1)S(1)}, u32[]{:S(2)}, u32[]{:S(2)}) collective-permute-start(bf16[272,1024]{1,0:T(8,128)(2,1)S(1)} %concatenate.38.refs_6_.refs_7_.refs_22_.refs_5_), channel_id=1, source_target_pairs={{0,1},{1,0},{2,3},{3,2},{4,5},{5,4},{6,7},{7,6},{8,9},{9,8},{10,11... | collective-permute-start | bytes 1671176 | tf_op jit(solution)/shard_map/ppermute | solution.py:759
  22.8 10.3 %collective-permute-start.3 = (bf16[272,1024]{1,0:T(8,128)(2,1)S(1)}, bf16[272,1024]{1,0:T(8,128)(2,1)S(1)}, u32[]{:S(2)}, u32[]{:S(2)}) collective-permute-start(bf16[272,1024]{1,0:T(8,128)(2,1)S(1)} %collective-permute-done.refs_10_.refs_11_.refs_24_.refs_9_), channel_id=1, source_target_pairs={{0,1},{1,0},{2,3},{3,2},{4,5},{5,4},{6,7},{7,6},{8,9},{9,8},{10,11... | collective-permute-start | bytes 1671176 | tf_op jit(solution)/shard_map/ppermute | solution.py:759
  22.9 10.2 %collective-permute-start.4 = (bf16[272,1024]{1,0:T(8,128)(2,1)S(1)}, bf16[272,1024]{1,0:T(8,128)(2,1)S(1)}, u32[]{:S(2)}, u32[]{:S(2)}) collective-permute-start(bf16[272,1024]{1,0:T(8,128)(2,1)S(1)} %collective-permute-done.1.refs_14_.refs_15_.refs_26_.refs_13_), channel_id=1, source_target_pairs={{0,1},{1,0},{2,3},{3,2},{4,5},{5,4},{6,7},{7,6},{8,9},{9,8},{10,11... | collective-permute-start | bytes 1671176 | tf_op jit(solution)/shard_map/ppermute | solution.py:759
  33.1 36.6 %collective-permute-start.9 = (bf16[704,1024]{1,0:T(8,128)(2,1)}, bf16[704,1024]{1,0:T(8,128)(2,1)S(1)}, u32[]{:S(2)}, u32[]{:S(2)}) collective-permute-start(bf16[704,1024]{1,0:T(8,128)(2,1)} %get-tuple-element.211.refs_5_.refs_4_.refs_9_), channel_id=1, source_target_pairs={{0,2},{1,3},{2,0},{3,1},{4,6},{5,7},{6,4},{7,5},{8,10},{9,11},{10,... | collective-permute-start | bytes 4325384 | tf_op jit(solution)/shard_map/ppermute | solution.py:759
  33.7 36.0 %collective-permute-start.10 = (bf16[704,1024]{1,0:T(8,128)(2,1)}, bf16[704,1024]{1,0:T(8,128)(2,1)S(1)}, u32[]{:S(2)}, u32[]{:S(2)}) collective-permute-start(bf16[704,1024]{1,0:T(8,128)(2,1)} %get-tuple-element.211.refs_5_.refs_4_.refs_9_), channel_id=1, source_target_pairs={{0,4},{1,5},{2,6},{3,7},{4,0},{5,1},{6,2},{7,3},{8,12},{9,13},{10,... | collective-permute-start | bytes 4325384 | tf_op jit(solution)/shard_map/ppermute | solution.py:759
  34.6 35.2 %collective-permute-start.11 = (bf16[704,1024]{1,0:T(8,128)(2,1)}, bf16[704,1024]{1,0:T(8,128)(2,1)S(1)}, u32[]{:S(2)}, u32[]{:S(2)}) collective-permute-start(bf16[704,1024]{1,0:T(8,128)(2,1)} %get-tuple-element.211.refs_5_.refs_4_.refs_9_), channel_id=1, source_target_pairs={{0,1},{1,0},{2,3},{3,2},{4,5},{5,4},{6,7},{7,6},{8,9},{9,8},{10,11... | collective-permute-start | bytes 4325384 | tf_op jit(solution)/shard_map/ppermute | solution.py:759
  69.8 20.4 %collective-permute-start.14 = (bf16[704,1024]{1,0:T(8,128)(2,1)S(1)}, bf16[704,1024]{1,0:T(8,128)(2,1)S(1)}, u32[]{:S(2)}, u32[]{:S(2)}) collective-permute-start(bf16[704,1024]{1,0:T(8,128)(2,1)S(1)} %collective-permute-done.9.refs_7_.refs_6_.refs_11_), channel_id=1, source_target_pairs={{0,1},{1,0},{2,3},{3,2},{4,5},{5,4},{6,7},{7,6},{8,9},{9,8},{10,11... | collective-permute-start | bytes 4325384 | tf_op jit(solution)/shard_map/ppermute | solution.py:759
  70.2 20.0 %collective-permute-start.15 = (bf16[704,1024]{1,0:T(8,128)(2,1)S(1)}, bf16[704,1024]{1,0:T(8,128)(2,1)S(1)}, u32[]{:S(2)}, u32[]{:S(2)}) collective-permute-start(bf16[704,1024]{1,0:T(8,128)(2,1)S(1)} %collective-permute-done.10.refs_9_.refs_8_.refs_13_), channel_id=1, source_target_pairs={{0,1},{1,0},{2,3},{3,2},{4,5},{5,4},{6,7},{7,6},{8,9},{9,8},{10,11... | collective-permute-start | bytes 4325384 | tf_op jit(solution)/shard_map/ppermute | solution.py:759
  70.5 18.5 %collective-permute-start.12 = (bf16[704,512]{1,0:T(8,128)(2,1)S(1)}, bf16[704,512]{1,0:T(8,128)(2,1)S(1)}, u32[]{:S(2)}, u32[]{:S(2)}) collective-permute-start(bf16[704,512]{1,0:T(8,128)(2,1)S(1)} %slice.65), channel_id=1, source_target_pairs={{0,2},{1,3},{2,0},{3,1},{4,6},{5,7},{6,4},{7,5},{8,10},{9,11},{10,... | collective-permute-start | bytes 2162696 | tf_op jit(solution)/shard_map/ppermute | solution.py:759
  72.1 18.1 %collective-permute-start.13 = (bf16[704,512]{1,0:T(8,128)(2,1)S(1)}, bf16[704,512]{1,0:T(8,128)(2,1)S(1)}, u32[]{:S(2)}, u32[]{:S(2)}) collective-permute-start(bf16[704,512]{1,0:T(8,128)(2,1)S(1)} %slice.66), channel_id=1, source_target_pairs={{0,4},{1,5},{2,6},{3,7},{4,0},{5,1},{6,2},{7,3},{8,12},{9,13},{10,... | collective-permute-start | bytes 2162696 | tf_op jit(solution)/shard_map/ppermute | solution.py:759
  91.3 61.3 %collective-permute-start.18 = (bf16[576,1024]{1,0:T(8,128)(2,1)}, bf16[576,1024]{1,0:T(8,128)(2,1)S(1)}, u32[]{:S(2)}, u32[]{:S(2)}) collective-permute-start(bf16[576,1024]{1,0:T(8,128)(2,1)} %get-tuple-element.234.refs_4_), channel_id=1, source_target_pairs={{0,1},{1,0},{2,3},{3,2},{4,5},{5,4},{6,7},{7,6},{8,9},{9,8},{10,11... | collective-permute-start | bytes 3538952 | tf_op jit(solution)/shard_map/ppermute | solution.py:759
  91.8 60.8 %collective-permute-start.19 = (bf16[576,1024]{1,0:T(8,128)(2,1)}, bf16[576,1024]{1,0:T(8,128)(2,1)}, u32[]{:S(2)}, u32[]{:S(2)}) collective-permute-start(bf16[576,1024]{1,0:T(8,128)(2,1)} %get-tuple-element.234.refs_4_), channel_id=1, source_target_pairs={{0,2},{1,3},{2,0},{3,1},{4,6},{5,7},{6,4},{7,5},{8,10},{9,11},{10,... | collective-permute-start | bytes 3538952 | tf_op jit(solution)/shard_map/ppermute | solution.py:759
  92.4 60.3 %collective-permute-start.20 = (bf16[576,1024]{1,0:T(8,128)(2,1)}, bf16[576,1024]{1,0:T(8,128)(2,1)}, u32[]{:S(2)}, u32[]{:S(2)}) collective-permute-start(bf16[576,1024]{1,0:T(8,128)(2,1)} %get-tuple-element.234.refs_4_), channel_id=1, source_target_pairs={{0,4},{1,5},{2,6},{3,7},{4,0},{5,1},{6,2},{7,3},{8,12},{9,13},{10,... | collective-permute-start | bytes 3538952 | tf_op jit(solution)/shard_map/ppermute | solution.py:759
  93.5 59.1 %collective-permute-start.21 = (bf16[576,1024]{1,0:T(8,128)(2,1)}, bf16[576,1024]{1,0:T(8,128)(2,1)}, u32[]{:S(2)}, u32[]{:S(2)}) collective-permute-start(bf16[576,1024]{1,0:T(8,128)(2,1)} %get-tuple-element.234.refs_4_), channel_id=1, source_target_pairs={{0,6},{1,7},{2,4},{3,5},{4,2},{5,3},{6,0},{7,1},{8,14},{9,15},{10,... | collective-permute-start | bytes 3538952 | tf_op jit(solution)/shard_map/ppermute | solution.py:759
  159.2 44.6 %collective-permute-start.25 = (bf16[4,576,1024]{2,1,0:T(8,128)(2,1)}, bf16[4,576,1024]{2,1,0:T(8,128)(2,1)}, u32[]{:S(2)}, u32[]{:S(2)}) collective-permute-start(bf16[4,576,1024]{2,1,0:T(8,128)(2,1)} %get-tuple-element.246), channel_id=1, source_target_pairs={{0,1},{1,0},{2,3},{3,2},{4,5},{5,4},{6,7},{7,6},{8,9},{9,8},{10,11... | collective-permute-start | bytes 14155784 | tf_op jit(solution)/shard_map/ppermute | solution.py:759
  159.3 44.4 %collective-permute-start.26 = (bf16[576,1024]{1,0:T(8,128)(2,1)S(1)}, bf16[576,1024]{1,0:T(8,128)(2,1)S(1)}, u32[]{:S(2)}, u32[]{:S(2)}) collective-permute-start(bf16[576,1024]{1,0:T(8,128)(2,1)S(1)} %copy-done.82), channel_id=1, source_target_pairs={{0,1},{1,0},{2,3},{3,2},{4,5},{5,4},{6,7},{7,6},{8,9},{9,8},{10,11... | collective-permute-start | bytes 3538952 | tf_op jit(solution)/shard_map/ppermute | solution.py:759
  159.7 44.1 %collective-permute-start.27 = (bf16[576,1024]{1,0:T(8,128)(2,1)S(1)}, bf16[576,1024]{1,0:T(8,128)(2,1)}, u32[]{:S(2)}, u32[]{:S(2)}) collective-permute-start(bf16[576,1024]{1,0:T(8,128)(2,1)S(1)} %copy-done.82), channel_id=1, source_target_pairs={{0,2},{1,3},{2,0},{3,1},{4,6},{5,7},{6,4},{7,5},{8,10},{9,11},{10,... | collective-permute-start | bytes 3538952 | tf_op jit(solution)/shard_map/ppermute | solution.py:759
  160.2 43.6 %collective-permute-start.28 = (bf16[576,1024]{1,0:T(8,128)(2,1)S(1)}, bf16[576,1024]{1,0:T(8,128)(2,1)}, u32[]{:S(2)}, u32[]{:S(2)}) collective-permute-start(bf16[576,1024]{1,0:T(8,128)(2,1)S(1)} %copy-done.82), channel_id=1, source_target_pairs={{0,4},{1,5},{2,6},{3,7},{4,0},{5,1},{6,2},{7,3},{8,12},{9,13},{10,... | collective-permute-start | bytes 3538952 | tf_op jit(solution)/shard_map/ppermute | solution.py:759
  161.4 52.3 %collective-permute-start.31 = (bf16[576,1024]{1,0:T(8,128)(2,1)S(1)}, bf16[576,1024]{1,0:T(8,128)(2,1)}, u32[]{:S(2)}, u32[]{:S(2)}) collective-permute-start(bf16[576,1024]{1,0:T(8,128)(2,1)S(1)} %copy-done.82), channel_id=1, source_target_pairs={{0,6},{1,7},{2,4},{3,5},{4,2},{5,3},{6,0},{7,1},{8,14},{9,15},{10,... | collective-permute-start | bytes 3538952 | tf_op jit(solution)/shard_map/ppermute | solution.py:759
  203.8 9.9 %collective-permute-start.29 = (bf16[576,1024]{1,0:T(8,128)(2,1)}, bf16[576,1024]{1,0:T(8,128)(2,1)S(1)}, u32[]{:S(2)}, u32[]{:S(2)}) collective-permute-start(bf16[576,1024]{1,0:T(8,128)(2,1)} %collective-permute-done.27.refs_6_), channel_id=1, source_target_pairs={{0,1},{1,0},{2,3},{3,2},{4,5},{5,4},{6,7},{7,6},{8,9},{9,8},{10,11... | collective-permute-start | bytes 3538952 | tf_op jit(solution)/shard_map/ppermute | solution.py:759
  203.9 9.8 %collective-permute-start.30 = (bf16[576,1024]{1,0:T(8,128)(2,1)}, bf16[576,1024]{1,0:T(8,128)(2,1)S(1)}, u32[]{:S(2)}, u32[]{:S(2)}) collective-permute-start(bf16[576,1024]{1,0:T(8,128)(2,1)} %collective-permute-done.28.refs_8_), channel_id=1, source_target_pairs={{0,1},{1,0},{2,3},{3,2},{4,5},{5,4},{6,7},{7,6},{8,9},{9,8},{10,11... | collective-permute-start | bytes 3538952 | tf_op jit(solution)/shard_map/ppermute | solution.py:759
  216.7 61.4 %collective-permute-start.33 = (bf16[4,576,1024]{2,1,0:T(8,128)(2,1)}, bf16[4,576,1024]{2,1,0:T(8,128)(2,1)}, u32[]{:S(2)}, u32[]{:S(2)}) collective-permute-start(bf16[4,576,1024]{2,1,0:T(8,128)(2,1)} %get-tuple-element.264), channel_id=1, source_target_pairs={{0,1},{1,0},{2,3},{3,2},{4,5},{5,4},{6,7},{7,6},{8,9},{9,8},{10,11... | collective-permute-start | bytes 14155784 | tf_op jit(solution)/shard_map/ppermute | solution.py:759
  216.9 50.0 %collective-permute-start.34 = (bf16[576,1024]{1,0:T(8,128)(2,1)}, bf16[576,1024]{1,0:T(8,128)(2,1)S(1)}, u32[]{:S(2)}, u32[]{:S(2)}) collective-permute-start(bf16[576,1024]{1,0:T(8,128)(2,1)} %get-tuple-element.265), channel_id=1, source_target_pairs={{0,2},{1,3},{2,0},{3,1},{4,6},{5,7},{6,4},{7,5},{8,10},{9,11},{10,... | collective-permute-start | bytes 3538952 | tf_op jit(solution)/shard_map/ppermute | solution.py:759
  224.6 53.4 %collective-permute-start.35 = (bf16[576,1024]{1,0:T(8,128)(2,1)}, bf16[576,1024]{1,0:T(8,128)(2,1)S(1)}, u32[]{:S(2)}, u32[]{:S(2)}) collective-permute-start(bf16[576,1024]{1,0:T(8,128)(2,1)} %get-tuple-element.266), channel_id=1, source_target_pairs={{0,4},{1,5},{2,6},{3,7},{4,0},{5,1},{6,2},{7,3},{8,12},{9,13},{10,... | collective-permute-start | bytes 3538952 | tf_op jit(solution)/shard_map/ppermute | solution.py:759
  225.8 52.3 %collective-permute-start.36 = (bf16[576,1024]{1,0:T(8,128)(2,1)}, bf16[576,1024]{1,0:T(8,128)(2,1)}, u32[]{:S(2)}, u32[]{:S(2)}) collective-permute-start(bf16[576,1024]{1,0:T(8,128)(2,1)} %get-tuple-element.267), channel_id=1, source_target_pairs={{0,6},{1,7},{2,4},{3,5},{4,2},{5,3},{6,0},{7,1},{8,14},{9,15},{10,... | collective-permute-start | bytes 3538952 | tf_op jit(solution)/shard_map/ppermute | solution.py:759
  278.1 47.0 %collective-permute-start.37 = (bf16[4,576,1024]{2,1,0:T(8,128)(2,1)}, bf16[4,576,1024]{2,1,0:T(8,128)(2,1)S(1)}, u32[]{:S(2)}, u32[]{:S(2)}) collective-permute-start(bf16[4,576,1024]{2,1,0:T(8,128)(2,1)} %get-tuple-element.280), channel_id=1, source_target_pairs={{0,1},{1,0},{2,3},{3,2},{4,5},{5,4},{6,7},{7,6},{8,9},{9,8},{10,11... | collective-permute-start | bytes 14155784 | tf_op jit(solution)/shard_map/ppermute | solution.py:759
  286.2 70.2 %collective-permute-start.38 = (bf16[576,1024]{1,0:T(8,128)(2,1)}, bf16[576,1024]{1,0:T(8,128)(2,1)}, u32[]{:S(2)}, u32[]{:S(2)}) collective-permute-start(bf16[576,1024]{1,0:T(8,128)(2,1)} %get-tuple-element.287), channel_id=1, source_target_pairs={{0,4},{1,5},{2,6},{3,7},{4,0},{5,1},{6,2},{7,3},{8,12},{9,13},{10,... | collective-permute-start | bytes 3538952 | tf_op jit(solution)/shard_map/ppermute | solution.py:759
  287.4 69.0 %collective-permute-start.40 = (bf16[576,1024]{1,0:T(8,128)(2,1)}, bf16[576,1024]{1,0:T(8,128)(2,1)}, u32[]{:S(2)}, u32[]{:S(2)}) collective-permute-start(bf16[576,1024]{1,0:T(8,128)(2,1)} %get-tuple-element.289.refs_10_), channel_id=1, source_target_pairs={{0,8},{24,16},{1,9},{25,17},{2,10},{26,18},{3,11},{27,19},{4,12},{... | collective-permute-start | bytes 3538952 | tf_op jit(solution)/shard_map/ppermute | solution.py:810
  330.1 27.9 %collective-permute-start.39 = (bf16[576,1024]{1,0:T(8,128)(2,1)S(1)}, bf16[576,1024]{1,0:T(8,128)(2,1)S(1)}, u32[]{:S(2)}, u32[]{:S(2)}) collective-permute-start(bf16[576,1024]{1,0:T(8,128)(2,1)S(1)} %combine.14), channel_id=1, source_target_pairs={{0,2},{1,3},{2,0},{3,1},{4,6},{5,7},{6,4},{7,5},{8,10},{9,11},{10,... | collective-permute-start | bytes 3538952 | tf_op jit(solution)/shard_map/ppermute | solution.py:759
  366.0 30.1 %collective-permute-start.41 = (bf16[576,1024]{1,0:T(8,128)(2,1)}, bf16[576,1024]{1,0:T(8,128)(2,1)S(1)}, u32[]{:S(2)}, u32[]{:S(2)}) collective-permute-start(bf16[576,1024]{1,0:T(8,128)(2,1)} %get-tuple-element.304), channel_id=1, source_target_pairs={{0,2},{1,3},{2,0},{3,1},{4,6},{5,7},{6,4},{7,5},{8,10},{9,11},{10,... | collective-permute-start | bytes 3538952 | tf_op jit(solution)/shard_map/ppermute | solution.py:759
  366.7 29.4 %collective-permute-start.42 = (bf16[576,1024]{1,0:T(8,128)(2,1)}, bf16[576,1024]{1,0:T(8,128)(2,1)S(1)}, u32[]{:S(2)}, u32[]{:S(2)}) collective-permute-start(bf16[576,1024]{1,0:T(8,128)(2,1)} %get-tuple-element.305), channel_id=1, source_target_pairs={{0,4},{1,5},{2,6},{3,7},{4,0},{5,1},{6,2},{7,3},{8,12},{9,13},{10,... | collective-permute-start | bytes 3538952 | tf_op jit(solution)/shard_map/ppermute | solution.py:759
  367.8 29.3 %collective-permute-start.43 = (bf16[576,1024]{1,0:T(8,128)(2,1)}, bf16[576,1024]{1,0:T(8,128)(2,1)}, u32[]{:S(2)}, u32[]{:S(2)}) collective-permute-start(bf16[576,1024]{1,0:T(8,128)(2,1)} %get-tuple-element.306.refs_4_), channel_id=1, source_target_pairs={{8,16},{16,8},{9,17},{17,9},{10,18},{18,10},{11,19},{19,11},{12,20... | collective-permute-start | bytes 3538952 | tf_op jit(solution)/shard_map/ppermute | solution.py:810
  369.5 60.6 %collective-permute-start.44 = (bf16[576,1024]{1,0:T(8,128)(2,1)}, bf16[576,1024]{1,0:T(8,128)(2,1)}, u32[]{:S(2)}, u32[]{:S(2)}) collective-permute-start(bf16[576,1024]{1,0:T(8,128)(2,1)} %get-tuple-element.323), channel_id=1, source_target_pairs={{0,2},{1,3},{2,0},{3,1},{4,6},{5,7},{6,4},{7,5},{8,10},{9,11},{10,... | collective-permute-start | bytes 3538952 | tf_op jit(solution)/shard_map/ppermute | solution.py:759
  370.6 59.6 %collective-permute-start.45 = (bf16[576,1024]{1,0:T(8,128)(2,1)}, bf16[576,1024]{1,0:T(8,128)(2,1)}, u32[]{:S(2)}, u32[]{:S(2)}) collective-permute-start(bf16[576,1024]{1,0:T(8,128)(2,1)} %get-tuple-element.324), channel_id=1, source_target_pairs={{0,4},{1,5},{2,6},{3,7},{4,0},{5,1},{6,2},{7,3},{8,12},{9,13},{10,... | collective-permute-start | bytes 3538952 | tf_op jit(solution)/shard_map/ppermute | solution.py:759
  401.8 28.3 %collective-permute-start.46 = (bf16[576,1024]{1,0:T(8,128)(2,1)}, bf16[576,1024]{1,0:T(8,128)(2,1)}, u32[]{:S(2)}, u32[]{:S(2)}) collective-permute-start(bf16[576,1024]{1,0:T(8,128)(2,1)} %get-tuple-element.325.refs_0_), channel_id=1, source_target_pairs={{0,8},{24,16},{1,9},{25,17},{2,10},{26,18},{3,11},{27,19},{4,12},{... | collective-permute-start | bytes 3538952 | tf_op jit(solution)/shard_map/ppermute | solution.py:810
  405.3 27.8 %collective-permute-start.47 = (bf16[576,1024]{1,0:T(8,128)(2,1)}, bf16[576,1024]{1,0:T(8,128)(2,1)}, u32[]{:S(2)}, u32[]{:S(2)}) collective-permute-start(bf16[576,1024]{1,0:T(8,128)(2,1)} %get-tuple-element.326.refs_0_), channel_id=1, source_target_pairs={{8,0},{16,24},{9,1},{17,25},{10,2},{18,26},{11,3},{19,27},{12,4},{... | collective-permute-start | bytes 3538952 | tf_op jit(solution)/shard_map/ppermute | solution.py:810
  439.5 18.3 %collective-permute-start.49 = (bf16[576,1024]{1,0:T(8,128)(2,1)S(1)}, bf16[576,1024]{1,0:T(8,128)(2,1)S(1)}, u32[]{:S(2)}, u32[]{:S(2)}) collective-permute-start(bf16[576,1024]{1,0:T(8,128)(2,1)S(1)} %get-tuple-element.334.refs_0_), channel_id=1, source_target_pairs={{8,16},{16,8},{9,17},{17,9},{10,18},{18,10},{11,19},{19,11},{12,20... | collective-permute-start | bytes 3538952 | tf_op jit(solution)/shard_map/ppermute | solution.py:810
  440.3 29.7 %collective-permute-start.50 = (bf16[576,1024]{1,0:T(8,128)(2,1)S(1)}, bf16[576,1024]{1,0:T(8,128)(2,1)S(1)}, u32[]{:S(2)}, u32[]{:S(2)}) collective-permute-start(bf16[576,1024]{1,0:T(8,128)(2,1)S(1)} %get-tuple-element.343.refs_2_), channel_id=1, source_target_pairs={{0,8},{24,16},{1,9},{25,17},{2,10},{26,18},{3,11},{27,19},{4,12},{... | collective-permute-start | bytes 3538952 | tf_op jit(solution)/shard_map/ppermute | solution.py:810
  446.8 31.0 %collective-permute-start.51 = (bf16[416,1024]{1,0:T(8,128)(2,1)}, bf16[416,1024]{1,0:T(8,128)(2,1)S(1)}, u32[]{:S(2)}, u32[]{:S(2)}) collective-permute-start(bf16[416,1024]{1,0:T(8,128)(2,1)} %get-tuple-element.352), channel_id=1, source_target_pairs={{0,2},{1,3},{2,0},{3,1},{4,6},{5,7},{6,4},{7,5},{8,10},{9,11},{10,... | collective-permute-start | bytes 2555912 | tf_op jit(solution)/shard_map/ppermute | solution.py:759
  447.9 38.6 %collective-permute-start.52 = (bf16[416,1024]{1,0:T(8,128)(2,1)}, bf16[416,1024]{1,0:T(8,128)(2,1)S(1)}, u32[]{:S(2)}, u32[]{:S(2)}) collective-permute-start(bf16[416,1024]{1,0:T(8,128)(2,1)} %get-tuple-element.353), channel_id=1, source_target_pairs={{0,4},{1,5},{2,6},{3,7},{4,0},{5,1},{6,2},{7,3},{8,12},{9,13},{10,... | collective-permute-start | bytes 2555912 | tf_op jit(solution)/shard_map/ppermute | solution.py:759
  448.7 38.7 %collective-permute-start.53 = (bf16[416,1024]{1,0:T(8,128)(2,1)}, bf16[416,1024]{1,0:T(8,128)(2,1)}, u32[]{:S(2)}, u32[]{:S(2)}) collective-permute-start(bf16[416,1024]{1,0:T(8,128)(2,1)} %get-tuple-element.354), channel_id=1, source_target_pairs={{0,6},{1,7},{2,4},{3,5},{4,2},{5,3},{6,0},{7,1},{8,14},{9,15},{10,... | collective-permute-start | bytes 2555912 | tf_op jit(solution)/shard_map/ppermute | solution.py:759
  470.6 21.1 %collective-permute-start.56 = (bf16[576,1024]{1,0:T(8,128)(2,1)S(1)}, bf16[576,1024]{1,0:T(8,128)(2,1)S(1)}, u32[]{:S(2)}, u32[]{:S(2)}) collective-permute-start(bf16[576,1024]{1,0:T(8,128)(2,1)S(1)} %get-tuple-element.362.refs_0_), channel_id=1, source_target_pairs={{8,16},{16,8},{9,17},{17,9},{10,18},{18,10},{11,19},{19,11},{12,20... | collective-permute-start | bytes 3538952 | tf_op jit(solution)/shard_map/ppermute | solution.py:810
  471.3 36.4 %collective-permute-start.55 = (bf16[576,1024]{1,0:T(8,128)(2,1)S(1)}, bf16[576,1024]{1,0:T(8,128)(2,1)S(1)}, u32[]{:S(2)}, u32[]{:S(2)}) collective-permute-start(bf16[576,1024]{1,0:T(8,128)(2,1)S(1)} %get-tuple-element.358.refs_2_), channel_id=1, source_target_pairs={{8,0},{16,24},{9,1},{17,25},{10,2},{18,26},{11,3},{19,27},{12,4},{... | collective-permute-start | bytes 3538952 | tf_op jit(solution)/shard_map/ppermute | solution.py:810
  490.1 17.6 %collective-permute-start.54 = (bf16[416,1024]{1,0:T(8,128)(2,1)S(1)}, bf16[416,1024]{1,0:T(8,128)(2,1)S(1)}, u32[]{:S(2)}, u32[]{:S(2)}) collective-permute-start(bf16[416,1024]{1,0:T(8,128)(2,1)S(1)} %combine.20.refs_0_), channel_id=1, source_target_pairs={{0,8},{24,16},{1,9},{25,17},{2,10},{26,18},{3,11},{27,19},{4,12},{... | collective-permute-start | bytes 2555912 | tf_op jit(solution)/shard_map/ppermute | solution.py:810
  492.0 36.0 %collective-permute-start.57 = (bf16[576,1024]{1,0:T(8,128)(2,1)S(1)}, bf16[576,1024]{1,0:T(8,128)(2,1)S(1)}, u32[]{:S(2)}, u32[]{:S(2)}) collective-permute-start(bf16[576,1024]{1,0:T(8,128)(2,1)S(1)} %combine.21.refs_4_), channel_id=1, source_target_pairs={{8,0},{16,24},{9,1},{17,25},{10,2},{18,26},{11,3},{19,27},{12,4},{... | collective-permute-start | bytes 3538952 | tf_op jit(solution)/shard_map/ppermute | solution.py:810
  529.0 20.6 %collective-permute-start.59 = (bf16[416,1024]{1,0:T(8,128)(2,1)S(1)}, bf16[416,1024]{1,0:T(8,128)(2,1)}, u32[]{:S(2)}, u32[]{:S(2)}) collective-permute-start(bf16[416,1024]{1,0:T(8,128)(2,1)S(1)} %combine.23), channel_id=1, source_target_pairs={{8,0},{16,24},{9,1},{17,25},{10,2},{18,26},{11,3},{19,27},{12,4},{... | collective-permute-start | bytes 2555912 | tf_op jit(solution)/shard_map/ppermute | solution.py:810
  (137 other events, 1059.5 us)
